TPU v7x, 32 devices: a whole 2x2x4 slice. The times are simulated.
32 devices in a mesh: dp: 4 (over y, x), row: 2 (over core), col: 4 (over z).
Axes of the slice: x: 2, y: 2, z: 4, core: 2. Of those that a mesh axis runs over, the one named last changes fastest.
Arguments:
- gradients: bfloat16 [4, 8192, 14336], P('dp', 'row', 'col'), may hold values from -6 to 6
- test_matrix: int32 [14336, 512], P('col'), may hold values from -3 to 3
- old_basis: float32 [8192, 512], P('row'), may hold values from -0.0625 to 0.0625
- first_moment: float32 [512, 14336], P(('dp', 'row'), 'col'), may hold values from -24 to 24
- second_moment: float32 [512, 14336], P(('dp', 'row'), 'col'), may hold values from 1 to 16
Outputs:
- projected: float32 [512, 14336], P(('dp', 'row'), 'col')
- first_moment_new: float32 [512, 14336], P(('dp', 'row'), 'col')
- second_moment_new: float32 [512, 14336], P(('dp', 'row'), 'col')
All inputs are finite; a program needn't handle non-finite values.
Results may differ from a plain program's by a relative error of at most 0.0023.
Values sent between devices are 32-bit elements; how exact they have to be, the bound alone decides.
No kernel may reach another device: no remote copies, remote signals or barrier semaphores. Data moves between devices by JAX's collectives and lax.ppermute only.
A program may use at most 128 MiB of HBM per device.

v0:
```python
import jax
import jax.numpy as jnp
from jax import lax
from jax.sharding import PartitionSpec as P

highest = lax.Precision.HIGHEST


def from_partner(value, axis, bit):
    return lax.ppermute(value, axis, [(i, i ^ 1 << bit) for i in range(lax.axis_size(axis))])


def gram_of(row_block):
    return lax.dot_general(
        row_block,
        row_block,
        (((0,), (0,)), ((), ())),
        precision=highest,
        preferred_element_type=jnp.float32,
    )


def basis_from(lower_factor, sketch_part):
    return jax.scipy.linalg.solve_triangular(lower_factor, sketch_part.T, lower=True).T


def local(gradients, test_matrix, old_basis, first_moment, second_moment):
    replica_grad = gradients[0]
    test_values = test_matrix.astype(jnp.bfloat16)
    partial_value = jnp.dot(replica_grad, test_values, preferred_element_type=jnp.float32)
    sketch = lax.psum(partial_value, ("dp", "col"))
    upper_factor = jnp.linalg.cholesky(gram_of(sketch)).T
    for bit_level in range(lax.axis_size("row").bit_length() - 1):
        partner = from_partner(upper_factor, "row", bit_level)
        upper_factor = jnp.linalg.cholesky(gram_of(upper_factor) + gram_of(partner)).T
    new_basis = basis_from(upper_factor.T, sketch)
    basis_low = new_basis.astype(jnp.bfloat16)
    local_correlation = lax.dot_general(
        new_basis,
        old_basis,
        (((0,), (0,)), ((), ())),
        precision=highest,
        preferred_element_type=jnp.float32,
    )
    correlation = lax.psum(local_correlation, "row")
    rank_dev = first_moment.shape[0]
    rank_start = lax.axis_index(("dp", "row")) * rank_dev
    projected = lax.psum_scatter(
        lax.dot_general(
            basis_low, replica_grad, (((0,), (0,)), ((), ())), preferred_element_type=jnp.float32
        ),
        ("dp", "row"),
        scatter_dimension=0,
        tiled=True,
    )
    own_rows = lax.dynamic_slice_in_dim(correlation, rank_start, rank_dev, 0)
    squared = own_rows * own_rows
    turned_first = jnp.dot(
        own_rows,
        lax.all_gather(first_moment, ("dp", "row"), axis=0, tiled=True),
        precision=highest,
        preferred_element_type=jnp.float32,
    )
    turned_second = jnp.dot(
        squared,
        lax.all_gather(second_moment, ("dp", "row"), axis=0, tiled=True),
        precision=highest,
        preferred_element_type=jnp.float32,
    )
    first_new = 0.9 * turned_first + 0.1 * projected
    second_new = 0.95 * turned_second + 0.05 * projected * projected
    return (projected, first_new, second_new)


def solution(mesh):
    in_specs = (
        P("dp", "row", "col"),
        P("col", None),
        P("row", None),
        P(("dp", "row"), "col"),
        P(("dp", "row"), "col"),
    )
    out_specs = (P(("dp", "row"), "col"), P(("dp", "row"), "col"), P(("dp", "row"), "col"))
    return jax.shard_map(local, mesh=mesh, in_specs=in_specs, out_specs=out_specs, check_vma=False)
```

profile of v0, /device:TPU:0, one launch (start us, length us, event | category | flops | bytes accessed | tf_op | source)
XLA Modules:
  0.0 776.1 jit_solution(16835528493540167930)
XLA Ops:
  8.0 23.3 %fusion.2 = f32[4096,512]{1,0:T(8,128)} fusion(bf16[1,4096,3584]{2,1,0:T(8,128)(2,1)} %param.6, s32[3584,512]{1,0:T(8,128)} %param.7), kind=kOutput, calls=%fused_computation.4 | convolution fusion | flops 15034220544 | bytes 45088768 | tf_op jit(solution)/shard_map/dot_general | solution.py:30
  31.4 259.1 %all-reduce.4.cloned.1.call-done = f32[4096,512]{1,0:T(8,128)} async-done(((f32[4096,512]{1,0:T(8,128)}), f32[4096,512]{1,0:T(8,128)}) %all-reduce.4.cloned.1.call-update) | async-done | bytes 8388624 | tf_op jit(solution)/shard_map/psum | solution.py:31
  290.5 17.6 %fusion.84 = f32[512,512]{1,0:T(8,128)S(1)} fusion(f32[4096,512]{1,0:T(8,128)} %all-reduce.4.cloned.1.call-done), kind=kOutput, calls=%fused_computation.136 | convolution fusion | flops 12884901888 | bytes 9437184 | tf_op jit(solution)/shard_map/dot_general | solution.py:14
  308.1 0.3 copy.8
  308.7 11.7 %cholesky.286 = f32[128,128]{1,0:T(8,128)S(1)} custom-call(f32[128,128]{1,0:T(8,128)S(1)} %cholesky.426), custom_call_target="Cholesky" | custom-call | tf_op jit(solution)/shard_map/jit(cholesky)/cholesky | solution.py:32
  320.5 9.8 %custom-call.28 = f32[1,128,128]{1,2,0:T(8,128)S(1)} custom-call(f32[1,128,128]{2,1,0:T(8,128)S(1)} %get-tuple-element.41), custom_call_target="InvertDiagBlocksLowerTriangular" | custom-call | tf_op jit(solution)/shard_map/jit(cholesky)/cholesky | solution.py:32
  330.4 0.3 constant_dynamic-update-slice_fusion.5
  330.7 0.3 convolution_subtract_fusion.2
  331.1 11.7 %cholesky.305 = f32[128,128]{1,0:T(8,128)S(1)} custom-call(f32[128,128]{1,0:T(8,128)S(1)} %cholesky.430), custom_call_target="Cholesky" | custom-call | tf_op jit(solution)/shard_map/jit(cholesky)/cholesky | solution.py:32
  342.8 10.2 %custom-call.29 = f32[1,128,128]{1,2,0:T(8,128)S(1)} custom-call(f32[1,128,128]{2,1,0:T(8,128)S(1)} %get-tuple-element.38), custom_call_target="InvertDiagBlocksLowerTriangular" | custom-call | tf_op jit(solution)/shard_map/jit(cholesky)/cholesky | solution.py:32
  353.3 0.4 convolution_subtract_fusion.3
  353.7 11.7 %cholesky.326 = f32[128,128]{1,0:T(8,128)S(1)} custom-call(f32[128,128]{1,0:T(8,128)S(1)} %cholesky.435), custom_call_target="Cholesky" | custom-call | tf_op jit(solution)/shard_map/jit(cholesky)/cholesky | solution.py:32
  365.4 0.6 compare_reduce_fusion.5
  366.1 9.8 %custom-call.30 = f32[1,128,128]{1,2,0:T(8,128)S(1)} custom-call(f32[1,128,128]{2,1,0:T(8,128)S(1)} %get-tuple-element.35), custom_call_target="InvertDiagBlocksLowerTriangular" | custom-call | tf_op jit(solution)/shard_map/jit(cholesky)/cholesky | solution.py:32
  376.1 0.4 convolution_subtract_fusion.4
  376.5 11.7 %cholesky.343 = f32[128,128]{1,0:T(8,128)S(1)} custom-call(f32[128,128]{1,0:T(8,128)S(1)} %convolution_subtract_fusion.4), custom_call_target="Cholesky" | custom-call | tf_op jit(solution)/shard_map/jit(cholesky)/cholesky | solution.py:32
  388.2 0.6 compare_reduce_fusion.4
  388.9 0.6 compare_reduce_fusion.6
  392.4 1.9 fusion.27
  394.3 0.7 collective-permute-done
  395.0 1.9 convolution_add_fusion
  396.9 0.3 copy.11
  397.5 11.7 %cholesky.358 = f32[128,128]{1,0:T(8,128)S(1)} custom-call(f32[128,128]{1,0:T(8,128)S(1)} %cholesky.439), custom_call_target="Cholesky" | custom-call | tf_op jit(solution)/shard_map/jit(cholesky)/cholesky | solution.py:35
  409.4 9.8 %custom-call.31 = f32[1,128,128]{1,2,0:T(8,128)S(1)} custom-call(f32[1,128,128]{2,1,0:T(8,128)S(1)} %get-tuple-element.31), custom_call_target="InvertDiagBlocksLowerTriangular" | custom-call | tf_op jit(solution)/shard_map/jit(cholesky)/cholesky | solution.py:35
  419.2 0.3 constant_dynamic-update-slice_fusion.3
  419.5 0.3 slice_subtract_fusion
  419.9 12.1 %cholesky.377 = f32[128,128]{1,0:T(8,128)S(1)} custom-call(f32[128,128]{1,0:T(8,128)S(1)} %cholesky.443), custom_call_target="Cholesky" | custom-call | tf_op jit(solution)/shard_map/jit(cholesky)/cholesky | solution.py:35
  432.0 0.6 compare_reduce_fusion.2
  432.6 0.6 compare_reduce_fusion.3
  433.3 9.8 %custom-call.32 = f32[1,128,128]{1,2,0:T(8,128)S(1)} custom-call(f32[1,128,128]{2,1,0:T(8,128)S(1)} %get-tuple-element.28), custom_call_target="InvertDiagBlocksLowerTriangular" | custom-call | tf_op jit(solution)/shard_map/jit(cholesky)/cholesky | solution.py:35
  443.3 0.4 slice_subtract_fusion.1
  443.7 11.7 %cholesky.398 = f32[128,128]{1,0:T(8,128)S(1)} custom-call(f32[128,128]{1,0:T(8,128)S(1)} %cholesky.448), custom_call_target="Cholesky" | custom-call | tf_op jit(solution)/shard_map/jit(cholesky)/cholesky | solution.py:35
  455.5 0.7 compare_reduce_fusion.1
  456.1 9.8 %custom-call.33 = f32[1,128,128]{1,2,0:T(8,128)S(1)} custom-call(f32[1,128,128]{2,1,0:T(8,128)S(1)} %get-tuple-element.25), custom_call_target="InvertDiagBlocksLowerTriangular" | custom-call | tf_op jit(solution)/shard_map/jit(cholesky)/cholesky | solution.py:35
  466.2 0.6 slice_subtract_fusion.2
  466.7 11.7 %cholesky.415 = f32[128,128]{1,0:T(8,128)S(1)} custom-call(f32[128,128]{1,0:T(8,128)S(1)} %slice_subtract_fusion.2), custom_call_target="Cholesky" | custom-call | tf_op jit(solution)/shard_map/jit(cholesky)/cholesky | solution.py:35
  478.5 0.6 compare_reduce_fusion
  481.7 10.2 %while.1 = (s32[]{:T(128)}, f32[512,512]{1,0:T(8,128)S(1)}, s32[4,2]{0,1:T(2,128)S(1)}, f32[4,128,128]{2,1,0:T(8,128)}, s32[]{:T(128)}) while((s32[]{:T(128)}, f32[512,512]{1,0:T(8,128)S(1)}, s32[4,2]{0,1:T(2,128)S(1)}, f32[4,128,128]{2,1,0:T(8,128)}, s32[]{:T(128)}) %tuple.39), condition=%wide.while_cond, body=%wide.while_body.sunk | while | flops 2 | bytes 132705 | solution.py:24
  481.8 0.5 fusion.99
  482.3 1.9 bitcast_dynamic-update-slice_fusion.2
  484.3 0.5 fusion.99
  484.8 1.9 bitcast_dynamic-update-slice_fusion.2
  486.8 0.5 fusion.99
  487.4 1.9 bitcast_dynamic-update-slice_fusion.2
  489.4 0.5 fusion.99
  489.9 1.9 bitcast_dynamic-update-slice_fusion.2
  491.8 40.1 %custom-call.24 = f32[4,128,128]{1,2,0:T(8,128)S(1)} custom-call(f32[4,128,128]{2,1,0:T(8,128)} %get-tuple-element.11), custom_call_target="InvertDiagBlocksLowerTriangular" | custom-call | tf_op jit(solution)/shard_map/jit(_solve_triangular)/triangular_solve | solution.py:24
  532.0 3.5 fusion.22
  535.5 5.1 convolution_subtract_fusion.1
  540.6 2.0 fusion.53
  542.6 9.9 %convolution_subtract_fusion = f32[128,4096]{0,1:T(8,128)S(1)} fusion(f32[128,4096]{1,0:T(8,128)S(1)} %fusion.53, f32[128,4096]{1,0:T(8,128)S(1)} %fusion.22, f32[512,4096]{0,1:T(8,128)} %bitcast.87, f32[512,512]{1,0:T(8,128)S(1)} %get-tuple-element.106), kind=kOutput, calls=%fused_computation.13 | convolution fusion | flops 1612185600 | bytes 8519680 | tf_op jit(solution)/shard_map/jit(_solve_triangular)/triangular_solve | solution.py:24
  552.5 2.0 fusion.51
  554.6 13.3 %fusion.12 = f32[128,4096]{0,1:T(8,128)S(1)} fusion(f32[128,4096]{1,0:T(8,128)S(1)} %fusion.51, f32[128,4096]{1,0:T(8,128)S(1)} %fusion.53, f32[128,4096]{1,0:T(8,128)S(1)} %fusion.22, f32[512,4096]{0,1:T(8,128)} %bitcast.88, f32[512,512]{1,0:T(8,128)S(1)} %get-tuple-element.106), kind=kOutput, calls=%fused_computation.17 | convolution fusion | flops 2419589120 | bytes 10682368 | tf_op jit(solution)/shard_map/jit(_solve_triangular)/triangular_solve | solution.py:24
  567.8 2.0 fusion.50
  569.8 1.3 copy-done.3
  571.1 15.1 %fusion.10 = f32[512,512]{1,0:T(8,128)} fusion(f32[4096,512]{1,0:T(8,128)S(1)} %bitcast.90, f32[128,4096]{1,0:T(8,128)S(1)} %fusion.50, f32[128,4096]{1,0:T(8,128)S(1)} %fusion.51, f32[128,4096]{1,0:T(8,128)S(1)} %fusion.53, f32[128,4096]{1,0:T(8,128)S(1)} %fusion.22), kind=kOutput, calls=%fused_computation.15 | convolution fusion | flops 12891193344 | bytes 17825792 | tf_op jit(solution)/shard_map/dot_general | solution.py:38
  586.3 0.5 all-gather.5.cloned.1.call-update
  586.9 24.3 %fusion = f32[512,3584]{1,0:T(8,128)} fusion(bf16[1,4096,3584]{2,1,0:T(8,128)(2,1)} %param.6, f32[128,4096]{1,0:T(8,128)} %copy-done.3, f32[128,4096]{1,0:T(8,128)} %copy-done.1, f32[128,4096]{1,0:T(8,128)} %copy-done, f32[128,4096]{1,0:T(8,128)S(1)} %fusion.22), kind=kOutput, calls=%fused_computation.2 | convolution fusion | flops 15049162752 | bytes 45088768 | tf_op jit(solution)/shard_map/dot_general | solution.py:49
  611.4 0.3 all-gather.3.cloned.1.call-update
  611.8 25.6 %all-gather.5.cloned.1.call-done = f32[512,3584]{1,0:T(8,128)} async-done(((f32[64,3584]{1,0:T(8,128)}), f32[512,3584]{1,0:T(8,128)}) %all-gather.5.cloned.1.call-update) | async-done | bytes 7340048 | tf_op jit(solution)/shard_map/all_gather | solution.py:66
  637.3 70.6 %reduce-scatter.2.cloned.1.call-done = f32[64,3584]{1,0:T(8,128)} async-done(((f32[512,3584]{1,0:T(8,128)}), f32[64,3584]{1,0:T(8,128)}) %reduce-scatter.2.cloned.1.call-update) | async-done | bytes 917520 | tf_op jit(solution)/shard_map/reduce_scatter | solution.py:48
  707.9 8.8 %fusion.15 = f32[64,3584]{1,0:T(8,128)} fusion(f32[512,3584]{1,0:T(8,128)} %all-gather.5.cloned.1.call-done, f32[64,3584]{1,0:T(8,128)} %reduce-scatter.2.cloned.1.call-done, f32[512,512]{1,0:T(8,128)} %all-reduce.6.cloned.1.call-done, s32[]{:T(128)S(6)} %select_n.6), kind=kOutput, calls=%fused_computation.19 | convolution fusion | flops 1410236416 | bytes 9306116 | tf_op jit(solution)/shard_map/dot_general | solution.py:64
  716.8 42.9 %all-gather.3.cloned.1.call-done = f32[512,3584]{1,0:T(8,128)} async-done(((f32[64,3584]{1,0:T(8,128)}), f32[512,3584]{1,0:T(8,128)}) %all-gather.3.cloned.1.call-update) | async-done | bytes 7340048 | tf_op jit(solution)/shard_map/all_gather | solution.py:60
  759.7 8.6 %fusion.16 = f32[64,3584]{1,0:T(8,128)} fusion(f32[512,3584]{1,0:T(8,128)} %all-gather.3.cloned.1.call-done, f32[64,3584]{1,0:T(8,128)S(1)} %copy-done.2, f32[512,512]{1,0:T(8,128)} %all-reduce.6.cloned.1.call-done, s32[]{:T(128)S(6)} %select_n.6), kind=kOutput, calls=%fused_computation.21 | convolution fusion | flops 1409974272 | bytes 9306116 | tf_op jit(solution)/shard_map/dot_general | solution.py:58
  (53 shorter events, 3.3 us)
Async XLA Ops:
  8.0 282.5 %all-reduce.4.cloned.1.call-start = ((), (), s32[]{:S(2)}) async-start(), calls=%async_computation.1 | async-start | bytes 16777216 | tf_op jit(solution)/shard_map/psum | solution.py:31
  31.4 580.4 %all-reduce.6.cloned.1.call-start = ((), (), s32[]{:S(2)}) async-start(), calls=%async_computation.3 | async-start | bytes 2097152 | tf_op jit(solution)/shard_map/psum | solution.py:45
  392.1 2.9 collective-permute-start
  542.6 27.2 %copy-start = (f32[128,4096]{1,0:T(8,128)}, f32[128,4096]{1,0:T(8,128)S(1)}, u32[]{:S(2)}) copy-start(f32[128,4096]{1,0:T(8,128)S(1)} %fusion.53) | copy-start | bytes 6291460
  552.5 18.6 %slice-start = ((s8[8388608]{0:T(1024)(128)(4,1)}), s8[4194304]{0:T(1024)(128)(4,1)S(1)}, s32[]{:S(2)}) async-start(s8[8388608]{0:T(1024)(128)(4,1)} %bitcast.89), calls=%async_computation.6 | async-start | bytes 8388608
  554.5 15.3 %copy-start.1 = (f32[128,4096]{1,0:T(8,128)}, f32[128,4096]{1,0:T(8,128)S(1)}, u32[]{:S(2)}) copy-start(f32[128,4096]{1,0:T(8,128)S(1)} %fusion.51) | copy-start | bytes 6291460
  554.5 16.6 %slice-start.1 = ((s8[8388608]{0:T(1024)(128)(4,1)}), s8[4194304]{0:T(1024)(128)(4,1)S(1)}, s32[]{:S(2)}) async-start(s8[8388608]{0:T(1024)(128)(4,1)} %bitcast.89), calls=%async_computation.7 | async-start | bytes 8388608
  569.8 1.3 copy-start.3
  586.2 51.1 %all-gather.5.cloned.1.call-start = ((), (), s32[]{:S(2)}) async-start(), calls=%async_computation.5 | async-start | bytes 8257536 | tf_op jit(solution)/shard_map/all_gather | solution.py:66
  586.8 121.1 %reduce-scatter.2.cloned.1.call-start = ((), (), s32[]{:S(2)}) async-start(), calls=%async_computation.2 | async-start | bytes 8257536 | tf_op jit(solution)/shard_map/reduce_scatter | solution.py:48
  611.2 148.5 %all-gather.3.cloned.1.call-start = ((), (), s32[]{:S(2)}) async-start(), calls=%async_computation.4 | async-start | bytes 8257536 | tf_op jit(solution)/shard_map/all_gather | solution.py:60
  707.9 51.7 %copy-start.2 = (f32[64,3584]{1,0:T(8,128)S(1)}, f32[64,3584]{1,0:T(8,128)}, u32[]{:S(2)}) copy-start(f32[64,3584]{1,0:T(8,128)} %reduce-scatter.2.cloned.1.call-done) | copy-start | bytes 2752516
Sparse Core Ops, SparseCore 0:
  31.5 258.9 all-reduce.3
  586.3 18.5 all-reduce.5
Sparse Core Ops, SparseCore 1:
  588.6 48.7 all-gather.4
  641.2 66.7 reduce-scatter.1
  709.9 49.7 all-gather.2
where the time goes:
time: 783 us; the launch traced here: 776 us
  waiting for transfers between devices  400 us (51%)
  other arithmetic  199 us (25%)
  matrix products  143 us (18%)
  between operations  21.3 us (3%)
  local copies, waits for them, and re-layouts  12.4 us (2%)
    psum x1, waiting for transfers between devices, local(): sketch = lax.psum(partial_value, ('dp', 'col'))  259 us
    another operation x15, other arithmetic, local(): jnp.linalg.cholesky(gram_of(upper_factor) + gram_of(partner))  79.4 us
    another operation x14, other arithmetic, local(): upper_factor = jnp.linalg.cholesky(gram_of(sketch)).T  78.7 us
    reduce_scatter x1, waiting for transfers between devices, local(): lax.psum_scatter(lax.dot_general(basis_low, replica_grad, (((0,), (0,)),...  70.6 us
    all_gather x1, waiting for transfers between devices, local(): lax.all_gather(first_moment, ('dp', 'row'), axis=0, tiled=True)  42.9 us
    another operation x3, other arithmetic, basis_from(): jax.scipy.linalg.solve_triangular(lower_factor, sketch_part.T, lower=True)  40.3 us
    another operation x7, matrix products, basis_from(): jax.scipy.linalg.solve_triangular(lower_factor, sketch_part.T, lower=True)  37.7 us
    all_gather x1, waiting for transfers between devices, local(): lax.all_gather(second_moment, ('dp', 'row'), axis=0, tiled=True)  25.6 us
  transfers between devices with their start and end apart: 6, of which 5 were waited for; matrix products, arithmetic and copies ran while one was open for 5% of the time, Pallas kernels for 0%

commit v1 on v0

v1 whole, which is shorter than its diff:
```python
import jax
import jax.numpy as jnp
from jax import lax
from jax.experimental import pallas as pl
from jax.experimental.pallas import tpu as pltpu
from jax.sharding import PartitionSpec as P

highest = lax.Precision.HIGHEST
BLOCK = 128


def contract(a, b, a_dim, b_dim):
    return lax.dot_general(
        a, b, (((a_dim,), (b_dim,)), ((), ())), precision=highest, preferred_element_type=jnp.float32
    )


def eliminate(block, inverse_ref):
    groups = BLOCK // 8
    left = [block[8 * g : 8 * g + 8] for g in range(groups)]
    row_ids = lax.broadcasted_iota(jnp.int32, (8, BLOCK), 0)
    lane_ids = lax.broadcasted_iota(jnp.int32, (8, BLOCK), 1)
    right = [(lane_ids == row_ids + 8 * g).astype(jnp.float32) for g in range(groups)]
    for j in range(BLOCK):
        own, sub = divmod(j, 8)
        row = left[own][sub : sub + 1]
        inv_row = right[own][sub : sub + 1]
        pivot = row[:, j : j + 1]
        recip = 1.0 / pivot
        inverse_ref[j : j + 1, :] = inv_row * lax.rsqrt(pivot)
        row_scaled = row * recip
        inv_scaled = inv_row * recip
        for g in range(own, groups):
            column = left[g][:, j : j + 1]
            if g == own:
                if sub == 7:
                    continue
                column = jnp.where(row_ids[:, :1] > sub, column, 0.0)
            left[g] = left[g] - column * row_scaled
            right[g] = right[g] - column * inv_scaled


def cholesky_kernel(gram_ref, inverse_ref, work_ref, rest_ref, diag_ref):
    size = gram_ref.shape[0]
    work_ref[...] = gram_ref[...]
    rows = lax.broadcasted_iota(jnp.int32, (size, size), 0)
    cols = lax.broadcasted_iota(jnp.int32, (size, size), 1)
    rest_ref[...] = (rows == cols).astype(jnp.float32)

    def step(k, _):
        at = pl.ds(pl.multiple_of(k * BLOCK, BLOCK), BLOCK)
        eliminate(work_ref[at, at], diag_ref)
        diag = diag_ref[...]
        below = lax.broadcasted_iota(jnp.int32, (size, BLOCK), 0) >= (k + 1) * BLOCK
        panel = jnp.where(below, work_ref[:, at], 0.0)
        factor = contract(panel, diag, 1, 1)
        done = contract(diag, rest_ref[at, :], 1, 0)
        inverse_ref[at, :] = done
        work_ref[...] -= contract(factor, factor, 1, 1)
        rest_ref[...] -= contract(factor, done, 1, 0)
        return 0

    lax.fori_loop(0, size // BLOCK, step, 0)


def inverse_cholesky(gram):
    size = gram.shape[0]
    return pl.pallas_call(
        cholesky_kernel,
        out_shape=jax.ShapeDtypeStruct((size, size), jnp.float32),
        in_specs=[pl.BlockSpec(memory_space=pltpu.VMEM)],
        out_specs=pl.BlockSpec(memory_space=pltpu.VMEM),
        scratch_shapes=[
            pltpu.VMEM((size, size), jnp.float32),
            pltpu.VMEM((size, size), jnp.float32),
            pltpu.VMEM((BLOCK, BLOCK), jnp.float32),
        ],
        compiler_params=pltpu.CompilerParams(vmem_limit_bytes=32 << 20),
        cost_estimate=pl.CostEstimate(flops=30_000_000_000, bytes_accessed=2_000_000, transcendentals=0),
    )(gram)


def bits_of(axis):
    return lax.axis_size(axis).bit_length() - 1


def own_bit(axis, bit):
    return (lax.axis_index(axis) >> bit) & 1


def swap(value, axis, bit):
    return lax.ppermute(value, axis, [(i, i ^ 1 << bit) for i in range(lax.axis_size(axis))])


def shifted(value, axis, by):
    size = lax.axis_size(axis)
    return lax.ppermute(value, axis, [(i, (i + by) % size) for i in range(size)])


def halve(value, axis, bit, dim=0):
    half = value.shape[dim] // 2
    me = own_bit(axis, bit)
    sent = lax.dynamic_slice_in_dim(value, (1 - me) * half, half, dim)
    kept = lax.dynamic_slice_in_dim(value, me * half, half, dim)
    return kept + swap(sent, axis, bit)


def double(value, axis, bit):
    other = swap(value, axis, bit)
    first = own_bit(axis, bit) == 0
    return jnp.concatenate([jnp.where(first, value, other), jnp.where(first, other, value)], 0)


def scatter_direct(value, axis):
    size = lax.axis_size(axis)
    part = value.shape[0] // size
    me = lax.axis_index(axis)
    total = lax.dynamic_slice_in_dim(value, me * part, part, 0)
    for by in range(1, size):
        total = total + shifted(
            lax.dynamic_slice_in_dim(value, (me + by) % size * part, part, 0), axis, by
        )
    return total


def gather_direct(value, axis):
    size = lax.axis_size(axis)
    me = lax.axis_index(axis)
    blocks = [value] + [shifted(value, axis, by) for by in range(1, size)]
    ordered = []
    for place in range(size):
        chosen = blocks[0]
        for by in range(1, size):
            chosen = jnp.where((me - by) % size == place, blocks[by], chosen)
        ordered.append(chosen)
    return jnp.concatenate(ordered, 0)


def scatter_ring(value, axis):
    size = lax.axis_size(axis)
    part = value.shape[0] // size
    me = lax.axis_index(axis)

    def block(place):
        return lax.dynamic_slice_in_dim(value, place % size * part, part, 0)

    total = block(me + size - 1)
    for step in range(1, size):
        total = shifted(total, axis, 1) + block(me + 2 * size - 1 - step)
    return total


def gather_ring(value, axis):
    size = lax.axis_size(axis)
    me = lax.axis_index(axis)
    blocks = [value]
    for _ in range(1, size):
        blocks.append(shifted(blocks[-1], axis, 1))
    ordered = []
    for place in range(size):
        chosen = blocks[0]
        for by in range(1, size):
            chosen = jnp.where((me - by) % size == place, blocks[by], chosen)
        ordered.append(chosen)
    return jnp.concatenate(ordered, 0)


def scatter_bits(value, axis, order):
    for bit in order:
        value = halve(value, axis, bit)
    return value


def gather_bits(value, axis, order):
    for bit in reversed(order):
        value = double(value, axis, bit)
    return value


def row_sum(value):
    for bit in range(bits_of("row")):
        value = value + swap(value, "row", bit)
    return value


def all_to_all(value):
    tail = value.shape[1:]
    dp_bits, row_bits = bits_of("dp"), bits_of("row")
    bits = [("dp", b) for b in reversed(range(dp_bits))] + [("row", b) for b in reversed(range(row_bits))]
    value = value.reshape((2,) * len(bits) + tail)
    for place in reversed(range(len(bits))):
        axis, bit = bits[place]
        me = own_bit(axis, bit)
        sent = lax.dynamic_index_in_dim(value, 1 - me, place, keepdims=True)
        kept = lax.dynamic_index_in_dim(value, me, place, keepdims=True)
        got = swap(sent, axis, bit)
        value = jnp.concatenate([jnp.where(me == 0, kept, got), jnp.where(me == 0, got, kept)], place)
    return value.reshape((1 << len(bits),) + tail)


def local(gradients, test_matrix, old_basis, first_moment, second_moment):
    grad = gradients[0]
    rows, cols = grad.shape
    rank_dev = first_moment.shape[0]
    group = lax.axis_size("dp") * lax.axis_size("row")
    rank = rank_dev * group
    wide = cols // group

    moments = jnp.stack([first_moment, second_moment])
    moments = moments.reshape(2, rank_dev, group, wide).transpose(2, 0, 1, 3)
    moments = all_to_all(moments)
    moments = moments.transpose(1, 0, 2, 3).reshape(2, rank, wide)

    test_values = test_matrix.astype(jnp.bfloat16)
    up = list(range(bits_of("dp")))
    down = up[::-1]
    unit = rows // 16
    plan = [(3, up), (3, down), (2, None), (3, up), (3, down), (2, None)]
    start = 0
    pieces = []
    for units, order in plan:
        size = units * unit
        part = jnp.dot(grad[start : start + size], test_values, preferred_element_type=jnp.float32)
        if order is None:
            part = scatter_bits(scatter_ring(part, "col"), "dp", up)
            part = gather_ring(gather_bits(part, "dp", up), "col")
        else:
            part = scatter_direct(scatter_bits(part, "dp", order), "col")
            part = gather_bits(gather_direct(part, "col"), "dp", order)
        pieces.append((start, size, part))
        start += size

    gram = 0.0
    inner = 0.0
    for start, size, part in pieces:
        gram = gram + contract(part, part, 0, 0)
        inner = inner + contract(part, old_basis[start : start + size], 0, 0)
    gram = row_sum(gram)
    inner = row_sum(inner)
    inverse = inverse_cholesky(gram)
    basis_low = jnp.concatenate(
        [contract(part, inverse, 1, 1).astype(jnp.bfloat16) for _, _, part in pieces], 0
    )

    correlation = contract(inverse, inner, 1, 0)
    turned = jnp.stack(
        [contract(correlation, moments[0], 1, 0), contract(correlation * correlation, moments[1], 1, 0)]
    )
    turned = turned.reshape(2, group, rank_dev, wide).transpose(1, 0, 2, 3)
    turned = all_to_all(turned)
    turned = turned.transpose(1, 2, 0, 3).reshape(2, rank_dev, cols)

    chunks = 4
    chunk = cols // chunks
    summed = []
    dp_bits, row_bits = bits_of("dp"), bits_of("row")
    for c in range(chunks):
        value = lax.dot_general(
            basis_low,
            grad[:, c * chunk : (c + 1) * chunk],
            (((0,), (0,)), ((), ())),
            preferred_element_type=jnp.float32,
        )
        value = value.reshape((2,) * (dp_bits + row_bits) + (rank_dev, chunk))
        places = [("row", b, dp_bits + row_bits - 1 - b) for b in range(row_bits)]
        dp_places = [("dp", b, dp_bits - 1 - b) for b in range(dp_bits)]
        for axis, bit, place in places + (dp_places if c % 2 else dp_places[::-1]):
            value = halve(value, axis, bit, place)
        summed.append(value.reshape(rank_dev, chunk))
    projected = jnp.concatenate(summed, 1)
    first_new = 0.9 * turned[0] + 0.1 * projected
    second_new = 0.95 * turned[1] + 0.05 * projected * projected
    return (projected, first_new, second_new)


def solution(mesh):
    in_specs = (
        P("dp", "row", "col"),
        P("col", None),
        P("row", None),
        P(("dp", "row"), "col"),
        P(("dp", "row"), "col"),
    )
    out_specs = (P(("dp", "row"), "col"), P(("dp", "row"), "col"), P(("dp", "row"), "col"))
    return jax.shard_map(local, mesh=mesh, in_specs=in_specs, out_specs=out_specs, check_vma=False)
```

time: 783 us -> 505 us (0.64)
  waiting for transfers between devices: 400 us -> 206 us
  other arithmetic: 199 us -> 29.8 us
  starting transfers between devices: 0.67 us -> 77.2 us
  Pallas kernels: 0 us -> 52.8 us
  matrix products: 143 us -> 115 us
  between operations: 21.3 us -> 2.36 us
    psum x2 -> x0, waiting for transfers between devices: 259 us -> none  [the longest x1 259 us: local(): sketch = lax.psum(partial_value, ('dp', 'col'))]
    ppermute x1 -> x80, waiting for transfers between devices: 0.73 us -> 206 us  [the longest x44 131 us: swap(): lax.ppermute(value, axis, [(i, i ^ 1 << bit) for i in range(lax.axis_size...]
    another operation x32 -> x1, other arithmetic: 198 us -> 0.2 us  [local(): jnp.stack([contract(correlation, moments[0], 1, 0), contract(correlation...]
    ppermute x1 -> x80, starting transfers between devices: 0.25 us -> 77.2 us  [the longest x36 42.9 us: shifted(): lax.ppermute(value, axis, [(i, (i + by) % size) for i in range(size)])]
    reduce_scatter x1 -> x0, waiting for transfers between devices: 70.6 us -> none  [local(): lax.psum_scatter(lax.dot_general(basis_low, replica_grad, (((0,), (0,)),...]
    all_gather x2 -> x0, waiting for transfers between devices: 68.5 us -> none  [the longest x1 42.9 us: local(): lax.all_gather(first_moment, ('dp', 'row'), axis=0, tiled=True)]
    pallas_call x0 -> x1, Pallas kernels: none -> 52.8 us  [inverse_cholesky(): pl.pallas_call(cholesky_kernel, out_shape=jax.ShapeDtypeStruct((size, siz...]
    another operation x19 -> x0, matrix products: 41.6 us -> none  [the longest x7 37.7 us: basis_from(): jax.scipy.linalg.solve_triangular(lower_factor, sketch_part.T, lower=True)]
  transfers between devices with their start and end apart: 6 -> 80, of which waited for: 5 -> 38; matrix products, arithmetic and copies ran while one was open for 5% -> 28% of each run, Pallas kernels for 0% -> 11%
where the time goes in v1:
time: 505 us; the launch traced here: 497 us
  waiting for transfers between devices  206 us (41%)
  matrix products  115 us (23%)
  starting transfers between devices  77.2 us (15%)
  Pallas kernels  52.8 us (10%)
  other arithmetic  29.8 us (6%)
  local copies, waits for them, and re-layouts  13.4 us (3%)
    ppermute x44, waiting for transfers between devices, swap(): lax.ppermute(value, axis, [(i, i ^ 1 << bit) for i in range(lax.axis_size...  131 us
    ppermute x36, waiting for transfers between devices, shifted(): lax.ppermute(value, axis, [(i, (i + by) % size) for i in range(size)])  75.2 us
    pallas_call x1, Pallas kernels, inverse_cholesky(): pl.pallas_call(cholesky_kernel, out_shape=jax.ShapeDtypeStruct((size, siz...  52.8 us
    dot_general x21, matrix products, contract(): lax.dot_general(a, b, (((a_dim,), (b_dim,)), ((), ())), precision=highest...  50 us
    ppermute x36, starting transfers between devices, shifted(): lax.ppermute(value, axis, [(i, (i + by) % size) for i in range(size)])  42.9 us
    dot_general x6, matrix products, local(): jnp.dot(grad[start:start + size], test_values, preferred_element_type=jnp...  34.8 us
    ppermute x44, starting transfers between devices, swap(): lax.ppermute(value, axis, [(i, i ^ 1 << bit) for i in range(lax.axis_size...  34.3 us
    dot_general x4, matrix products, local(): lax.dot_general(basis_low, grad[:, c * chunk:(c + 1) * chunk], (((0,), (0...  30.3 us
  transfers between devices with their start and end apart: 80, of which 38 were waited for; matrix products, arithmetic and copies ran while one was open for 28% of the time, Pallas kernels for 11%

profile of v1, /device:TPU:0, one launch (start us, length us, event | category | flops | bytes accessed | tf_op | source)
XLA Modules:
  0.0 496.7 jit_solution(16531760521035017348)
XLA Ops:
  0.6 6.0 %convert_element_type.21 = bf16[3584,512]{1,0:T(8,128)(2,1)} convert(s32[3584,512]{1,0:T(8,128)} %param.6) | non-fusion elementwise | flops 1835008 | bytes 11010048 | tf_op jit(solution)/shard_map/convert_element_type | solution.py:214
  6.6 5.3 %fusion.20 = f32[512,512]{1,0:T(8,128)S(1)} fusion(bf16[3584,512]{1,0:T(8,128)(2,1)} %convert_element_type.21, bf16[1,4096,3584]{2,1,0:T(8,128)(2,1)} %param.5), kind=kOutput, calls=%fused_computation.20 | convolution fusion | flops 1879048192 | bytes 8388608 | tf_op jit(solution)/shard_map/dot_general | solution.py:223
  13.0 3.0 collective-permute-start.50
  16.1 4.1 fusion.22
  22.8 6.1 %fusion.14 = f32[768,512]{1,0:T(8,128)S(1)} fusion(bf16[3584,512]{1,0:T(8,128)(2,1)} %convert_element_type.21, bf16[1,4096,3584]{2,1,0:T(8,128)(2,1)} %param.5), kind=kOutput, calls=%fused_computation.14 | convolution fusion | flops 2818572288 | bytes 10747904 | tf_op jit(solution)/shard_map/dot_general | solution.py:223
  31.4 6.1 %fusion.12 = f32[768,512]{1,0:T(8,128)S(1)} fusion(bf16[3584,512]{1,0:T(8,128)(2,1)} %convert_element_type.21, bf16[1,4096,3584]{2,1,0:T(8,128)(2,1)} %param.5), kind=kOutput, calls=%fused_computation.12 | convolution fusion | flops 2818572288 | bytes 10747904 | tf_op jit(solution)/shard_map/dot_general | solution.py:223
  40.1 6.6 %fusion.10 = f32[768,512]{1,0:T(8,128)S(1)} fusion(bf16[3584,512]{1,0:T(8,128)(2,1)} %convert_element_type.21, bf16[1,4096,3584]{2,1,0:T(8,128)(2,1)} %param.5), kind=kOutput, calls=%fused_computation.10 | convolution fusion | flops 2818572288 | bytes 10747904 | tf_op jit(solution)/shard_map/dot_general | solution.py:223
  49.4 6.7 %fusion.8 = f32[768,512]{1,0:T(8,128)} fusion(bf16[3584,512]{1,0:T(8,128)(2,1)S(1)} %copy-done.2, bf16[1,4096,3584]{2,1,0:T(8,128)(2,1)} %param.5), kind=kOutput, calls=%fused_computation.8 | convolution fusion | flops 2818572288 | bytes 10747904 | tf_op jit(solution)/shard_map/dot_general | solution.py:223
  64.8 7.4 %collective-permute-done.51 = f32[128,512]{1,0:T(8,128)} collective-permute-done((f32[128,512]{1,0:T(8,128)}, f32[128,512]{1,0:T(8,128)}, u32[]{:S(2)}, u32[]{:S(2)}) %collective-permute-start.51) | collective-permute-done | bytes 262176 | tf_op jit(solution)/shard_map/ppermute | solution.py:97
  74.8 2.1 collective-permute-done.21
  78.5 3.8 collective-permute-done.52
  83.5 7.1 %collective-permute-done.22 = f32[128,512]{1,0:T(8,128)S(1)} collective-permute-done((f32[128,512]{1,0:T(8,128)S(1)}, f32[128,512]{1,0:T(8,128)S(1)}, u32[]{:S(2)}, u32[]{:S(2)}) %collective-permute-start.22) | collective-permute-done | bytes 262176 | tf_op jit(solution)/shard_map/ppermute | solution.py:97
  103.4 14.0 %collective-permute-done.54 = f32[32,512]{1,0:T(8,128)S(1)} collective-permute-done((f32[32,512]{1,0:T(8,128)S(1)}, f32[32,512]{1,0:T(8,128)S(1)}, u32[]{:S(2)}, u32[]{:S(2)}) %collective-permute-start.54) | collective-permute-done | bytes 65568 | tf_op jit(solution)/shard_map/ppermute | solution.py:92
  117.9 3.7 collective-permute-done.24
  122.2 4.3 collective-permute-done.55
  127.0 3.7 collective-permute-done.25
  132.2 3.9 collective-permute-done.56
  137.6 4.9 collective-permute-done.26
  144.4 4.4 collective-permute-start.3
  149.2 7.8 %collective-permute-done.2 = f32[48,512]{1,0:T(8,128)S(1)} collective-permute-done((f32[48,512]{1,0:T(8,128)S(1)}, f32[48,512]{1,0:T(8,128)S(1)}, u32[]{:S(2)}, u32[]{:S(2)}) %collective-permute-start.2) | collective-permute-done | bytes 98336 | tf_op jit(solution)/shard_map/ppermute | solution.py:97
  157.0 3.4 collective-permute-done.3
  165.3 2.6 collective-permute-done.13
  167.9 3.1 collective-permute-done.14
  173.2 2.5 collective-permute-done.33
  177.4 5.5 %collective-permute-start.44 = (f32[48,512]{1,0:T(8,128)S(1)}, f32[48,512]{1,0:T(8,128)S(1)}, u32[]{:S(2)}, u32[]{:S(2)}) collective-permute-start(f32[48,512]{1,0:T(8,128)S(1)} %get-tuple-element.69), channel_id=1, source_target_pairs={{0,3},{1,0},{2,1},{3,2},{4,7},{5,4},{6,5},{7,6},{8,11},{9,8},{10,9... | collective-permute-start | bytes 294920 | tf_op jit(solution)/shard_map/ppermute | solution.py:97
  186.2 6.1 %collective-permute-start.7 = (f32[48,512]{1,0:T(8,128)S(1)}, f32[48,512]{1,0:T(8,128)S(1)}, u32[]{:S(2)}, u32[]{:S(2)}) collective-permute-start(f32[48,512]{1,0:T(8,128)S(1)} %add_add_fusion.3), channel_id=1, source_target_pairs={{0,1},{1,2},{2,3},{3,0},{4,5},{5,6},{6,7},{7,4},{8,9},{9,10},{10,1... | collective-permute-start | bytes 294920 | tf_op jit(solution)/shard_map/ppermute | solution.py:97
  192.6 5.5 %collective-permute-done.6 = f32[48,512]{1,0:T(8,128)S(1)} collective-permute-done((f32[48,512]{1,0:T(8,128)S(1)}, f32[48,512]{1,0:T(8,128)S(1)}, u32[]{:S(2)}, u32[]{:S(2)}) %collective-permute-start.6) | collective-permute-done | bytes 98336 | tf_op jit(solution)/shard_map/ppermute | solution.py:97
  202.1 8.7 %collective-permute-done.16 = f32[48,512]{1,0:T(8,128)S(1)} collective-permute-done((f32[48,512]{1,0:T(8,128)S(1)}, f32[48,512]{1,0:T(8,128)S(1)}, u32[]{:S(2)}, u32[]{:S(2)}) %collective-permute-start.16) | collective-permute-done | bytes 98336 | tf_op jit(solution)/shard_map/ppermute | solution.py:97
  210.8 3.9 collective-permute-start.45
  214.7 4.3 collective-permute-done.36
  220.9 5.7 %collective-permute-start.27 = (f32[128,512]{1,0:T(8,128)S(1)}, f32[128,512]{1,0:T(8,128)S(1)}, u32[]{:S(2)}, u32[]{:S(2)}) collective-permute-start(f32[128,512]{1,0:T(8,128)S(1)} %pad_maximum_fusion.30), channel_id=1, source_target_pairs={{0,1},{1,2},{2,3},{3,0},{4,5},{5,6},{6,7},{7,4},{8,9},{9,10},{10,1... | collective-permute-start | bytes 786440 | tf_op jit(solution)/shard_map/ppermute | solution.py:97
  226.7 8.9 %collective-permute-done.46 = f32[48,512]{1,0:T(8,128)S(1)} collective-permute-done((f32[48,512]{1,0:T(8,128)S(1)}, f32[48,512]{1,0:T(8,128)S(1)}, u32[]{:S(2)}, u32[]{:S(2)}) %collective-permute-start.46) | collective-permute-done | bytes 98336 | tf_op jit(solution)/shard_map/ppermute | solution.py:97
  235.9 11.7 %collective-permute-done.8 = f32[192,512]{1,0:T(8,128)S(1)} collective-permute-done((f32[192,512]{1,0:T(8,128)S(1)}, f32[192,512]{1,0:T(8,128)S(1)}, u32[]{:S(2)}, u32[]{:S(2)}) %collective-permute-start.8) | collective-permute-done | bytes 393248 | tf_op jit(solution)/shard_map/ppermute | solution.py:92
  248.4 11.3 %collective-permute-done.38 = f32[192,512]{1,0:T(8,128)S(1)} collective-permute-done((f32[192,512]{1,0:T(8,128)S(1)}, f32[192,512]{1,0:T(8,128)S(1)}, u32[]{:S(2)}, u32[]{:S(2)}) %collective-permute-start.38) | collective-permute-done | bytes 393248 | tf_op jit(solution)/shard_map/ppermute | solution.py:92
  260.1 2.1 collective-permute-start.39
  262.5 2.1 collective-permute-start.49
  265.2 10.5 %collective-permute-done.19 = f32[384,512]{1,0:T(8,128)S(1)} collective-permute-done((f32[384,512]{1,0:T(8,128)S(1)}, f32[384,512]{1,0:T(8,128)S(1)}, u32[]{:S(2)}, u32[]{:S(2)}) %collective-permute-start.19) | collective-permute-done | bytes 786464 | tf_op jit(solution)/shard_map/ppermute | solution.py:92
  275.8 2.7 fusion.61
  280.3 3.7 collective-permute-done.49
  284.2 2.7 fusion.60
  286.9 2.7 fusion.59
  289.6 3.2 fusion.30
  292.8 2.7 fusion.28
  295.7 2.7 convolution_add_fusion.4
  298.4 2.0 fusion.43
  302.4 2.9 fusion.38
  305.2 2.7 fusion.26
  307.9 2.0 fusion.44
  313.2 52.8 %shard_map.76 = f32[512,512]{1,0:T(8,128)S(1)} custom-call(f32[512,512]{1,0:T(8,128)S(1)} %add.532.gram_ref), custom_call_target="tpu_custom_call" | custom-call | flops 30000001024 | bytes 2000000 | tf_op jit(solution)/shard_map/pallas_call | solution.py:68
  366.1 2.7 fusion.37
  368.7 2.7 fusion.36
  373.3 2.7 fusion.35
  375.9 2.9 fusion.34
  380.7 7.5 %fusion.6 = f32[512,896]{1,0:T(8,128)S(1)} fusion(bf16[4096,512]{1,0:T(8,128)(2,1)S(1)} %fusion.45, bf16[4096,3584]{1,0:T(8,128)(2,1)} %bitcast.102), kind=kOutput, calls=%fused_computation.6 | convolution fusion | flops 3758096384 | bytes 13369344 | tf_op jit(solution)/shard_map/dot_general | solution.py:258
  388.2 7.5 %fusion.4 = f32[512,896]{1,0:T(8,128)S(1)} fusion(bf16[4096,512]{1,0:T(8,128)(2,1)S(1)} %fusion.45, bf16[4096,3584]{1,0:T(8,128)(2,1)} %bitcast.103), kind=kOutput, calls=%fused_computation.4 | convolution fusion | flops 3758096384 | bytes 13369344 | tf_op jit(solution)/shard_map/dot_general | solution.py:258
  395.7 7.6 %fusion.2 = f32[512,896]{1,0:T(8,128)S(1)} fusion(bf16[4096,512]{1,0:T(8,128)(2,1)S(1)} %fusion.45, bf16[4096,3584]{1,0:T(8,128)(2,1)} %bitcast.104), kind=kOutput, calls=%fused_computation.2 | convolution fusion | flops 3758096384 | bytes 13369344 | tf_op jit(solution)/shard_map/dot_general | solution.py:258
  404.3 7.7 %fusion = f32[512,896]{1,0:T(8,128)S(1)} fusion(bf16[4096,512]{1,0:T(8,128)(2,1)S(1)} %fusion.45, bf16[4096,3584]{1,0:T(8,128)(2,1)} %bitcast.105), kind=kOutput, calls=%fused_computation | convolution fusion | flops 3758096384 | bytes 13369344 | tf_op jit(solution)/shard_map/dot_general | solution.py:258
  425.5 6.7 %collective-permute-done.62 = f32[1,2,1,64,896]{4,3,2,1,0:T(8,128)S(1)} collective-permute-done((f32[1,2,1,64,896]{4,3,2,1,0:T(8,128)S(1)}, f32[1,2,1,64,896]{4,3,2,1,0:T(8,128)S(1)}, u32[]{:S(2)}, u32[]{:S(2)}) %collective-permute-start.62) | collective-permute-done | bytes 458784 | tf_op jit(solution)/shard_map/ppermute | solution.py:92
  434.7 7.4 %collective-permute-done.68 = f32[1,2,1,64,896]{4,3,2,1,0:T(8,128)S(1)} collective-permute-done((f32[1,2,1,64,896]{4,3,2,1,0:T(8,128)S(1)}, f32[1,2,1,64,896]{4,3,2,1,0:T(8,128)S(1)}, u32[]{:S(2)}, u32[]{:S(2)}) %collective-permute-start.68) | collective-permute-done | bytes 458784 | tf_op jit(solution)/shard_map/ppermute | solution.py:92
  444.5 21.6 %collective-permute-done.78 = f32[2,1,2,2,64,448]{5,4,2,1,0,3:T(8,128)S(1)} collective-permute-done((f32[2,1,2,2,64,448]{5,4,2,1,0,3:T(8,128)S(1)}, f32[2,1,2,2,64,448]{5,4,2,1,0,3:T(8,128)S(1)}, u32[]{:S(2)}, u32[]{:S(2)}) %collective-permute-start.78) | collective-permute-done | bytes 917536 | tf_op jit(solution)/shard_map/ppermute | solution.py:92
  467.3 3.8 collective-permute-done.63
  471.1 4.1 collective-permute-done.69
  476.6 13.6 %collective-permute-done.79 = f32[1,2,2,2,64,448]{5,4,2,1,0,3:T(8,128)S(1)} collective-permute-done((f32[1,2,2,2,64,448]{5,4,2,1,0,3:T(8,128)S(1)}, f32[1,2,2,2,64,448]{5,4,2,1,0,3:T(8,128)S(1)}, u32[]{:S(2)}, u32[]{:S(2)}) %collective-permute-start.79) | collective-permute-done | bytes 917536 | tf_op jit(solution)/shard_map/ppermute | solution.py:92
  493.1 2.1 fusion.62
  (287 shorter events, 102.3 us)
Async XLA Ops:
  13.0 46.1 %collective-permute-start.50 = (f32[128,512]{1,0:T(8,128)}, f32[128,512]{1,0:T(8,128)}, u32[]{:S(2)}, u32[]{:S(2)}) collective-permute-start(f32[128,512]{1,0:T(8,128)} %constant_dynamic-slice_fusion.16), channel_id=1, source_target_pairs={{0,1},{1,2},{2,3},{3,0},{4,5},{5,6},{6,7},{7,4},{8,9},{9,10},{10,1... | collective-permute-start | bytes 786440 | tf_op jit(solution)/shard_map/ppermute | solution.py:97
  21.2 41.5 %collective-permute-start.20 = (f32[128,512]{1,0:T(8,128)S(1)}, f32[128,512]{1,0:T(8,128)}, u32[]{:S(2)}, u32[]{:S(2)}) collective-permute-start(f32[128,512]{1,0:T(8,128)S(1)} %constant_dynamic-slice_fusion.29), channel_id=1, source_target_pairs={{0,1},{1,2},{2,3},{3,0},{4,5},{5,6},{6,7},{7,4},{8,9},{9,10},{10,1... | collective-permute-start | bytes 786440 | tf_op jit(solution)/shard_map/ppermute | solution.py:97
  29.9 61.7 %collective-permute-start = (f32[384,512]{1,0:T(8,128)}, f32[384,512]{1,0:T(8,128)}, u32[]{:S(2)}, u32[]{:S(2)}) collective-permute-start(f32[384,512]{1,0:T(8,128)} %constant_dynamic-slice_fusion.39), channel_id=1, source_target_pairs={{0,8},{8,0},{16,24},{24,16},{1,9},{9,1},{17,25},{25,17},{2,10},{10... | collective-permute-start | bytes 2359304 | tf_op jit(solution)/shard_map/ppermute | solution.py:92
  38.5 55.9 %collective-permute-start.10 = (f32[384,512]{1,0:T(8,128)}, f32[384,512]{1,0:T(8,128)}, u32[]{:S(2)}, u32[]{:S(2)}) collective-permute-start(f32[384,512]{1,0:T(8,128)} %constant_dynamic-slice_fusion.34), channel_id=1, source_target_pairs={{0,16},{8,24},{16,0},{24,8},{1,17},{9,25},{17,1},{25,9},{2,18},{10... | collective-permute-start | bytes 2359304 | tf_op jit(solution)/shard_map/ppermute | solution.py:92
  48.8 47.6 %collective-permute-start.30 = (f32[384,512]{1,0:T(8,128)}, f32[384,512]{1,0:T(8,128)}, u32[]{:S(2)}, u32[]{:S(2)}) collective-permute-start(f32[384,512]{1,0:T(8,128)} %constant_dynamic-slice_fusion.26), channel_id=1, source_target_pairs={{0,8},{8,0},{16,24},{24,16},{1,9},{9,1},{17,25},{25,17},{2,10},{10... | collective-permute-start | bytes 2359304 | tf_op jit(solution)/shard_map/ppermute | solution.py:92
  61.0 11.2 %collective-permute-start.51 = (f32[128,512]{1,0:T(8,128)}, f32[128,512]{1,0:T(8,128)}, u32[]{:S(2)}, u32[]{:S(2)}) collective-permute-start(f32[128,512]{1,0:T(8,128)} %dynamic-slice_add_fusion.18), channel_id=1, source_target_pairs={{0,1},{1,2},{2,3},{3,0},{4,5},{5,6},{6,7},{7,4},{8,9},{9,10},{10,1... | collective-permute-start | bytes 786440 | tf_op jit(solution)/shard_map/ppermute | solution.py:97
  64.5 12.4 %collective-permute-start.21 = (f32[128,512]{1,0:T(8,128)}, f32[128,512]{1,0:T(8,128)}, u32[]{:S(2)}, u32[]{:S(2)}) collective-permute-start(f32[128,512]{1,0:T(8,128)} %dynamic-slice_add_fusion.21), channel_id=1, source_target_pairs={{0,1},{1,2},{2,3},{3,0},{4,5},{5,6},{6,7},{7,4},{8,9},{9,10},{10,1... | collective-permute-start | bytes 786440 | tf_op jit(solution)/shard_map/ppermute | solution.py:97
  73.9 8.4 %collective-permute-start.52 = (f32[128,512]{1,0:T(8,128)}, f32[128,512]{1,0:T(8,128)S(1)}, u32[]{:S(2)}, u32[]{:S(2)}) collective-permute-start(f32[128,512]{1,0:T(8,128)} %dynamic-slice_add_fusion.17), channel_id=1, source_target_pairs={{0,1},{1,2},{2,3},{3,0},{4,5},{5,6},{6,7},{7,4},{8,9},{9,10},{10,1... | collective-permute-start | bytes 786440 | tf_op jit(solution)/shard_map/ppermute | solution.py:97
  76.9 21.4 %collective-permute-start.40 = (f32[384,512]{1,0:T(8,128)}, f32[384,512]{1,0:T(8,128)S(1)}, u32[]{:S(2)}, u32[]{:S(2)}) collective-permute-start(f32[384,512]{1,0:T(8,128)} %constant_dynamic-slice_fusion.21), channel_id=1, source_target_pairs={{0,16},{8,24},{16,0},{24,8},{1,17},{9,25},{17,1},{25,9},{2,18},{10... | collective-permute-start | bytes 2359304 | tf_op jit(solution)/shard_map/ppermute | solution.py:92
  82.3 8.3 %collective-permute-start.22 = (f32[128,512]{1,0:T(8,128)S(1)}, f32[128,512]{1,0:T(8,128)S(1)}, u32[]{:S(2)}, u32[]{:S(2)}) collective-permute-start(f32[128,512]{1,0:T(8,128)S(1)} %dynamic-slice_add_fusion.20), channel_id=1, source_target_pairs={{0,1},{1,2},{2,3},{3,0},{4,5},{5,6},{6,7},{7,4},{8,9},{9,10},{10,1... | collective-permute-start | bytes 786440 | tf_op jit(solution)/shard_map/ppermute | solution.py:97
  90.6 11.8 %collective-permute-start.74 = (f32[2,2,1,2,64,448]{5,4,2,1,0,3:T(8,128)S(1)}, f32[2,2,1,2,64,448]{5,4,2,1,0,3:T(8,128)S(1)}, u32[]{:S(2)}, u32[]{:S(2)}) collective-permute-start(f32[2,2,1,2,64,448]{5,4,2,1,0,3:T(8,128)S(1)} %constant_dynamic-slice_fusion.1), channel_id=1, source_target_pairs={{0,4},{4,0},{1,5},{5,1},{2,6},{6,2},{3,7},{7,3},{8,12},{12,8},{9,1... | collective-permute-start | bytes 2752520 | tf_op jit(solution)/shard_map/ppermute | solution.py:92
  91.6 8.5 %collective-permute-start.53 = (f32[64,512]{1,0:T(8,128)S(1)}, f32[64,512]{1,0:T(8,128)S(1)}, u32[]{:S(2)}, u32[]{:S(2)}) collective-permute-start(f32[64,512]{1,0:T(8,128)S(1)} %constant_dynamic-slice_fusion.15), channel_id=1, source_target_pairs={{0,8},{8,0},{16,24},{24,16},{1,9},{9,1},{17,25},{25,17},{2,10},{10... | collective-permute-start | bytes 393224 | tf_op jit(solution)/shard_map/ppermute | solution.py:92
  96.5 47.6 %collective-permute-start.1 = (f32[192,512]{1,0:T(8,128)S(1)}, f32[192,512]{1,0:T(8,128)S(1)}, u32[]{:S(2)}, u32[]{:S(2)}) collective-permute-start(f32[192,512]{1,0:T(8,128)S(1)} %constant_dynamic-slice_fusion.38), channel_id=1, source_target_pairs={{0,16},{8,24},{16,0},{24,8},{1,17},{9,25},{17,1},{25,9},{2,18},{10... | collective-permute-start | bytes 1179656 | tf_op jit(solution)/shard_map/ppermute | solution.py:92
  98.3 45.9 %collective-permute-start.11 = (f32[192,512]{1,0:T(8,128)S(1)}, f32[192,512]{1,0:T(8,128)S(1)}, u32[]{:S(2)}, u32[]{:S(2)}) collective-permute-start(f32[192,512]{1,0:T(8,128)S(1)} %constant_dynamic-slice_fusion.33), channel_id=1, source_target_pairs={{0,8},{8,0},{16,24},{24,16},{1,9},{9,1},{17,25},{25,17},{2,10},{10... | collective-permute-start | bytes 1179656 | tf_op jit(solution)/shard_map/ppermute | solution.py:92
  100.1 44.3 %collective-permute-start.31 = (f32[192,512]{1,0:T(8,128)S(1)}, f32[192,512]{1,0:T(8,128)S(1)}, u32[]{:S(2)}, u32[]{:S(2)}) collective-permute-start(f32[192,512]{1,0:T(8,128)S(1)} %constant_dynamic-slice_fusion.25), channel_id=1, source_target_pairs={{0,16},{8,24},{16,0},{24,8},{1,17},{9,25},{17,1},{25,9},{2,18},{10... | collective-permute-start | bytes 1179656 | tf_op jit(solution)/shard_map/ppermute | solution.py:92
  101.7 47.2 %collective-permute-start.41 = (f32[192,512]{1,0:T(8,128)S(1)}, f32[192,512]{1,0:T(8,128)S(1)}, u32[]{:S(2)}, u32[]{:S(2)}) collective-permute-start(f32[192,512]{1,0:T(8,128)S(1)} %constant_dynamic-slice_fusion.20), channel_id=1, source_target_pairs={{0,8},{8,0},{16,24},{24,16},{1,9},{9,1},{17,25},{25,17},{2,10},{10... | collective-permute-start | bytes 1179656 | tf_op jit(solution)/shard_map/ppermute | solution.py:92
  102.4 14.9 %collective-permute-start.54 = (f32[32,512]{1,0:T(8,128)S(1)}, f32[32,512]{1,0:T(8,128)S(1)}, u32[]{:S(2)}, u32[]{:S(2)}) collective-permute-start(f32[32,512]{1,0:T(8,128)S(1)} %constant_dynamic-slice_fusion.14), channel_id=1, source_target_pairs={{0,16},{8,24},{16,0},{24,8},{1,17},{9,25},{17,1},{25,9},{2,18},{10... | collective-permute-start | bytes 196616 | tf_op jit(solution)/shard_map/ppermute | solution.py:92
  142.5 117.5 %collective-permute-start.75 = (f32[2,1,2,2,64,448]{5,4,2,1,0,3:T(8,128)S(1)}, f32[2,1,2,2,64,448]{5,4,2,1,0,3:T(8,128)S(1)}, u32[]{:S(2)}, u32[]{:S(2)}) collective-permute-start(f32[2,1,2,2,64,448]{5,4,2,1,0,3:T(8,128)S(1)} %fusion.53), channel_id=1, source_target_pairs={{0,8},{8,0},{16,24},{24,16},{1,9},{9,1},{17,25},{25,17},{2,10},{10... | collective-permute-start | bytes 2752520 | tf_op jit(solution)/shard_map/ppermute | solution.py:92
  144.1 91.6 %collective-permute-start.57 = (f32[128,512]{1,0:T(8,128)S(1)}, f32[128,512]{1,0:T(8,128)S(1)}, u32[]{:S(2)}, u32[]{:S(2)}) collective-permute-start(f32[128,512]{1,0:T(8,128)S(1)} %pad_maximum_fusion.31), channel_id=1, source_target_pairs={{0,1},{1,2},{2,3},{3,0},{4,5},{5,6},{6,7},{7,4},{8,9},{9,10},{10,1... | collective-permute-start | bytes 786440 | tf_op jit(solution)/shard_map/ppermute | solution.py:97
  144.3 12.8 %collective-permute-start.2 = (f32[48,512]{1,0:T(8,128)S(1)}, f32[48,512]{1,0:T(8,128)S(1)}, u32[]{:S(2)}, u32[]{:S(2)}) collective-permute-start(f32[48,512]{1,0:T(8,128)S(1)} %get-tuple-element.47), channel_id=1, source_target_pairs={{0,1},{1,2},{2,3},{3,0},{4,5},{5,6},{6,7},{7,4},{8,9},{9,10},{10,1... | collective-permute-start | bytes 294920 | tf_op jit(solution)/shard_map/ppermute | solution.py:97
  144.4 16.0 %collective-permute-start.3 = (f32[48,512]{1,0:T(8,128)S(1)}, f32[48,512]{1,0:T(8,128)S(1)}, u32[]{:S(2)}, u32[]{:S(2)}) collective-permute-start(f32[48,512]{1,0:T(8,128)S(1)} %get-tuple-element.49), channel_id=1, source_target_pairs={{0,2},{1,3},{2,0},{3,1},{4,6},{5,7},{6,4},{7,5},{8,10},{9,11},{10,... | collective-permute-start | bytes 294920 | tf_op jit(solution)/shard_map/ppermute | solution.py:97
  149.0 11.5 %collective-permute-start.4 = (f32[48,512]{1,0:T(8,128)S(1)}, f32[48,512]{1,0:T(8,128)S(1)}, u32[]{:S(2)}, u32[]{:S(2)}) collective-permute-start(f32[48,512]{1,0:T(8,128)S(1)} %get-tuple-element.48), channel_id=1, source_target_pairs={{0,3},{1,0},{2,1},{3,2},{4,7},{5,4},{6,5},{7,6},{8,11},{9,8},{10,9... | collective-permute-start | bytes 294920 | tf_op jit(solution)/shard_map/ppermute | solution.py:97
  160.4 10.5 %collective-permute-start.14 = (f32[48,512]{1,0:T(8,128)S(1)}, f32[48,512]{1,0:T(8,128)S(1)}, u32[]{:S(2)}, u32[]{:S(2)}) collective-permute-start(f32[48,512]{1,0:T(8,128)S(1)} %get-tuple-element.55), channel_id=1, source_target_pairs={{0,3},{1,0},{2,1},{3,2},{4,7},{5,4},{6,5},{7,6},{8,11},{9,8},{10,9... | collective-permute-start | bytes 294920 | tf_op jit(solution)/shard_map/ppermute | solution.py:97
  171.4 11.6 %collective-permute-start.42 = (f32[48,512]{1,0:T(8,128)S(1)}, f32[48,512]{1,0:T(8,128)S(1)}, u32[]{:S(2)}, u32[]{:S(2)}) collective-permute-start(f32[48,512]{1,0:T(8,128)S(1)} %get-tuple-element.68), channel_id=1, source_target_pairs={{0,1},{1,2},{2,3},{3,0},{4,5},{5,6},{6,7},{7,4},{8,9},{9,10},{10,1... | collective-permute-start | bytes 294920 | tf_op jit(solution)/shard_map/ppermute | solution.py:97
  177.4 8.7 %collective-permute-start.44 = (f32[48,512]{1,0:T(8,128)S(1)}, f32[48,512]{1,0:T(8,128)S(1)}, u32[]{:S(2)}, u32[]{:S(2)}) collective-permute-start(f32[48,512]{1,0:T(8,128)S(1)} %get-tuple-element.69), channel_id=1, source_target_pairs={{0,3},{1,0},{2,1},{3,2},{4,7},{5,4},{6,5},{7,6},{8,11},{9,8},{10,9... | collective-permute-start | bytes 294920 | tf_op jit(solution)/shard_map/ppermute | solution.py:97
  183.0 9.3 %collective-permute-start.5 = (f32[48,512]{1,0:T(8,128)S(1)}, f32[48,512]{1,0:T(8,128)S(1)}, u32[]{:S(2)}, u32[]{:S(2)}) collective-permute-start(f32[48,512]{1,0:T(8,128)S(1)} %add_add_fusion.3), channel_id=1, source_target_pairs={{0,3},{1,0},{2,1},{3,2},{4,7},{5,4},{6,5},{7,6},{8,11},{9,8},{10,9... | collective-permute-start | bytes 294920 | tf_op jit(solution)/shard_map/ppermute | solution.py:97
  183.6 14.5 %collective-permute-start.6 = (f32[48,512]{1,0:T(8,128)S(1)}, f32[48,512]{1,0:T(8,128)S(1)}, u32[]{:S(2)}, u32[]{:S(2)}) collective-permute-start(f32[48,512]{1,0:T(8,128)S(1)} %add_add_fusion.3), channel_id=1, source_target_pairs={{0,2},{1,3},{2,0},{3,1},{4,6},{5,7},{6,4},{7,5},{8,10},{9,11},{10,... | collective-permute-start | bytes 294920 | tf_op jit(solution)/shard_map/ppermute | solution.py:97
  186.2 11.9 %collective-permute-start.7 = (f32[48,512]{1,0:T(8,128)S(1)}, f32[48,512]{1,0:T(8,128)S(1)}, u32[]{:S(2)}, u32[]{:S(2)}) collective-permute-start(f32[48,512]{1,0:T(8,128)S(1)} %add_add_fusion.3), channel_id=1, source_target_pairs={{0,1},{1,2},{2,3},{3,0},{4,5},{5,6},{6,7},{7,4},{8,9},{9,10},{10,1... | collective-permute-start | bytes 294920 | tf_op jit(solution)/shard_map/ppermute | solution.py:97
  198.1 12.6 %collective-permute-start.16 = (f32[48,512]{1,0:T(8,128)S(1)}, f32[48,512]{1,0:T(8,128)S(1)}, u32[]{:S(2)}, u32[]{:S(2)}) collective-permute-start(f32[48,512]{1,0:T(8,128)S(1)} %add_add_fusion.2), channel_id=1, source_target_pairs={{0,2},{1,3},{2,0},{3,1},{4,6},{5,7},{6,4},{7,5},{8,10},{9,11},{10,... | collective-permute-start | bytes 294920 | tf_op jit(solution)/shard_map/ppermute | solution.py:97
  198.1 12.6 %collective-permute-start.17 = (f32[48,512]{1,0:T(8,128)S(1)}, f32[48,512]{1,0:T(8,128)S(1)}, u32[]{:S(2)}, u32[]{:S(2)}) collective-permute-start(f32[48,512]{1,0:T(8,128)S(1)} %add_add_fusion.2), channel_id=1, source_target_pairs={{0,1},{1,2},{2,3},{3,0},{4,5},{5,6},{6,7},{7,4},{8,9},{9,10},{10,1... | collective-permute-start | bytes 294920 | tf_op jit(solution)/shard_map/ppermute | solution.py:97
  200.3 10.5 %collective-permute-start.35 = (f32[48,512]{1,0:T(8,128)S(1)}, f32[48,512]{1,0:T(8,128)S(1)}, u32[]{:S(2)}, u32[]{:S(2)}) collective-permute-start(f32[48,512]{1,0:T(8,128)S(1)} %add_add_fusion.1), channel_id=1, source_target_pairs={{0,3},{1,0},{2,1},{3,2},{4,7},{5,4},{6,5},{7,6},{8,11},{9,8},{10,9... | collective-permute-start | bytes 294920 | tf_op jit(solution)/shard_map/ppermute | solution.py:97
  210.8 10.1 %collective-permute-start.45 = (f32[48,512]{1,0:T(8,128)S(1)}, f32[48,512]{1,0:T(8,128)S(1)}, u32[]{:S(2)}, u32[]{:S(2)}) collective-permute-start(f32[48,512]{1,0:T(8,128)S(1)} %add_add_fusion), channel_id=1, source_target_pairs={{0,3},{1,0},{2,1},{3,2},{4,7},{5,4},{6,5},{7,6},{8,11},{9,8},{10,9... | collective-permute-start | bytes 294920 | tf_op jit(solution)/shard_map/ppermute | solution.py:97
  219.0 16.6 %collective-permute-start.46 = (f32[48,512]{1,0:T(8,128)S(1)}, f32[48,512]{1,0:T(8,128)S(1)}, u32[]{:S(2)}, u32[]{:S(2)}) collective-permute-start(f32[48,512]{1,0:T(8,128)S(1)} %add_add_fusion), channel_id=1, source_target_pairs={{0,2},{1,3},{2,0},{3,1},{4,6},{5,7},{6,4},{7,5},{8,10},{9,11},{10,... | collective-permute-start | bytes 294920 | tf_op jit(solution)/shard_map/ppermute | solution.py:97
  219.0 16.6 %collective-permute-start.47 = (f32[48,512]{1,0:T(8,128)S(1)}, f32[48,512]{1,0:T(8,128)S(1)}, u32[]{:S(2)}, u32[]{:S(2)}) collective-permute-start(f32[48,512]{1,0:T(8,128)S(1)} %add_add_fusion), channel_id=1, source_target_pairs={{0,1},{1,2},{2,3},{3,0},{4,5},{5,6},{6,7},{7,4},{8,9},{9,10},{10,1... | collective-permute-start | bytes 294920 | tf_op jit(solution)/shard_map/ppermute | solution.py:97
  220.9 14.8 %collective-permute-start.27 = (f32[128,512]{1,0:T(8,128)S(1)}, f32[128,512]{1,0:T(8,128)S(1)}, u32[]{:S(2)}, u32[]{:S(2)}) collective-permute-start(f32[128,512]{1,0:T(8,128)S(1)} %pad_maximum_fusion.30), channel_id=1, source_target_pairs={{0,1},{1,2},{2,3},{3,0},{4,5},{5,6},{6,7},{7,4},{8,9},{9,10},{10,1... | collective-permute-start | bytes 786440 | tf_op jit(solution)/shard_map/ppermute | solution.py:97
  235.6 12.1 %collective-permute-start.8 = (f32[192,512]{1,0:T(8,128)S(1)}, f32[192,512]{1,0:T(8,128)S(1)}, u32[]{:S(2)}, u32[]{:S(2)}) collective-permute-start(f32[192,512]{1,0:T(8,128)S(1)} %pad_maximum_fusion.26), channel_id=1, source_target_pairs={{0,16},{8,24},{16,0},{24,8},{1,17},{9,25},{17,1},{25,9},{2,18},{10... | collective-permute-start | bytes 1179656 | tf_op jit(solution)/shard_map/ppermute | solution.py:92
  235.6 12.3 %collective-permute-start.18 = (f32[192,512]{1,0:T(8,128)S(1)}, f32[192,512]{1,0:T(8,128)S(1)}, u32[]{:S(2)}, u32[]{:S(2)}) collective-permute-start(f32[192,512]{1,0:T(8,128)S(1)} %pad_maximum_fusion.27), channel_id=1, source_target_pairs={{0,8},{8,0},{16,24},{24,16},{1,9},{9,1},{17,25},{25,17},{2,10},{10... | collective-permute-start | bytes 1179656 | tf_op jit(solution)/shard_map/ppermute | solution.py:92
  235.7 12.0 %collective-permute-start.58 = (f32[128,512]{1,0:T(8,128)S(1)}, f32[128,512]{1,0:T(8,128)S(1)}, u32[]{:S(2)}, u32[]{:S(2)}) collective-permute-start(f32[128,512]{1,0:T(8,128)S(1)} %collective-permute-done.57), channel_id=1, source_target_pairs={{0,1},{1,2},{2,3},{3,0},{4,5},{5,6},{6,7},{7,4},{8,9},{9,10},{10,1... | collective-permute-start | bytes 786440 | tf_op jit(solution)/shard_map/ppermute | solution.py:97
  235.8 12.0 %collective-permute-start.28 = (f32[128,512]{1,0:T(8,128)S(1)}, f32[128,512]{1,0:T(8,128)S(1)}, u32[]{:S(2)}, u32[]{:S(2)}) collective-permute-start(f32[128,512]{1,0:T(8,128)S(1)} %collective-permute-done.27), channel_id=1, source_target_pairs={{0,1},{1,2},{2,3},{3,0},{4,5},{5,6},{6,7},{7,4},{8,9},{9,10},{10,1... | collective-permute-start | bytes 786440 | tf_op jit(solution)/shard_map/ppermute | solution.py:97
  247.6 12.1 %collective-permute-start.38 = (f32[192,512]{1,0:T(8,128)S(1)}, f32[192,512]{1,0:T(8,128)S(1)}, u32[]{:S(2)}, u32[]{:S(2)}) collective-permute-start(f32[192,512]{1,0:T(8,128)S(1)} %pad_maximum_fusion.28), channel_id=1, source_target_pairs={{0,16},{8,24},{16,0},{24,8},{1,17},{9,25},{17,1},{25,9},{2,18},{10... | collective-permute-start | bytes 1179656 | tf_op jit(solution)/shard_map/ppermute | solution.py:92
  247.7 12.1 %collective-permute-start.48 = (f32[192,512]{1,0:T(8,128)S(1)}, f32[192,512]{1,0:T(8,128)S(1)}, u32[]{:S(2)}, u32[]{:S(2)}) collective-permute-start(f32[192,512]{1,0:T(8,128)S(1)} %pad_maximum_fusion.29), channel_id=1, source_target_pairs={{0,8},{8,0},{16,24},{24,16},{1,9},{9,1},{17,25},{25,17},{2,10},{10... | collective-permute-start | bytes 1179656 | tf_op jit(solution)/shard_map/ppermute | solution.py:92
  247.8 14.7 %collective-permute-start.59 = (f32[128,512]{1,0:T(8,128)S(1)}, f32[128,512]{1,0:T(8,128)S(1)}, u32[]{:S(2)}, u32[]{:S(2)}) collective-permute-start(f32[128,512]{1,0:T(8,128)S(1)} %collective-permute-done.58), channel_id=1, source_target_pairs={{0,1},{1,2},{2,3},{3,0},{4,5},{5,6},{6,7},{7,4},{8,9},{9,10},{10,1... | collective-permute-start | bytes 786440 | tf_op jit(solution)/shard_map/ppermute | solution.py:97
  247.9 16.8 %collective-permute-start.29 = (f32[128,512]{1,0:T(8,128)S(1)}, f32[128,512]{1,0:T(8,128)S(1)}, u32[]{:S(2)}, u32[]{:S(2)}) collective-permute-start(f32[128,512]{1,0:T(8,128)S(1)} %collective-permute-done.28), channel_id=1, source_target_pairs={{0,1},{1,2},{2,3},{3,0},{4,5},{5,6},{6,7},{7,4},{8,9},{9,10},{10,1... | collective-permute-start | bytes 786440 | tf_op jit(solution)/shard_map/ppermute | solution.py:97
  259.7 35.8 %collective-permute-start.9 = (f32[384,512]{1,0:T(8,128)S(1)}, f32[384,512]{1,0:T(8,128)S(1)}, u32[]{:S(2)}, u32[]{:S(2)}) collective-permute-start(f32[384,512]{1,0:T(8,128)S(1)} %pad_maximum_fusion.22), channel_id=1, source_target_pairs={{0,8},{8,0},{16,24},{24,16},{1,9},{9,1},{17,25},{25,17},{2,10},{10... | collective-permute-start | bytes 2359304 | tf_op jit(solution)/shard_map/ppermute | solution.py:92
  259.8 15.8 %collective-permute-start.19 = (f32[384,512]{1,0:T(8,128)S(1)}, f32[384,512]{1,0:T(8,128)S(1)}, u32[]{:S(2)}, u32[]{:S(2)}) collective-permute-start(f32[384,512]{1,0:T(8,128)S(1)} %pad_maximum_fusion.23), channel_id=1, source_target_pairs={{0,16},{8,24},{16,0},{24,8},{1,17},{9,25},{17,1},{25,9},{2,18},{10... | collective-permute-start | bytes 2359304 | tf_op jit(solution)/shard_map/ppermute | solution.py:92
  260.1 20.0 %collective-permute-start.39 = (f32[384,512]{1,0:T(8,128)S(1)}, f32[384,512]{1,0:T(8,128)S(1)}, u32[]{:S(2)}, u32[]{:S(2)}) collective-permute-start(f32[384,512]{1,0:T(8,128)S(1)} %pad_maximum_fusion.24), channel_id=1, source_target_pairs={{0,8},{8,0},{16,24},{24,16},{1,9},{9,1},{17,25},{25,17},{2,10},{10... | collective-permute-start | bytes 2359304 | tf_op jit(solution)/shard_map/ppermute | solution.py:92
  262.5 21.5 %collective-permute-start.49 = (f32[384,512]{1,0:T(8,128)S(1)}, f32[384,512]{1,0:T(8,128)S(1)}, u32[]{:S(2)}, u32[]{:S(2)}) collective-permute-start(f32[384,512]{1,0:T(8,128)S(1)} %pad_maximum_fusion.25), channel_id=1, source_target_pairs={{0,16},{8,24},{16,0},{24,8},{1,17},{9,25},{17,1},{25,9},{2,18},{10... | collective-permute-start | bytes 2359304 | tf_op jit(solution)/shard_map/ppermute | solution.py:92
  264.8 47.6 %collective-permute-start.76 = (f32[1,2,2,2,64,448]{5,4,2,1,0,3:T(8,128)S(1)}, f32[1,2,2,2,64,448]{5,4,2,1,0,3:T(8,128)S(1)}, u32[]{:S(2)}, u32[]{:S(2)}) collective-permute-start(f32[1,2,2,2,64,448]{5,4,2,1,0,3:T(8,128)S(1)} %fusion.51), channel_id=1, source_target_pairs={{0,16},{8,24},{16,0},{24,8},{1,17},{9,25},{17,1},{25,9},{2,18},{10... | collective-permute-start | bytes 2752520 | tf_op jit(solution)/shard_map/ppermute | solution.py:92
  302.3 10.7 %collective-permute-start.60 = (f32[512,512]{1,0:T(8,128)S(1)}, f32[512,512]{1,0:T(8,128)S(1)}, u32[]{:S(2)}, u32[]{:S(2)}) collective-permute-start(f32[512,512]{1,0:T(8,128)S(1)} %convolution_add_fusion.2), channel_id=1, source_target_pairs={{0,4},{4,0},{1,5},{5,1},{2,6},{6,2},{3,7},{7,3},{8,12},{12,8},{9,1... | collective-permute-start | bytes 3145736 | tf_op jit(solution)/shard_map/ppermute | solution.py:92
  311.8 100.8 %collective-permute-start.73 = (f32[512,512]{1,0:T(8,128)S(1)}, f32[512,512]{1,0:T(8,128)S(1)}, u32[]{:S(2)}, u32[]{:S(2)}) collective-permute-start(f32[512,512]{1,0:T(8,128)S(1)} %convolution_add_fusion), channel_id=1, source_target_pairs={{0,4},{4,0},{1,5},{5,1},{2,6},{6,2},{3,7},{7,3},{8,12},{12,8},{9,1... | collective-permute-start | bytes 3145736 | tf_op jit(solution)/shard_map/ppermute | solution.py:92
  403.4 15.2 %collective-permute-start.61 = (f32[2,2,1,64,896]{4,3,2,1,0:T(8,128)S(1)}, f32[2,2,1,64,896]{4,3,2,1,0:T(8,128)S(1)}, u32[]{:S(2)}, u32[]{:S(2)}) collective-permute-start(f32[2,2,1,64,896]{4,3,2,1,0:T(8,128)S(1)} %constant_dynamic-slice_fusion.13), channel_id=1, source_target_pairs={{0,4},{4,0},{1,5},{5,1},{2,6},{6,2},{3,7},{7,3},{8,12},{12,8},{9,1... | collective-permute-start | bytes 2752520 | tf_op jit(solution)/shard_map/ppermute | solution.py:92
  403.6 16.6 %collective-permute-start.64 = (f32[2,2,1,64,896]{4,3,2,1,0:T(8,128)S(1)}, f32[2,2,1,64,896]{4,3,2,1,0:T(8,128)S(1)}, u32[]{:S(2)}, u32[]{:S(2)}) collective-permute-start(f32[2,2,1,64,896]{4,3,2,1,0:T(8,128)S(1)} %constant_dynamic-slice_fusion.10), channel_id=1, source_target_pairs={{0,4},{4,0},{1,5},{5,1},{2,6},{6,2},{3,7},{7,3},{8,12},{12,8},{9,1... | collective-permute-start | bytes 2752520 | tf_op jit(solution)/shard_map/ppermute | solution.py:92
  404.2 16.8 %collective-permute-start.67 = (f32[2,2,1,64,896]{4,3,2,1,0:T(8,128)S(1)}, f32[2,2,1,64,896]{4,3,2,1,0:T(8,128)S(1)}, u32[]{:S(2)}, u32[]{:S(2)}) collective-permute-start(f32[2,2,1,64,896]{4,3,2,1,0:T(8,128)S(1)} %constant_dynamic-slice_fusion.7), channel_id=1, source_target_pairs={{0,4},{4,0},{1,5},{5,1},{2,6},{6,2},{3,7},{7,3},{8,12},{12,8},{9,1... | collective-permute-start | bytes 2752520 | tf_op jit(solution)/shard_map/ppermute | solution.py:92
  412.1 10.7 %collective-permute-start.70 = (f32[2,2,1,64,896]{4,3,2,1,0:T(8,128)S(1)}, f32[2,2,1,64,896]{4,3,2,1,0:T(8,128)S(1)}, u32[]{:S(2)}, u32[]{:S(2)}) collective-permute-start(f32[2,2,1,64,896]{4,3,2,1,0:T(8,128)S(1)} %constant_dynamic-slice_fusion.4), channel_id=1, source_target_pairs={{0,4},{4,0},{1,5},{5,1},{2,6},{6,2},{3,7},{7,3},{8,12},{12,8},{9,1... | collective-permute-start | bytes 2752520 | tf_op jit(solution)/shard_map/ppermute | solution.py:92
  418.8 13.4 %collective-permute-start.62 = (f32[1,2,1,64,896]{4,3,2,1,0:T(8,128)S(1)}, f32[1,2,1,64,896]{4,3,2,1,0:T(8,128)S(1)}, u32[]{:S(2)}, u32[]{:S(2)}) collective-permute-start(f32[1,2,1,64,896]{4,3,2,1,0:T(8,128)S(1)} %constant_dynamic-slice_fusion.12), channel_id=1, source_target_pairs={{0,16},{8,24},{16,0},{24,8},{1,17},{9,25},{17,1},{25,9},{2,18},{10... | collective-permute-start | bytes 1376264 | tf_op jit(solution)/shard_map/ppermute | solution.py:92
  420.4 13.4 %collective-permute-start.65 = (f32[2,1,1,64,896]{4,3,2,1,0:T(8,128)S(1)}, f32[2,1,1,64,896]{4,3,2,1,0:T(8,128)S(1)}, u32[]{:S(2)}, u32[]{:S(2)}) collective-permute-start(f32[2,1,1,64,896]{4,3,2,1,0:T(8,128)S(1)} %constant_dynamic-slice_fusion.9), channel_id=1, source_target_pairs={{0,8},{8,0},{16,24},{24,16},{1,9},{9,1},{17,25},{25,17},{2,10},{10... | collective-permute-start | bytes 1376264 | tf_op jit(solution)/shard_map/ppermute | solution.py:92
  421.2 20.8 %collective-permute-start.68 = (f32[1,2,1,64,896]{4,3,2,1,0:T(8,128)S(1)}, f32[1,2,1,64,896]{4,3,2,1,0:T(8,128)S(1)}, u32[]{:S(2)}, u32[]{:S(2)}) collective-permute-start(f32[1,2,1,64,896]{4,3,2,1,0:T(8,128)S(1)} %constant_dynamic-slice_fusion.6), channel_id=1, source_target_pairs={{0,16},{8,24},{16,0},{24,8},{1,17},{9,25},{17,1},{25,9},{2,18},{10... | collective-permute-start | bytes 1376264 | tf_op jit(solution)/shard_map/ppermute | solution.py:92
  422.9 20.7 %collective-permute-start.71 = (f32[2,1,1,64,896]{4,3,2,1,0:T(8,128)S(1)}, f32[2,1,1,64,896]{4,3,2,1,0:T(8,128)S(1)}, u32[]{:S(2)}, u32[]{:S(2)}) collective-permute-start(f32[2,1,1,64,896]{4,3,2,1,0:T(8,128)S(1)} %constant_dynamic-slice_fusion.3), channel_id=1, source_target_pairs={{0,8},{8,0},{16,24},{24,16},{1,9},{9,1},{17,25},{25,17},{2,10},{10... | collective-permute-start | bytes 1376264 | tf_op jit(solution)/shard_map/ppermute | solution.py:92
  424.0 42.1 %collective-permute-start.78 = (f32[2,1,2,2,64,448]{5,4,2,1,0,3:T(8,128)S(1)}, f32[2,1,2,2,64,448]{5,4,2,1,0,3:T(8,128)S(1)}, u32[]{:S(2)}, u32[]{:S(2)}) collective-permute-start(f32[2,1,2,2,64,448]{5,4,2,1,0,3:T(8,128)S(1)} %fusion.49), channel_id=1, source_target_pairs={{0,8},{8,0},{16,24},{24,16},{1,9},{9,1},{17,25},{25,17},{2,10},{10... | collective-permute-start | bytes 2752520 | tf_op jit(solution)/shard_map/ppermute | solution.py:92
  432.3 38.7 %collective-permute-start.63 = (f32[1,1,1,64,896]{4,3,2,1,0:T(8,128)S(1)}, f32[1,1,1,64,896]{4,3,2,1,0:T(8,128)S(1)}, u32[]{:S(2)}, u32[]{:S(2)}) collective-permute-start(f32[1,1,1,64,896]{4,3,2,1,0:T(8,128)S(1)} %constant_dynamic-slice_fusion.11), channel_id=1, source_target_pairs={{0,8},{8,0},{16,24},{24,16},{1,9},{9,1},{17,25},{25,17},{2,10},{10... | collective-permute-start | bytes 688136 | tf_op jit(solution)/shard_map/ppermute | solution.py:92
  433.9 37.2 %collective-permute-start.66 = (f32[1,1,1,64,896]{4,3,2,1,0:T(8,128)S(1)}, f32[1,1,1,64,896]{4,3,2,1,0:T(8,128)S(1)}, u32[]{:S(2)}, u32[]{:S(2)}) collective-permute-start(f32[1,1,1,64,896]{4,3,2,1,0:T(8,128)S(1)} %constant_dynamic-slice_fusion.8), channel_id=1, source_target_pairs={{0,16},{8,24},{16,0},{24,8},{1,17},{9,25},{17,1},{25,9},{2,18},{10... | collective-permute-start | bytes 688136 | tf_op jit(solution)/shard_map/ppermute | solution.py:92
  442.1 33.1 %collective-permute-start.69 = (f32[1,1,1,64,896]{4,3,2,1,0:T(8,128)S(1)}, f32[1,1,1,64,896]{4,3,2,1,0:T(8,128)S(1)}, u32[]{:S(2)}, u32[]{:S(2)}) collective-permute-start(f32[1,1,1,64,896]{4,3,2,1,0:T(8,128)S(1)} %constant_dynamic-slice_fusion.5), channel_id=1, source_target_pairs={{0,8},{8,0},{16,24},{24,16},{1,9},{9,1},{17,25},{25,17},{2,10},{10... | collective-permute-start | bytes 688136 | tf_op jit(solution)/shard_map/ppermute | solution.py:92
  443.7 32.2 %collective-permute-start.72 = (f32[1,1,1,64,896]{4,3,2,1,0:T(8,128)S(1)}, f32[1,1,1,64,896]{4,3,2,1,0:T(8,128)S(1)}, u32[]{:S(2)}, u32[]{:S(2)}) collective-permute-start(f32[1,1,1,64,896]{4,3,2,1,0:T(8,128)S(1)} %constant_dynamic-slice_fusion.2), channel_id=1, source_target_pairs={{0,16},{8,24},{16,0},{24,8},{1,17},{9,25},{17,1},{25,9},{2,18},{10... | collective-permute-start | bytes 688136 | tf_op jit(solution)/shard_map/ppermute | solution.py:92
  466.5 23.8 %collective-permute-start.79 = (f32[1,2,2,2,64,448]{5,4,2,1,0,3:T(8,128)S(1)}, f32[1,2,2,2,64,448]{5,4,2,1,0,3:T(8,128)S(1)}, u32[]{:S(2)}, u32[]{:S(2)}) collective-permute-start(f32[1,2,2,2,64,448]{5,4,2,1,0,3:T(8,128)S(1)} %fusion.47), channel_id=1, source_target_pairs={{0,16},{8,24},{16,0},{24,8},{1,17},{9,25},{17,1},{25,9},{2,18},{10... | collective-permute-start | bytes 2752520 | tf_op jit(solution)/shard_map/ppermute | solution.py:92
  (33 other events, 229.6 us)

commit v2 on v0

v2 whole, which is shorter than its diff:
```python
import functools

import jax
import jax.numpy as jnp
from jax import lax
from jax.experimental import pallas as pl
from jax.experimental.pallas import tpu as pltpu
from jax.sharding import PartitionSpec as P

highest = lax.Precision.HIGHEST
BLOCK = 128


def contract(a, b, a_dim, b_dim):
    return lax.dot_general(
        a, b, (((a_dim,), (b_dim,)), ((), ())), precision=highest, preferred_element_type=jnp.float32
    )


def eliminate(block, inverse_ref):
    groups = BLOCK // 8
    left = [block[8 * g : 8 * g + 8] for g in range(groups)]
    row_ids = lax.broadcasted_iota(jnp.int32, (8, BLOCK), 0)
    lane_ids = lax.broadcasted_iota(jnp.int32, (8, BLOCK), 1)
    right = [(lane_ids == row_ids + 8 * g).astype(jnp.float32) for g in range(groups)]
    for own in range(groups):
        at = 8 * own
        spread = {
            g: [jnp.broadcast_to(left[g][:, at + k : at + k + 1], (8, BLOCK)) for k in range(8)]
            for g in range(own, groups)
        }
        scaled = []
        for i in range(8):
            pivot = spread[own][i][i : i + 1]
            recip = 1.0 / pivot
            row, inv_row = left[own][i : i + 1], right[own][i : i + 1]
            inverse_ref[at + i : at + i + 1, :] = inv_row * lax.rsqrt(pivot)
            row, inv_row = row * recip, inv_row * recip
            scaled.append((row, inv_row))
            if i == 7:
                continue
            ratio = {k: spread[own][k][i : i + 1] * recip for k in range(i + 1, 8)}
            below = jnp.where(row_ids > i, spread[own][i], 0.0)
            left[own] = left[own] - below * row
            right[own] = right[own] - below * inv_row
            for g in range(own, groups):
                column = below if g == own else spread[g][i]
                for k in range(i + 1, 8):
                    spread[g][k] = spread[g][k] - column * ratio[k]
        for g in range(own + 1, groups):
            for i, (row, inv_row) in enumerate(scaled):
                left[g] = left[g] - spread[g][i] * row
                right[g] = right[g] - spread[g][i] * inv_row


def cholesky_kernel(index, work_in, rest_in, inverse_in, work_ref, rest_ref, inverse_ref, diag_ref):
    size = work_ref.shape[0]
    at = slice(index * BLOCK, (index + 1) * BLOCK)
    if index == 0:
        rows = lax.broadcasted_iota(jnp.int32, (size, size), 0)
        cols = lax.broadcasted_iota(jnp.int32, (size, size), 1)
        rest = (rows == cols).astype(jnp.float32)
    else:
        rest = rest_in[...]
        inverse_ref[...] = inverse_in[...]
    eliminate(work_in[at, at], diag_ref)
    diag = diag_ref[...]
    done = contract(diag, rest[at], 1, 0)
    inverse_ref[at, :] = done
    if index < size // BLOCK - 1:
        below = slice((index + 1) * BLOCK, size)
        factor = contract(work_in[below, at], diag, 1, 1)
        work_ref[below, below] = work_in[below, below] - contract(factor, factor, 1, 1)
        rest_ref[below, :] = rest[below] - contract(factor, done, 1, 0)


def cholesky_step(index, work, rest, inverse):
    size = work.shape[0]
    whole = jax.ShapeDtypeStruct((size, size), jnp.float32)
    spec = pl.BlockSpec(memory_space=pltpu.VMEM)
    return pl.pallas_call(
        functools.partial(cholesky_kernel, index),
        out_shape=[whole] * 3,
        in_specs=[spec] * 3,
        out_specs=[spec] * 3,
        scratch_shapes=[pltpu.VMEM((BLOCK, BLOCK), jnp.float32)],
        compiler_params=pltpu.CompilerParams(vmem_limit_bytes=32 << 20),
        cost_estimate=pl.CostEstimate(flops=7_000_000_000, bytes_accessed=6_000_000, transcendentals=0),
    )(work, rest, inverse)


def join(*values):
    return lax.optimization_barrier(values)


def bits_of(axis):
    return lax.axis_size(axis).bit_length() - 1


def own_bit(axis, bit):
    return (lax.axis_index(axis) >> bit) & 1


def flipped(value, axis, mask):
    return lax.ppermute(value, axis, [(i, i ^ mask) for i in range(lax.axis_size(axis))])


def swap(value, axis, bit):
    return flipped(value, axis, 1 << bit)


def shifted(value, axis):
    size = lax.axis_size(axis)
    return lax.ppermute(value, axis, [(i, (i + 1) % size) for i in range(size)])


def split_half(value, axis, bit, dim=0):
    half = value.shape[dim] // 2
    me = own_bit(axis, bit)
    sent = lax.dynamic_slice_in_dim(value, (1 - me) * half, half, dim)
    kept = lax.dynamic_slice_in_dim(value, me * half, half, dim)
    return sent, kept


def in_order(value, other, axis, bit):
    first = own_bit(axis, bit) == 0
    return jnp.concatenate([jnp.where(first, value, other), jnp.where(first, other, value)], 0)


def scatter_sends(value, axis):
    me = lax.axis_index(axis)
    kept = lax.dynamic_index_in_dim(value, me, 0, keepdims=False)
    return kept, [
        lax.dynamic_index_in_dim(value, me ^ mask, 0, keepdims=False)
        for mask in range(1, lax.axis_size(axis))
    ]


def flip_all(sends, axis):
    return [flipped(send, axis, mask) for mask, send in enumerate(sends, 1)]


def copies_to_all(value, axis):
    return flip_all([value] * (lax.axis_size(axis) - 1), axis)


def placed(value, others, axis):
    me = lax.axis_index(axis)
    blocks = [value] + list(others)
    return jnp.stack(
        [lax.select_n(me, *[blocks[p ^ i] for i in range(len(blocks))]) for p in range(len(blocks))]
    )


def ring_placed(blocks, axis):
    me = lax.axis_index(axis)
    size = len(blocks)
    return jnp.concatenate(
        [lax.select_n(me, *[blocks[(i - p) % size] for i in range(size)]) for p in range(size)], 0
    )


class Sum:
    def __init__(self, value):
        self.value = value
        self.steps = [("half", b) for b in range(bits_of("row"))]
        self.steps += [("scatter", "dp"), ("scatter", "col"), ("gather", "col"), ("gather", "dp")]
        self.steps += [("double", b) for b in reversed(range(bits_of("row")))]

    def start(self):
        kind, what = self.steps[0]
        if kind == "half":
            sent, self.kept = split_half(self.value, "row", what)
            self.got = [swap(sent, "row", what)]
        elif kind == "double":
            self.got = [swap(self.value, "row", what)]
        elif kind == "scatter":
            size = lax.axis_size(what)
            self.kept, sends = scatter_sends(self.value.reshape((size, -1) + self.value.shape[1:]), what)
            self.got = flip_all(sends, what)
        else:
            self.got = copies_to_all(self.value, what)

    def finish(self):
        kind, what = self.steps.pop(0)
        if kind in ("half", "scatter"):
            self.value = self.kept + sum(self.got)
        elif kind == "double":
            self.value = in_order(self.value, self.got[0], "row", what)
        else:
            self.value = placed(self.value, self.got, what).reshape((-1,) + self.value.shape[1:])


class Exchange:
    def __init__(self, value):
        self.tail = value.shape[1:]
        bits = [("dp", b) for b in reversed(range(bits_of("dp")))]
        self.bits = bits + [("row", b) for b in reversed(range(bits_of("row")))]
        self.value = value.reshape((2,) * len(self.bits) + self.tail)
        self.left = list(range(len(self.bits)))

    def start(self):
        place = self.left[-1]
        axis, bit = self.bits[place]
        me = own_bit(axis, bit)
        sent = lax.dynamic_index_in_dim(self.value, 1 - me, place, keepdims=True)
        self.kept = lax.dynamic_index_in_dim(self.value, me, place, keepdims=True)
        self.got = swap(sent, axis, bit)

    def finish(self):
        place = self.left.pop()
        me = own_bit(*self.bits[place])
        kept, got = self.kept, self.got
        self.value = jnp.concatenate([jnp.where(me == 0, kept, got), jnp.where(me == 0, got, kept)], place)

    def result(self):
        return self.value.reshape((1 << len(self.bits),) + self.tail)


def local(gradients, test_matrix, old_basis, first_moment, second_moment):
    grad = gradients[0]
    rows, cols = grad.shape
    rank_dev = first_moment.shape[0]
    dp_size, row_size, col_size = (lax.axis_size(a) for a in ("dp", "row", "col"))
    group = dp_size * row_size
    rank = rank_dev * group
    wide = cols // group
    dp_bits, row_bits = bits_of("dp"), bits_of("row")

    moments = jnp.stack([first_moment, second_moment])
    moments = moments.reshape(2, rank_dev, group, wide).transpose(2, 0, 1, 3)
    turn_in = Exchange(moments)

    test_values = test_matrix.astype(jnp.bfloat16)
    unit = rows // 32
    size_c, size_a, size_b = 10 * unit, 11 * unit, 11 * unit
    range_c, range_a, range_b = (0, size_c), (size_c, size_a), (size_c + size_a, size_b)

    def sketch(span):
        return jnp.dot(
            grad[span[0] : span[0] + span[1]], test_values, preferred_element_type=jnp.float32
        )

    low, high = 0, dp_bits - 1
    me_col = lax.axis_index("col")
    part_c = sketch(range_c)

    def block_c(back):
        return lax.dynamic_slice_in_dim(
            part_c, (me_col + 2 * col_size - back) % col_size * (size_c // col_size), size_c // col_size, 0
        )

    ring = shifted(block_c(1), "col")
    part_a, kept_a = split_half(sketch(range_a), "dp", low)
    got_a = swap(part_a, "dp", low)
    part_b, kept_b = split_half(sketch(range_b), "dp", high)
    got_b = swap(part_b, "dp", high)
    turn_in.start()
    ring, turn_in.got = join(ring, turn_in.got)
    turn_in.finish()
    ring = shifted(ring + block_c(2), "col")
    ring, got_a, got_b = join(ring, got_a, got_b)
    part_a, kept_a = split_half(kept_a + got_a, "dp", high)
    part_b, kept_b = split_half(kept_b + got_b, "dp", low)
    ring = shifted(ring + block_c(3), "col")
    got_a = swap(part_a, "dp", high)
    got_b = swap(part_b, "dp", low)
    ring, got_a, got_b = join(ring, got_a, got_b)
    part_ab = jnp.concatenate(
        [(kept_a + got_a).reshape(col_size, -1, rank), (kept_b + got_b).reshape(col_size, -1, rank)], 1
    )
    rows_ab = part_ab.shape[1]
    part_c = (ring + block_c(4)).reshape(dp_size, -1, rank)
    kept_ab, sends_ab = scatter_sends(part_ab, "col")
    kept_c, sends_c = scatter_sends(part_c, "dp")
    got_ab = flip_all(sends_ab, "col")
    got_c = flip_all(sends_c, "dp")
    turn_in.start()
    got_ab, got_c, turn_in.got = join(got_ab, got_c, turn_in.got)
    turn_in.finish()
    own_ab = kept_ab + sum(got_ab)
    own_c = kept_c + sum(got_c)

    own = jnp.concatenate([own_ab, own_c], 0)
    gram = Sum(contract(own, own, 0, 0))
    half = rows_ab // 2
    me_dp = lax.axis_index("dp")
    low_bit, high_bit = me_dp & 1, me_dp >> high & 1
    start_a = range_a[0] + low_bit * (size_a // 2) + high_bit * (size_a // 4) + me_col * half
    start_b = range_b[0] + high_bit * (size_b // 2) + low_bit * (size_b // 4) + me_col * half
    start_c = me_col * (size_c // col_size) + me_dp * (size_c // col_size // dp_size)
    own_old = jnp.concatenate(
        [
            lax.dynamic_slice_in_dim(old_basis, start_a, half, 0),
            lax.dynamic_slice_in_dim(old_basis, start_b, half, 0),
            lax.dynamic_slice_in_dim(old_basis, start_c, own_c.shape[0], 0),
        ],
        0,
    )
    inner = Sum(contract(own, own_old, 0, 0))

    for _ in range(row_bits):
        gram.start()
        (gram.got,) = join(gram.got)
        gram.finish()
    gram.start()
    got_ab = copies_to_all(own_ab, "col")
    got_c = copies_to_all(own_c, "dp")
    (gram.got,) = join(gram.got)
    gram.finish()
    gram.start()
    (gram.got,) = join(gram.got)
    gram.finish()
    gram.start()
    gram.got, got_ab, got_c, inner.value = join(gram.got, got_ab, got_c, inner.value)
    gram.finish()
    whole_ab = placed(own_ab, got_ab, "col")
    part_a = whole_ab[:, :half].reshape(-1, rank)
    part_b = whole_ab[:, half:].reshape(-1, rank)
    ring_c = [placed(own_c, got_c, "dp").reshape(-1, rank)]
    gram.start()
    got_a = swap(part_a, "dp", high)
    got_b = swap(part_b, "dp", low)
    ring_c.append(shifted(ring_c[0], "col"))
    (gram.got,) = join(gram.got)
    gram.finish()
    for _ in range(row_bits):
        gram.start()
        inner.start()
        gram.got, inner.got = join(gram.got, inner.got)
        gram.finish()
        inner.finish()
    work = gram.value
    rest = jnp.zeros_like(work)
    inverse = rest
    inner.start()
    work, rest, inverse = cholesky_step(0, work, rest, inverse)
    work, inner.got, got_a, got_b, ring_c[1] = join(work, inner.got, got_a, got_b, ring_c[1])
    inner.finish()
    part_a = in_order(part_a, got_a, "dp", high)
    part_b = in_order(part_b, got_b, "dp", low)
    got_a = swap(part_a, "dp", low)
    got_b = swap(part_b, "dp", high)
    ring_c.append(shifted(ring_c[1], "col"))
    inner.start()
    work, rest, inverse = cholesky_step(1, work, rest, inverse)
    work, inner.got, ring_c[2] = join(work, inner.got, ring_c[2])
    inner.finish()
    ring_c.append(shifted(ring_c[2], "col"))
    inner.start()
    work, rest, inverse = cholesky_step(2, work, rest, inverse)
    work, inner.got = join(work, inner.got)
    inner.finish()
    inner.start()
    work, rest, inverse = cholesky_step(3, work, rest, inverse)
    inverse, inner.got, got_a, got_b, ring_c[3] = join(inverse, inner.got, got_a, got_b, ring_c[3])
    inner.finish()

    def basis(part):
        return contract(part, inverse, 1, 1).astype(jnp.bfloat16)

    basis_low = jnp.concatenate(
        [
            ring_placed([basis(part) for part in ring_c], "col"),
            in_order(basis(part_a), basis(got_a), "dp", low),
            in_order(basis(part_b), basis(got_b), "dp", high),
        ],
        0,
    )

    chunks = 4
    chunk = cols // chunks

    def project(c):
        value = lax.dot_general(
            basis_low,
            grad[:, c * chunk : (c + 1) * chunk],
            (((0,), (0,)), ((), ())),
            preferred_element_type=jnp.float32,
        )
        return value.reshape((dp_size,) + (2,) * row_bits + (rank_dev, chunk))

    while len(turn_in.left) > 0:
        turn_in.start()
        inner_steps = len(inner.steps) > 0
        if inner_steps:
            inner.start()
            turn_in.got, inner.got = join(turn_in.got, inner.got)
            inner.finish()
        else:
            (turn_in.got,) = join(turn_in.got)
        turn_in.finish()
    while len(inner.steps) > 0:
        inner.start()
        (inner.got,) = join(inner.got)
        inner.finish()
    correlation = contract(inverse, inner.value, 1, 0)
    moments = turn_in.result().transpose(1, 0, 2, 3).reshape(2, rank, wide)
    turned = jnp.stack(
        [contract(correlation, moments[0], 1, 0), contract(correlation * correlation, moments[1], 1, 0)]
    )
    turn_out = Exchange(turned.reshape(2, group, rank_dev, wide).transpose(1, 0, 2, 3))

    values = [None] * chunks
    gots = [None] * chunks
    kepts = [None] * chunks
    values[0] = project(0)
    for r in range(chunks + 2):
        waits = []
        if 0 <= r - 1 < chunks:
            c = r - 1
            kepts[c], sends = scatter_sends(values[c], "dp")
            gots[c] = flip_all(sends, "dp")
        if r < chunks:
            value = values[r]
            for bit in range(row_bits):
                sent, kept = split_half(value, "row", bit, row_bits - bit)
                value = kept + swap(sent, "row", bit)
            values[r] = value
        if r + 1 < chunks:
            values[r + 1] = project(r + 1)
        if len(turn_out.left) > 0:
            turn_out.start()
        flat = (values, gots, turn_out.got)
        values, gots, turn_out.got = join(*flat)
        if len(turn_out.left) > 0:
            turn_out.finish()
        if 0 <= r - 1 < chunks:
            values[r - 1] = kepts[r - 1] + sum(gots[r - 1])
            gots[r - 1] = None
    while len(turn_out.left) > 0:
        turn_out.start()
        turn_out.finish()
    projected = jnp.concatenate([value.reshape(rank_dev, chunk) for value in values], 1)
    turned = turn_out.result().transpose(1, 2, 0, 3).reshape(2, rank_dev, cols)
    first_new = 0.9 * turned[0] + 0.1 * projected
    second_new = 0.95 * turned[1] + 0.05 * projected * projected
    return (projected, first_new, second_new)


def solution(mesh):
    in_specs = (
        P("dp", "row", "col"),
        P("col", None),
        P("row", None),
        P(("dp", "row"), "col"),
        P(("dp", "row"), "col"),
    )
    out_specs = (P(("dp", "row"), "col"), P(("dp", "row"), "col"), P(("dp", "row"), "col"))
    return jax.shard_map(local, mesh=mesh, in_specs=in_specs, out_specs=out_specs, check_vma=False)
```

time: 783 us -> 443 us (0.57)
  waiting for transfers between devices: 400 us -> 180 us
  other arithmetic: 199 us -> 33.5 us
  starting transfers between devices: 0.67 us -> 85.7 us
  matrix products: 143 us -> 87.1 us
  between operations: 21.3 us -> 2.16 us
  Pallas kernels: 0 us -> 18.2 us
  local copies, waits for them, and re-layouts: 12.4 us -> 28.2 us
    psum x2 -> x0, waiting for transfers between devices: 259 us -> none  [the longest x1 259 us: local(): sketch = lax.psum(partial_value, ('dp', 'col'))]
    another operation x32 -> x13, other arithmetic: 198 us -> 1.97 us  [the longest x12 1.7 us: placed(): jnp.stack([lax.select_n(me, *[blocks[p ^ i] for i in range(len(blocks))])...]
    ppermute x1 -> x76, waiting for transfers between devices: 0.73 us -> 180 us  [the longest x70 150 us: flipped(): lax.ppermute(value, axis, [(i, i ^ mask) for i in range(lax.axis_size(axi...]
    ppermute x1 -> x76, starting transfers between devices: 0.25 us -> 85.7 us  [the longest x70 78.6 us: flipped(): lax.ppermute(value, axis, [(i, i ^ mask) for i in range(lax.axis_size(axi...]
    reduce_scatter x1 -> x0, waiting for transfers between devices: 70.6 us -> none  [local(): lax.psum_scatter(lax.dot_general(basis_low, replica_grad, (((0,), (0,)),...]
    all_gather x2 -> x0, waiting for transfers between devices: 68.5 us -> none  [the longest x1 42.9 us: local(): lax.all_gather(first_moment, ('dp', 'row'), axis=0, tiled=True)]
    another operation x19 -> x0, matrix products: 41.6 us -> none  [the longest x7 37.7 us: basis_from(): jax.scipy.linalg.solve_triangular(lower_factor, sketch_part.T, lower=True)]
    add x0 -> x24, other arithmetic: none -> 23.8 us  [the longest x4 2.8 us: local(): value = kept + swap(sent, 'row', bit)]
  transfers between devices with their start and end apart: 6 -> 76, of which waited for: 5 -> 33; matrix products, arithmetic and copies ran while one was open for 5% -> 28% of each run, Pallas kernels for 0% -> 4%
where the time goes in v2:
time: 443 us; the launch traced here: 434 us
  waiting for transfers between devices  180 us (41%)
  matrix products  87.1 us (20%)
  starting transfers between devices  85.7 us (19%)
  other arithmetic  33.5 us (8%)
  local copies, waits for them, and re-layouts  28.2 us (6%)
  Pallas kernels  18.2 us (4%)
    ppermute x70, waiting for transfers between devices, flipped(): lax.ppermute(value, axis, [(i, i ^ mask) for i in range(lax.axis_size(axi...  150 us
    ppermute x70, starting transfers between devices, flipped(): lax.ppermute(value, axis, [(i, i ^ mask) for i in range(lax.axis_size(axi...  78.6 us
    dot_general x3, matrix products, sketch(): jnp.dot(grad[span[0]:span[0] + span[1]], test_values, preferred_element_t...  31.4 us
    dot_general x4, matrix products, project(): lax.dot_general(basis_low, grad[:, c * chunk:(c + 1) * chunk], (((0,), (0...  31 us
    ppermute x6, waiting for transfers between devices, shifted(): return lax.ppermute(value, axis, [(i, (i + 1) % size) for i in range(size)])  29.9 us
    dot_general x13, matrix products, contract(): lax.dot_general(a, b, (((a_dim,), (b_dim,)), ((), ())), precision=highest...  24.7 us
    pallas_call x4, Pallas kernels, cholesky_step(): pl.pallas_call(functools.partial(cholesky_kernel, index), out_shape=[whol...  18.2 us
  transfers between devices with their start and end apart: 76, of which 33 were waited for; matrix products, arithmetic and copies ran while one was open for 28% of the time, Pallas kernels for 4%

profile of v2, /device:TPU:0, one launch (start us, length us, event | category | flops | bytes accessed | tf_op | source)
XLA Modules:
  0.0 434.5 jit_solution(8485858977516536455)
XLA Ops:
  0.6 1.7 stack.104
  6.0 9.6 %fusion.6 = f32[1280,512]{1,0:T(8,128)S(1)} fusion(bf16[1,4096,3584]{2,1,0:T(8,128)(2,1)} %param.5, s32[3584,512]{1,0:T(8,128)} %param.6), kind=kOutput, calls=%fused_computation.6 | convolution fusion | flops 4699455488 | bytes 19136512 | tf_op jit(solution)/shard_map/dot_general | solution.py:240
  17.3 2.6 collective-permute-start
  19.9 10.2 %fusion.2 = f32[1408,512]{1,0:T(8,128)S(1)} fusion(bf16[1,4096,3584]{2,1,0:T(8,128)(2,1)} %param.5, s32[3584,512]{1,0:T(8,128)} %param.6), kind=kOutput, calls=%fused_computation.2 | convolution fusion | flops 5169217536 | bytes 20316160 | tf_op jit(solution)/shard_map/dot_general | solution.py:240
  32.8 11.7 %fusion = f32[1408,512]{1,0:T(8,128)} fusion(bf16[1,4096,3584]{2,1,0:T(8,128)(2,1)} %param.5, s32[3584,512]{1,0:T(8,128)} %param.6), kind=kOutput, calls=%fused_computation | convolution fusion | flops 5169217536 | bytes 20316160 | tf_op jit(solution)/shard_map/dot_general | solution.py:240
  44.5 2.6 constant_dynamic-slice_fusion.12
  48.6 2.0 dynamic-slice_add_fusion.10
  52.2 13.2 %collective-permute-done.3 = f32[704,512]{1,0:T(8,128)} collective-permute-done((f32[704,512]{1,0:T(8,128)}, f32[704,512]{1,0:T(8,128)}, u32[]{:S(2)}, u32[]{:S(2)}) %collective-permute-start.3) | collective-permute-done | bytes 1441824 | tf_op jit(solution)/shard_map/ppermute | solution.py:105
  65.4 15.5 %collective-permute-done.4 = f32[704,512]{1,0:T(8,128)} collective-permute-done((f32[704,512]{1,0:T(8,128)}, f32[704,512]{1,0:T(8,128)}, u32[]{:S(2)}, u32[]{:S(2)}) %collective-permute-start.4) | collective-permute-done | bytes 1441824 | tf_op jit(solution)/shard_map/ppermute | solution.py:105
  80.8 2.1 dynamic-slice_add_fusion
  88.8 2.0 dynamic-slice_add_fusion.9
  90.8 1.7 collective-permute-start.5
  92.5 1.9 dynamic-slice_select_fusion.2
  96.1 12.0 %collective-permute-done.5 = f32[320,512]{1,0:T(8,128)S(1)} collective-permute-done((f32[320,512]{1,0:T(8,128)}, f32[320,512]{1,0:T(8,128)S(1)}, u32[]{:S(2)}, u32[]{:S(2)}) %collective-permute-start.5) | collective-permute-done | bytes 655392 | tf_op jit(solution)/shard_map/ppermute | solution.py:114
  113.0 3.0 collective-permute-start.9
  120.3 5.2 %collective-permute-done.14 = f32[2,1,2,2,64,448]{5,4,2,1,0,3:T(8,128)S(1)} collective-permute-done((f32[2,1,2,2,64,448]{5,4,2,1,0,3:T(8,128)S(1)}, f32[2,1,2,2,64,448]{5,4,2,1,0,3:T(8,128)S(1)}, u32[]{:S(2)}, u32[]{:S(2)}) %collective-permute-start.14) | collective-permute-done | bytes 917536 | tf_op jit(solution)/shard_map/ppermute | solution.py:105
  129.0 3.2 collective-permute-done.12
  132.1 1.9 collective-permute-done.11
  134.1 8.4 %collective-permute-done.9 = f32[176,512]{1,0:T(8,128)} collective-permute-done((f32[176,512]{1,0:T(8,128)}, f32[176,512]{1,0:T(8,128)}, u32[]{:S(2)}, u32[]{:S(2)}) %collective-permute-start.9) | collective-permute-done | bytes 360480 | tf_op jit(solution)/shard_map/ppermute | solution.py:105
  143.8 2.0 bitcast_add_fusion.4
  145.8 2.0 fusion.36
  148.7 2.2 collective-permute-done.15
  161.2 2.5 collective-permute-start.27
  164.9 2.2 collective-permute-start.21
  167.1 2.3 collective-permute-start.19
  169.7 4.1 collective-permute-done.21
  175.4 4.8 %collective-permute-done.20 = f32[16,512]{1,0:T(8,128)S(1)} collective-permute-done((f32[16,512]{1,0:T(8,128)S(1)}, f32[16,512]{1,0:T(8,128)S(1)}, u32[]{:S(2)}, u32[]{:S(2)}) %collective-permute-start.20) | collective-permute-done | bytes 32800 | tf_op jit(solution)/shard_map/ppermute | solution.py:105
  182.6 2.5 collective-permute-start.24
  185.7 1.7 collective-permute-start.23
  187.6 1.9 fusion.30
  189.6 9.0 %collective-permute-done.26 = f32[176,512]{1,0:T(8,128)S(1)} collective-permute-done((f32[176,512]{1,0:T(8,128)S(1)}, f32[176,512]{1,0:T(8,128)S(1)}, u32[]{:S(2)}, u32[]{:S(2)}) %collective-permute-start.26) | collective-permute-done | bytes 360480 | tf_op jit(solution)/shard_map/ppermute | solution.py:105
  200.0 2.3 collective-permute-start.33
  206.3 2.6 collective-permute-done.32
  215.2 8.5 %collective-permute-done.41 = f32[320,512]{1,0:T(8,128)S(1)} collective-permute-done((f32[320,512]{1,0:T(8,128)S(1)}, f32[320,512]{1,0:T(8,128)S(1)}, u32[]{:S(2)}, u32[]{:S(2)}) %collective-permute-start.41) | collective-permute-done | bytes 655392 | tf_op jit(solution)/shard_map/ppermute | solution.py:114
  225.4 5.3 %shard_map.76 = (f32[512,512]{1,0:T(8,128)S(1)}, f32[512,512]{1,0:T(8,128)S(1)}, f32[512,512]{1,0:T(8,128)S(1)}) custom-call(f32[512,512]{1,0:T(8,128)S(1)} %pad_maximum_fusion.6.work_in, f32[512,512]{1,0:T(8,128)S(1)} %broadcast_in_dim.3.rest_in.inverse_in, f32[512,512]{1,0:T(8,128)S(1)} %broadcast_in_dim.3.rest_in.inverse_in), custom_call_target="tpu_custom_call" | custom-call | flops 7000000000 | bytes 6000000 | tf_op jit(solution)/shard_map/pallas_call | solution.py:81
  230.7 2.5 collective-permute-done.38
  236.7 3.0 collective-permute-start.42
  241.2 4.9 %shard_map.77 = (f32[512,512]{1,0:T(8,128)S(1)}, f32[512,512]{1,0:T(8,128)S(1)}, f32[512,512]{1,0:T(8,128)S(1)}) custom-call(f32[512,512]{1,0:T(8,128)S(1)} %get-tuple-element.142.work_in, f32[512,512]{1,0:T(8,128)S(1)} %get-tuple-element.143.rest_in, f32[512,512]{1,0:T(8,128)S(1)} %get-tuple-element.144.inverse_in), custom_call_target="tpu_custom_call" | custom-call | flops 7000000000 | bytes 6000000 | tf_op jit(solution)/shard_map/pallas_call | solution.py:81
  247.7 9.4 %collective-permute-done.45 = f32[320,512]{1,0:T(8,128)S(1)} collective-permute-done((f32[320,512]{1,0:T(8,128)S(1)}, f32[320,512]{1,0:T(8,128)S(1)}, u32[]{:S(2)}, u32[]{:S(2)}) %collective-permute-start.45) | collective-permute-done | bytes 655392 | tf_op jit(solution)/shard_map/ppermute | solution.py:114
  257.5 4.1 collective-permute-start.46
  261.6 4.5 %shard_map.78 = (f32[512,512]{1,0:T(8,128)S(1)}, f32[512,512]{1,0:T(8,128)S(1)}, f32[512,512]{1,0:T(8,128)S(1)}) custom-call(f32[512,512]{1,0:T(8,128)S(1)} %get-tuple-element.150.work_in, f32[512,512]{1,0:T(8,128)S(1)} %get-tuple-element.151.rest_in, f32[512,512]{1,0:T(8,128)S(1)} %get-tuple-element.152.inverse_in), custom_call_target="tpu_custom_call" | custom-call | flops 7000000000 | bytes 6000000 | tf_op jit(solution)/shard_map/pallas_call | solution.py:81
  269.0 6.5 %collective-permute-done.51 = f32[64,512]{1,0:T(8,128)S(1)} collective-permute-done((f32[64,512]{1,0:T(8,128)S(1)}, f32[64,512]{1,0:T(8,128)S(1)}, u32[]{:S(2)}, u32[]{:S(2)}) %collective-permute-start.51) | collective-permute-done | bytes 131104 | tf_op jit(solution)/shard_map/ppermute | solution.py:105
  277.1 3.6 shard_map.79
  280.7 3.0 collective-permute-done.50
  289.1 2.5 convolution_convert_fusion.2
  291.6 2.6 convolution_convert_fusion
  296.1 2.5 select_dynamic-update-slice_fusion.3
  298.8 2.5 select_dynamic-update-slice_fusion.1
  301.5 8.2 %fusion.15 = f32[512,896]{1,0:T(8,128)S(1)} fusion(bf16[4096,512]{1,0:T(8,128)(2,1)S(1)} %select_dynamic-update-slice_fusion, bf16[4096,3584]{1,0:T(8,128)(2,1)} %bitcast.279), kind=kOutput, calls=%fused_computation.15 | convolution fusion | flops 3758096384 | bytes 13369344 | tf_op jit(solution)/shard_map/dot_general | solution.py:375
  311.3 1.9 fusion.54
  313.2 1.9 convolution_bitcast_fusion
  315.0 1.9 convolution_bitcast_fusion.1
  317.3 7.7 %fusion.13 = f32[512,896]{1,0:T(8,128)S(1)} fusion(bf16[4096,512]{1,0:T(8,128)(2,1)S(1)} %select_dynamic-update-slice_fusion, bf16[4096,3584]{1,0:T(8,128)(2,1)} %bitcast.280), kind=kOutput, calls=%fused_computation.13 | convolution fusion | flops 3758096384 | bytes 13369344 | tf_op jit(solution)/shard_map/dot_general | solution.py:375
  326.8 7.6 %fusion.11 = f32[512,896]{1,0:T(8,128)S(1)} fusion(bf16[4096,512]{1,0:T(8,128)(2,1)S(1)} %select_dynamic-update-slice_fusion, bf16[4096,3584]{1,0:T(8,128)(2,1)} %bitcast.281), kind=kOutput, calls=%fused_computation.11 | convolution fusion | flops 3758096384 | bytes 13369344 | tf_op jit(solution)/shard_map/dot_general | solution.py:375
  338.1 19.1 %collective-permute-done.62 = f32[1,64,896]{2,1,0:T(8,128)S(1)} collective-permute-done((f32[1,64,896]{2,1,0:T(8,128)S(1)}, f32[1,64,896]{2,1,0:T(8,128)S(1)}, u32[]{:S(2)}, u32[]{:S(2)}) %collective-permute-start.62) | collective-permute-done | bytes 229408 | tf_op jit(solution)/shard_map/ppermute | solution.py:105
  357.3 4.0 collective-permute-done.60
  362.5 7.5 %fusion.9 = f32[512,896]{1,0:T(8,128)S(1)} fusion(bf16[4096,512]{1,0:T(8,128)(2,1)S(1)} %select_dynamic-update-slice_fusion, bf16[4096,3584]{1,0:T(8,128)(2,1)} %bitcast.282), kind=kOutput, calls=%fused_computation.9 | convolution fusion | flops 3758096384 | bytes 13369344 | tf_op jit(solution)/shard_map/dot_general | solution.py:375
  374.7 4.8 %collective-permute-done.67 = f32[1,64,896]{2,1,0:T(8,128)S(1)} collective-permute-done((f32[1,64,896]{2,1,0:T(8,128)S(1)}, f32[1,64,896]{2,1,0:T(8,128)S(1)}, u32[]{:S(2)}, u32[]{:S(2)}) %collective-permute-start.67) | collective-permute-done | bytes 229408 | tf_op jit(solution)/shard_map/ppermute | solution.py:105
  379.5 17.8 %collective-permute-done.66 = f32[1,64,896]{2,1,0:T(8,128)S(1)} collective-permute-done((f32[1,64,896]{2,1,0:T(8,128)S(1)}, f32[1,64,896]{2,1,0:T(8,128)S(1)}, u32[]{:S(2)}, u32[]{:S(2)}) %collective-permute-start.66) | collective-permute-done | bytes 229408 | tf_op jit(solution)/shard_map/ppermute | solution.py:105
  401.8 2.0 dynamic-slice_bitcast_fusion.3
  410.4 3.1 collective-permute-done.72
  413.5 4.5 %collective-permute-done.71 = f32[1,64,896]{2,1,0:T(8,128)} collective-permute-done((f32[1,64,896]{2,1,0:T(8,128)}, f32[1,64,896]{2,1,0:T(8,128)}, u32[]{:S(2)}, u32[]{:S(2)}) %collective-permute-start.71) | collective-permute-done | bytes 229408 | tf_op jit(solution)/shard_map/ppermute | solution.py:105
  422.9 4.6 %collective-permute-done.75 = f32[1,64,896]{2,1,0:T(8,128)S(1)} collective-permute-done((f32[1,64,896]{2,1,0:T(8,128)S(1)}, f32[1,64,896]{2,1,0:T(8,128)S(1)}, u32[]{:S(2)}, u32[]{:S(2)}) %collective-permute-start.75) | collective-permute-done | bytes 229408 | tf_op jit(solution)/shard_map/ppermute | solution.py:105
  427.5 4.0 collective-permute-done.74
  (251 shorter events, 113.8 us)
Async XLA Ops:
  5.5 43.1 %collective-permute-start.1 = (f32[2,2,1,2,64,448]{5,4,2,1,0,3:T(8,128)}, f32[2,2,1,2,64,448]{5,4,2,1,0,3:T(8,128)}, u32[]{:S(2)}, u32[]{:S(2)}) collective-permute-start(f32[2,2,1,2,64,448]{5,4,2,1,0,3:T(8,128)} %constant_dynamic-slice_fusion.14), channel_id=1, source_target_pairs={{0,4},{4,0},{1,5},{5,1},{2,6},{6,2},{3,7},{7,3},{8,12},{12,8},{9,1... | collective-permute-start | bytes 2752520 | tf_op jit(solution)/shard_map/ppermute | solution.py:105
  17.3 31.3 %collective-permute-start = (f32[320,512]{1,0:T(8,128)}, f32[320,512]{1,0:T(8,128)S(1)}, u32[]{:S(2)}, u32[]{:S(2)}) collective-permute-start(f32[320,512]{1,0:T(8,128)} %constant_dynamic-slice_fusion.15), channel_id=1, source_target_pairs={{0,1},{1,2},{2,3},{3,0},{4,5},{5,6},{6,7},{7,4},{8,9},{9,10},{10,1... | collective-permute-start | bytes 1966088 | tf_op jit(solution)/shard_map/ppermute | solution.py:114
  31.3 34.0 %collective-permute-start.3 = (f32[704,512]{1,0:T(8,128)}, f32[704,512]{1,0:T(8,128)}, u32[]{:S(2)}, u32[]{:S(2)}) collective-permute-start(f32[704,512]{1,0:T(8,128)} %constant_dynamic-slice_fusion.13), channel_id=1, source_target_pairs={{0,8},{8,0},{16,24},{24,16},{1,9},{9,1},{17,25},{25,17},{2,10},{10... | collective-permute-start | bytes 4325384 | tf_op jit(solution)/shard_map/ppermute | solution.py:105
  47.1 33.8 %collective-permute-start.4 = (f32[704,512]{1,0:T(8,128)}, f32[704,512]{1,0:T(8,128)}, u32[]{:S(2)}, u32[]{:S(2)}) collective-permute-start(f32[704,512]{1,0:T(8,128)} %constant_dynamic-slice_fusion.12), channel_id=1, source_target_pairs={{0,16},{8,24},{16,0},{24,8},{1,17},{9,25},{17,1},{25,9},{2,18},{10... | collective-permute-start | bytes 4325384 | tf_op jit(solution)/shard_map/ppermute | solution.py:105
  50.6 30.2 %collective-permute-start.2 = (f32[320,512]{1,0:T(8,128)}, f32[320,512]{1,0:T(8,128)S(1)}, u32[]{:S(2)}, u32[]{:S(2)}) collective-permute-start(f32[320,512]{1,0:T(8,128)} %dynamic-slice_add_fusion.10), channel_id=1, source_target_pairs={{0,1},{1,2},{2,3},{3,0},{4,5},{5,6},{6,7},{7,4},{8,9},{9,10},{10,1... | collective-permute-start | bytes 1966088 | tf_op jit(solution)/shard_map/ppermute | solution.py:114
  83.9 24.2 %collective-permute-start.7 = (f32[352,512]{1,0:T(8,128)}, f32[352,512]{1,0:T(8,128)}, u32[]{:S(2)}, u32[]{:S(2)}) collective-permute-start(f32[352,512]{1,0:T(8,128)} %constant_dynamic-slice_fusion.10), channel_id=1, source_target_pairs={{0,8},{8,0},{16,24},{24,16},{1,9},{9,1},{17,25},{25,17},{2,10},{10... | collective-permute-start | bytes 2162696 | tf_op jit(solution)/shard_map/ppermute | solution.py:105
  87.3 21.7 %collective-permute-start.6 = (f32[352,512]{1,0:T(8,128)S(1)}, f32[352,512]{1,0:T(8,128)}, u32[]{:S(2)}, u32[]{:S(2)}) collective-permute-start(f32[352,512]{1,0:T(8,128)S(1)} %constant_dynamic-slice_fusion.11), channel_id=1, source_target_pairs={{0,16},{8,24},{16,0},{24,8},{1,17},{9,25},{17,1},{25,9},{2,18},{10... | collective-permute-start | bytes 2162696 | tf_op jit(solution)/shard_map/ppermute | solution.py:105
  90.8 17.3 %collective-permute-start.5 = (f32[320,512]{1,0:T(8,128)}, f32[320,512]{1,0:T(8,128)S(1)}, u32[]{:S(2)}, u32[]{:S(2)}) collective-permute-start(f32[320,512]{1,0:T(8,128)} %dynamic-slice_add_fusion.9), channel_id=1, source_target_pairs={{0,1},{1,2},{2,3},{3,0},{4,5},{5,6},{6,7},{7,4},{8,9},{9,10},{10,1... | collective-permute-start | bytes 1966088 | tf_op jit(solution)/shard_map/ppermute | solution.py:114
  94.6 30.9 %collective-permute-start.14 = (f32[2,1,2,2,64,448]{5,4,2,1,0,3:T(8,128)S(1)}, f32[2,1,2,2,64,448]{5,4,2,1,0,3:T(8,128)S(1)}, u32[]{:S(2)}, u32[]{:S(2)}) collective-permute-start(f32[2,1,2,2,64,448]{5,4,2,1,0,3:T(8,128)S(1)} %fusion.24), channel_id=1, source_target_pairs={{0,8},{8,0},{16,24},{24,16},{1,9},{9,1},{17,25},{25,17},{2,10},{10... | collective-permute-start | bytes 2752520 | tf_op jit(solution)/shard_map/ppermute | solution.py:105
  111.7 22.4 %collective-permute-start.10 = (f32[176,512]{1,0:T(8,128)}, f32[176,512]{1,0:T(8,128)}, u32[]{:S(2)}, u32[]{:S(2)}) collective-permute-start(f32[176,512]{1,0:T(8,128)} %get-tuple-element.239), channel_id=1, source_target_pairs={{0,3},{1,2},{2,1},{3,0},{4,7},{5,6},{6,5},{7,4},{8,11},{9,10},{10,... | collective-permute-start | bytes 1081352 | tf_op jit(solution)/shard_map/ppermute | solution.py:105
  112.2 21.8 %collective-permute-start.8 = (f32[176,512]{1,0:T(8,128)}, f32[176,512]{1,0:T(8,128)}, u32[]{:S(2)}, u32[]{:S(2)}) collective-permute-start(f32[176,512]{1,0:T(8,128)} %get-tuple-element.240), channel_id=1, source_target_pairs={{0,1},{1,0},{2,3},{3,2},{4,5},{5,4},{6,7},{7,6},{8,9},{9,8},{10,11... | collective-permute-start | bytes 1081352 | tf_op jit(solution)/shard_map/ppermute | solution.py:105
  113.0 29.4 %collective-permute-start.9 = (f32[176,512]{1,0:T(8,128)}, f32[176,512]{1,0:T(8,128)}, u32[]{:S(2)}, u32[]{:S(2)}) collective-permute-start(f32[176,512]{1,0:T(8,128)} %get-tuple-element.241), channel_id=1, source_target_pairs={{0,2},{1,3},{2,0},{3,1},{4,6},{5,7},{6,4},{7,5},{8,10},{9,11},{10,... | collective-permute-start | bytes 1081352 | tf_op jit(solution)/shard_map/ppermute | solution.py:105
  118.9 9.5 %collective-permute-start.13 = (f32[80,512]{1,0:T(8,128)S(1)}, f32[80,512]{1,0:T(8,128)}, u32[]{:S(2)}, u32[]{:S(2)}) collective-permute-start(f32[80,512]{1,0:T(8,128)S(1)} %get-tuple-element.262), channel_id=1, source_target_pairs={{0,24},{8,16},{16,8},{24,0},{1,25},{9,17},{17,9},{25,1},{2,26},{10... | collective-permute-start | bytes 491528 | tf_op jit(solution)/shard_map/ppermute | solution.py:105
  153.6 10.1 %collective-permute-start.18 = (f32[64,512]{1,0:T(8,128)}, f32[64,512]{1,0:T(8,128)}, u32[]{:S(2)}, u32[]{:S(2)}) collective-permute-start(f32[64,512]{1,0:T(8,128)} %get-tuple-element.276), channel_id=1, source_target_pairs={{0,24},{8,16},{16,8},{24,0},{1,25},{9,17},{17,9},{25,1},{2,26},{10... | collective-permute-start | bytes 393224 | tf_op jit(solution)/shard_map/ppermute | solution.py:105
  155.0 8.7 %collective-permute-start.17 = (f32[64,512]{1,0:T(8,128)}, f32[64,512]{1,0:T(8,128)}, u32[]{:S(2)}, u32[]{:S(2)}) collective-permute-start(f32[64,512]{1,0:T(8,128)} %get-tuple-element.277), channel_id=1, source_target_pairs={{0,16},{8,24},{16,0},{24,8},{1,17},{9,25},{17,1},{25,9},{2,18},{10... | collective-permute-start | bytes 393224 | tf_op jit(solution)/shard_map/ppermute | solution.py:105
  159.7 22.6 %collective-permute-start.30 = (f32[80,512]{1,0:T(8,128)}, f32[80,512]{1,0:T(8,128)S(1)}, u32[]{:S(2)}, u32[]{:S(2)}) collective-permute-start(f32[80,512]{1,0:T(8,128)} %bitcast_add_fusion.4), channel_id=1, source_target_pairs={{0,24},{8,16},{16,8},{24,0},{1,25},{9,17},{17,9},{25,1},{2,26},{10... | collective-permute-start | bytes 491528 | tf_op jit(solution)/shard_map/ppermute | solution.py:105
  161.2 26.2 %collective-permute-start.27 = (f32[176,512]{1,0:T(8,128)S(1)}, f32[176,512]{1,0:T(8,128)S(1)}, u32[]{:S(2)}, u32[]{:S(2)}) collective-permute-start(f32[176,512]{1,0:T(8,128)S(1)} %copy-done.6), channel_id=1, source_target_pairs={{0,3},{1,2},{2,1},{3,0},{4,7},{5,6},{6,5},{7,4},{8,11},{9,10},{10,... | collective-permute-start | bytes 1081352 | tf_op jit(solution)/shard_map/ppermute | solution.py:105
  164.9 9.0 %collective-permute-start.21 = (f32[16,512]{1,0:T(8,128)S(1)}, f32[16,512]{1,0:T(8,128)S(1)}, u32[]{:S(2)}, u32[]{:S(2)}) collective-permute-start(f32[16,512]{1,0:T(8,128)S(1)} %get-tuple-element.290), channel_id=1, source_target_pairs={{0,3},{1,2},{2,1},{3,0},{4,7},{5,6},{6,5},{7,4},{8,11},{9,10},{10,... | collective-permute-start | bytes 98312 | tf_op jit(solution)/shard_map/ppermute | solution.py:105
  167.1 13.1 %collective-permute-start.20 = (f32[16,512]{1,0:T(8,128)S(1)}, f32[16,512]{1,0:T(8,128)S(1)}, u32[]{:S(2)}, u32[]{:S(2)}) collective-permute-start(f32[16,512]{1,0:T(8,128)S(1)} %get-tuple-element.291), channel_id=1, source_target_pairs={{0,2},{1,3},{2,0},{3,1},{4,6},{5,7},{6,4},{7,5},{8,10},{9,11},{10,... | collective-permute-start | bytes 98312 | tf_op jit(solution)/shard_map/ppermute | solution.py:105
  167.1 13.6 %collective-permute-start.19 = (f32[16,512]{1,0:T(8,128)S(1)}, f32[16,512]{1,0:T(8,128)S(1)}, u32[]{:S(2)}, u32[]{:S(2)}) collective-permute-start(f32[16,512]{1,0:T(8,128)S(1)} %get-tuple-element.292), channel_id=1, source_target_pairs={{0,1},{1,0},{2,3},{3,2},{4,5},{5,4},{6,7},{7,6},{8,9},{9,8},{10,11... | collective-permute-start | bytes 98312 | tf_op jit(solution)/shard_map/ppermute | solution.py:105
  173.8 8.8 %collective-permute-start.29 = (f32[80,512]{1,0:T(8,128)}, f32[80,512]{1,0:T(8,128)S(1)}, u32[]{:S(2)}, u32[]{:S(2)}) collective-permute-start(f32[80,512]{1,0:T(8,128)} %bitcast_add_fusion.4), channel_id=1, source_target_pairs={{0,16},{8,24},{16,0},{24,8},{1,17},{9,25},{17,1},{25,9},{2,18},{10... | collective-permute-start | bytes 491528 | tf_op jit(solution)/shard_map/ppermute | solution.py:105
  180.7 17.9 %collective-permute-start.26 = (f32[176,512]{1,0:T(8,128)S(1)}, f32[176,512]{1,0:T(8,128)S(1)}, u32[]{:S(2)}, u32[]{:S(2)}) collective-permute-start(f32[176,512]{1,0:T(8,128)S(1)} %copy-done.6), channel_id=1, source_target_pairs={{0,2},{1,3},{2,0},{3,1},{4,6},{5,7},{6,4},{7,5},{8,10},{9,11},{10,... | collective-permute-start | bytes 1081352 | tf_op jit(solution)/shard_map/ppermute | solution.py:105
  182.3 16.2 %collective-permute-start.25 = (f32[176,512]{1,0:T(8,128)S(1)}, f32[176,512]{1,0:T(8,128)S(1)}, u32[]{:S(2)}, u32[]{:S(2)}) collective-permute-start(f32[176,512]{1,0:T(8,128)S(1)} %copy-done.6), channel_id=1, source_target_pairs={{0,1},{1,0},{2,3},{3,2},{4,5},{5,4},{6,7},{7,6},{8,9},{9,8},{10,11... | collective-permute-start | bytes 1081352 | tf_op jit(solution)/shard_map/ppermute | solution.py:105
  182.6 16.9 %collective-permute-start.24 = (f32[16,512]{1,0:T(8,128)S(1)}, f32[16,512]{1,0:T(8,128)S(1)}, u32[]{:S(2)}, u32[]{:S(2)}) collective-permute-start(f32[16,512]{1,0:T(8,128)S(1)} %bitcast_add_fusion.8), channel_id=1, source_target_pairs={{0,3},{1,2},{2,1},{3,0},{4,7},{5,6},{6,5},{7,4},{8,11},{9,10},{10,... | collective-permute-start | bytes 98312 | tf_op jit(solution)/shard_map/ppermute | solution.py:105
  185.7 14.3 %collective-permute-start.23 = (f32[16,512]{1,0:T(8,128)S(1)}, f32[16,512]{1,0:T(8,128)S(1)}, u32[]{:S(2)}, u32[]{:S(2)}) collective-permute-start(f32[16,512]{1,0:T(8,128)S(1)} %bitcast_add_fusion.8), channel_id=1, source_target_pairs={{0,2},{1,3},{2,0},{3,1},{4,6},{5,7},{6,4},{7,5},{8,10},{9,11},{10,... | collective-permute-start | bytes 98312 | tf_op jit(solution)/shard_map/ppermute | solution.py:105
  187.4 12.6 %collective-permute-start.22 = (f32[16,512]{1,0:T(8,128)S(1)}, f32[16,512]{1,0:T(8,128)S(1)}, u32[]{:S(2)}, u32[]{:S(2)}) collective-permute-start(f32[16,512]{1,0:T(8,128)S(1)} %bitcast_add_fusion.8), channel_id=1, source_target_pairs={{0,1},{1,0},{2,3},{3,2},{4,5},{5,4},{6,7},{7,6},{8,9},{9,8},{10,11... | collective-permute-start | bytes 98312 | tf_op jit(solution)/shard_map/ppermute | solution.py:105
  204.8 19.0 %collective-permute-start.41 = (f32[320,512]{1,0:T(8,128)S(1)}, f32[320,512]{1,0:T(8,128)S(1)}, u32[]{:S(2)}, u32[]{:S(2)}) collective-permute-start(f32[320,512]{1,0:T(8,128)S(1)} %bitcast.247), channel_id=1, source_target_pairs={{0,1},{1,2},{2,3},{3,0},{4,5},{5,6},{6,7},{7,4},{8,9},{9,10},{10,1... | collective-permute-start | bytes 1966088 | tf_op jit(solution)/shard_map/ppermute | solution.py:114
  209.8 20.8 %collective-permute-start.39 = (f32[352,512]{1,0:T(8,128)S(1)}, f32[352,512]{1,0:T(8,128)S(1)}, u32[]{:S(2)}, u32[]{:S(2)}) collective-permute-start(f32[352,512]{1,0:T(8,128)S(1)} %bitcast.245), channel_id=1, source_target_pairs={{0,16},{8,24},{16,0},{24,8},{1,17},{9,25},{17,1},{25,9},{2,18},{10... | collective-permute-start | bytes 2162696 | tf_op jit(solution)/shard_map/ppermute | solution.py:105
  211.3 19.3 %collective-permute-start.40 = (f32[352,512]{1,0:T(8,128)S(1)}, f32[352,512]{1,0:T(8,128)S(1)}, u32[]{:S(2)}, u32[]{:S(2)}) collective-permute-start(f32[352,512]{1,0:T(8,128)S(1)} %bitcast.246), channel_id=1, source_target_pairs={{0,8},{8,0},{16,24},{24,16},{1,9},{9,1},{17,25},{25,17},{2,10},{10... | collective-permute-start | bytes 2162696 | tf_op jit(solution)/shard_map/ppermute | solution.py:105
  212.2 21.0 %collective-permute-start.38 = (f32[64,512]{1,0:T(8,128)S(1)}, f32[64,512]{1,0:T(8,128)S(1)}, u32[]{:S(2)}, u32[]{:S(2)}) collective-permute-start(f32[64,512]{1,0:T(8,128)S(1)} %get-tuple-element.269), channel_id=1, source_target_pairs={{0,24},{8,16},{16,8},{24,0},{1,25},{9,17},{17,9},{25,1},{2,26},{10... | collective-permute-start | bytes 393224 | tf_op jit(solution)/shard_map/ppermute | solution.py:105
  213.6 20.5 %collective-permute-start.37 = (f32[64,512]{1,0:T(8,128)S(1)}, f32[64,512]{1,0:T(8,128)S(1)}, u32[]{:S(2)}, u32[]{:S(2)}) collective-permute-start(f32[64,512]{1,0:T(8,128)S(1)} %get-tuple-element.270), channel_id=1, source_target_pairs={{0,16},{8,24},{16,0},{24,8},{1,17},{9,25},{17,1},{25,9},{2,18},{10... | collective-permute-start | bytes 393224 | tf_op jit(solution)/shard_map/ppermute | solution.py:105
  223.7 11.5 %collective-permute-start.36 = (f32[64,512]{1,0:T(8,128)S(1)}, f32[64,512]{1,0:T(8,128)S(1)}, u32[]{:S(2)}, u32[]{:S(2)}) collective-permute-start(f32[64,512]{1,0:T(8,128)S(1)} %get-tuple-element.271), channel_id=1, source_target_pairs={{0,8},{8,0},{16,24},{24,16},{1,9},{9,1},{17,25},{25,17},{2,10},{10... | collective-permute-start | bytes 393224 | tf_op jit(solution)/shard_map/ppermute | solution.py:105
  235.3 10.9 %collective-permute-start.44 = (f32[16,512]{1,0:T(8,128)S(1)}, f32[16,512]{1,0:T(8,128)S(1)}, u32[]{:S(2)}, u32[]{:S(2)}) collective-permute-start(f32[16,512]{1,0:T(8,128)S(1)} %get-tuple-element.283), channel_id=1, source_target_pairs={{0,3},{1,2},{2,1},{3,0},{4,7},{5,6},{6,5},{7,4},{8,11},{9,10},{10,... | collective-permute-start | bytes 98312 | tf_op jit(solution)/shard_map/ppermute | solution.py:105
  236.7 11.0 %collective-permute-start.43 = (f32[16,512]{1,0:T(8,128)S(1)}, f32[16,512]{1,0:T(8,128)S(1)}, u32[]{:S(2)}, u32[]{:S(2)}) collective-permute-start(f32[16,512]{1,0:T(8,128)S(1)} %get-tuple-element.284), channel_id=1, source_target_pairs={{0,2},{1,3},{2,0},{3,1},{4,6},{5,7},{6,4},{7,5},{8,10},{9,11},{10,... | collective-permute-start | bytes 98312 | tf_op jit(solution)/shard_map/ppermute | solution.py:105
  236.7 11.0 %collective-permute-start.42 = (f32[16,512]{1,0:T(8,128)S(1)}, f32[16,512]{1,0:T(8,128)S(1)}, u32[]{:S(2)}, u32[]{:S(2)}) collective-permute-start(f32[16,512]{1,0:T(8,128)S(1)} %get-tuple-element.285), channel_id=1, source_target_pairs={{0,1},{1,0},{2,3},{3,2},{4,5},{5,4},{6,7},{7,6},{8,9},{9,8},{10,11... | collective-permute-start | bytes 98312 | tf_op jit(solution)/shard_map/ppermute | solution.py:105
  239.8 17.4 %collective-permute-start.45 = (f32[320,512]{1,0:T(8,128)S(1)}, f32[320,512]{1,0:T(8,128)S(1)}, u32[]{:S(2)}, u32[]{:S(2)}) collective-permute-start(f32[320,512]{1,0:T(8,128)S(1)} %collective-permute-done.41), channel_id=1, source_target_pairs={{0,1},{1,2},{2,3},{3,0},{4,5},{5,6},{6,7},{7,4},{8,9},{9,10},{10,1... | collective-permute-start | bytes 1966088 | tf_op jit(solution)/shard_map/ppermute | solution.py:114
  240.5 44.6 %collective-permute-start.52 = (f32[704,512]{1,0:T(8,128)S(1)}, f32[704,512]{1,0:T(8,128)S(1)}, u32[]{:S(2)}, u32[]{:S(2)}) collective-permute-start(f32[704,512]{1,0:T(8,128)S(1)} %pad_maximum_fusion.4), channel_id=1, source_target_pairs={{0,8},{8,0},{16,24},{24,16},{1,9},{9,1},{17,25},{25,17},{2,10},{10... | collective-permute-start | bytes 4325384 | tf_op jit(solution)/shard_map/ppermute | solution.py:105
  246.2 38.9 %collective-permute-start.53 = (f32[704,512]{1,0:T(8,128)S(1)}, f32[704,512]{1,0:T(8,128)S(1)}, u32[]{:S(2)}, u32[]{:S(2)}) collective-permute-start(f32[704,512]{1,0:T(8,128)S(1)} %pad_maximum_fusion.5), channel_id=1, source_target_pairs={{0,16},{8,24},{16,0},{24,8},{1,17},{9,25},{17,1},{25,9},{2,18},{10... | collective-permute-start | bytes 4325384 | tf_op jit(solution)/shard_map/ppermute | solution.py:105
  257.2 8.9 %collective-permute-start.48 = (f32[16,512]{1,0:T(8,128)S(1)}, f32[16,512]{1,0:T(8,128)S(1)}, u32[]{:S(2)}, u32[]{:S(2)}) collective-permute-start(f32[16,512]{1,0:T(8,128)S(1)} %bitcast_add_fusion.7), channel_id=1, source_target_pairs={{0,3},{1,2},{2,1},{3,0},{4,7},{5,6},{6,5},{7,4},{8,11},{9,10},{10,... | collective-permute-start | bytes 98312 | tf_op jit(solution)/shard_map/ppermute | solution.py:105
  257.3 8.8 %collective-permute-start.47 = (f32[16,512]{1,0:T(8,128)S(1)}, f32[16,512]{1,0:T(8,128)S(1)}, u32[]{:S(2)}, u32[]{:S(2)}) collective-permute-start(f32[16,512]{1,0:T(8,128)S(1)} %bitcast_add_fusion.7), channel_id=1, source_target_pairs={{0,2},{1,3},{2,0},{3,1},{4,6},{5,7},{6,4},{7,5},{8,10},{9,11},{10,... | collective-permute-start | bytes 98312 | tf_op jit(solution)/shard_map/ppermute | solution.py:105
  266.2 9.4 %collective-permute-start.51 = (f32[64,512]{1,0:T(8,128)S(1)}, f32[64,512]{1,0:T(8,128)S(1)}, u32[]{:S(2)}, u32[]{:S(2)}) collective-permute-start(f32[64,512]{1,0:T(8,128)S(1)} %bitcast.269), channel_id=1, source_target_pairs={{0,24},{8,16},{16,8},{24,0},{1,25},{9,17},{17,9},{25,1},{2,26},{10... | collective-permute-start | bytes 393224 | tf_op jit(solution)/shard_map/ppermute | solution.py:105
  267.8 17.3 %collective-permute-start.54 = (f32[320,512]{1,0:T(8,128)S(1)}, f32[320,512]{1,0:T(8,128)S(1)}, u32[]{:S(2)}, u32[]{:S(2)}) collective-permute-start(f32[320,512]{1,0:T(8,128)S(1)} %collective-permute-done.45), channel_id=1, source_target_pairs={{0,1},{1,2},{2,3},{3,0},{4,5},{5,6},{6,7},{7,4},{8,9},{9,10},{10,1... | collective-permute-start | bytes 1966088 | tf_op jit(solution)/shard_map/ppermute | solution.py:114
  268.3 15.4 %collective-permute-start.50 = (f32[64,512]{1,0:T(8,128)S(1)}, f32[64,512]{1,0:T(8,128)S(1)}, u32[]{:S(2)}, u32[]{:S(2)}) collective-permute-start(f32[64,512]{1,0:T(8,128)S(1)} %bitcast.270), channel_id=1, source_target_pairs={{0,16},{8,24},{16,0},{24,8},{1,17},{9,25},{17,1},{25,9},{2,18},{10... | collective-permute-start | bytes 393224 | tf_op jit(solution)/shard_map/ppermute | solution.py:105
  275.5 9.6 %collective-permute-start.49 = (f32[64,512]{1,0:T(8,128)S(1)}, f32[64,512]{1,0:T(8,128)S(1)}, u32[]{:S(2)}, u32[]{:S(2)}) collective-permute-start(f32[64,512]{1,0:T(8,128)S(1)} %bitcast.271), channel_id=1, source_target_pairs={{0,8},{8,0},{16,24},{24,16},{1,9},{9,1},{17,25},{25,17},{2,10},{10... | collective-permute-start | bytes 393224 | tf_op jit(solution)/shard_map/ppermute | solution.py:105
  283.7 26.7 %collective-permute-start.56 = (f32[1,2,2,2,64,448]{5,4,2,1,0,3:T(8,128)S(1)}, f32[1,2,2,2,64,448]{5,4,2,1,0,3:T(8,128)S(1)}, u32[]{:S(2)}, u32[]{:S(2)}) collective-permute-start(f32[1,2,2,2,64,448]{5,4,2,1,0,3:T(8,128)S(1)} %fusion.22), channel_id=1, source_target_pairs={{0,16},{8,24},{16,0},{24,8},{1,17},{9,25},{17,1},{25,9},{2,18},{10... | collective-permute-start | bytes 2752520 | tf_op jit(solution)/shard_map/ppermute | solution.py:105
  289.0 21.3 %collective-permute-start.57 = (f32[256,512]{1,0:T(8,128)S(1)}, f32[256,512]{1,0:T(8,128)S(1)}, u32[]{:S(2)}, u32[]{:S(2)}) collective-permute-start(f32[256,512]{1,0:T(8,128)S(1)} %bitcast.251), channel_id=1, source_target_pairs={{0,4},{4,0},{1,5},{5,1},{2,6},{6,2},{3,7},{7,3},{8,12},{12,8},{9,1... | collective-permute-start | bytes 1572872 | tf_op jit(solution)/shard_map/ppermute | solution.py:105
  309.8 15.3 %collective-permute-start.55 = (f32[4,1,64,896]{3,2,1,0:T(8,128)S(1)}, f32[4,1,64,896]{3,2,1,0:T(8,128)S(1)}, u32[]{:S(2)}, u32[]{:S(2)}) collective-permute-start(f32[4,1,64,896]{3,2,1,0:T(8,128)S(1)} %constant_dynamic-slice_fusion.4), channel_id=1, source_target_pairs={{0,4},{4,0},{1,5},{5,1},{2,6},{6,2},{3,7},{7,3},{8,12},{12,8},{9,1... | collective-permute-start | bytes 2752520 | tf_op jit(solution)/shard_map/ppermute | solution.py:105
  325.6 12.4 %collective-permute-start.59 = (f32[4,1,64,896]{3,2,1,0:T(8,128)S(1)}, f32[4,1,64,896]{3,2,1,0:T(8,128)S(1)}, u32[]{:S(2)}, u32[]{:S(2)}) collective-permute-start(f32[4,1,64,896]{3,2,1,0:T(8,128)S(1)} %constant_dynamic-slice_fusion.2), channel_id=1, source_target_pairs={{0,4},{4,0},{1,5},{5,1},{2,6},{6,2},{3,7},{7,3},{8,12},{12,8},{9,1... | collective-permute-start | bytes 2752520 | tf_op jit(solution)/shard_map/ppermute | solution.py:105
  326.2 35.0 %collective-permute-start.63 = (f32[2,1,2,2,64,448]{5,4,2,1,0,3:T(8,128)S(1)}, f32[2,1,2,2,64,448]{5,4,2,1,0,3:T(8,128)S(1)}, u32[]{:S(2)}, u32[]{:S(2)}) collective-permute-start(f32[2,1,2,2,64,448]{5,4,2,1,0,3:T(8,128)S(1)} %fusion.20), channel_id=1, source_target_pairs={{0,8},{8,0},{16,24},{24,16},{1,9},{9,1},{17,25},{25,17},{2,10},{10... | collective-permute-start | bytes 2752520 | tf_op jit(solution)/shard_map/ppermute | solution.py:105
  334.5 22.8 %collective-permute-start.62 = (f32[1,64,896]{2,1,0:T(8,128)S(1)}, f32[1,64,896]{2,1,0:T(8,128)S(1)}, u32[]{:S(2)}, u32[]{:S(2)}) collective-permute-start(f32[1,64,896]{2,1,0:T(8,128)S(1)} %get-tuple-element.255), channel_id=1, source_target_pairs={{0,24},{8,16},{16,8},{24,0},{1,25},{9,17},{17,9},{25,1},{2,26},{10... | collective-permute-start | bytes 688136 | tf_op jit(solution)/shard_map/ppermute | solution.py:105
  336.1 21.2 %collective-permute-start.61 = (f32[1,64,896]{2,1,0:T(8,128)S(1)}, f32[1,64,896]{2,1,0:T(8,128)S(1)}, u32[]{:S(2)}, u32[]{:S(2)}) collective-permute-start(f32[1,64,896]{2,1,0:T(8,128)S(1)} %get-tuple-element.256), channel_id=1, source_target_pairs={{0,16},{8,24},{16,0},{24,8},{1,17},{9,25},{17,1},{25,9},{2,18},{10... | collective-permute-start | bytes 688136 | tf_op jit(solution)/shard_map/ppermute | solution.py:105
  337.5 23.7 %collective-permute-start.60 = (f32[1,64,896]{2,1,0:T(8,128)S(1)}, f32[1,64,896]{2,1,0:T(8,128)S(1)}, u32[]{:S(2)}, u32[]{:S(2)}) collective-permute-start(f32[1,64,896]{2,1,0:T(8,128)S(1)} %get-tuple-element.257), channel_id=1, source_target_pairs={{0,8},{8,0},{16,24},{24,16},{1,9},{9,1},{17,25},{25,17},{2,10},{10... | collective-permute-start | bytes 688136 | tf_op jit(solution)/shard_map/ppermute | solution.py:105
  361.6 12.0 %collective-permute-start.64 = (f32[4,1,64,896]{3,2,1,0:T(8,128)S(1)}, f32[4,1,64,896]{3,2,1,0:T(8,128)S(1)}, u32[]{:S(2)}, u32[]{:S(2)}) collective-permute-start(f32[4,1,64,896]{3,2,1,0:T(8,128)S(1)} %constant_dynamic-slice_fusion.1), channel_id=1, source_target_pairs={{0,4},{4,0},{1,5},{5,1},{2,6},{6,2},{3,7},{7,3},{8,12},{12,8},{9,1... | collective-permute-start | bytes 2752520 | tf_op jit(solution)/shard_map/ppermute | solution.py:105
  361.8 35.5 %collective-permute-start.68 = (f32[1,2,2,2,64,448]{5,4,2,1,0,3:T(8,128)S(1)}, f32[1,2,2,2,64,448]{5,4,2,1,0,3:T(8,128)S(1)}, u32[]{:S(2)}, u32[]{:S(2)}) collective-permute-start(f32[1,2,2,2,64,448]{5,4,2,1,0,3:T(8,128)S(1)} %fusion.18), channel_id=1, source_target_pairs={{0,16},{8,24},{16,0},{24,8},{1,17},{9,25},{17,1},{25,9},{2,18},{10... | collective-permute-start | bytes 2752520 | tf_op jit(solution)/shard_map/ppermute | solution.py:105
  370.0 9.5 %collective-permute-start.67 = (f32[1,64,896]{2,1,0:T(8,128)S(1)}, f32[1,64,896]{2,1,0:T(8,128)S(1)}, u32[]{:S(2)}, u32[]{:S(2)}) collective-permute-start(f32[1,64,896]{2,1,0:T(8,128)S(1)} %get-tuple-element.252), channel_id=1, source_target_pairs={{0,24},{8,16},{16,8},{24,0},{1,25},{9,17},{17,9},{25,1},{2,26},{10... | collective-permute-start | bytes 688136 | tf_op jit(solution)/shard_map/ppermute | solution.py:105
  371.5 25.8 %collective-permute-start.66 = (f32[1,64,896]{2,1,0:T(8,128)S(1)}, f32[1,64,896]{2,1,0:T(8,128)S(1)}, u32[]{:S(2)}, u32[]{:S(2)}) collective-permute-start(f32[1,64,896]{2,1,0:T(8,128)S(1)} %get-tuple-element.253), channel_id=1, source_target_pairs={{0,16},{8,24},{16,0},{24,8},{1,17},{9,25},{17,1},{25,9},{2,18},{10... | collective-permute-start | bytes 688136 | tf_op jit(solution)/shard_map/ppermute | solution.py:105
  372.9 24.3 %collective-permute-start.65 = (f32[1,64,896]{2,1,0:T(8,128)S(1)}, f32[1,64,896]{2,1,0:T(8,128)S(1)}, u32[]{:S(2)}, u32[]{:S(2)}) collective-permute-start(f32[1,64,896]{2,1,0:T(8,128)S(1)} %get-tuple-element.254), channel_id=1, source_target_pairs={{0,8},{8,0},{16,24},{24,16},{1,9},{9,1},{17,25},{25,17},{2,10},{10... | collective-permute-start | bytes 688136 | tf_op jit(solution)/shard_map/ppermute | solution.py:105
  398.3 10.5 %collective-permute-start.69 = (f32[4,1,64,896]{3,2,1,0:T(8,128)}, f32[4,1,64,896]{3,2,1,0:T(8,128)}, u32[]{:S(2)}, u32[]{:S(2)}) collective-permute-start(f32[4,1,64,896]{3,2,1,0:T(8,128)} %constant_dynamic-slice_fusion), channel_id=1, source_target_pairs={{0,4},{4,0},{1,5},{5,1},{2,6},{6,2},{3,7},{7,3},{8,12},{12,8},{9,1... | collective-permute-start | bytes 2752520 | tf_op jit(solution)/shard_map/ppermute | solution.py:105
  403.8 9.7 %collective-permute-start.72 = (f32[1,64,896]{2,1,0:T(8,128)}, f32[1,64,896]{2,1,0:T(8,128)}, u32[]{:S(2)}, u32[]{:S(2)}) collective-permute-start(f32[1,64,896]{2,1,0:T(8,128)} %get-tuple-element.249), channel_id=1, source_target_pairs={{0,24},{8,16},{16,8},{24,0},{1,25},{9,17},{17,9},{25,1},{2,26},{10... | collective-permute-start | bytes 688136 | tf_op jit(solution)/shard_map/ppermute | solution.py:105
  405.2 12.8 %collective-permute-start.71 = (f32[1,64,896]{2,1,0:T(8,128)}, f32[1,64,896]{2,1,0:T(8,128)}, u32[]{:S(2)}, u32[]{:S(2)}) collective-permute-start(f32[1,64,896]{2,1,0:T(8,128)} %get-tuple-element.250), channel_id=1, source_target_pairs={{0,16},{8,24},{16,0},{24,8},{1,17},{9,25},{17,1},{25,9},{2,18},{10... | collective-permute-start | bytes 688136 | tf_op jit(solution)/shard_map/ppermute | solution.py:105
  405.8 12.2 %collective-permute-start.70 = (f32[1,64,896]{2,1,0:T(8,128)}, f32[1,64,896]{2,1,0:T(8,128)}, u32[]{:S(2)}, u32[]{:S(2)}) collective-permute-start(f32[1,64,896]{2,1,0:T(8,128)} %get-tuple-element.251), channel_id=1, source_target_pairs={{0,8},{8,0},{16,24},{24,16},{1,9},{9,1},{17,25},{25,17},{2,10},{10... | collective-permute-start | bytes 688136 | tf_op jit(solution)/shard_map/ppermute | solution.py:105
  418.0 9.5 %collective-permute-start.75 = (f32[1,64,896]{2,1,0:T(8,128)S(1)}, f32[1,64,896]{2,1,0:T(8,128)S(1)}, u32[]{:S(2)}, u32[]{:S(2)}) collective-permute-start(f32[1,64,896]{2,1,0:T(8,128)S(1)} %get-tuple-element.246), channel_id=1, source_target_pairs={{0,24},{8,16},{16,8},{24,0},{1,25},{9,17},{17,9},{25,1},{2,26},{10... | collective-permute-start | bytes 688136 | tf_op jit(solution)/shard_map/ppermute | solution.py:105
  419.5 12.0 %collective-permute-start.74 = (f32[1,64,896]{2,1,0:T(8,128)S(1)}, f32[1,64,896]{2,1,0:T(8,128)S(1)}, u32[]{:S(2)}, u32[]{:S(2)}) collective-permute-start(f32[1,64,896]{2,1,0:T(8,128)S(1)} %get-tuple-element.247), channel_id=1, source_target_pairs={{0,16},{8,24},{16,0},{24,8},{1,17},{9,25},{17,1},{25,9},{2,18},{10... | collective-permute-start | bytes 688136 | tf_op jit(solution)/shard_map/ppermute | solution.py:105
  420.1 11.4 %collective-permute-start.73 = (f32[1,64,896]{2,1,0:T(8,128)S(1)}, f32[1,64,896]{2,1,0:T(8,128)S(1)}, u32[]{:S(2)}, u32[]{:S(2)}) collective-permute-start(f32[1,64,896]{2,1,0:T(8,128)S(1)} %get-tuple-element.248), channel_id=1, source_target_pairs={{0,8},{8,0},{16,24},{24,16},{1,9},{9,1},{17,25},{25,17},{2,10},{10... | collective-permute-start | bytes 688136 | tf_op jit(solution)/shard_map/ppermute | solution.py:105
  (33 other events, 215.9 us)

commit v3 on v2

v3 whole, which is shorter than its diff:
```python
import functools

import jax
import jax.numpy as jnp
from jax import lax
from jax.experimental import pallas as pl
from jax.experimental.pallas import tpu as pltpu
from jax.sharding import PartitionSpec as P

highest = lax.Precision.HIGHEST
near = lax.Precision.HIGH
BLOCK = 128


def contract(a, b, a_dim, b_dim, precision=highest):
    return lax.dot_general(
        a, b, (((a_dim,), (b_dim,)), ((), ())), precision=precision, preferred_element_type=jnp.float32
    )


def eliminate(block, inverse_ref):
    groups = BLOCK // 8
    left = [block[8 * g : 8 * g + 8] for g in range(groups)]
    row_ids = lax.broadcasted_iota(jnp.int32, (8, BLOCK), 0)
    lane_ids = lax.broadcasted_iota(jnp.int32, (8, BLOCK), 1)
    right = [(lane_ids == row_ids + 8 * g).astype(jnp.float32) for g in range(groups)]
    for own in range(groups):
        at = 8 * own
        spread = {
            g: [jnp.broadcast_to(left[g][:, at + k : at + k + 1], (8, BLOCK)) for k in range(8)]
            for g in range(own, groups)
        }
        scaled = []
        for i in range(8):
            pivot = spread[own][i][i : i + 1]
            recip = 1.0 / pivot
            row, inv_row = left[own][i : i + 1], right[own][i : i + 1]
            inverse_ref[at + i : at + i + 1, :] = inv_row * lax.rsqrt(pivot)
            row, inv_row = row * recip, inv_row * recip
            scaled.append((row, inv_row))
            if i == 7:
                continue
            ratio = {k: spread[own][k][i : i + 1] * recip for k in range(i + 1, 8)}
            below = jnp.where(row_ids > i, spread[own][i], 0.0)
            left[own] = left[own] - below * row
            right[own] = right[own] - below * inv_row
            for g in range(own, groups):
                column = below if g == own else spread[g][i]
                for k in range(i + 1, 8):
                    spread[g][k] = spread[g][k] - column * ratio[k]
        for g in range(own + 1, groups):
            for i, (row, inv_row) in enumerate(scaled):
                left[g] = left[g] - spread[g][i] * row
                right[g] = right[g] - spread[g][i] * inv_row


def cholesky_kernel(index, work_in, rest_in, inverse_in, work_ref, rest_ref, inverse_ref, diag_ref):
    size = work_ref.shape[0]
    at = slice(index * BLOCK, (index + 1) * BLOCK)
    if index == 0:
        rows = lax.broadcasted_iota(jnp.int32, (size, size), 0)
        cols = lax.broadcasted_iota(jnp.int32, (size, size), 1)
        rest = (rows == cols).astype(jnp.float32)
    else:
        rest = rest_in[...]
        inverse_ref[...] = inverse_in[...]
    eliminate(work_in[at, at], diag_ref)
    diag = diag_ref[...]
    done = contract(diag, rest[at], 1, 0)
    inverse_ref[at, :] = done
    if index < size // BLOCK - 1:
        below = slice((index + 1) * BLOCK, size)
        factor = contract(work_in[below, at], diag, 1, 1)
        work_ref[below, below] = work_in[below, below] - contract(factor, factor, 1, 1)
        rest_ref[below, :] = rest[below] - contract(factor, done, 1, 0)


def cholesky_step(index, work, rest, inverse):
    size = work.shape[0]
    whole = jax.ShapeDtypeStruct((size, size), jnp.float32)
    spec = pl.BlockSpec(memory_space=pltpu.VMEM)
    return pl.pallas_call(
        functools.partial(cholesky_kernel, index),
        out_shape=[whole] * 3,
        in_specs=[spec] * 3,
        out_specs=[spec] * 3,
        scratch_shapes=[pltpu.VMEM((BLOCK, BLOCK), jnp.float32)],
        compiler_params=pltpu.CompilerParams(vmem_limit_bytes=32 << 20),
        cost_estimate=pl.CostEstimate(flops=1_000_000, bytes_accessed=100_000, transcendentals=0),
    )(work, rest, inverse)


def projection_kernel(sizes, first, tile, starts_ref, basis_ref, grad_ref, out_ref, held_ref, sems):
    step = pl.program_id(0)
    steps = pl.num_programs(0)

    def copies(index, slot):
        at = 0
        made = []
        for k, size in enumerate(sizes):
            source = grad_ref.at[
                pl.ds(pl.multiple_of(starts_ref[k], 16), size),
                pl.ds(pl.multiple_of(first + index * tile, 128), tile),
            ]
            made.append(pltpu.make_async_copy(source, held_ref.at[slot, pl.ds(at, size)], sems.at[slot, k]))
            at += size
        return made

    @pl.when(step == 0)
    def _():
        for copy in copies(0, 0):
            copy.start()

    @pl.when(step + 1 < steps)
    def _():
        for copy in copies(step + 1, (step + 1) % 2):
            copy.start()

    slot = step % 2
    for copy in copies(step, slot):
        copy.wait()
    out_ref[...] = lax.dot_general(
        basis_ref[...], held_ref[slot], (((0,), (0,)), ((), ())), preferred_element_type=jnp.float32
    )


def projection(starts, basis, grad, sizes, first, width, tile):
    rows, rank = basis.shape
    return pl.pallas_call(
        functools.partial(projection_kernel, sizes, first, tile),
        grid=(width // tile,),
        out_shape=jax.ShapeDtypeStruct((rank, width), jnp.float32),
        in_specs=[
            pl.BlockSpec(memory_space=pltpu.SMEM),
            pl.BlockSpec((rows, rank), lambda i: (0, 0), pipeline_mode=pl.Buffered(1)),
            pl.BlockSpec(memory_space=pl.ANY),
        ],
        out_specs=pl.BlockSpec((rank, tile), lambda i: (0, i)),
        scratch_shapes=[pltpu.VMEM((2, rows, tile), jnp.bfloat16), pltpu.SemaphoreType.DMA((2, len(sizes)))],
        compiler_params=pltpu.CompilerParams(vmem_limit_bytes=40 << 20),
        cost_estimate=pl.CostEstimate(flops=1_000_000, bytes_accessed=100_000, transcendentals=0),
    )(starts, basis, grad)


class Order:
    def __init__(self):
        self.mark = jnp.zeros((8, 128), jnp.float32)

    def __call__(self, *values):
        self.mark, *values = lax.optimization_barrier((self.mark,) + values)
        return values


def bits_of(axis):
    return lax.axis_size(axis).bit_length() - 1


def own_bit(axis, bit):
    return (lax.axis_index(axis) >> bit) & 1


def flipped(value, axis, mask):
    return lax.ppermute(value, axis, [(i, i ^ mask) for i in range(lax.axis_size(axis))])


def swap(value, axis, bit):
    return flipped(value, axis, 1 << bit)


def shifted(value, axis):
    size = lax.axis_size(axis)
    return lax.ppermute(value, axis, [(i, (i + 1) % size) for i in range(size)])


def split_half(value, axis, bit, dim=0):
    half = value.shape[dim] // 2
    me = own_bit(axis, bit)
    sent = lax.dynamic_slice_in_dim(value, (1 - me) * half, half, dim)
    kept = lax.dynamic_slice_in_dim(value, me * half, half, dim)
    return sent, kept


def in_order(value, other, axis, bit):
    first = own_bit(axis, bit) == 0
    return jnp.concatenate([jnp.where(first, value, other), jnp.where(first, other, value)], 0)


def scatter_sends(value, axis):
    me = lax.axis_index(axis)
    kept = lax.dynamic_index_in_dim(value, me, 0, keepdims=False)
    return kept, [
        lax.dynamic_index_in_dim(value, me ^ mask, 0, keepdims=False)
        for mask in range(1, lax.axis_size(axis))
    ]


def flip_all(sends, axis):
    return [flipped(send, axis, mask) for mask, send in enumerate(sends, 1)]


def copies_to_all(value, axis):
    return flip_all([value] * (lax.axis_size(axis) - 1), axis)


def placed(value, others, axis):
    me = lax.axis_index(axis)
    blocks = [value] + list(others)
    return jnp.stack(
        [lax.select_n(me, *[blocks[p ^ i] for i in range(len(blocks))]) for p in range(len(blocks))]
    )


def ring_placed(blocks, axis):
    me = lax.axis_index(axis)
    size = len(blocks)
    return jnp.concatenate(
        [lax.select_n(me, *[blocks[(i - p) % size] for i in range(size)]) for p in range(size)], 0
    )


class Sum:
    def __init__(self, value):
        self.value = value
        row = [("half", b) for b in range(bits_of("row"))]
        self.steps = row + [("scatter", "dp"), ("all", "col"), ("gather", "dp")]
        self.steps += [("double", b) for _, b in reversed(row)]

    def start(self):
        kind, what = self.steps[0]
        if kind == "half":
            sent, self.kept = split_half(self.value, "row", what)
            self.got = swap(sent, "row", what)
        elif kind == "double":
            self.got = swap(self.value, "row", what)
        elif kind == "scatter":
            size = lax.axis_size(what)
            self.kept, sends = scatter_sends(self.value.reshape((size, -1) + self.value.shape[1:]), what)
            self.got = flip_all(sends, what)
        else:
            self.got = copies_to_all(self.value, what)

    def finish(self):
        kind, what = self.steps.pop(0)
        if kind == "half":
            self.value = self.kept + self.got
        elif kind == "scatter":
            self.value = self.kept + sum(self.got)
        elif kind == "all":
            self.value = placed(self.value, self.got, what).sum(0)
        elif kind == "double":
            self.value = in_order(self.value, self.got, "row", what)
        else:
            self.value = placed(self.value, self.got, what).reshape((-1,) + self.value.shape[1:])


class Exchange:
    def __init__(self, value, dp_order):
        self.tail = value.shape[1:]
        dp_bits, row_bits = bits_of("dp"), bits_of("row")
        self.bits = [("dp", b) for b in reversed(range(dp_bits))] + [("row", b) for b in reversed(range(row_bits))]
        self.value = value.reshape((2,) * len(self.bits) + self.tail)
        self.left = [("row", b) for b in range(row_bits)] + [("dp", b) for b in dp_order]

    def start(self):
        axis, bit = self.left[0]
        place = self.bits.index((axis, bit))
        me = own_bit(axis, bit)
        sent = lax.dynamic_index_in_dim(self.value, 1 - me, place, keepdims=True)
        self.kept = lax.dynamic_index_in_dim(self.value, me, place, keepdims=True)
        self.got = swap(sent, axis, bit)

    def finish(self):
        axis, bit = self.left.pop(0)
        place = self.bits.index((axis, bit))
        me = own_bit(axis, bit)
        kept, got = self.kept, self.got
        self.value = jnp.concatenate([jnp.where(me == 0, kept, got), jnp.where(me == 0, got, kept)], place)

    def start_row(self):
        while self.left[1][0] == "row":
            self.start()
            self.finish()
        self.start()

    def result(self):
        return self.value.reshape((1 << len(self.bits),) + self.tail)


def exchanges(value, rank_dev, low, high):
    half = rank_dev // 2
    return [Exchange(value[:, :half], [low, high]), Exchange(value[:, half:], [high, low])]


def local(gradients, test_matrix, old_basis, first_moment, second_moment):
    join = Order()
    grad = gradients[0]
    rows, cols = grad.shape
    rank_dev = first_moment.shape[0]
    dp_size, row_size, col_size = (lax.axis_size(a) for a in ("dp", "row", "col"))
    group = dp_size * row_size
    rank = rank_dev * group
    wide = 2 * cols // group
    dp_bits, row_bits = bits_of("dp"), bits_of("row")
    low, high = 0, dp_bits - 1
    me_col, me_dp = lax.axis_index("col"), lax.axis_index("dp")
    at_low, at_high = own_bit("dp", low), own_bit("dp", high)

    test_values = test_matrix.astype(jnp.bfloat16)
    unit = rows // 32
    size_c, size = 10 * unit, 11 * unit
    base_a, base_b = size_c, size_c + size
    quarter_c = size_c // col_size
    half = size // 2

    both = jnp.concatenate([first_moment, second_moment], 1).reshape(rank_dev, group, wide).transpose(1, 0, 2)
    turns = exchanges(both, rank_dev, low, high)
    for turn in turns:
        turn.start_row()
    whole = jnp.dot(grad, test_values, preferred_element_type=jnp.float32)
    whole, turns[0].got, turns[1].got = join(whole, turns[0].got, turns[1].got)

    def block_c(back):
        return lax.dynamic_slice_in_dim(whole, (me_col + 2 * col_size - back) % col_size * quarter_c, quarter_c, 0)

    got_a = swap(lax.dynamic_slice_in_dim(whole, base_a + (1 - at_low) * half, half, 0), "dp", low)
    got_b = swap(lax.dynamic_slice_in_dim(whole, base_b + (1 - at_high) * half, half, 0), "dp", high)
    ring = shifted(block_c(1), "col")
    (ring,) = join(ring)
    ring = shifted(ring + block_c(2), "col")
    for turn in turns:
        turn.finish()
    got_a, got_b = join(got_a, got_b)
    kept_a = lax.dynamic_slice_in_dim(whole, base_a + at_low * half, half, 0)
    kept_b = lax.dynamic_slice_in_dim(whole, base_b + at_high * half, half, 0)
    sent_a, kept_a = split_half(kept_a + got_a, "dp", high)
    sent_b, kept_b = split_half(kept_b + got_b, "dp", low)
    got_a = swap(sent_a, "dp", high)
    got_b = swap(sent_b, "dp", low)
    (ring,) = join(ring)
    ring = shifted(ring + block_c(3), "col")
    got_a, got_b = join(got_a, got_b)
    part_ab = jnp.concatenate(
        [(kept_a + got_a).reshape(col_size, -1, rank), (kept_b + got_b).reshape(col_size, -1, rank)], 1
    ).reshape(2, 2, -1, rank)
    sent_ab, kept_ab = split_half(part_ab, "col", 0, 1)
    got_ab = swap(sent_ab, "col", 0)
    for turn in turns:
        turn.start()
    (ring,) = join(ring)
    sent_c, kept_c = split_half(ring + block_c(4), "dp", low)
    got_c = swap(sent_c, "dp", low)
    got_ab, got_c, turns[0].got, turns[1].got = join(got_ab, got_c, turns[0].got, turns[1].got)
    sent_ab, kept_ab = split_half(kept_ab + got_ab, "col", 1, 0)
    got_ab = swap(sent_ab, "col", 1)
    sent_c, kept_c = split_half(kept_c + got_c, "dp", high)
    got_c = swap(sent_c, "dp", high)
    for turn in turns:
        turn.finish()
        turn.start()
    got_ab, got_c, turns[0].got, turns[1].got = join(got_ab, got_c, turns[0].got, turns[1].got)
    own_ab = (kept_ab + got_ab).reshape(-1, rank)
    own_c = kept_c + got_c

    got_ab = swap(own_ab, "col", 1)
    got_c = swap(own_c, "dp", high)
    own = jnp.concatenate([own_ab, own_c], 0)
    gram = Sum(contract(own, own, 0, 0))
    for _ in range(row_bits - 1):
        gram.start()
        (gram.got,) = join(gram.got)
        gram.finish()
    gram.start()
    gram.got, got_c = join(gram.got, got_c)
    gram.finish()
    own_c = in_order(own_c, got_c, "dp", high)
    gram.start()
    got_c = swap(own_c, "dp", low)
    gram.got, got_c, got_ab = join(gram.got, got_c, got_ab)
    gram.finish()
    gram.start()
    own_ab = in_order(own_ab, got_ab, "col", 1)
    got_ab = swap(own_ab, "col", 0)
    (gram.got,) = join(gram.got)
    gram.finish()
    gram.start()
    ring_c = [in_order(own_c, got_c, "dp", low)]
    ring_c.append(shifted(ring_c[0], "col"))
    (gram.got,) = join(gram.got)
    gram.finish()
    for _ in range(row_bits):
        gram.start()
        (gram.got,) = join(gram.got)
        gram.finish()
    (got_ab,) = join(got_ab)

    def part_of(which):
        first = own_bit("col", 0) == 0
        mine, other = (block.reshape(2, 2, -1, rank)[:, which] for block in (own_ab, got_ab))
        pair = jnp.stack([jnp.where(first, mine, other), jnp.where(first, other, mine)], 1)
        return pair.reshape(-1, rank)

    part_a, part_b = part_of(0), part_of(1)
    got_a = swap(part_a, "dp", high)
    got_b = swap(part_b, "dp", low)
    for turn in turns:
        turn.finish()
    work = gram.value
    rest = jnp.zeros_like(work)
    inverse = rest
    work, rest, inverse = cholesky_step(0, work, rest, inverse)
    work, rest, inverse = cholesky_step(1, work, rest, inverse)
    work, got_a, got_b, ring_c[1] = join(work, got_a, got_b, ring_c[1])
    part_a = in_order(part_a, got_a, "dp", high)
    part_b = in_order(part_b, got_b, "dp", low)
    got_a = swap(part_a, "dp", low)
    got_b = swap(part_b, "dp", high)
    ring_c.append(shifted(ring_c[1], "col"))
    work, rest, inverse = cholesky_step(2, work, rest, inverse)
    work, rest, inverse = cholesky_step(3, work, rest, inverse)
    inverse, ring_c[2] = join(inverse, ring_c[2])
    ring_c.append(shifted(ring_c[2], "col"))

    def old_rows(base, bit):
        return lax.dynamic_slice_in_dim(old_basis, base + bit * half, half, 0)

    def old_ring(back):
        return lax.dynamic_slice_in_dim(old_basis, (me_col + col_size - back) % col_size * quarter_c, quarter_c, 0)

    def basis(part):
        return contract(part, inverse, 1, 1, near).astype(jnp.bfloat16)

    basis_a, basis_b = basis(part_a), basis(part_b)
    basis_c = [basis(ring_c[0]), basis(ring_c[1]), basis(ring_c[2])]
    inner = contract(part_a, old_rows(base_a, at_low), 0, 0, near)
    inner = inner + contract(part_b, old_rows(base_b, at_high), 0, 0, near)
    for back in range(3):
        inner = inner + contract(ring_c[back], old_ring(back), 0, 0, near)
    got_a, got_b, ring_c[3], inner, basis_a, basis_b, basis_c = join(
        got_a, got_b, ring_c[3], inner, basis_a, basis_b, basis_c
    )
    inner = inner + contract(got_a, old_rows(base_a, 1 - at_low), 0, 0, near)
    inner = inner + contract(got_b, old_rows(base_b, 1 - at_high), 0, 0, near)
    inner = inner + contract(ring_c[3], old_ring(3), 0, 0, near)
    inner_got = swap(inner, "row", 0)
    basis_low = jnp.concatenate(basis_c + [basis(ring_c[3]), basis_a, basis(got_a), basis_b, basis(got_b)], 0)
    starts = [(me_col + col_size - back) % col_size * quarter_c for back in range(col_size)]
    starts += [base_a + at_low * half, base_a + (1 - at_low) * half]
    starts += [base_b + at_high * half, base_b + (1 - at_high) * half]
    starts = jnp.stack(starts).astype(jnp.int32)
    sizes = [quarter_c] * col_size + [half] * 4
    basis_low, inner_got = join(basis_low, inner_got)
    inner = inner + inner_got
    for bit in range(1, row_bits):
        inner = inner + swap(inner, "row", bit)
    correlation = contract(inverse, inner, 1, 0)
    place = me_dp * row_size + lax.axis_index("row")
    turner = jnp.where(place < group // 2, correlation, correlation * correlation)
    turned = jnp.concatenate([turn.result() for turn in turns], 1).reshape(rank, wide)
    turned = contract(turner, turned, 1, 0)
    turns = exchanges(turned.reshape(group, rank_dev, wide), rank_dev, low, high)

    chunks = 4
    tile = cols // 7
    widths = [2 * tile, 2 * tile, 2 * tile, tile]
    values, kepts, gots = [None] * chunks, [None] * chunks, [None] * chunks

    def project(c):
        value = projection(starts, basis_low, grad, sizes, sum(widths[:c]), widths[c], tile)
        values[c] = value.reshape((2,) * (dp_bits + row_bits) + (rank_dev, widths[c]))

    def start(c, axis, bit):
        place = dp_bits - 1 - bit if axis == "dp" else dp_bits + row_bits - 1 - bit
        sent, kepts[c] = split_half(values[c], axis, bit, place)
        gots[c] = swap(sent, axis, bit)

    def finish(c):
        values[c] = kepts[c] + gots[c]

    def start_row(c):
        for bit in range(row_bits):
            if bit > 0:
                finish(c)
            start(c, "row", bit)

    for turn in turns:
        turn.start_row()
    project(0)
    basis_low, values[0], turns[0].got, turns[1].got = join(basis_low, values[0], turns[0].got, turns[1].got)
    for turn in turns:
        turn.finish()
        turn.start()
    start_row(0)
    project(1)
    basis_low, values[1], gots[0] = join(basis_low, values[1], gots[0])
    finish(0)
    start(0, "dp", low)
    start_row(1)
    project(2)
    basis_low, values[2], gots[1], turns[0].got, turns[1].got = join(
        basis_low, values[2], gots[1], turns[0].got, turns[1].got
    )
    finish(1)
    start(1, "dp", high)
    for turn in turns:
        turn.finish()
        turn.start()
    start_row(2)
    project(3)
    values[3], gots[2], gots[0] = join(values[3], gots[2], gots[0])
    finish(2)
    finish(0)
    start_row(3)
    start(2, "dp", low)
    gots[3], gots[1], turns[0].got, turns[1].got = join(gots[3], gots[1], turns[0].got, turns[1].got)
    finish(1)
    finish(3)
    start(0, "dp", high)
    start(1, "dp", low)
    start(3, "dp", high)
    for turn in turns:
        turn.finish()
    gots[0], gots[2] = join(gots[0], gots[2])
    finish(0)
    finish(2)
    start(2, "dp", high)
    gots[1], gots[3] = join(gots[1], gots[3])
    finish(1)
    finish(3)
    start(3, "dp", low)
    gots[2], gots[3] = join(gots[2], gots[3])
    finish(2)
    finish(3)
    projected = jnp.concatenate([value.reshape(rank_dev, width) for value, width in zip(values, widths, strict=True)], 1)
    turned = jnp.concatenate([turn.result() for turn in turns], 1).reshape(2, group // 2, rank_dev, wide).transpose(0, 2, 1, 3).reshape(2, rank_dev, cols)
    first_new = 0.9 * turned[0] + 0.1 * projected
    second_new = 0.95 * turned[1] + 0.05 * projected * projected
    return (projected, first_new, second_new)


def solution(mesh):
    in_specs = (
        P("dp", "row", "col"),
        P("col", None),
        P("row", None),
        P(("dp", "row"), "col"),
        P(("dp", "row"), "col"),
    )
    out_specs = (P(("dp", "row"), "col"), P(("dp", "row"), "col"), P(("dp", "row"), "col"))
    return jax.shard_map(local, mesh=mesh, in_specs=in_specs, out_specs=out_specs, check_vma=False)
```

time: 443 us -> 344 us (0.78)
  waiting for transfers between devices: 180 us -> 141 us
  matrix products: 87.1 us -> 48.6 us
  starting transfers between devices: 85.7 us -> 55.7 us
  Pallas kernels: 18.2 us -> 47.4 us
  local copies, waits for them, and re-layouts: 28.2 us -> 13.9 us
  other arithmetic: 33.5 us -> 28.7 us
    ppermute x70 -> x52, waiting for transfers between devices: 150 us -> 108 us  [flipped(): lax.ppermute(value, axis, [(i, i ^ mask) for i in range(lax.axis_size(axi...]
    dot_general x20, matrix products: 87.1 us -> 48.6 us  [the longest x19 25.1 us: contract(): lax.dot_general(a, b, (((a_dim,), (b_dim,)), ((), ())), precision=precisi...]
    pallas_call x0 -> x4, Pallas kernels: none -> 29.2 us  [projection(): pl.pallas_call(functools.partial(projection_kernel, sizes, first, tile),...]
    ppermute x70 -> x52, starting transfers between devices: 78.6 us -> 51 us  [flipped(): lax.ppermute(value, axis, [(i, i ^ mask) for i in range(lax.axis_size(axi...]
    add x13 -> x14, other arithmetic: 13.6 us -> 7.36 us  [the longest x1 2.91 us: local(): sent_b, kept_b = split_half(kept_b + got_b, 'dp', low)]
  transfers between devices with their start and end apart: 76 -> 58, of which waited for: 33 -> 35; matrix products, arithmetic and copies ran while one was open for 28% -> 20% of each run, Pallas kernels for 4% -> 14%
where the time goes in v3:
time: 344 us; the launch traced here: 338 us
  waiting for transfers between devices  141 us (41%)
  starting transfers between devices  55.7 us (16%)
  matrix products  48.6 us (14%)
  Pallas kernels  47.4 us (14%)
  other arithmetic  28.7 us (8%)
  local copies, waits for them, and re-layouts  13.9 us (4%)
    ppermute x52, waiting for transfers between devices, flipped(): lax.ppermute(value, axis, [(i, i ^ mask) for i in range(lax.axis_size(axi...  108 us
    ppermute x52, starting transfers between devices, flipped(): lax.ppermute(value, axis, [(i, i ^ mask) for i in range(lax.axis_size(axi...  51 us
    ppermute x6, waiting for transfers between devices, shifted(): return lax.ppermute(value, axis, [(i, (i + 1) % size) for i in range(size)])  33.3 us
    pallas_call x4, Pallas kernels, projection(): pl.pallas_call(functools.partial(projection_kernel, sizes, first, tile),...  29.2 us
    dot_general x19, matrix products, contract(): lax.dot_general(a, b, (((a_dim,), (b_dim,)), ((), ())), precision=precisi...  25.1 us
    dot_general x1, matrix products, local(): whole = jnp.dot(grad, test_values, preferred_element_type=jnp.float32)  23.5 us
    pallas_call x4, Pallas kernels, cholesky_step(): pl.pallas_call(functools.partial(cholesky_kernel, index), out_shape=[whol...  18.2 us
  transfers between devices with their start and end apart: 58, of which 35 were waited for; matrix products, arithmetic and copies ran while one was open for 20% of the time, Pallas kernels for 14%

profile of v3, /device:TPU:0, one launch (start us, length us, event | category | flops | bytes accessed | tf_op | source)
XLA Modules:
  0.0 337.7 jit_solution(10310186948923646280)
XLA Ops:
  0.6 1.6 pad_maximum_fusion
  3.8 23.5 %fusion = f32[4096,512]{1,0:T(8,128)} fusion(s32[3584,512]{1,0:T(8,128)} %param.6, bf16[1,4096,3584]{2,1,0:T(8,128)(2,1)} %param.5), kind=kOutput, calls=%fused_computation | convolution fusion | flops 15034220544 | bytes 45088768 | tf_op jit(solution)/shard_map/dot_general | solution.py:319
  27.3 3.8 %constant_dynamic-slice_fusion.20 = (f32[704,512]{1,0:T(8,128)}, f32[704,512]{1,0:T(8,128)}) fusion(f32[4096,512]{1,0:T(8,128)} %fusion, s32[]{:T(128)S(6)} %select_n.559, s32[]{:T(128)S(6)} %select_n.558), kind=kLoop, calls=%fused_computation.217 | loop fusion | bytes 5767176 | tf_op jit(solution)/shard_map/dynamic_slice | solution.py:326
  31.2 2.8 collective-permute-start.3
  34.0 1.5 collective-permute-start.4
  36.6 1.6 collective-permute-start.2
  38.2 16.7 %collective-permute-done.2 = f32[320,512]{1,0:T(8,128)} collective-permute-done((f32[320,512]{1,0:T(8,128)S(1)}, f32[320,512]{1,0:T(8,128)}, u32[]{:S(2)}, u32[]{:S(2)}) %collective-permute-start.2) | collective-permute-done | bytes 655392 | tf_op jit(solution)/shard_map/ppermute | solution.py:172
  56.4 9.7 %collective-permute-done.3 = f32[704,512]{1,0:T(8,128)S(1)} collective-permute-done((f32[704,512]{1,0:T(8,128)}, f32[704,512]{1,0:T(8,128)S(1)}, u32[]{:S(2)}, u32[]{:S(2)}) %collective-permute-start.3) | collective-permute-done | bytes 1441824 | tf_op jit(solution)/shard_map/ppermute | solution.py:163
  66.1 1.6 collective-permute-done.4
  67.7 2.9 dynamic-slice_add_fusion
  70.7 1.6 collective-permute-start.6
  74.8 1.5 collective-permute-start.11
  77.5 1.8 collective-permute-start.8
  79.5 8.4 %collective-permute-done.6 = f32[352,512]{1,0:T(8,128)S(1)} collective-permute-done((f32[352,512]{1,0:T(8,128)S(1)}, f32[352,512]{1,0:T(8,128)S(1)}, u32[]{:S(2)}, u32[]{:S(2)}) %collective-permute-start.6) | collective-permute-done | bytes 720928 | tf_op jit(solution)/shard_map/ppermute | solution.py:163
  87.9 3.6 %collective-permute-done.7 = f32[352,512]{1,0:T(8,128)S(1)} collective-permute-done((f32[352,512]{1,0:T(8,128)S(1)}, f32[352,512]{1,0:T(8,128)S(1)}, u32[]{:S(2)}, u32[]{:S(2)}) %collective-permute-start.7) | collective-permute-done | bytes 720928 | tf_op jit(solution)/shard_map/ppermute | solution.py:163
  92.7 1.6 collective-permute-start.9
  100.6 3.3 collective-permute-done.12
  103.8 2.3 collective-permute-done.10
  106.2 3.9 %collective-permute-done.9 = f32[2,1,176,512]{3,2,1,0:T(8,128)} collective-permute-done((f32[2,1,176,512]{3,2,1,0:T(8,128)}, f32[2,1,176,512]{3,2,1,0:T(8,128)}, u32[]{:S(2)}, u32[]{:S(2)}) %collective-permute-start.9) | collective-permute-done | bytes 720928 | tf_op jit(solution)/shard_map/ppermute | solution.py:163
  118.7 1.5 collective-permute-start.14
  120.2 8.2 %collective-permute-done.14 = f32[80,512]{1,0:T(8,128)S(1)} collective-permute-done((f32[80,512]{1,0:T(8,128)}, f32[80,512]{1,0:T(8,128)S(1)}, u32[]{:S(2)}, u32[]{:S(2)}) %collective-permute-start.14) | collective-permute-done | bytes 163872 | tf_op jit(solution)/shard_map/ppermute | solution.py:163
  131.2 2.7 collective-permute-start.23
  138.7 1.5 collective-permute-start.20
  141.0 5.9 %collective-permute-done.23 = f32[176,512]{1,0:T(8,128)S(1)} collective-permute-done((f32[176,512]{1,0:T(8,128)S(1)}, f32[176,512]{1,0:T(8,128)S(1)}, u32[]{:S(2)}, u32[]{:S(2)}) %collective-permute-start.23) | collective-permute-done | bytes 360480 | tf_op jit(solution)/shard_map/ppermute | solution.py:163
  146.8 2.9 collective-permute-done.19
  149.8 3.4 collective-permute-done.21
  154.1 3.6 %collective-permute-start.27 = (f32[64,512]{1,0:T(8,128)S(1)}, f32[64,512]{1,0:T(8,128)S(1)}, u32[]{:S(2)}, u32[]{:S(2)}) collective-permute-start(f32[64,512]{1,0:T(8,128)S(1)} %bitcast_add_fusion), channel_id=1, source_target_pairs={{0,3},{1,2},{2,1},{3,0},{4,7},{5,6},{6,5},{7,4},{8,11},{9,10},{10,... | collective-permute-start | bytes 393224 | tf_op jit(solution)/shard_map/ppermute | solution.py:163
  157.9 3.5 %collective-permute-done.25 = f32[64,512]{1,0:T(8,128)S(1)} collective-permute-done((f32[64,512]{1,0:T(8,128)S(1)}, f32[64,512]{1,0:T(8,128)S(1)}, u32[]{:S(2)}, u32[]{:S(2)}) %collective-permute-start.25) | collective-permute-done | bytes 131104 | tf_op jit(solution)/shard_map/ppermute | solution.py:163
  161.4 4.8 %collective-permute-done.26 = f32[64,512]{1,0:T(8,128)S(1)} collective-permute-done((f32[64,512]{1,0:T(8,128)S(1)}, f32[64,512]{1,0:T(8,128)S(1)}, u32[]{:S(2)}, u32[]{:S(2)}) %collective-permute-start.26) | collective-permute-done | bytes 131104 | tf_op jit(solution)/shard_map/ppermute | solution.py:163
  167.6 2.2 collective-permute-start.30
  171.9 1.5 collective-permute-done.30
  173.7 5.8 %collective-permute-done.24 = f32[352,512]{1,0:T(8,128)S(1)} collective-permute-done((f32[352,512]{1,0:T(8,128)S(1)}, f32[352,512]{1,0:T(8,128)S(1)}, u32[]{:S(2)}, u32[]{:S(2)}) %collective-permute-start.24) | collective-permute-done | bytes 720928 | tf_op jit(solution)/shard_map/ppermute | solution.py:163
  183.4 5.3 %shard_map.76 = (f32[512,512]{1,0:T(8,128)S(1)}, f32[512,512]{1,0:T(8,128)S(1)}, f32[512,512]{1,0:T(8,128)S(1)}) custom-call(f32[512,512]{1,0:T(8,128)S(1)} %pad_maximum_fusion.4.work_in, f32[512,512]{1,0:T(8,128)S(1)} %broadcast_in_dim.7.rest_in.inverse_in, f32[512,512]{1,0:T(8,128)S(1)} %broadcast_in_dim.7.rest_in.inverse_in), custom_call_target="tpu_custom_call" | custom-call | flops 1000000 | bytes 100000 | tf_op jit(solution)/shard_map/pallas_call | solution.py:82
  188.7 4.9 %shard_map.77 = (f32[512,512]{1,0:T(8,128)S(1)}, f32[512,512]{1,0:T(8,128)S(1)}, f32[512,512]{1,0:T(8,128)S(1)}) custom-call(f32[512,512]{1,0:T(8,128)S(1)} %get-tuple-element.136.work_in, f32[512,512]{1,0:T(8,128)S(1)} %get-tuple-element.137.rest_in, f32[512,512]{1,0:T(8,128)S(1)} %get-tuple-element.138.inverse_in), custom_call_target="tpu_custom_call" | custom-call | flops 1000000 | bytes 100000 | tf_op jit(solution)/shard_map/pallas_call | solution.py:82
  193.5 5.2 %collective-permute-done.34 = f32[320,512]{1,0:T(8,128)S(1)} collective-permute-done((f32[320,512]{1,0:T(8,128)S(1)}, f32[320,512]{1,0:T(8,128)S(1)}, u32[]{:S(2)}, u32[]{:S(2)}) %collective-permute-start.34) | collective-permute-done | bytes 655392 | tf_op jit(solution)/shard_map/ppermute | solution.py:172
  201.2 1.6 collective-permute-start.36
  202.8 4.5 %shard_map.78 = (f32[512,512]{1,0:T(8,128)S(1)}, f32[512,512]{1,0:T(8,128)S(1)}, f32[512,512]{1,0:T(8,128)S(1)}) custom-call(f32[512,512]{1,0:T(8,128)S(1)} %get-tuple-element.143.work_in, f32[512,512]{1,0:T(8,128)S(1)} %get-tuple-element.144.rest_in, f32[512,512]{1,0:T(8,128)S(1)} %get-tuple-element.145.inverse_in), custom_call_target="tpu_custom_call" | custom-call | flops 1000000 | bytes 100000 | tf_op jit(solution)/shard_map/pallas_call | solution.py:82
  207.3 3.6 %shard_map.79 = (f32[512,512]{1,0:T(8,128)}, f32[512,512]{1,0:T(8,128)}, f32[512,512]{1,0:T(8,128)S(1)}) custom-call(f32[512,512]{1,0:T(8,128)S(1)} %get-tuple-element.146.work_in, f32[512,512]{1,0:T(8,128)S(1)} %get-tuple-element.147.rest_in, f32[512,512]{1,0:T(8,128)S(1)} %get-tuple-element.148.inverse_in), custom_call_target="tpu_custom_call" | custom-call | flops 1000000 | bytes 100000 | tf_op jit(solution)/shard_map/pallas_call | solution.py:82
  212.4 1.5 fusion.15
  213.9 3.1 collective-permute-done.37
  224.2 8.1 %collective-permute-done.38 = f32[320,512]{1,0:T(8,128)S(1)} collective-permute-done((f32[320,512]{1,0:T(8,128)S(1)}, f32[320,512]{1,0:T(8,128)S(1)}, u32[]{:S(2)}, u32[]{:S(2)}) %collective-permute-start.38) | collective-permute-done | bytes 655392 | tf_op jit(solution)/shard_map/ppermute | solution.py:172
  232.4 1.5 fusion.2
  237.4 1.6 fusion.11
  240.4 1.9 multiply_select_fusion
  242.4 3.5 %fusion.69 = f32[8,64,896]{2,1,0:T(8,128)S(1)} fusion(f32[8,64,512]{2,1,0:T(8,128)S(1)} %bitcast.121, f32[512,896,1]{1,0,2:T(8,128)S(1)} %bitcast.114), kind=kOutput, calls=%fused_computation.231 | convolution fusion | flops 2818572288 | bytes 4718592 | tf_op jit(solution)/shard_map/dot_general | solution.py:16
  246.9 2.2 copy-done.1
  249.1 8.1 %shard_map.80 = f32[512,1024]{1,0:T(8,128)S(1)} custom-call(s32[8]{0:T(128)S(1)} %stack.72.starts_ref, bf16[4096,512]{1,0:T(8,128)(2,1)S(1)} %copy-done.1, bf16[4096,3584]{1,0:T(8,128)(2,1)} %bitcast.108), custom_call_target="tpu_custom_call" | custom-call | flops 1000000 | bytes 100000 | tf_op jit(solution)/shard_map/pallas_call | solution.py:129
  257.9 7.8 %shard_map.81 = f32[512,1024]{1,0:T(8,128)S(1)} custom-call(s32[8]{0:T(128)S(1)} %stack.72.starts_ref, bf16[4096,512]{1,0:T(8,128)(2,1)S(1)} %copy-done.1, bf16[4096,3584]{1,0:T(8,128)(2,1)} %bitcast.109), custom_call_target="tpu_custom_call" | custom-call | flops 1000000 | bytes 100000 | tf_op jit(solution)/shard_map/pallas_call | solution.py:129
  267.9 1.6 collective-permute-start.45
  269.7 1.5 collective-permute-start.47
  271.2 8.1 %shard_map.82 = f32[512,1024]{1,0:T(8,128)S(1)} custom-call(s32[8]{0:T(128)S(1)} %stack.72.starts_ref, bf16[4096,512]{1,0:T(8,128)(2,1)S(1)} %copy-done.1, bf16[4096,3584]{1,0:T(8,128)(2,1)} %bitcast.110), custom_call_target="tpu_custom_call" | custom-call | flops 1000000 | bytes 100000 | tf_op jit(solution)/shard_map/pallas_call | solution.py:129
  281.0 1.6 collective-permute-start.51
  283.4 1.5 collective-permute-start.53
  284.9 5.2 %shard_map.83 = f32[512,512]{1,0:T(8,128)S(1)} custom-call(s32[8]{0:T(128)S(1)} %stack.72.starts_ref, bf16[4096,512]{1,0:T(8,128)(2,1)S(1)} %copy-done.1, bf16[4096,3584]{1,0:T(8,128)(2,1)} %bitcast.111), custom_call_target="tpu_custom_call" | custom-call | flops 1000000 | bytes 100000 | tf_op jit(solution)/shard_map/pallas_call | solution.py:129
  290.1 1.6 collective-permute-done.47
  291.9 1.6 collective-permute-start.48
  293.7 11.8 %collective-permute-done.52 = f32[1,2,2,32,896]{4,3,2,1,0:T(8,128)S(1)} collective-permute-done((f32[1,2,2,32,896]{4,3,2,1,0:T(8,128)S(1)}, f32[1,2,2,32,896]{4,3,2,1,0:T(8,128)S(1)}, u32[]{:S(2)}, u32[]{:S(2)}) %collective-permute-start.52) | collective-permute-done | bytes 458784 | tf_op jit(solution)/shard_map/ppermute | solution.py:163
  310.8 7.9 %collective-permute-done.49 = f32[2,1,1,64,1024]{4,3,2,1,0:T(8,128)S(1)} collective-permute-done((f32[2,1,1,64,1024]{4,3,2,1,0:T(8,128)S(1)}, f32[2,1,1,64,1024]{4,3,2,1,0:T(8,128)S(1)}, u32[]{:S(2)}, u32[]{:S(2)}) %collective-permute-start.49) | collective-permute-done | bytes 524320 | tf_op jit(solution)/shard_map/ppermute | solution.py:163
  318.9 1.5 collective-permute-start.54
  320.5 1.6 collective-permute-start.55
  322.9 2.7 collective-permute-done.54
  325.6 4.1 %collective-permute-done.55 = f32[1,2,1,64,512]{4,3,2,1,0:T(8,128)S(1)} collective-permute-done((f32[1,2,1,64,512]{4,3,2,1,0:T(8,128)S(1)}, f32[1,2,1,64,512]{4,3,2,1,0:T(8,128)S(1)}, u32[]{:S(2)}, u32[]{:S(2)}) %collective-permute-start.55) | collective-permute-done | bytes 262176 | tf_op jit(solution)/shard_map/ppermute | solution.py:163
  330.5 2.0 collective-permute-done.56
  332.5 2.3 collective-permute-done.57
  (220 shorter events, 73.3 us)
Async XLA Ops:
  2.9 24.4 %collective-permute-start = (f32[2,2,1,32,896]{4,3,2,1,0:T(8,128)S(1)}, f32[2,2,1,32,896]{4,3,2,1,0:T(8,128)}, u32[]{:S(2)}, u32[]{:S(2)}) collective-permute-start(f32[2,2,1,32,896]{4,3,2,1,0:T(8,128)S(1)} %constant_dynamic-slice_fusion.24), channel_id=1, source_target_pairs={{0,4},{4,0},{1,5},{5,1},{2,6},{6,2},{3,7},{7,3},{8,12},{12,8},{9,1... | collective-permute-start | bytes 1376264 | tf_op jit(solution)/shard_map/ppermute | solution.py:163
  3.6 23.7 %copy-start.2 = (f32[8,32,896]{2,1,0:T(8,128)}, f32[8,32,896]{2,1,0:T(8,128)S(1)}, u32[]{:S(2)}) copy-start(f32[8,32,896]{2,1,0:T(8,128)S(1)} %copy.9) | copy-start | bytes 2752516
  3.7 23.6 %collective-permute-start.1 = (f32[2,2,1,32,896]{4,3,2,1,0:T(8,128)S(1)}, f32[2,2,1,32,896]{4,3,2,1,0:T(8,128)S(1)}, u32[]{:S(2)}, u32[]{:S(2)}) collective-permute-start(f32[2,2,1,32,896]{4,3,2,1,0:T(8,128)S(1)} %constant_dynamic-slice_fusion.23), channel_id=1, source_target_pairs={{0,4},{4,0},{1,5},{5,1},{2,6},{6,2},{3,7},{7,3},{8,12},{12,8},{9,1... | collective-permute-start | bytes 1376264 | tf_op jit(solution)/shard_map/ppermute | solution.py:163
  27.3 3.8 %copy-start.9 = (f32[2,2,1,32,896]{4,3,2,1,0:T(8,128)}, f32[2,2,1,32,896]{4,3,2,1,0:T(8,128)S(1)}, u32[]{:S(2)}) copy-start(f32[2,2,1,32,896]{4,3,2,1,0:T(8,128)S(1)} %collective-permute-done.1) | copy-start | bytes 1376260
  31.2 35.0 %collective-permute-start.3 = (f32[704,512]{1,0:T(8,128)}, f32[704,512]{1,0:T(8,128)S(1)}, u32[]{:S(2)}, u32[]{:S(2)}) collective-permute-start(f32[704,512]{1,0:T(8,128)} %get-tuple-element.196), channel_id=1, source_target_pairs={{0,8},{8,0},{16,24},{24,16},{1,9},{9,1},{17,25},{25,17},{2,10},{10... | collective-permute-start | bytes 4325384 | tf_op jit(solution)/shard_map/ppermute | solution.py:163
  34.0 33.7 %collective-permute-start.4 = (f32[704,512]{1,0:T(8,128)}, f32[704,512]{1,0:T(8,128)}, u32[]{:S(2)}, u32[]{:S(2)}) collective-permute-start(f32[704,512]{1,0:T(8,128)} %get-tuple-element.195), channel_id=1, source_target_pairs={{0,16},{8,24},{16,0},{24,8},{1,17},{9,25},{17,1},{25,9},{2,18},{10... | collective-permute-start | bytes 4325384 | tf_op jit(solution)/shard_map/ppermute | solution.py:163
  36.6 18.3 %collective-permute-start.2 = (f32[320,512]{1,0:T(8,128)S(1)}, f32[320,512]{1,0:T(8,128)}, u32[]{:S(2)}, u32[]{:S(2)}) collective-permute-start(f32[320,512]{1,0:T(8,128)S(1)} %constant_dynamic-slice_fusion.22), channel_id=1, source_target_pairs={{0,1},{1,2},{2,3},{3,0},{4,5},{5,6},{6,7},{7,4},{8,9},{9,10},{10,1... | collective-permute-start | bytes 1966088 | tf_op jit(solution)/shard_map/ppermute | solution.py:172
  56.3 20.0 %collective-permute-start.5 = (f32[320,512]{1,0:T(8,128)S(1)}, f32[320,512]{1,0:T(8,128)S(1)}, u32[]{:S(2)}, u32[]{:S(2)}) collective-permute-start(f32[320,512]{1,0:T(8,128)S(1)} %dynamic-slice_add_fusion.9), channel_id=1, source_target_pairs={{0,1},{1,2},{2,3},{3,0},{4,5},{5,6},{6,7},{7,4},{8,9},{9,10},{10,1... | collective-permute-start | bytes 1966088 | tf_op jit(solution)/shard_map/ppermute | solution.py:172
  70.7 17.2 %collective-permute-start.6 = (f32[352,512]{1,0:T(8,128)S(1)}, f32[352,512]{1,0:T(8,128)S(1)}, u32[]{:S(2)}, u32[]{:S(2)}) collective-permute-start(f32[352,512]{1,0:T(8,128)S(1)} %constant_dynamic-slice_fusion.19), channel_id=1, source_target_pairs={{0,16},{8,24},{16,0},{24,8},{1,17},{9,25},{17,1},{25,9},{2,18},{10... | collective-permute-start | bytes 2162696 | tf_op jit(solution)/shard_map/ppermute | solution.py:163
  72.3 19.1 %collective-permute-start.7 = (f32[352,512]{1,0:T(8,128)S(1)}, f32[352,512]{1,0:T(8,128)S(1)}, u32[]{:S(2)}, u32[]{:S(2)}) collective-permute-start(f32[352,512]{1,0:T(8,128)S(1)} %constant_dynamic-slice_fusion.18), channel_id=1, source_target_pairs={{0,8},{8,0},{16,24},{24,16},{1,9},{9,1},{17,25},{25,17},{2,10},{10... | collective-permute-start | bytes 2162696 | tf_op jit(solution)/shard_map/ppermute | solution.py:163
  74.0 5.4 %copy-start.3 = (f32[8,32,896]{2,1,0:T(8,128)S(1)}, f32[8,32,896]{2,1,0:T(8,128)}, u32[]{:S(2)}) copy-start(f32[8,32,896]{2,1,0:T(8,128)} %copy-done.2) | copy-start | bytes 2752516
  74.0 5.4 %copy-start.10 = (f32[2,2,1,32,896]{4,3,2,1,0:T(8,128)S(1)}, f32[2,2,1,32,896]{4,3,2,1,0:T(8,128)}, u32[]{:S(2)}) copy-start(f32[2,2,1,32,896]{4,3,2,1,0:T(8,128)} %copy-done.9) | copy-start | bytes 1376260
  74.8 25.7 %collective-permute-start.11 = (f32[2,1,2,32,896]{4,3,2,1,0:T(8,128)}, f32[2,1,2,32,896]{4,3,2,1,0:T(8,128)}, u32[]{:S(2)}, u32[]{:S(2)}) collective-permute-start(f32[2,1,2,32,896]{4,3,2,1,0:T(8,128)} %fusion.56), channel_id=1, source_target_pairs={{0,8},{8,0},{16,24},{24,16},{1,9},{9,1},{17,25},{25,17},{2,10},{10... | collective-permute-start | bytes 1376264 | tf_op jit(solution)/shard_map/ppermute | solution.py:163
  77.5 18.3 %collective-permute-start.8 = (f32[320,512]{1,0:T(8,128)S(1)}, f32[320,512]{1,0:T(8,128)S(1)}, u32[]{:S(2)}, u32[]{:S(2)}) collective-permute-start(f32[320,512]{1,0:T(8,128)S(1)} %dynamic-slice_add_fusion.8), channel_id=1, source_target_pairs={{0,1},{1,2},{2,3},{3,0},{4,5},{5,6},{6,7},{7,4},{8,9},{9,10},{10,1... | collective-permute-start | bytes 1966088 | tf_op jit(solution)/shard_map/ppermute | solution.py:172
  92.7 17.4 %collective-permute-start.9 = (f32[2,1,176,512]{3,2,1,0:T(8,128)}, f32[2,1,176,512]{3,2,1,0:T(8,128)}, u32[]{:S(2)}, u32[]{:S(2)}) collective-permute-start(f32[2,1,176,512]{3,2,1,0:T(8,128)} %fusion.25), channel_id=1, source_target_pairs={{0,1},{1,0},{2,3},{3,2},{4,5},{5,4},{6,7},{7,6},{8,9},{9,8},{10,11... | collective-permute-start | bytes 2162696 | tf_op jit(solution)/shard_map/ppermute | solution.py:163
  95.0 8.8 %collective-permute-start.12 = (f32[1,2,2,32,896]{4,3,2,1,0:T(8,128)}, f32[1,2,2,32,896]{4,3,2,1,0:T(8,128)}, u32[]{:S(2)}, u32[]{:S(2)}) collective-permute-start(f32[1,2,2,32,896]{4,3,2,1,0:T(8,128)} %fusion.54), channel_id=1, source_target_pairs={{0,16},{8,24},{16,0},{24,8},{1,17},{9,25},{17,1},{25,9},{2,18},{10... | collective-permute-start | bytes 1376264 | tf_op jit(solution)/shard_map/ppermute | solution.py:163
  98.7 7.5 %collective-permute-start.10 = (f32[160,512]{1,0:T(8,128)}, f32[160,512]{1,0:T(8,128)}, u32[]{:S(2)}, u32[]{:S(2)}) collective-permute-start(f32[160,512]{1,0:T(8,128)} %constant_dynamic-slice_fusion.17), channel_id=1, source_target_pairs={{0,8},{8,0},{16,24},{24,16},{1,9},{9,1},{17,25},{25,17},{2,10},{10... | collective-permute-start | bytes 983048 | tf_op jit(solution)/shard_map/ppermute | solution.py:163
  112.2 16.4 %collective-permute-start.13 = (f32[1,1,176,512]{3,2,1,0:T(8,128)}, f32[1,1,176,512]{3,2,1,0:T(8,128)}, u32[]{:S(2)}, u32[]{:S(2)}) collective-permute-start(f32[1,1,176,512]{3,2,1,0:T(8,128)} %constant_dynamic-slice_fusion.16), channel_id=1, source_target_pairs={{0,2},{1,3},{2,0},{3,1},{4,6},{5,7},{6,4},{7,5},{8,10},{9,11},{10,... | collective-permute-start | bytes 1081352 | tf_op jit(solution)/shard_map/ppermute | solution.py:163
  114.6 13.9 %collective-permute-start.15 = (f32[1,2,2,32,896]{4,3,2,1,0:T(8,128)}, f32[1,2,2,32,896]{4,3,2,1,0:T(8,128)}, u32[]{:S(2)}, u32[]{:S(2)}) collective-permute-start(f32[1,2,2,32,896]{4,3,2,1,0:T(8,128)} %fusion.52), channel_id=1, source_target_pairs={{0,16},{8,24},{16,0},{24,8},{1,17},{9,25},{17,1},{25,9},{2,18},{10... | collective-permute-start | bytes 1376264 | tf_op jit(solution)/shard_map/ppermute | solution.py:163
  116.2 12.9 %copy-start.6 = (f32[2,1,176,512]{3,2,1,0:T(8,128)S(1)}, f32[2,1,176,512]{3,2,1,0:T(8,128)}, u32[]{:S(2)}) copy-start(f32[2,1,176,512]{3,2,1,0:T(8,128)} %copy-done.5) | copy-start | bytes 2162692
  116.3 12.2 %collective-permute-start.16 = (f32[2,1,2,32,896]{4,3,2,1,0:T(8,128)S(1)}, f32[2,1,2,32,896]{4,3,2,1,0:T(8,128)}, u32[]{:S(2)}, u32[]{:S(2)}) collective-permute-start(f32[2,1,2,32,896]{4,3,2,1,0:T(8,128)S(1)} %fusion.50), channel_id=1, source_target_pairs={{0,8},{8,0},{16,24},{24,16},{1,9},{9,1},{17,25},{25,17},{2,10},{10... | collective-permute-start | bytes 1376264 | tf_op jit(solution)/shard_map/ppermute | solution.py:163
  118.7 9.7 %collective-permute-start.14 = (f32[80,512]{1,0:T(8,128)}, f32[80,512]{1,0:T(8,128)S(1)}, u32[]{:S(2)}, u32[]{:S(2)}) collective-permute-start(f32[80,512]{1,0:T(8,128)} %constant_dynamic-slice_fusion.15), channel_id=1, source_target_pairs={{0,16},{8,24},{16,0},{24,8},{1,17},{9,25},{17,1},{25,9},{2,18},{10... | collective-permute-start | bytes 491528 | tf_op jit(solution)/shard_map/ppermute | solution.py:163
  128.6 7.8 %collective-permute-start.18 = (f32[80,512]{1,0:T(8,128)S(1)}, f32[80,512]{1,0:T(8,128)S(1)}, u32[]{:S(2)}, u32[]{:S(2)}) collective-permute-start(f32[80,512]{1,0:T(8,128)S(1)} %dynamic-slice_add_fusion.17), channel_id=1, source_target_pairs={{0,16},{8,24},{16,0},{24,8},{1,17},{9,25},{17,1},{25,9},{2,18},{10... | collective-permute-start | bytes 491528 | tf_op jit(solution)/shard_map/ppermute | solution.py:163
  131.2 15.6 %collective-permute-start.23 = (f32[176,512]{1,0:T(8,128)S(1)}, f32[176,512]{1,0:T(8,128)S(1)}, u32[]{:S(2)}, u32[]{:S(2)}) collective-permute-start(f32[176,512]{1,0:T(8,128)S(1)} %add_bitcast_fusion), channel_id=1, source_target_pairs={{0,2},{1,3},{2,0},{3,1},{4,6},{5,7},{6,4},{7,5},{8,10},{9,11},{10,... | collective-permute-start | bytes 1081352 | tf_op jit(solution)/shard_map/ppermute | solution.py:163
  134.0 2.4 collective-permute-start.17
  136.4 16.7 %collective-permute-start.22 = (f32[160,512]{1,0:T(8,128)S(1)}, f32[160,512]{1,0:T(8,128)S(1)}, u32[]{:S(2)}, u32[]{:S(2)}) collective-permute-start(f32[160,512]{1,0:T(8,128)S(1)} %pad_maximum_fusion.15), channel_id=1, source_target_pairs={{0,8},{8,0},{16,24},{24,16},{1,9},{9,1},{17,25},{25,17},{2,10},{10... | collective-permute-start | bytes 983048 | tf_op jit(solution)/shard_map/ppermute | solution.py:163
  137.3 12.4 %collective-permute-start.19 = (f32[64,512]{1,0:T(8,128)S(1)}, f32[64,512]{1,0:T(8,128)S(1)}, u32[]{:S(2)}, u32[]{:S(2)}) collective-permute-start(f32[64,512]{1,0:T(8,128)S(1)} %get-tuple-element.247), channel_id=1, source_target_pairs={{0,8},{8,0},{16,24},{24,16},{1,9},{9,1},{17,25},{25,17},{2,10},{10... | collective-permute-start | bytes 393224 | tf_op jit(solution)/shard_map/ppermute | solution.py:163
  138.7 11.1 %collective-permute-start.20 = (f32[64,512]{1,0:T(8,128)S(1)}, f32[64,512]{1,0:T(8,128)S(1)}, u32[]{:S(2)}, u32[]{:S(2)}) collective-permute-start(f32[64,512]{1,0:T(8,128)S(1)} %get-tuple-element.246), channel_id=1, source_target_pairs={{0,16},{8,24},{16,0},{24,8},{1,17},{9,25},{17,1},{25,9},{2,18},{10... | collective-permute-start | bytes 393224 | tf_op jit(solution)/shard_map/ppermute | solution.py:163
  140.2 12.9 %collective-permute-start.21 = (f32[64,512]{1,0:T(8,128)S(1)}, f32[64,512]{1,0:T(8,128)S(1)}, u32[]{:S(2)}, u32[]{:S(2)}) collective-permute-start(f32[64,512]{1,0:T(8,128)S(1)} %get-tuple-element.245), channel_id=1, source_target_pairs={{0,24},{8,16},{16,8},{24,0},{1,25},{9,17},{17,9},{25,1},{2,26},{10... | collective-permute-start | bytes 393224 | tf_op jit(solution)/shard_map/ppermute | solution.py:163
  153.2 8.2 %collective-permute-start.25 = (f32[64,512]{1,0:T(8,128)S(1)}, f32[64,512]{1,0:T(8,128)S(1)}, u32[]{:S(2)}, u32[]{:S(2)}) collective-permute-start(f32[64,512]{1,0:T(8,128)S(1)} %bitcast_add_fusion), channel_id=1, source_target_pairs={{0,1},{1,0},{2,3},{3,2},{4,5},{5,4},{6,7},{7,6},{8,9},{9,8},{10,11... | collective-permute-start | bytes 393224 | tf_op jit(solution)/shard_map/ppermute | solution.py:163
  153.3 12.9 %collective-permute-start.26 = (f32[64,512]{1,0:T(8,128)S(1)}, f32[64,512]{1,0:T(8,128)S(1)}, u32[]{:S(2)}, u32[]{:S(2)}) collective-permute-start(f32[64,512]{1,0:T(8,128)S(1)} %bitcast_add_fusion), channel_id=1, source_target_pairs={{0,2},{1,3},{2,0},{3,1},{4,6},{5,7},{6,4},{7,5},{8,10},{9,11},{10,... | collective-permute-start | bytes 393224 | tf_op jit(solution)/shard_map/ppermute | solution.py:163
  154.1 12.1 %collective-permute-start.27 = (f32[64,512]{1,0:T(8,128)S(1)}, f32[64,512]{1,0:T(8,128)S(1)}, u32[]{:S(2)}, u32[]{:S(2)}) collective-permute-start(f32[64,512]{1,0:T(8,128)S(1)} %bitcast_add_fusion), channel_id=1, source_target_pairs={{0,3},{1,2},{2,1},{3,0},{4,7},{5,6},{6,5},{7,4},{8,11},{9,10},{10,... | collective-permute-start | bytes 393224 | tf_op jit(solution)/shard_map/ppermute | solution.py:163
  157.7 24.3 %slice-start = ((s8[8388608]{0:T(1024)(128)(4,1)}), s8[4194304]{0:T(1024)(128)(4,1)S(1)}, s32[]{:S(2)}) async-start(s8[8388608]{0:T(1024)(128)(4,1)} %bitcast.112), calls=%async_computation | async-start | bytes 8388608
  157.8 21.7 %collective-permute-start.24 = (f32[352,512]{1,0:T(8,128)S(1)}, f32[352,512]{1,0:T(8,128)S(1)}, u32[]{:S(2)}, u32[]{:S(2)}) collective-permute-start(f32[352,512]{1,0:T(8,128)S(1)} %pad_maximum_fusion.10), channel_id=1, source_target_pairs={{0,1},{1,0},{2,3},{3,2},{4,5},{5,4},{6,7},{7,6},{8,9},{9,8},{10,11... | collective-permute-start | bytes 2162696 | tf_op jit(solution)/shard_map/ppermute | solution.py:163
  166.3 5.0 %collective-permute-start.28 = (f32[64,512]{1,0:T(8,128)S(1)}, f32[64,512]{1,0:T(8,128)S(1)}, u32[]{:S(2)}, u32[]{:S(2)}) collective-permute-start(f32[64,512]{1,0:T(8,128)S(1)} %select_add_fusion), channel_id=1, source_target_pairs={{0,8},{8,0},{16,24},{24,16},{1,9},{9,1},{17,25},{25,17},{2,10},{10... | collective-permute-start | bytes 393224 | tf_op jit(solution)/shard_map/ppermute | solution.py:163
  167.0 5.0 %collective-permute-start.29 = (f32[64,512]{1,0:T(8,128)S(1)}, f32[64,512]{1,0:T(8,128)S(1)}, u32[]{:S(2)}, u32[]{:S(2)}) collective-permute-start(f32[64,512]{1,0:T(8,128)S(1)} %select_add_fusion), channel_id=1, source_target_pairs={{0,16},{8,24},{16,0},{24,8},{1,17},{9,25},{17,1},{25,9},{2,18},{10... | collective-permute-start | bytes 393224 | tf_op jit(solution)/shard_map/ppermute | solution.py:163
  167.6 5.9 %collective-permute-start.30 = (f32[64,512]{1,0:T(8,128)S(1)}, f32[64,512]{1,0:T(8,128)S(1)}, u32[]{:S(2)}, u32[]{:S(2)}) collective-permute-start(f32[64,512]{1,0:T(8,128)S(1)} %select_add_fusion), channel_id=1, source_target_pairs={{0,24},{8,16},{16,8},{24,0},{1,25},{9,17},{17,9},{25,1},{2,26},{10... | collective-permute-start | bytes 393224 | tf_op jit(solution)/shard_map/ppermute | solution.py:163
  173.6 9.4 %collective-permute-start.31 = (f32[256,512]{1,0:T(8,128)S(1)}, f32[256,512]{1,0:T(8,128)S(1)}, u32[]{:S(2)}, u32[]{:S(2)}) collective-permute-start(f32[256,512]{1,0:T(8,128)S(1)} %bitcast.141), channel_id=1, source_target_pairs={{0,4},{4,0},{1,5},{5,1},{2,6},{6,2},{3,7},{7,3},{8,12},{12,8},{9,1... | collective-permute-start | bytes 1572872 | tf_op jit(solution)/shard_map/ppermute | solution.py:163
  179.7 19.0 %collective-permute-start.32 = (f32[352,512]{1,0:T(8,128)S(1)}, f32[352,512]{1,0:T(8,128)S(1)}, u32[]{:S(2)}, u32[]{:S(2)}) collective-permute-start(f32[352,512]{1,0:T(8,128)S(1)} %bitcast.140), channel_id=1, source_target_pairs={{0,16},{8,24},{16,0},{24,8},{1,17},{9,25},{17,1},{25,9},{2,18},{10... | collective-permute-start | bytes 2162696 | tf_op jit(solution)/shard_map/ppermute | solution.py:163
  180.3 18.4 %collective-permute-start.33 = (f32[352,512]{1,0:T(8,128)S(1)}, f32[352,512]{1,0:T(8,128)S(1)}, u32[]{:S(2)}, u32[]{:S(2)}) collective-permute-start(f32[352,512]{1,0:T(8,128)S(1)} %bitcast.139), channel_id=1, source_target_pairs={{0,8},{8,0},{16,24},{24,16},{1,9},{9,1},{17,25},{25,17},{2,10},{10... | collective-permute-start | bytes 2162696 | tf_op jit(solution)/shard_map/ppermute | solution.py:163
  181.2 17.5 %collective-permute-start.34 = (f32[320,512]{1,0:T(8,128)S(1)}, f32[320,512]{1,0:T(8,128)S(1)}, u32[]{:S(2)}, u32[]{:S(2)}) collective-permute-start(f32[320,512]{1,0:T(8,128)S(1)} %pad_maximum_fusion.13), channel_id=1, source_target_pairs={{0,1},{1,2},{2,3},{3,0},{4,5},{5,6},{6,7},{7,4},{8,9},{9,10},{10,1... | collective-permute-start | bytes 1966088 | tf_op jit(solution)/shard_map/ppermute | solution.py:172
  199.0 33.2 %collective-permute-start.35 = (f32[704,512]{1,0:T(8,128)S(1)}, f32[704,512]{1,0:T(8,128)S(1)}, u32[]{:S(2)}, u32[]{:S(2)}) collective-permute-start(f32[704,512]{1,0:T(8,128)S(1)} %pad_maximum_fusion.2), channel_id=1, source_target_pairs={{0,8},{8,0},{16,24},{24,16},{1,9},{9,1},{17,25},{25,17},{2,10},{10... | collective-permute-start | bytes 4325384 | tf_op jit(solution)/shard_map/ppermute | solution.py:163
  200.4 16.5 %collective-permute-start.37 = (f32[320,512]{1,0:T(8,128)S(1)}, f32[320,512]{1,0:T(8,128)S(1)}, u32[]{:S(2)}, u32[]{:S(2)}) collective-permute-start(f32[320,512]{1,0:T(8,128)S(1)} %collective-permute-done.34), channel_id=1, source_target_pairs={{0,1},{1,2},{2,3},{3,0},{4,5},{5,6},{6,7},{7,4},{8,9},{9,10},{10,1... | collective-permute-start | bytes 1966088 | tf_op jit(solution)/shard_map/ppermute | solution.py:172
  201.2 31.2 %collective-permute-start.36 = (f32[704,512]{1,0:T(8,128)S(1)}, f32[704,512]{1,0:T(8,128)S(1)}, u32[]{:S(2)}, u32[]{:S(2)}) collective-permute-start(f32[704,512]{1,0:T(8,128)S(1)} %pad_maximum_fusion.3), channel_id=1, source_target_pairs={{0,16},{8,24},{16,0},{24,8},{1,17},{9,25},{17,1},{25,9},{2,18},{10... | collective-permute-start | bytes 4325384 | tf_op jit(solution)/shard_map/ppermute | solution.py:163
  217.0 15.3 %collective-permute-start.38 = (f32[320,512]{1,0:T(8,128)S(1)}, f32[320,512]{1,0:T(8,128)S(1)}, u32[]{:S(2)}, u32[]{:S(2)}) collective-permute-start(f32[320,512]{1,0:T(8,128)S(1)} %collective-permute-done.37), channel_id=1, source_target_pairs={{0,1},{1,2},{2,3},{3,0},{4,5},{5,6},{6,7},{7,4},{8,9},{9,10},{10,1... | collective-permute-start | bytes 1966088 | tf_op jit(solution)/shard_map/ppermute | solution.py:172
  236.5 3.9 %collective-permute-start.39 = (f32[512,512]{1,0:T(8,128)S(1)}, f32[512,512]{1,0:T(8,128)S(1)}, u32[]{:S(2)}, u32[]{:S(2)}) collective-permute-start(f32[512,512]{1,0:T(8,128)S(1)} %add_add_fusion), channel_id=1, source_target_pairs={{0,4},{4,0},{1,5},{5,1},{2,6},{6,2},{3,7},{7,3},{8,12},{12,8},{9,1... | collective-permute-start | bytes 3145736 | tf_op jit(solution)/shard_map/ppermute | solution.py:163
  246.1 11.0 %collective-permute-start.40 = (f32[2,2,1,32,896]{4,3,2,1,0:T(8,128)S(1)}, f32[2,2,1,32,896]{4,3,2,1,0:T(8,128)}, u32[]{:S(2)}, u32[]{:S(2)}) collective-permute-start(f32[2,2,1,32,896]{4,3,2,1,0:T(8,128)S(1)} %constant_dynamic-slice_fusion.13), channel_id=1, source_target_pairs={{0,4},{4,0},{1,5},{5,1},{2,6},{6,2},{3,7},{7,3},{8,12},{12,8},{9,1... | collective-permute-start | bytes 1376264 | tf_op jit(solution)/shard_map/ppermute | solution.py:163
  246.7 10.5 %collective-permute-start.41 = (f32[2,2,1,32,896]{4,3,2,1,0:T(8,128)S(1)}, f32[2,2,1,32,896]{4,3,2,1,0:T(8,128)S(1)}, u32[]{:S(2)}, u32[]{:S(2)}) collective-permute-start(f32[2,2,1,32,896]{4,3,2,1,0:T(8,128)S(1)} %constant_dynamic-slice_fusion.12), channel_id=1, source_target_pairs={{0,4},{4,0},{1,5},{5,1},{2,6},{6,2},{3,7},{7,3},{8,12},{12,8},{9,1... | collective-permute-start | bytes 1376264 | tf_op jit(solution)/shard_map/ppermute | solution.py:163
  257.3 8.3 %collective-permute-start.42 = (f32[2,2,1,64,1024]{4,3,2,1,0:T(8,128)S(1)}, f32[2,2,1,64,1024]{4,3,2,1,0:T(8,128)S(1)}, u32[]{:S(2)}, u32[]{:S(2)}) collective-permute-start(f32[2,2,1,64,1024]{4,3,2,1,0:T(8,128)S(1)} %constant_dynamic-slice_fusion.11), channel_id=1, source_target_pairs={{0,4},{4,0},{1,5},{5,1},{2,6},{6,2},{3,7},{7,3},{8,12},{12,8},{9,1... | collective-permute-start | bytes 3145736 | tf_op jit(solution)/shard_map/ppermute | solution.py:163
  265.8 14.7 %collective-permute-start.43 = (f32[2,2,1,64,1024]{4,3,2,1,0:T(8,128)S(1)}, f32[2,2,1,64,1024]{4,3,2,1,0:T(8,128)S(1)}, u32[]{:S(2)}, u32[]{:S(2)}) collective-permute-start(f32[2,2,1,64,1024]{4,3,2,1,0:T(8,128)S(1)} %constant_dynamic-slice_fusion.10), channel_id=1, source_target_pairs={{0,4},{4,0},{1,5},{5,1},{2,6},{6,2},{3,7},{7,3},{8,12},{12,8},{9,1... | collective-permute-start | bytes 3145736 | tf_op jit(solution)/shard_map/ppermute | solution.py:163
  267.0 13.4 %collective-permute-start.44 = (f32[2,1,2,32,896]{4,3,2,1,0:T(8,128)S(1)}, f32[2,1,2,32,896]{4,3,2,1,0:T(8,128)S(1)}, u32[]{:S(2)}, u32[]{:S(2)}) collective-permute-start(f32[2,1,2,32,896]{4,3,2,1,0:T(8,128)S(1)} %fusion.48), channel_id=1, source_target_pairs={{0,8},{8,0},{16,24},{24,16},{1,9},{9,1},{17,25},{25,17},{2,10},{10... | collective-permute-start | bytes 1376264 | tf_op jit(solution)/shard_map/ppermute | solution.py:163
  267.9 12.7 %collective-permute-start.45 = (f32[1,2,2,32,896]{4,3,2,1,0:T(8,128)S(1)}, f32[1,2,2,32,896]{4,3,2,1,0:T(8,128)S(1)}, u32[]{:S(2)}, u32[]{:S(2)}) collective-permute-start(f32[1,2,2,32,896]{4,3,2,1,0:T(8,128)S(1)} %fusion.46), channel_id=1, source_target_pairs={{0,16},{8,24},{16,0},{24,8},{1,17},{9,25},{17,1},{25,9},{2,18},{10... | collective-permute-start | bytes 1376264 | tf_op jit(solution)/shard_map/ppermute | solution.py:163
  269.7 22.0 %collective-permute-start.47 = (f32[2,1,1,64,1024]{4,3,2,1,0:T(8,128)S(1)}, f32[2,1,1,64,1024]{4,3,2,1,0:T(8,128)S(1)}, u32[]{:S(2)}, u32[]{:S(2)}) collective-permute-start(f32[2,1,1,64,1024]{4,3,2,1,0:T(8,128)S(1)} %constant_dynamic-slice_fusion.8), channel_id=1, source_target_pairs={{0,8},{8,0},{16,24},{24,16},{1,9},{9,1},{17,25},{25,17},{2,10},{10... | collective-permute-start | bytes 1572872 | tf_op jit(solution)/shard_map/ppermute | solution.py:163
  280.6 11.0 %collective-permute-start.46 = (f32[2,2,1,64,1024]{4,3,2,1,0:T(8,128)S(1)}, f32[2,2,1,64,1024]{4,3,2,1,0:T(8,128)S(1)}, u32[]{:S(2)}, u32[]{:S(2)}) collective-permute-start(f32[2,2,1,64,1024]{4,3,2,1,0:T(8,128)S(1)} %constant_dynamic-slice_fusion.9), channel_id=1, source_target_pairs={{0,4},{4,0},{1,5},{5,1},{2,6},{6,2},{3,7},{7,3},{8,12},{12,8},{9,1... | collective-permute-start | bytes 3145736 | tf_op jit(solution)/shard_map/ppermute | solution.py:163
  281.0 26.1 %collective-permute-start.51 = (f32[1,2,1,64,1024]{4,3,2,1,0:T(8,128)S(1)}, f32[1,2,1,64,1024]{4,3,2,1,0:T(8,128)S(1)}, u32[]{:S(2)}, u32[]{:S(2)}) collective-permute-start(f32[1,2,1,64,1024]{4,3,2,1,0:T(8,128)S(1)} %constant_dynamic-slice_fusion.4), channel_id=1, source_target_pairs={{0,16},{8,24},{16,0},{24,8},{1,17},{9,25},{17,1},{25,9},{2,18},{10... | collective-permute-start | bytes 1572872 | tf_op jit(solution)/shard_map/ppermute | solution.py:163
  282.7 22.9 %collective-permute-start.52 = (f32[1,2,2,32,896]{4,3,2,1,0:T(8,128)S(1)}, f32[1,2,2,32,896]{4,3,2,1,0:T(8,128)S(1)}, u32[]{:S(2)}, u32[]{:S(2)}) collective-permute-start(f32[1,2,2,32,896]{4,3,2,1,0:T(8,128)S(1)} %fusion.44), channel_id=1, source_target_pairs={{0,16},{8,24},{16,0},{24,8},{1,17},{9,25},{17,1},{25,9},{2,18},{10... | collective-permute-start | bytes 1376264 | tf_op jit(solution)/shard_map/ppermute | solution.py:163
  283.4 23.6 %collective-permute-start.53 = (f32[2,1,2,32,896]{4,3,2,1,0:T(8,128)S(1)}, f32[2,1,2,32,896]{4,3,2,1,0:T(8,128)S(1)}, u32[]{:S(2)}, u32[]{:S(2)}) collective-permute-start(f32[2,1,2,32,896]{4,3,2,1,0:T(8,128)S(1)} %fusion.42), channel_id=1, source_target_pairs={{0,8},{8,0},{16,24},{24,16},{1,9},{9,1},{17,25},{25,17},{2,10},{10... | collective-permute-start | bytes 1376264 | tf_op jit(solution)/shard_map/ppermute | solution.py:163
  291.7 15.3 %collective-permute-start.50 = (f32[2,2,1,64,512]{4,3,2,1,0:T(8,128)S(1)}, f32[2,2,1,64,512]{4,3,2,1,0:T(8,128)S(1)}, u32[]{:S(2)}, u32[]{:S(2)}) collective-permute-start(f32[2,2,1,64,512]{4,3,2,1,0:T(8,128)S(1)} %constant_dynamic-slice_fusion.5), channel_id=1, source_target_pairs={{0,4},{4,0},{1,5},{5,1},{2,6},{6,2},{3,7},{7,3},{8,12},{12,8},{9,1... | collective-permute-start | bytes 1572872 | tf_op jit(solution)/shard_map/ppermute | solution.py:163
  291.9 18.9 %collective-permute-start.48 = (f32[1,1,1,64,1024]{4,3,2,1,0:T(8,128)S(1)}, f32[1,1,1,64,1024]{4,3,2,1,0:T(8,128)S(1)}, u32[]{:S(2)}, u32[]{:S(2)}) collective-permute-start(f32[1,1,1,64,1024]{4,3,2,1,0:T(8,128)S(1)} %constant_dynamic-slice_fusion.7), channel_id=1, source_target_pairs={{0,16},{8,24},{16,0},{24,8},{1,17},{9,25},{17,1},{25,9},{2,18},{10... | collective-permute-start | bytes 786440 | tf_op jit(solution)/shard_map/ppermute | solution.py:163
  305.6 13.1 %collective-permute-start.49 = (f32[2,1,1,64,1024]{4,3,2,1,0:T(8,128)S(1)}, f32[2,1,1,64,1024]{4,3,2,1,0:T(8,128)S(1)}, u32[]{:S(2)}, u32[]{:S(2)}) collective-permute-start(f32[2,1,1,64,1024]{4,3,2,1,0:T(8,128)S(1)} %constant_dynamic-slice_fusion.6), channel_id=1, source_target_pairs={{0,8},{8,0},{16,24},{24,16},{1,9},{9,1},{17,25},{25,17},{2,10},{10... | collective-permute-start | bytes 1572872 | tf_op jit(solution)/shard_map/ppermute | solution.py:163
  318.9 6.7 %collective-permute-start.54 = (f32[1,1,1,64,1024]{4,3,2,1,0:T(8,128)S(1)}, f32[1,1,1,64,1024]{4,3,2,1,0:T(8,128)S(1)}, u32[]{:S(2)}, u32[]{:S(2)}) collective-permute-start(f32[1,1,1,64,1024]{4,3,2,1,0:T(8,128)S(1)} %constant_dynamic-slice_fusion.3), channel_id=1, source_target_pairs={{0,8},{8,0},{16,24},{24,16},{1,9},{9,1},{17,25},{25,17},{2,10},{10... | collective-permute-start | bytes 786440 | tf_op jit(solution)/shard_map/ppermute | solution.py:163
  320.5 9.2 %collective-permute-start.55 = (f32[1,2,1,64,512]{4,3,2,1,0:T(8,128)S(1)}, f32[1,2,1,64,512]{4,3,2,1,0:T(8,128)S(1)}, u32[]{:S(2)}, u32[]{:S(2)}) collective-permute-start(f32[1,2,1,64,512]{4,3,2,1,0:T(8,128)S(1)} %constant_dynamic-slice_fusion.2), channel_id=1, source_target_pairs={{0,16},{8,24},{16,0},{24,8},{1,17},{9,25},{17,1},{25,9},{2,18},{10... | collective-permute-start | bytes 786440 | tf_op jit(solution)/shard_map/ppermute | solution.py:163
  322.2 10.3 %collective-permute-start.56 = (f32[1,1,1,64,1024]{4,3,2,1,0:T(8,128)S(1)}, f32[1,1,1,64,1024]{4,3,2,1,0:T(8,128)S(1)}, u32[]{:S(2)}, u32[]{:S(2)}) collective-permute-start(f32[1,1,1,64,1024]{4,3,2,1,0:T(8,128)S(1)} %constant_dynamic-slice_fusion.1), channel_id=1, source_target_pairs={{0,16},{8,24},{16,0},{24,8},{1,17},{9,25},{17,1},{25,9},{2,18},{10... | collective-permute-start | bytes 786440 | tf_op jit(solution)/shard_map/ppermute | solution.py:163
  329.8 5.0 %collective-permute-start.57 = (f32[1,1,1,64,512]{4,3,2,1,0:T(8,128)S(1)}, f32[1,1,1,64,512]{4,3,2,1,0:T(8,128)S(1)}, u32[]{:S(2)}, u32[]{:S(2)}) collective-permute-start(f32[1,1,1,64,512]{4,3,2,1,0:T(8,128)S(1)} %constant_dynamic-slice_fusion), channel_id=1, source_target_pairs={{0,8},{8,0},{16,24},{24,16},{1,9},{9,1},{17,25},{25,17},{2,10},{10... | collective-permute-start | bytes 393224 | tf_op jit(solution)/shard_map/ppermute | solution.py:163
  (7 other events, 14.4 us)

commit v4 on v3

--- a/solution.py
+++ b/solution.py
@@ -254,12 +254,12 @@
 
 
 class Exchange:
-    def __init__(self, value, dp_order):
+    def __init__(self, value, dp_order, row=True):
         self.tail = value.shape[1:]
         dp_bits, row_bits = bits_of("dp"), bits_of("row")
         self.bits = [("dp", b) for b in reversed(range(dp_bits))] + [("row", b) for b in reversed(range(row_bits))]
         self.value = value.reshape((2,) * len(self.bits) + self.tail)
-        self.left = [("row", b) for b in range(row_bits)] + [("dp", b) for b in dp_order]
+        self.left = [("row", b) for b in range(row_bits) if row] + [("dp", b) for b in dp_order]
 
     def start(self):
         axis, bit = self.left[0]
@@ -277,18 +277,45 @@
         self.value = jnp.concatenate([jnp.where(me == 0, kept, got), jnp.where(me == 0, got, kept)], place)
 
     def start_row(self):
-        while self.left[1][0] == "row":
+        while len(self.left) > 1 and self.left[1][0] == "row":
             self.start()
             self.finish()
         self.start()
 
+    def split(self, low, high):
+        half = self.tail[0] // 2
+        return [
+            Exchange(self.result()[:, at : at + half], order, False)
+            for at, order in ((0, [low, high]), (half, [high, low]))
+        ]
+
     def result(self):
         return self.value.reshape((1 << len(self.bits),) + self.tail)
 
 
-def exchanges(value, rank_dev, low, high):
-    half = rank_dev // 2
-    return [Exchange(value[:, :half], [low, high]), Exchange(value[:, half:], [high, low])]
+class Part:
+    def __init__(self, value, dp_bits, row_bits):
+        self.value = value
+        self.bits = (dp_bits, row_bits)
+
+    def start(self, axis, bit):
+        dp_bits, row_bits = self.bits
+        place = dp_bits - 1 - bit if axis == "dp" else dp_bits + row_bits - 1 - bit
+        sent, self.kept = split_half(self.value, axis, bit, place)
+        self.got = swap(sent, axis, bit)
+
+    def finish(self):
+        self.value = self.kept + self.got
+
+    def start_row(self):
+        for bit in range(self.bits[1]):
+            if bit > 0:
+                self.finish()
+            self.start("row", bit)
+
+    def halves(self):
+        cut = self.value.shape[-1] // 2
+        return [Part(self.value[..., :cut], *self.bits), Part(self.value[..., cut:], *self.bits)]
 
 
 def local(gradients, test_matrix, old_basis, first_moment, second_moment):
@@ -313,11 +340,10 @@
     half = size // 2
 
     both = jnp.concatenate([first_moment, second_moment], 1).reshape(rank_dev, group, wide).transpose(1, 0, 2)
-    turns = exchanges(both, rank_dev, low, high)
-    for turn in turns:
-        turn.start_row()
+    turn = Exchange(both, [])
+    turn.start_row()
     whole = jnp.dot(grad, test_values, preferred_element_type=jnp.float32)
-    whole, turns[0].got, turns[1].got = join(whole, turns[0].got, turns[1].got)
+    whole, turn.got = join(whole, turn.got)
 
     def block_c(back):
         return lax.dynamic_slice_in_dim(whole, (me_col + 2 * col_size - back) % col_size * quarter_c, quarter_c, 0)
@@ -327,8 +353,8 @@
     ring = shifted(block_c(1), "col")
     (ring,) = join(ring)
     ring = shifted(ring + block_c(2), "col")
-    for turn in turns:
-        turn.finish()
+    turn.finish()
+    turns = turn.split(low, high)
     got_a, got_b = join(got_a, got_b)
     kept_a = lax.dynamic_slice_in_dim(whole, base_a + at_low * half, half, 0)
     kept_b = lax.dynamic_slice_in_dim(whole, base_b + at_high * half, half, 0)
@@ -456,82 +482,57 @@
     place = me_dp * row_size + lax.axis_index("row")
     turner = jnp.where(place < group // 2, correlation, correlation * correlation)
     turned = jnp.concatenate([turn.result() for turn in turns], 1).reshape(rank, wide)
-    turned = contract(turner, turned, 1, 0)
-    turns = exchanges(turned.reshape(group, rank_dev, wide), rank_dev, low, high)
-
-    chunks = 4
+    turned = contract(turner, turned, 1, 0, near)
+    turn = Exchange(turned.reshape(group, rank_dev, wide), [])
+    turn.start_row()
+    turn.got, basis_low = join(turn.got, basis_low)
+    turn.finish()
+    turns = turn.split(low, high)
+    for turn in turns:
+        turn.start()
+
     tile = cols // 7
-    widths = [2 * tile, 2 * tile, 2 * tile, tile]
-    values, kepts, gots = [None] * chunks, [None] * chunks, [None] * chunks
+    widths = [3 * tile, 4 * tile]
 
     def project(c):
         value = projection(starts, basis_low, grad, sizes, sum(widths[:c]), widths[c], tile)
-        values[c] = value.reshape((2,) * (dp_bits + row_bits) + (rank_dev, widths[c]))
-
-    def start(c, axis, bit):
-        place = dp_bits - 1 - bit if axis == "dp" else dp_bits + row_bits - 1 - bit
-        sent, kepts[c] = split_half(values[c], axis, bit, place)
-        gots[c] = swap(sent, axis, bit)
-
-    def finish(c):
-        values[c] = kepts[c] + gots[c]
-
-    def start_row(c):
-        for bit in range(row_bits):
-            if bit > 0:
-                finish(c)
-            start(c, "row", bit)
-
-    for turn in turns:
-        turn.start_row()
-    project(0)
-    basis_low, values[0], turns[0].got, turns[1].got = join(basis_low, values[0], turns[0].got, turns[1].got)
+        return Part(value.reshape((2,) * (dp_bits + row_bits) + (rank_dev, widths[c])), dp_bits, row_bits)
+
+    front = project(0)
+    front.value, basis_low, turns[0].got, turns[1].got = join(front.value, basis_low, turns[0].got, turns[1].got)
+    front.start_row()
     for turn in turns:
         turn.finish()
         turn.start()
-    start_row(0)
-    project(1)
-    basis_low, values[1], gots[0] = join(basis_low, values[1], gots[0])
-    finish(0)
-    start(0, "dp", low)
-    start_row(1)
-    project(2)
-    basis_low, values[2], gots[1], turns[0].got, turns[1].got = join(
-        basis_low, values[2], gots[1], turns[0].got, turns[1].got
-    )
-    finish(1)
-    start(1, "dp", high)
+    back = project(1)
+    back.value, front.got, turns[0].got, turns[1].got = join(back.value, front.got, turns[0].got, turns[1].got)
+    front.finish()
+    front = front.halves()
+    for part, bit in zip(front, (low, high), strict=True):
+        part.start("dp", bit)
+    back.start_row()
     for turn in turns:
         turn.finish()
-        turn.start()
-    start_row(2)
-    project(3)
-    values[3], gots[2], gots[0] = join(values[3], gots[2], gots[0])
-    finish(2)
-    finish(0)
-    start_row(3)
-    start(2, "dp", low)
-    gots[3], gots[1], turns[0].got, turns[1].got = join(gots[3], gots[1], turns[0].got, turns[1].got)
-    finish(1)
-    finish(3)
-    start(0, "dp", high)
-    start(1, "dp", low)
-    start(3, "dp", high)
-    for turn in turns:
-        turn.finish()
-    gots[0], gots[2] = join(gots[0], gots[2])
-    finish(0)
-    finish(2)
-    start(2, "dp", high)
-    gots[1], gots[3] = join(gots[1], gots[3])
-    finish(1)
-    finish(3)
-    start(3, "dp", low)
-    gots[2], gots[3] = join(gots[2], gots[3])
-    finish(2)
-    finish(3)
-    projected = jnp.concatenate([value.reshape(rank_dev, width) for value, width in zip(values, widths, strict=True)], 1)
-    turned = jnp.concatenate([turn.result() for turn in turns], 1).reshape(2, group // 2, rank_dev, wide).transpose(0, 2, 1, 3).reshape(2, rank_dev, cols)
+    front[0].got, front[1].got, back.got = join(front[0].got, front[1].got, back.got)
+    back.finish()
+    back = back.halves()
+    for part, bit in zip(back, (low, high), strict=True):
+        part.start("dp", bit)
+    for part, bit in zip(front, (high, low), strict=True):
+        part.finish()
+        part.start("dp", bit)
+    back[0].got, back[1].got, front[0].got, front[1].got = join(back[0].got, back[1].got, front[0].got, front[1].got)
+    for part, bit in zip(back, (high, low), strict=True):
+        part.finish()
+        part.start("dp", bit)
+    for part in front:
+        part.finish()
+    back[0].got, back[1].got = join(back[0].got, back[1].got)
+    for part in back:
+        part.finish()
+    projected = jnp.concatenate([part.value.reshape(rank_dev, -1) for part in front + back], 1)
+    turned = jnp.concatenate([turn.result() for turn in turns], 1).reshape(2, group // 2, rank_dev, wide)
+    turned = turned.transpose(0, 2, 1, 3).reshape(2, rank_dev, cols)
     first_new = 0.9 * turned[0] + 0.1 * projected
     second_new = 0.95 * turned[1] + 0.05 * projected * projected
     return (projected, first_new, second_new)

time: 344 us -> 328 us (0.953)
  waiting for transfers between devices: 141 us -> 132 us
  Pallas kernels: 47.4 us -> 41.3 us
    ppermute x52 -> x48, waiting for transfers between devices: 108 us -> 98.1 us  [flipped(): lax.ppermute(value, axis, [(i, i ^ mask) for i in range(lax.axis_size(axi...]
    pallas_call x4 -> x2, Pallas kernels: 29.2 us -> 23.1 us  [projection(): pl.pallas_call(functools.partial(projection_kernel, sizes, first, tile),...]
    ppermute x52 -> x48, starting transfers between devices: 51 us -> 52.4 us  [flipped(): lax.ppermute(value, axis, [(i, i ^ mask) for i in range(lax.axis_size(axi...]
  transfers between devices with their start and end apart: 58 -> 54, of which waited for: 35 -> 30; matrix products, arithmetic and copies ran while one was open for 20% -> 21% of each run, Pallas kernels for 14% -> 13%
where the time goes in v4:
time: 328 us; the launch traced here: 322 us
  waiting for transfers between devices  132 us (40%)
  starting transfers between devices  56.5 us (17%)
  matrix products  46.8 us (14%)
  Pallas kernels  41.3 us (13%)
  other arithmetic  27.2 us (8%)
  local copies, waits for them, and re-layouts  16.1 us (5%)
    ppermute x48, waiting for transfers between devices, flipped(): lax.ppermute(value, axis, [(i, i ^ mask) for i in range(lax.axis_size(axi...  98.1 us
    ppermute x48, starting transfers between devices, flipped(): lax.ppermute(value, axis, [(i, i ^ mask) for i in range(lax.axis_size(axi...  52.4 us
    ppermute x6, waiting for transfers between devices, shifted(): return lax.ppermute(value, axis, [(i, (i + 1) % size) for i in range(size)])  34.2 us
    dot_general x19, matrix products, contract(): lax.dot_general(a, b, (((a_dim,), (b_dim,)), ((), ())), precision=precisi...  23.4 us
    dot_general x1, matrix products, local(): whole = jnp.dot(grad, test_values, preferred_element_type=jnp.float32)  23.4 us
    pallas_call x2, Pallas kernels, projection(): pl.pallas_call(functools.partial(projection_kernel, sizes, first, tile),...  23.1 us
    pallas_call x4, Pallas kernels, cholesky_step(): pl.pallas_call(functools.partial(cholesky_kernel, index), out_shape=[whol...  18.2 us
  transfers between devices with their start and end apart: 54, of which 30 were waited for; matrix products, arithmetic and copies ran while one was open for 21% of the time, Pallas kernels for 13%

profile of v4, /device:TPU:0, one launch (start us, length us, event | category | flops | bytes accessed | tf_op | source)
XLA Modules:
  0.0 322.1 jit_solution(15877670626313324523)
XLA Ops:
  0.6 1.6 pad_maximum_fusion
  3.0 23.4 %fusion = f32[4096,512]{1,0:T(8,128)} fusion(s32[3584,512]{1,0:T(8,128)} %param.6, bf16[1,4096,3584]{2,1,0:T(8,128)(2,1)} %param.5), kind=kOutput, calls=%fused_computation | convolution fusion | flops 15034220544 | bytes 45088768 | tf_op jit(solution)/shard_map/dot_general | solution.py:345
  26.3 3.6 %constant_dynamic-slice_fusion.21 = (f32[704,512]{1,0:T(8,128)}, f32[704,512]{1,0:T(8,128)}) fusion(f32[4096,512]{1,0:T(8,128)} %fusion, s32[]{:T(128)S(6)} %select_n.546, s32[]{:T(128)S(6)} %select_n.545), kind=kLoop, calls=%fused_computation.191 | loop fusion | bytes 5767176 | tf_op jit(solution)/shard_map/dynamic_slice | solution.py:352
  30.0 2.5 collective-permute-start.2
  32.5 1.5 collective-permute-start.3
  34.0 2.0 constant_dynamic-slice_fusion.23
  36.0 1.6 collective-permute-start.1
  38.9 15.8 %collective-permute-done.1 = f32[320,512]{1,0:T(8,128)} collective-permute-done((f32[320,512]{1,0:T(8,128)}, f32[320,512]{1,0:T(8,128)}, u32[]{:S(2)}, u32[]{:S(2)}) %collective-permute-start.1) | collective-permute-done | bytes 655392 | tf_op jit(solution)/shard_map/ppermute | solution.py:172
  54.7 1.4 dynamic-slice_add_fusion.8
  56.2 8.8 %collective-permute-done.2 = f32[704,512]{1,0:T(8,128)S(1)} collective-permute-done((f32[704,512]{1,0:T(8,128)}, f32[704,512]{1,0:T(8,128)S(1)}, u32[]{:S(2)}, u32[]{:S(2)}) %collective-permute-start.2) | collective-permute-done | bytes 1441824 | tf_op jit(solution)/shard_map/ppermute | solution.py:163
  64.9 1.6 collective-permute-done.3
  66.5 2.9 dynamic-slice_add_fusion.2
  69.9 1.8 collective-permute-start.5
  72.0 1.7 collective-permute-done.4
  76.6 10.3 %collective-permute-done.6 = f32[352,512]{1,0:T(8,128)S(1)} collective-permute-done((f32[352,512]{1,0:T(8,128)S(1)}, f32[352,512]{1,0:T(8,128)S(1)}, u32[]{:S(2)}, u32[]{:S(2)}) %collective-permute-start.6) | collective-permute-done | bytes 720928 | tf_op jit(solution)/shard_map/ppermute | solution.py:163
  87.0 2.1 collective-permute-done.5
  89.4 1.9 collective-permute-start.8
  92.1 1.5 collective-permute-start.10
  97.4 7.1 %collective-permute-done.10 = f32[2,1,2,32,896]{4,3,2,1,0:T(8,128)} collective-permute-done((f32[2,1,2,32,896]{4,3,2,1,0:T(8,128)}, f32[2,1,2,32,896]{4,3,2,1,0:T(8,128)}, u32[]{:S(2)}, u32[]{:S(2)}) %collective-permute-start.10) | collective-permute-done | bytes 458784 | tf_op jit(solution)/shard_map/ppermute | solution.py:163
  104.4 3.5 %collective-permute-done.9 = f32[160,512]{1,0:T(8,128)} collective-permute-done((f32[160,512]{1,0:T(8,128)}, f32[160,512]{1,0:T(8,128)}, u32[]{:S(2)}, u32[]{:S(2)}) %collective-permute-start.9) | collective-permute-done | bytes 327712 | tf_op jit(solution)/shard_map/ppermute | solution.py:163
  109.8 1.4 collective-permute-start.15
  113.2 1.5 collective-permute-start.14
  116.9 2.7 collective-permute-start.12
  121.8 5.0 %collective-permute-done.13 = f32[80,512]{1,0:T(8,128)S(1)} collective-permute-done((f32[80,512]{1,0:T(8,128)}, f32[80,512]{1,0:T(8,128)S(1)}, u32[]{:S(2)}, u32[]{:S(2)}) %collective-permute-start.13) | collective-permute-done | bytes 163872 | tf_op jit(solution)/shard_map/ppermute | solution.py:163
  126.9 3.5 %collective-permute-done.12 = f32[1,1,176,512]{3,2,1,0:T(8,128)} collective-permute-done((f32[1,1,176,512]{3,2,1,0:T(8,128)S(1)}, f32[1,1,176,512]{3,2,1,0:T(8,128)}, u32[]{:S(2)}, u32[]{:S(2)}) %collective-permute-start.12) | collective-permute-done | bytes 360480 | tf_op jit(solution)/shard_map/ppermute | solution.py:163
  130.4 1.6 collective-permute-start.17
  136.7 1.8 collective-permute-start.21
  139.7 2.5 collective-permute-start.20
  142.3 6.8 %collective-permute-done.22 = f32[176,512]{1,0:T(8,128)S(1)} collective-permute-done((f32[176,512]{1,0:T(8,128)S(1)}, f32[176,512]{1,0:T(8,128)S(1)}, u32[]{:S(2)}, u32[]{:S(2)}) %collective-permute-start.22) | collective-permute-done | bytes 360480 | tf_op jit(solution)/shard_map/ppermute | solution.py:163
  150.1 2.3 collective-permute-done.20
  152.5 3.2 collective-permute-start.23
  155.6 2.4 collective-permute-start.25
  159.6 8.3 %collective-permute-done.24 = f32[64,512]{1,0:T(8,128)S(1)} collective-permute-done((f32[64,512]{1,0:T(8,128)S(1)}, f32[64,512]{1,0:T(8,128)S(1)}, u32[]{:S(2)}, u32[]{:S(2)}) %collective-permute-start.24) | collective-permute-done | bytes 131104 | tf_op jit(solution)/shard_map/ppermute | solution.py:163
  171.6 1.4 collective-permute-done.26
  174.2 2.0 collective-permute-done.28
  176.4 3.8 %collective-permute-done.30 = f32[352,512]{1,0:T(8,128)S(1)} collective-permute-done((f32[352,512]{1,0:T(8,128)S(1)}, f32[352,512]{1,0:T(8,128)S(1)}, u32[]{:S(2)}, u32[]{:S(2)}) %collective-permute-start.30) | collective-permute-done | bytes 720928 | tf_op jit(solution)/shard_map/ppermute | solution.py:163
  182.5 1.4 collective-permute-start.33
  185.5 5.3 %shard_map.76 = (f32[512,512]{1,0:T(8,128)S(1)}, f32[512,512]{1,0:T(8,128)S(1)}, f32[512,512]{1,0:T(8,128)S(1)}) custom-call(f32[512,512]{1,0:T(8,128)S(1)} %pad_maximum_fusion.6.work_in, f32[512,512]{1,0:T(8,128)S(1)} %broadcast_in_dim.7.rest_in.inverse_in, f32[512,512]{1,0:T(8,128)S(1)} %broadcast_in_dim.7.rest_in.inverse_in), custom_call_target="tpu_custom_call" | custom-call | flops 1000000 | bytes 100000 | tf_op jit(solution)/shard_map/pallas_call | solution.py:82
  190.8 4.9 %shard_map.77 = (f32[512,512]{1,0:T(8,128)S(1)}, f32[512,512]{1,0:T(8,128)S(1)}, f32[512,512]{1,0:T(8,128)S(1)}) custom-call(f32[512,512]{1,0:T(8,128)S(1)} %get-tuple-element.123.work_in, f32[512,512]{1,0:T(8,128)S(1)} %get-tuple-element.124.rest_in, f32[512,512]{1,0:T(8,128)S(1)} %get-tuple-element.125.inverse_in), custom_call_target="tpu_custom_call" | custom-call | flops 1000000 | bytes 100000 | tf_op jit(solution)/shard_map/pallas_call | solution.py:82
  195.6 4.4 %collective-permute-done.33 = f32[320,512]{1,0:T(8,128)S(1)} collective-permute-done((f32[320,512]{1,0:T(8,128)S(1)}, f32[320,512]{1,0:T(8,128)S(1)}, u32[]{:S(2)}, u32[]{:S(2)}) %collective-permute-start.33) | collective-permute-done | bytes 655392 | tf_op jit(solution)/shard_map/ppermute | solution.py:172
  201.6 1.5 collective-permute-start.35
  203.2 4.5 %shard_map.78 = (f32[512,512]{1,0:T(8,128)S(1)}, f32[512,512]{1,0:T(8,128)S(1)}, f32[512,512]{1,0:T(8,128)S(1)}) custom-call(f32[512,512]{1,0:T(8,128)S(1)} %get-tuple-element.129.work_in, f32[512,512]{1,0:T(8,128)S(1)} %get-tuple-element.130.rest_in, f32[512,512]{1,0:T(8,128)S(1)} %get-tuple-element.131.inverse_in), custom_call_target="tpu_custom_call" | custom-call | flops 1000000 | bytes 100000 | tf_op jit(solution)/shard_map/pallas_call | solution.py:82
  207.7 3.6 %shard_map.79 = (f32[512,512]{1,0:T(8,128)}, f32[512,512]{1,0:T(8,128)}, f32[512,512]{1,0:T(8,128)S(1)}) custom-call(f32[512,512]{1,0:T(8,128)S(1)} %get-tuple-element.132.work_in, f32[512,512]{1,0:T(8,128)S(1)} %get-tuple-element.133.rest_in, f32[512,512]{1,0:T(8,128)S(1)} %get-tuple-element.134.inverse_in), custom_call_target="tpu_custom_call" | custom-call | flops 1000000 | bytes 100000 | tf_op jit(solution)/shard_map/pallas_call | solution.py:82
  211.3 1.5 fusion.6
  212.8 1.5 fusion.15
  214.3 2.5 collective-permute-done.34
  224.1 9.7 %collective-permute-done.37 = f32[320,512]{1,0:T(8,128)S(1)} collective-permute-done((f32[320,512]{1,0:T(8,128)S(1)}, f32[320,512]{1,0:T(8,128)S(1)}, u32[]{:S(2)}, u32[]{:S(2)}) %collective-permute-start.37) | collective-permute-done | bytes 655392 | tf_op jit(solution)/shard_map/ppermute | solution.py:172
  233.8 1.5 fusion.4
  235.3 1.5 fusion.2
  240.2 1.6 fusion.10.basis_ref
  241.8 1.9 multiply_select_fusion
  243.8 1.8 fusion.63
  246.3 2.1 collective-permute-done.39
  250.5 2.2 copy-done.1
  252.7 10.3 %shard_map.80 = f32[512,1536]{1,0:T(8,128)S(1)} custom-call(s32[8]{0:T(128)S(1)} %stack.65.starts_ref, bf16[4096,512]{1,0:T(8,128)(2,1)S(1)} %copy-done.1, bf16[4096,3584]{1,0:T(8,128)(2,1)} %bitcast.109), custom_call_target="tpu_custom_call" | custom-call | flops 1000000 | bytes 100000 | tf_op jit(solution)/shard_map/pallas_call | solution.py:129
  265.8 1.5 collective-permute-start.43
  267.3 12.8 %shard_map.81 = f32[512,2048]{1,0:T(8,128)S(1)} custom-call(s32[8]{0:T(128)S(1)} %stack.65.starts_ref, bf16[4096,512]{1,0:T(8,128)(2,1)S(1)} %copy-done.1, bf16[4096,3584]{1,0:T(8,128)(2,1)} %bitcast.110), custom_call_target="tpu_custom_call" | custom-call | flops 1000000 | bytes 100000 | tf_op jit(solution)/shard_map/pallas_call | solution.py:129
  284.2 8.2 %collective-permute-done.46 = f32[1,2,1,64,768]{4,3,2,1,0:T(8,128)S(1)} collective-permute-done((f32[1,2,1,64,768]{4,3,2,1,0:T(8,128)S(1)}, f32[1,2,1,64,768]{4,3,2,1,0:T(8,128)S(1)}, u32[]{:S(2)}, u32[]{:S(2)}) %collective-permute-start.46) | collective-permute-done | bytes 393248 | tf_op jit(solution)/shard_map/ppermute | solution.py:163
  295.4 1.8 collective-permute-start.48
  298.5 2.2 collective-permute-done.51
  300.7 10.8 %collective-permute-done.50 = f32[1,1,1,64,768]{4,3,2,1,0:T(8,128)S(1)} collective-permute-done((f32[1,1,1,64,768]{4,3,2,1,0:T(8,128)S(1)}, f32[1,1,1,64,768]{4,3,2,1,0:T(8,128)S(1)}, u32[]{:S(2)}, u32[]{:S(2)}) %collective-permute-start.50) | collective-permute-done | bytes 196640 | tf_op jit(solution)/shard_map/ppermute | solution.py:163
  313.1 1.5 collective-permute-start.52
  314.6 3.4 %collective-permute-done.53 = f32[1,1,1,64,1024]{4,3,2,1,0:T(8,128)S(1)} collective-permute-done((f32[1,1,1,64,1024]{4,3,2,1,0:T(8,128)S(1)}, f32[1,1,1,64,1024]{4,3,2,1,0:T(8,128)S(1)}, u32[]{:S(2)}, u32[]{:S(2)}) %collective-permute-start.53) | collective-permute-done | bytes 262176 | tf_op jit(solution)/shard_map/ppermute | solution.py:163
  318.1 1.4 collective-permute-done.52
  (198 shorter events, 66.0 us)
Async XLA Ops:
  2.4 23.9 %collective-permute-start = (f32[2,2,1,64,896]{4,3,2,1,0:T(8,128)S(1)}, f32[2,2,1,64,896]{4,3,2,1,0:T(8,128)}, u32[]{:S(2)}, u32[]{:S(2)}) collective-permute-start(f32[2,2,1,64,896]{4,3,2,1,0:T(8,128)S(1)} %constant_dynamic-slice_fusion.24), channel_id=1, source_target_pairs={{0,4},{4,0},{1,5},{5,1},{2,6},{6,2},{3,7},{7,3},{8,12},{12,8},{9,1... | collective-permute-start | bytes 2752520 | tf_op jit(solution)/shard_map/ppermute | solution.py:163
  30.0 35.0 %collective-permute-start.2 = (f32[704,512]{1,0:T(8,128)}, f32[704,512]{1,0:T(8,128)S(1)}, u32[]{:S(2)}, u32[]{:S(2)}) collective-permute-start(f32[704,512]{1,0:T(8,128)} %get-tuple-element.178), channel_id=1, source_target_pairs={{0,8},{8,0},{16,24},{24,16},{1,9},{9,1},{17,25},{25,17},{2,10},{10... | collective-permute-start | bytes 4325384 | tf_op jit(solution)/shard_map/ppermute | solution.py:163
  32.5 34.0 %collective-permute-start.3 = (f32[704,512]{1,0:T(8,128)}, f32[704,512]{1,0:T(8,128)}, u32[]{:S(2)}, u32[]{:S(2)}) collective-permute-start(f32[704,512]{1,0:T(8,128)} %get-tuple-element.177), channel_id=1, source_target_pairs={{0,16},{8,24},{16,0},{24,8},{1,17},{9,25},{17,1},{25,9},{2,18},{10... | collective-permute-start | bytes 4325384 | tf_op jit(solution)/shard_map/ppermute | solution.py:163
  36.0 18.7 %collective-permute-start.1 = (f32[320,512]{1,0:T(8,128)}, f32[320,512]{1,0:T(8,128)}, u32[]{:S(2)}, u32[]{:S(2)}) collective-permute-start(f32[320,512]{1,0:T(8,128)} %constant_dynamic-slice_fusion.23), channel_id=1, source_target_pairs={{0,1},{1,2},{2,3},{3,0},{4,5},{5,6},{6,7},{7,4},{8,9},{9,10},{10,1... | collective-permute-start | bytes 1966088 | tf_op jit(solution)/shard_map/ppermute | solution.py:172
  56.1 17.6 %collective-permute-start.4 = (f32[320,512]{1,0:T(8,128)S(1)}, f32[320,512]{1,0:T(8,128)S(1)}, u32[]{:S(2)}, u32[]{:S(2)}) collective-permute-start(f32[320,512]{1,0:T(8,128)S(1)} %dynamic-slice_add_fusion.8), channel_id=1, source_target_pairs={{0,1},{1,2},{2,3},{3,0},{4,5},{5,6},{6,7},{7,4},{8,9},{9,10},{10,1... | collective-permute-start | bytes 1966088 | tf_op jit(solution)/shard_map/ppermute | solution.py:172
  69.5 17.5 %collective-permute-start.6 = (f32[352,512]{1,0:T(8,128)S(1)}, f32[352,512]{1,0:T(8,128)S(1)}, u32[]{:S(2)}, u32[]{:S(2)}) collective-permute-start(f32[352,512]{1,0:T(8,128)S(1)} %constant_dynamic-slice_fusion.19), channel_id=1, source_target_pairs={{0,8},{8,0},{16,24},{24,16},{1,9},{9,1},{17,25},{25,17},{2,10},{10... | collective-permute-start | bytes 2162696 | tf_op jit(solution)/shard_map/ppermute | solution.py:163
  69.9 19.1 %collective-permute-start.5 = (f32[352,512]{1,0:T(8,128)S(1)}, f32[352,512]{1,0:T(8,128)S(1)}, u32[]{:S(2)}, u32[]{:S(2)}) collective-permute-start(f32[352,512]{1,0:T(8,128)S(1)} %constant_dynamic-slice_fusion.20), channel_id=1, source_target_pairs={{0,16},{8,24},{16,0},{24,8},{1,17},{9,25},{17,1},{25,9},{2,18},{10... | collective-permute-start | bytes 2162696 | tf_op jit(solution)/shard_map/ppermute | solution.py:163
  72.0 19.3 %copy-start.2 = (f32[8,32,896]{2,1,0:T(8,128)}, f32[8,32,896]{2,1,0:T(8,128)S(1)}, u32[]{:S(2)}) copy-start(f32[8,32,896]{2,1,0:T(8,128)S(1)} %get-tuple-element.190) | copy-start | bytes 2752516
  74.9 18.7 %collective-permute-start.7 = (f32[320,512]{1,0:T(8,128)S(1)}, f32[320,512]{1,0:T(8,128)S(1)}, u32[]{:S(2)}, u32[]{:S(2)}) collective-permute-start(f32[320,512]{1,0:T(8,128)S(1)} %dynamic-slice_add_fusion.7), channel_id=1, source_target_pairs={{0,1},{1,2},{2,3},{3,0},{4,5},{5,6},{6,7},{7,4},{8,9},{9,10},{10,1... | collective-permute-start | bytes 1966088 | tf_op jit(solution)/shard_map/ppermute | solution.py:172
  76.1 21.2 %collective-permute-start.11 = (f32[1,2,2,32,896]{4,3,2,1,0:T(8,128)}, f32[1,2,2,32,896]{4,3,2,1,0:T(8,128)}, u32[]{:S(2)}, u32[]{:S(2)}) collective-permute-start(f32[1,2,2,32,896]{4,3,2,1,0:T(8,128)} %constant_dynamic-slice_fusion.16), channel_id=1, source_target_pairs={{0,16},{8,24},{16,0},{24,8},{1,17},{9,25},{17,1},{25,9},{2,18},{10... | collective-permute-start | bytes 1376264 | tf_op jit(solution)/shard_map/ppermute | solution.py:163
  89.4 18.5 %collective-permute-start.8 = (f32[2,1,176,512]{3,2,1,0:T(8,128)S(1)}, f32[2,1,176,512]{3,2,1,0:T(8,128)}, u32[]{:S(2)}, u32[]{:S(2)}) collective-permute-start(f32[2,1,176,512]{3,2,1,0:T(8,128)S(1)} %fusion.25), channel_id=1, source_target_pairs={{0,1},{1,0},{2,3},{3,2},{4,5},{5,4},{6,7},{7,6},{8,9},{9,8},{10,11... | collective-permute-start | bytes 2162696 | tf_op jit(solution)/shard_map/ppermute | solution.py:163
  92.1 12.3 %collective-permute-start.10 = (f32[2,1,2,32,896]{4,3,2,1,0:T(8,128)}, f32[2,1,2,32,896]{4,3,2,1,0:T(8,128)}, u32[]{:S(2)}, u32[]{:S(2)}) collective-permute-start(f32[2,1,2,32,896]{4,3,2,1,0:T(8,128)} %constant_dynamic-slice_fusion.17), channel_id=1, source_target_pairs={{0,8},{8,0},{16,24},{24,16},{1,9},{9,1},{17,25},{25,17},{2,10},{10... | collective-permute-start | bytes 1376264 | tf_op jit(solution)/shard_map/ppermute | solution.py:163
  94.8 0.8 copy-start.6
  96.4 11.6 %collective-permute-start.9 = (f32[160,512]{1,0:T(8,128)}, f32[160,512]{1,0:T(8,128)}, u32[]{:S(2)}, u32[]{:S(2)}) collective-permute-start(f32[160,512]{1,0:T(8,128)} %constant_dynamic-slice_fusion.18), channel_id=1, source_target_pairs={{0,8},{8,0},{16,24},{24,16},{1,9},{9,1},{17,25},{25,17},{2,10},{10... | collective-permute-start | bytes 983048 | tf_op jit(solution)/shard_map/ppermute | solution.py:163
  109.8 20.6 %collective-permute-start.15 = (f32[2,1,2,32,896]{4,3,2,1,0:T(8,128)}, f32[2,1,2,32,896]{4,3,2,1,0:T(8,128)}, u32[]{:S(2)}, u32[]{:S(2)}) collective-permute-start(f32[2,1,2,32,896]{4,3,2,1,0:T(8,128)} %fusion.46), channel_id=1, source_target_pairs={{0,8},{8,0},{16,24},{24,16},{1,9},{9,1},{17,25},{25,17},{2,10},{10... | collective-permute-start | bytes 1376264 | tf_op jit(solution)/shard_map/ppermute | solution.py:163
  113.2 6.4 %copy-start.7 = (f32[320,512]{1,0:T(8,128)S(1)}, f32[320,512]{1,0:T(8,128)}, u32[]{:S(2)}) copy-start(f32[320,512]{1,0:T(8,128)} %copy-done.6) | copy-start | bytes 1966084
  113.2 17.2 %collective-permute-start.14 = (f32[1,2,2,32,896]{4,3,2,1,0:T(8,128)}, f32[1,2,2,32,896]{4,3,2,1,0:T(8,128)}, u32[]{:S(2)}, u32[]{:S(2)}) collective-permute-start(f32[1,2,2,32,896]{4,3,2,1,0:T(8,128)} %fusion.48), channel_id=1, source_target_pairs={{0,16},{8,24},{16,0},{24,8},{1,17},{9,25},{17,1},{25,9},{2,18},{10... | collective-permute-start | bytes 1376264 | tf_op jit(solution)/shard_map/ppermute | solution.py:163
  116.0 0.9 copy-start.4
  116.9 15.2 %copy-start.5 = (f32[2,1,176,512]{3,2,1,0:T(8,128)S(1)}, f32[2,1,176,512]{3,2,1,0:T(8,128)}, u32[]{:S(2)}) copy-start(f32[2,1,176,512]{3,2,1,0:T(8,128)} %copy-done.4) | copy-start | bytes 2162692
  116.9 13.5 %collective-permute-start.12 = (f32[1,1,176,512]{3,2,1,0:T(8,128)S(1)}, f32[1,1,176,512]{3,2,1,0:T(8,128)}, u32[]{:S(2)}, u32[]{:S(2)}) collective-permute-start(f32[1,1,176,512]{3,2,1,0:T(8,128)S(1)} %constant_dynamic-slice_fusion.15), channel_id=1, source_target_pairs={{0,2},{1,3},{2,0},{3,1},{4,6},{5,7},{6,4},{7,5},{8,10},{9,11},{10,... | collective-permute-start | bytes 1081352 | tf_op jit(solution)/shard_map/ppermute | solution.py:163
  121.3 5.5 %collective-permute-start.13 = (f32[80,512]{1,0:T(8,128)}, f32[80,512]{1,0:T(8,128)S(1)}, u32[]{:S(2)}, u32[]{:S(2)}) collective-permute-start(f32[80,512]{1,0:T(8,128)} %constant_dynamic-slice_fusion.14), channel_id=1, source_target_pairs={{0,16},{8,24},{16,0},{24,8},{1,17},{9,25},{17,1},{25,9},{2,18},{10... | collective-permute-start | bytes 491528 | tf_op jit(solution)/shard_map/ppermute | solution.py:163
  130.4 6.2 %collective-permute-start.17 = (f32[80,512]{1,0:T(8,128)S(1)}, f32[80,512]{1,0:T(8,128)S(1)}, u32[]{:S(2)}, u32[]{:S(2)}) collective-permute-start(f32[80,512]{1,0:T(8,128)S(1)} %dynamic-slice_add_fusion.15), channel_id=1, source_target_pairs={{0,16},{8,24},{16,0},{24,8},{1,17},{9,25},{17,1},{25,9},{2,18},{10... | collective-permute-start | bytes 491528 | tf_op jit(solution)/shard_map/ppermute | solution.py:163
  134.1 14.9 %collective-permute-start.22 = (f32[176,512]{1,0:T(8,128)S(1)}, f32[176,512]{1,0:T(8,128)S(1)}, u32[]{:S(2)}, u32[]{:S(2)}) collective-permute-start(f32[176,512]{1,0:T(8,128)S(1)} %add_bitcast_fusion), channel_id=1, source_target_pairs={{0,2},{1,3},{2,0},{3,1},{4,6},{5,7},{6,4},{7,5},{8,10},{9,11},{10,... | collective-permute-start | bytes 1081352 | tf_op jit(solution)/shard_map/ppermute | solution.py:163
  134.3 2.4 collective-permute-start.16
  136.7 15.7 %collective-permute-start.21 = (f32[160,512]{1,0:T(8,128)S(1)}, f32[160,512]{1,0:T(8,128)S(1)}, u32[]{:S(2)}, u32[]{:S(2)}) collective-permute-start(f32[160,512]{1,0:T(8,128)S(1)} %pad_maximum_fusion.17), channel_id=1, source_target_pairs={{0,8},{8,0},{16,24},{24,16},{1,9},{9,1},{17,25},{25,17},{2,10},{10... | collective-permute-start | bytes 983048 | tf_op jit(solution)/shard_map/ppermute | solution.py:163
  138.6 11.4 %collective-permute-start.18 = (f32[64,512]{1,0:T(8,128)S(1)}, f32[64,512]{1,0:T(8,128)S(1)}, u32[]{:S(2)}, u32[]{:S(2)}) collective-permute-start(f32[64,512]{1,0:T(8,128)S(1)} %get-tuple-element.229), channel_id=1, source_target_pairs={{0,8},{8,0},{16,24},{24,16},{1,9},{9,1},{17,25},{25,17},{2,10},{10... | collective-permute-start | bytes 393224 | tf_op jit(solution)/shard_map/ppermute | solution.py:163
  139.0 11.1 %collective-permute-start.19 = (f32[64,512]{1,0:T(8,128)S(1)}, f32[64,512]{1,0:T(8,128)S(1)}, u32[]{:S(2)}, u32[]{:S(2)}) collective-permute-start(f32[64,512]{1,0:T(8,128)S(1)} %get-tuple-element.228), channel_id=1, source_target_pairs={{0,16},{8,24},{16,0},{24,8},{1,17},{9,25},{17,1},{25,9},{2,18},{10... | collective-permute-start | bytes 393224 | tf_op jit(solution)/shard_map/ppermute | solution.py:163
  139.7 12.7 %collective-permute-start.20 = (f32[64,512]{1,0:T(8,128)S(1)}, f32[64,512]{1,0:T(8,128)S(1)}, u32[]{:S(2)}, u32[]{:S(2)}) collective-permute-start(f32[64,512]{1,0:T(8,128)S(1)} %get-tuple-element.227), channel_id=1, source_target_pairs={{0,24},{8,16},{16,8},{24,0},{1,25},{9,17},{17,9},{25,1},{2,26},{10... | collective-permute-start | bytes 393224 | tf_op jit(solution)/shard_map/ppermute | solution.py:163
  152.5 7.1 %collective-permute-start.23 = (f32[64,512]{1,0:T(8,128)S(1)}, f32[64,512]{1,0:T(8,128)S(1)}, u32[]{:S(2)}, u32[]{:S(2)}) collective-permute-start(f32[64,512]{1,0:T(8,128)S(1)} %bitcast_add_fusion), channel_id=1, source_target_pairs={{0,1},{1,0},{2,3},{3,2},{4,5},{5,4},{6,7},{7,6},{8,9},{9,8},{10,11... | collective-permute-start | bytes 393224 | tf_op jit(solution)/shard_map/ppermute | solution.py:163
  155.6 12.3 %collective-permute-start.24 = (f32[64,512]{1,0:T(8,128)S(1)}, f32[64,512]{1,0:T(8,128)S(1)}, u32[]{:S(2)}, u32[]{:S(2)}) collective-permute-start(f32[64,512]{1,0:T(8,128)S(1)} %bitcast_add_fusion), channel_id=1, source_target_pairs={{0,2},{1,3},{2,0},{3,1},{4,6},{5,7},{6,4},{7,5},{8,10},{9,11},{10,... | collective-permute-start | bytes 393224 | tf_op jit(solution)/shard_map/ppermute | solution.py:163
  155.6 12.2 %collective-permute-start.25 = (f32[64,512]{1,0:T(8,128)S(1)}, f32[64,512]{1,0:T(8,128)S(1)}, u32[]{:S(2)}, u32[]{:S(2)}) collective-permute-start(f32[64,512]{1,0:T(8,128)S(1)} %bitcast_add_fusion), channel_id=1, source_target_pairs={{0,3},{1,2},{2,1},{3,0},{4,7},{5,6},{6,5},{7,4},{8,11},{9,10},{10,... | collective-permute-start | bytes 393224 | tf_op jit(solution)/shard_map/ppermute | solution.py:163
  158.1 26.0 %slice-start = ((s8[8388608]{0:T(1024)(128)(4,1)}), s8[4194304]{0:T(1024)(128)(4,1)S(1)}, s32[]{:S(2)}) async-start(s8[8388608]{0:T(1024)(128)(4,1)} %bitcast.111), calls=%async_computation | async-start | bytes 8388608
  158.2 22.1 %collective-permute-start.30 = (f32[352,512]{1,0:T(8,128)S(1)}, f32[352,512]{1,0:T(8,128)S(1)}, u32[]{:S(2)}, u32[]{:S(2)}) collective-permute-start(f32[352,512]{1,0:T(8,128)S(1)} %pad_maximum_fusion.12), channel_id=1, source_target_pairs={{0,1},{1,0},{2,3},{3,2},{4,5},{5,4},{6,7},{7,6},{8,9},{9,8},{10,11... | collective-permute-start | bytes 2162696 | tf_op jit(solution)/shard_map/ppermute | solution.py:163
  167.9 5.0 %collective-permute-start.26 = (f32[64,512]{1,0:T(8,128)S(1)}, f32[64,512]{1,0:T(8,128)S(1)}, u32[]{:S(2)}, u32[]{:S(2)}) collective-permute-start(f32[64,512]{1,0:T(8,128)S(1)} %select_add_fusion), channel_id=1, source_target_pairs={{0,8},{8,0},{16,24},{24,16},{1,9},{9,1},{17,25},{25,17},{2,10},{10... | collective-permute-start | bytes 393224 | tf_op jit(solution)/shard_map/ppermute | solution.py:163
  169.2 5.0 %collective-permute-start.27 = (f32[64,512]{1,0:T(8,128)S(1)}, f32[64,512]{1,0:T(8,128)S(1)}, u32[]{:S(2)}, u32[]{:S(2)}) collective-permute-start(f32[64,512]{1,0:T(8,128)S(1)} %select_add_fusion), channel_id=1, source_target_pairs={{0,16},{8,24},{16,0},{24,8},{1,17},{9,25},{17,1},{25,9},{2,18},{10... | collective-permute-start | bytes 393224 | tf_op jit(solution)/shard_map/ppermute | solution.py:163
  170.3 5.9 %collective-permute-start.28 = (f32[64,512]{1,0:T(8,128)S(1)}, f32[64,512]{1,0:T(8,128)S(1)}, u32[]{:S(2)}, u32[]{:S(2)}) collective-permute-start(f32[64,512]{1,0:T(8,128)S(1)} %select_add_fusion), channel_id=1, source_target_pairs={{0,24},{8,16},{16,8},{24,0},{1,25},{9,17},{17,9},{25,1},{2,26},{10... | collective-permute-start | bytes 393224 | tf_op jit(solution)/shard_map/ppermute | solution.py:163
  176.3 8.8 %collective-permute-start.29 = (f32[256,512]{1,0:T(8,128)S(1)}, f32[256,512]{1,0:T(8,128)S(1)}, u32[]{:S(2)}, u32[]{:S(2)}) collective-permute-start(f32[256,512]{1,0:T(8,128)S(1)} %bitcast.143), channel_id=1, source_target_pairs={{0,4},{4,0},{1,5},{5,1},{2,6},{6,2},{3,7},{7,3},{8,12},{12,8},{9,1... | collective-permute-start | bytes 1572872 | tf_op jit(solution)/shard_map/ppermute | solution.py:163
  180.3 3.8 %slice-start.1 = ((s8[8388608]{0:T(1024)(128)(4,1)}), s8[4194304]{0:T(1024)(128)(4,1)S(1)}, s32[]{:S(2)}) async-start(s8[8388608]{0:T(1024)(128)(4,1)} %bitcast.111), calls=%async_computation.1 | async-start | bytes 8388608
  180.5 19.5 %collective-permute-start.32 = (f32[352,512]{1,0:T(8,128)S(1)}, f32[352,512]{1,0:T(8,128)S(1)}, u32[]{:S(2)}, u32[]{:S(2)}) collective-permute-start(f32[352,512]{1,0:T(8,128)S(1)} %bitcast.141), channel_id=1, source_target_pairs={{0,8},{8,0},{16,24},{24,16},{1,9},{9,1},{17,25},{25,17},{2,10},{10... | collective-permute-start | bytes 2162696 | tf_op jit(solution)/shard_map/ppermute | solution.py:163
  181.2 18.8 %collective-permute-start.31 = (f32[352,512]{1,0:T(8,128)S(1)}, f32[352,512]{1,0:T(8,128)S(1)}, u32[]{:S(2)}, u32[]{:S(2)}) collective-permute-start(f32[352,512]{1,0:T(8,128)S(1)} %bitcast.142), channel_id=1, source_target_pairs={{0,16},{8,24},{16,0},{24,8},{1,17},{9,25},{17,1},{25,9},{2,18},{10... | collective-permute-start | bytes 2162696 | tf_op jit(solution)/shard_map/ppermute | solution.py:163
  182.5 17.6 %collective-permute-start.33 = (f32[320,512]{1,0:T(8,128)S(1)}, f32[320,512]{1,0:T(8,128)S(1)}, u32[]{:S(2)}, u32[]{:S(2)}) collective-permute-start(f32[320,512]{1,0:T(8,128)S(1)} %pad_maximum_fusion.15), channel_id=1, source_target_pairs={{0,1},{1,2},{2,3},{3,0},{4,5},{5,6},{6,7},{7,4},{8,9},{9,10},{10,1... | collective-permute-start | bytes 1966088 | tf_op jit(solution)/shard_map/ppermute | solution.py:172
  200.0 16.8 %collective-permute-start.34 = (f32[320,512]{1,0:T(8,128)S(1)}, f32[320,512]{1,0:T(8,128)S(1)}, u32[]{:S(2)}, u32[]{:S(2)}) collective-permute-start(f32[320,512]{1,0:T(8,128)S(1)} %collective-permute-done.33), channel_id=1, source_target_pairs={{0,1},{1,2},{2,3},{3,0},{4,5},{5,6},{6,7},{7,4},{8,9},{9,10},{10,1... | collective-permute-start | bytes 1966088 | tf_op jit(solution)/shard_map/ppermute | solution.py:172
  201.0 32.8 %collective-permute-start.36 = (f32[704,512]{1,0:T(8,128)S(1)}, f32[704,512]{1,0:T(8,128)S(1)}, u32[]{:S(2)}, u32[]{:S(2)}) collective-permute-start(f32[704,512]{1,0:T(8,128)S(1)} %pad_maximum_fusion.5), channel_id=1, source_target_pairs={{0,16},{8,24},{16,0},{24,8},{1,17},{9,25},{17,1},{25,9},{2,18},{10... | collective-permute-start | bytes 4325384 | tf_op jit(solution)/shard_map/ppermute | solution.py:163
  201.6 32.2 %collective-permute-start.35 = (f32[704,512]{1,0:T(8,128)S(1)}, f32[704,512]{1,0:T(8,128)S(1)}, u32[]{:S(2)}, u32[]{:S(2)}) collective-permute-start(f32[704,512]{1,0:T(8,128)S(1)} %pad_maximum_fusion.4), channel_id=1, source_target_pairs={{0,8},{8,0},{16,24},{24,16},{1,9},{9,1},{17,25},{25,17},{2,10},{10... | collective-permute-start | bytes 4325384 | tf_op jit(solution)/shard_map/ppermute | solution.py:163
  218.1 15.7 %collective-permute-start.37 = (f32[320,512]{1,0:T(8,128)S(1)}, f32[320,512]{1,0:T(8,128)S(1)}, u32[]{:S(2)}, u32[]{:S(2)}) collective-permute-start(f32[320,512]{1,0:T(8,128)S(1)} %collective-permute-done.34), channel_id=1, source_target_pairs={{0,1},{1,2},{2,3},{3,0},{4,5},{5,6},{6,7},{7,4},{8,9},{9,10},{10,1... | collective-permute-start | bytes 1966088 | tf_op jit(solution)/shard_map/ppermute | solution.py:172
  237.9 3.9 %collective-permute-start.38 = (f32[512,512]{1,0:T(8,128)S(1)}, f32[512,512]{1,0:T(8,128)S(1)}, u32[]{:S(2)}, u32[]{:S(2)}) collective-permute-start(f32[512,512]{1,0:T(8,128)S(1)} %add_add_fusion), channel_id=1, source_target_pairs={{0,4},{4,0},{1,5},{5,1},{2,6},{6,2},{3,7},{7,3},{8,12},{12,8},{9,1... | collective-permute-start | bytes 3145736 | tf_op jit(solution)/shard_map/ppermute | solution.py:163
  241.8 2.0 copy-start
  245.8 2.6 collective-permute-start.39
  248.9 14.1 %collective-permute-start.41 = (f32[1,2,2,32,896]{4,3,2,1,0:T(8,128)S(1)}, f32[1,2,2,32,896]{4,3,2,1,0:T(8,128)}, u32[]{:S(2)}, u32[]{:S(2)}) collective-permute-start(f32[1,2,2,32,896]{4,3,2,1,0:T(8,128)S(1)} %constant_dynamic-slice_fusion.10), channel_id=1, source_target_pairs={{0,16},{8,24},{16,0},{24,8},{1,17},{9,25},{17,1},{25,9},{2,18},{10... | collective-permute-start | bytes 1376264 | tf_op jit(solution)/shard_map/ppermute | solution.py:163
  249.6 13.4 %collective-permute-start.40 = (f32[2,1,2,32,896]{4,3,2,1,0:T(8,128)S(1)}, f32[2,1,2,32,896]{4,3,2,1,0:T(8,128)S(1)}, u32[]{:S(2)}, u32[]{:S(2)}) collective-permute-start(f32[2,1,2,32,896]{4,3,2,1,0:T(8,128)S(1)} %constant_dynamic-slice_fusion.11), channel_id=1, source_target_pairs={{0,8},{8,0},{16,24},{24,16},{1,9},{9,1},{17,25},{25,17},{2,10},{10... | collective-permute-start | bytes 1376264 | tf_op jit(solution)/shard_map/ppermute | solution.py:163
  250.5 2.2 copy-start.1
  263.1 17.0 %collective-permute-start.42 = (f32[2,2,1,64,1536]{4,3,2,1,0:T(8,128)S(1)}, f32[2,2,1,64,1536]{4,3,2,1,0:T(8,128)S(1)}, u32[]{:S(2)}, u32[]{:S(2)}) collective-permute-start(f32[2,2,1,64,1536]{4,3,2,1,0:T(8,128)S(1)} %constant_dynamic-slice_fusion.9), channel_id=1, source_target_pairs={{0,4},{4,0},{1,5},{5,1},{2,6},{6,2},{3,7},{7,3},{8,12},{12,8},{9,1... | collective-permute-start | bytes 4718600 | tf_op jit(solution)/shard_map/ppermute | solution.py:163
  264.4 15.8 %collective-permute-start.44 = (f32[2,1,2,32,896]{4,3,2,1,0:T(8,128)S(1)}, f32[2,1,2,32,896]{4,3,2,1,0:T(8,128)S(1)}, u32[]{:S(2)}, u32[]{:S(2)}) collective-permute-start(f32[2,1,2,32,896]{4,3,2,1,0:T(8,128)S(1)} %fusion.42), channel_id=1, source_target_pairs={{0,8},{8,0},{16,24},{24,16},{1,9},{9,1},{17,25},{25,17},{2,10},{10... | collective-permute-start | bytes 1376264 | tf_op jit(solution)/shard_map/ppermute | solution.py:163
  265.8 14.3 %collective-permute-start.43 = (f32[1,2,2,32,896]{4,3,2,1,0:T(8,128)S(1)}, f32[1,2,2,32,896]{4,3,2,1,0:T(8,128)S(1)}, u32[]{:S(2)}, u32[]{:S(2)}) collective-permute-start(f32[1,2,2,32,896]{4,3,2,1,0:T(8,128)S(1)} %fusion.44), channel_id=1, source_target_pairs={{0,16},{8,24},{16,0},{24,8},{1,17},{9,25},{17,1},{25,9},{2,18},{10... | collective-permute-start | bytes 1376264 | tf_op jit(solution)/shard_map/ppermute | solution.py:163
  280.3 12.4 %collective-permute-start.47 = (f32[2,2,1,64,2048]{4,3,2,1,0:T(8,128)S(1)}, f32[2,2,1,64,2048]{4,3,2,1,0:T(8,128)S(1)}, u32[]{:S(2)}, u32[]{:S(2)}) collective-permute-start(f32[2,2,1,64,2048]{4,3,2,1,0:T(8,128)S(1)} %constant_dynamic-slice_fusion.6), channel_id=1, source_target_pairs={{0,4},{4,0},{1,5},{5,1},{2,6},{6,2},{3,7},{7,3},{8,12},{12,8},{9,1... | collective-permute-start | bytes 6291464 | tf_op jit(solution)/shard_map/ppermute | solution.py:163
  280.8 11.6 %collective-permute-start.46 = (f32[1,2,1,64,768]{4,3,2,1,0:T(8,128)S(1)}, f32[1,2,1,64,768]{4,3,2,1,0:T(8,128)S(1)}, u32[]{:S(2)}, u32[]{:S(2)}) collective-permute-start(f32[1,2,1,64,768]{4,3,2,1,0:T(8,128)S(1)} %constant_dynamic-slice_fusion.7), channel_id=1, source_target_pairs={{0,16},{8,24},{16,0},{24,8},{1,17},{9,25},{17,1},{25,9},{2,18},{10... | collective-permute-start | bytes 1179656 | tf_op jit(solution)/shard_map/ppermute | solution.py:163
  281.5 11.3 %collective-permute-start.45 = (f32[2,1,1,64,768]{4,3,2,1,0:T(8,128)S(1)}, f32[2,1,1,64,768]{4,3,2,1,0:T(8,128)S(1)}, u32[]{:S(2)}, u32[]{:S(2)}) collective-permute-start(f32[2,1,1,64,768]{4,3,2,1,0:T(8,128)S(1)} %constant_dynamic-slice_fusion.8), channel_id=1, source_target_pairs={{0,8},{8,0},{16,24},{24,16},{1,9},{9,1},{17,25},{25,17},{2,10},{10... | collective-permute-start | bytes 1179656 | tf_op jit(solution)/shard_map/ppermute | solution.py:163
  292.8 7.9 %collective-permute-start.51 = (f32[1,1,1,64,768]{4,3,2,1,0:T(8,128)S(1)}, f32[1,1,1,64,768]{4,3,2,1,0:T(8,128)S(1)}, u32[]{:S(2)}, u32[]{:S(2)}) collective-permute-start(f32[1,1,1,64,768]{4,3,2,1,0:T(8,128)S(1)} %constant_dynamic-slice_fusion.2), channel_id=1, source_target_pairs={{0,8},{8,0},{16,24},{24,16},{1,9},{9,1},{17,25},{25,17},{2,10},{10... | collective-permute-start | bytes 589832 | tf_op jit(solution)/shard_map/ppermute | solution.py:163
  294.3 17.2 %collective-permute-start.49 = (f32[1,2,1,64,1024]{4,3,2,1,0:T(8,128)S(1)}, f32[1,2,1,64,1024]{4,3,2,1,0:T(8,128)S(1)}, u32[]{:S(2)}, u32[]{:S(2)}) collective-permute-start(f32[1,2,1,64,1024]{4,3,2,1,0:T(8,128)S(1)} %constant_dynamic-slice_fusion.4), channel_id=1, source_target_pairs={{0,16},{8,24},{16,0},{24,8},{1,17},{9,25},{17,1},{25,9},{2,18},{10... | collective-permute-start | bytes 1572872 | tf_op jit(solution)/shard_map/ppermute | solution.py:163
  295.4 16.1 %collective-permute-start.48 = (f32[2,1,1,64,1024]{4,3,2,1,0:T(8,128)S(1)}, f32[2,1,1,64,1024]{4,3,2,1,0:T(8,128)S(1)}, u32[]{:S(2)}, u32[]{:S(2)}) collective-permute-start(f32[2,1,1,64,1024]{4,3,2,1,0:T(8,128)S(1)} %constant_dynamic-slice_fusion.5), channel_id=1, source_target_pairs={{0,8},{8,0},{16,24},{24,16},{1,9},{9,1},{17,25},{25,17},{2,10},{10... | collective-permute-start | bytes 1572872 | tf_op jit(solution)/shard_map/ppermute | solution.py:163
  297.3 14.2 %collective-permute-start.50 = (f32[1,1,1,64,768]{4,3,2,1,0:T(8,128)S(1)}, f32[1,1,1,64,768]{4,3,2,1,0:T(8,128)S(1)}, u32[]{:S(2)}, u32[]{:S(2)}) collective-permute-start(f32[1,1,1,64,768]{4,3,2,1,0:T(8,128)S(1)} %constant_dynamic-slice_fusion.3), channel_id=1, source_target_pairs={{0,16},{8,24},{16,0},{24,8},{1,17},{9,25},{17,1},{25,9},{2,18},{10... | collective-permute-start | bytes 589832 | tf_op jit(solution)/shard_map/ppermute | solution.py:163
  311.6 6.5 %collective-permute-start.53 = (f32[1,1,1,64,1024]{4,3,2,1,0:T(8,128)S(1)}, f32[1,1,1,64,1024]{4,3,2,1,0:T(8,128)S(1)}, u32[]{:S(2)}, u32[]{:S(2)}) collective-permute-start(f32[1,1,1,64,1024]{4,3,2,1,0:T(8,128)S(1)} %constant_dynamic-slice_fusion), channel_id=1, source_target_pairs={{0,8},{8,0},{16,24},{24,16},{1,9},{9,1},{17,25},{25,17},{2,10},{10... | collective-permute-start | bytes 786440 | tf_op jit(solution)/shard_map/ppermute | solution.py:163
  313.1 6.4 %collective-permute-start.52 = (f32[1,1,1,64,1024]{4,3,2,1,0:T(8,128)S(1)}, f32[1,1,1,64,1024]{4,3,2,1,0:T(8,128)S(1)}, u32[]{:S(2)}, u32[]{:S(2)}) collective-permute-start(f32[1,1,1,64,1024]{4,3,2,1,0:T(8,128)S(1)} %constant_dynamic-slice_fusion.1), channel_id=1, source_target_pairs={{0,16},{8,24},{16,0},{24,8},{1,17},{9,25},{17,1},{25,9},{2,18},{10... | collective-permute-start | bytes 786440 | tf_op jit(solution)/shard_map/ppermute | solution.py:163
  320.6 1.2 copy-start.3

commit v5 on v4

--- a/solution.py
+++ b/solution.py
@@ -293,6 +293,24 @@
         return self.value.reshape((1 << len(self.bits),) + self.tail)
 
 
+def lower_blocks(square):
+    count = square.shape[0] // BLOCK
+    return [
+        square[i * BLOCK : (i + 1) * BLOCK, k * BLOCK : (k + 1) * BLOCK] for i in range(count) for k in range(i + 1)
+    ]
+
+
+def from_lower_blocks(stacked, size):
+    count = size // BLOCK
+    rows = []
+    at = 0
+    for i in range(count):
+        blocks = [stacked[at + k * BLOCK : at + (k + 1) * BLOCK] for k in range(i + 1)]
+        at += (i + 1) * BLOCK
+        rows.append(jnp.concatenate(blocks + [jnp.zeros_like(blocks[0])] * (count - 1 - i), 1))
+    return jnp.concatenate(rows, 0)
+
+
 class Part:
     def __init__(self, value, dp_bits, row_bits):
         self.value = value
@@ -377,6 +395,7 @@
     got_c = swap(sent_c, "dp", low)
     got_ab, got_c, turns[0].got, turns[1].got = join(got_ab, got_c, turns[0].got, turns[1].got)
     sent_ab, kept_ab = split_half(kept_ab + got_ab, "col", 1, 0)
+    sent_ab, turns[0].got, turns[1].got, got_c = join(sent_ab, turns[0].got, turns[1].got, got_c)
     got_ab = swap(sent_ab, "col", 1)
     sent_c, kept_c = split_half(kept_c + got_c, "dp", high)
     got_c = swap(sent_c, "dp", high)
@@ -390,7 +409,7 @@
     got_ab = swap(own_ab, "col", 1)
     got_c = swap(own_c, "dp", high)
     own = jnp.concatenate([own_ab, own_c], 0)
-    gram = Sum(contract(own, own, 0, 0))
+    gram = Sum(jnp.concatenate(lower_blocks(contract(own, own, 0, 0)), 0))
     for _ in range(row_bits - 1):
         gram.start()
         (gram.got,) = join(gram.got)
@@ -430,7 +449,7 @@
     got_b = swap(part_b, "dp", low)
     for turn in turns:
         turn.finish()
-    work = gram.value
+    work = from_lower_blocks(gram.value, rank)
     rest = jnp.zeros_like(work)
     inverse = rest
     work, rest, inverse = cholesky_step(0, work, rest, inverse)
@@ -478,7 +497,7 @@
     inner = inner + inner_got
     for bit in range(1, row_bits):
         inner = inner + swap(inner, "row", bit)
-    correlation = contract(inverse, inner, 1, 0)
+    correlation = contract(inverse, inner, 1, 0, near)
     place = me_dp * row_size + lax.axis_index("row")
     turner = jnp.where(place < group // 2, correlation, correlation * correlation)
     turned = jnp.concatenate([turn.result() for turn in turns], 1).reshape(rank, wide)

time: 328 us -> 325 us (level)
  waiting for transfers between devices: 132 us -> 126 us
  starting transfers between devices: 56.5 us -> 61.2 us
    ppermute x6, waiting for transfers between devices: 34.2 us -> 22 us  [shifted(): return lax.ppermute(value, axis, [(i, (i + 1) % size) for i in range(size)])]
    ppermute x48, waiting for transfers between devices: 98.1 us -> 104 us  [flipped(): lax.ppermute(value, axis, [(i, i ^ mask) for i in range(lax.axis_size(axi...]
    ppermute x6, starting transfers between devices: 4.09 us -> 10.3 us  [shifted(): return lax.ppermute(value, axis, [(i, (i + 1) % size) for i in range(size)])]
  transfers between devices with their start and end apart: 54 -> 54, of which waited for: 30 -> 33; matrix products, arithmetic and copies ran while one was open for 21% -> 20% of each run, Pallas kernels for 13% -> 13%
where the time goes in v5:
time: 325 us; the launch traced here: 319 us
  waiting for transfers between devices  126 us (39%)
  starting transfers between devices  61.2 us (19%)
  matrix products  45.9 us (14%)
  Pallas kernels  41.3 us (13%)
  other arithmetic  26.2 us (8%)
  local copies, waits for them, and re-layouts  16.2 us (5%)
    ppermute x48, waiting for transfers between devices, flipped(): lax.ppermute(value, axis, [(i, i ^ mask) for i in range(lax.axis_size(axi...  104 us
    ppermute x48, starting transfers between devices, flipped(): lax.ppermute(value, axis, [(i, i ^ mask) for i in range(lax.axis_size(axi...  50.9 us
    dot_general x1, matrix products, local(): whole = jnp.dot(grad, test_values, preferred_element_type=jnp.float32)  23.4 us
    pallas_call x2, Pallas kernels, projection(): pl.pallas_call(functools.partial(projection_kernel, sizes, first, tile),...  23.1 us
    dot_general x19, matrix products, contract(): lax.dot_general(a, b, (((a_dim,), (b_dim,)), ((), ())), precision=precisi...  22.5 us
    ppermute x6, waiting for transfers between devices, shifted(): return lax.ppermute(value, axis, [(i, (i + 1) % size) for i in range(size)])  22 us
    pallas_call x4, Pallas kernels, cholesky_step(): pl.pallas_call(functools.partial(cholesky_kernel, index), out_shape=[whol...  18.2 us
    ppermute x6, starting transfers between devices, shifted(): return lax.ppermute(value, axis, [(i, (i + 1) % size) for i in range(size)])  10.3 us
  transfers between devices with their start and end apart: 54, of which 33 were waited for; matrix products, arithmetic and copies ran while one was open for 20% of the time, Pallas kernels for 13%

profile of v5, /device:TPU:0, one launch (start us, length us, event | category | flops | bytes accessed | tf_op | source)
XLA Modules:
  0.0 319.0 jit_solution(15679961645748907643)
XLA Ops:
  0.6 1.6 pad_maximum_fusion
  3.0 23.4 %fusion = f32[4096,512]{1,0:T(8,128)} fusion(s32[3584,512]{1,0:T(8,128)} %param.6, bf16[1,4096,3584]{2,1,0:T(8,128)(2,1)} %param.5), kind=kOutput, calls=%fused_computation | convolution fusion | flops 15034220544 | bytes 45088768 | tf_op jit(solution)/shard_map/dot_general | solution.py:363
  26.3 3.6 %constant_dynamic-slice_fusion.21 = (f32[704,512]{1,0:T(8,128)}, f32[704,512]{1,0:T(8,128)}) fusion(f32[4096,512]{1,0:T(8,128)} %fusion, s32[]{:T(128)S(6)} %select_n.546, s32[]{:T(128)S(6)} %select_n.545), kind=kLoop, calls=%fused_computation.208 | loop fusion | bytes 5767176 | tf_op jit(solution)/shard_map/dynamic_slice | solution.py:370
  30.0 2.5 collective-permute-start.2
  32.5 1.5 collective-permute-start.3
  34.0 2.0 constant_dynamic-slice_fusion.23
  36.0 1.6 collective-permute-start.1
  38.9 15.8 %collective-permute-done.1 = f32[320,512]{1,0:T(8,128)} collective-permute-done((f32[320,512]{1,0:T(8,128)}, f32[320,512]{1,0:T(8,128)}, u32[]{:S(2)}, u32[]{:S(2)}) %collective-permute-start.1) | collective-permute-done | bytes 655392 | tf_op jit(solution)/shard_map/ppermute | solution.py:172
  54.7 1.4 dynamic-slice_add_fusion.8
  56.2 8.8 %collective-permute-done.2 = f32[704,512]{1,0:T(8,128)S(1)} collective-permute-done((f32[704,512]{1,0:T(8,128)}, f32[704,512]{1,0:T(8,128)S(1)}, u32[]{:S(2)}, u32[]{:S(2)}) %collective-permute-start.2) | collective-permute-done | bytes 1441824 | tf_op jit(solution)/shard_map/ppermute | solution.py:163
  64.9 1.6 collective-permute-done.3
  66.5 2.9 dynamic-slice_add_fusion.2
  69.9 1.8 collective-permute-start.5
  72.0 1.7 collective-permute-done.4
  76.6 10.3 %collective-permute-done.6 = f32[352,512]{1,0:T(8,128)S(1)} collective-permute-done((f32[352,512]{1,0:T(8,128)S(1)}, f32[352,512]{1,0:T(8,128)S(1)}, u32[]{:S(2)}, u32[]{:S(2)}) %collective-permute-start.6) | collective-permute-done | bytes 720928 | tf_op jit(solution)/shard_map/ppermute | solution.py:163
  87.0 2.1 collective-permute-done.5
  89.4 1.9 collective-permute-start.8
  92.1 1.5 collective-permute-start.10
  97.4 7.1 %collective-permute-done.10 = f32[2,1,2,32,896]{4,3,2,1,0:T(8,128)} collective-permute-done((f32[2,1,2,32,896]{4,3,2,1,0:T(8,128)}, f32[2,1,2,32,896]{4,3,2,1,0:T(8,128)}, u32[]{:S(2)}, u32[]{:S(2)}) %collective-permute-start.10) | collective-permute-done | bytes 458784 | tf_op jit(solution)/shard_map/ppermute | solution.py:163
  104.4 3.4 %collective-permute-done.9 = f32[160,512]{1,0:T(8,128)S(1)} collective-permute-done((f32[160,512]{1,0:T(8,128)}, f32[160,512]{1,0:T(8,128)S(1)}, u32[]{:S(2)}, u32[]{:S(2)}) %collective-permute-start.9) | collective-permute-done | bytes 327712 | tf_op jit(solution)/shard_map/ppermute | solution.py:163
  107.9 1.4 fusion.29
  112.0 1.4 collective-permute-start.15
  115.3 1.5 collective-permute-start.14
  116.8 2.6 collective-permute-start.12
  120.1 8.4 %collective-permute-done.13 = f32[80,512]{1,0:T(8,128)} collective-permute-done((f32[80,512]{1,0:T(8,128)S(1)}, f32[80,512]{1,0:T(8,128)}, u32[]{:S(2)}, u32[]{:S(2)}) %collective-permute-start.13) | collective-permute-done | bytes 163872 | tf_op jit(solution)/shard_map/ppermute | solution.py:163
  128.4 2.0 collective-permute-done.12
  131.4 1.6 collective-permute-start.17
  137.2 1.7 collective-permute-start.21
  140.6 2.0 collective-permute-start.20
  142.7 6.5 %collective-permute-done.22 = f32[176,512]{1,0:T(8,128)S(1)} collective-permute-done((f32[176,512]{1,0:T(8,128)S(1)}, f32[176,512]{1,0:T(8,128)S(1)}, u32[]{:S(2)}, u32[]{:S(2)}) %collective-permute-start.22) | collective-permute-done | bytes 360480 | tf_op jit(solution)/shard_map/ppermute | solution.py:163
  150.6 3.2 %collective-permute-start.23 = (f32[160,128]{1,0:T(8,128)S(1)}, f32[160,128]{1,0:T(8,128)S(1)}, u32[]{:S(2)}, u32[]{:S(2)}) collective-permute-start(f32[160,128]{1,0:T(8,128)S(1)} %bitcast_add_fusion), channel_id=1, source_target_pairs={{0,1},{1,0},{2,3},{3,2},{4,5},{5,4},{6,7},{7,6},{8,9},{9,8},{10,11... | collective-permute-start | bytes 245768 | tf_op jit(solution)/shard_map/ppermute | solution.py:163
  153.8 2.4 collective-permute-start.25
  156.4 5.9 %collective-permute-done.24 = f32[160,128]{1,0:T(8,128)S(1)} collective-permute-done((f32[160,128]{1,0:T(8,128)S(1)}, f32[160,128]{1,0:T(8,128)S(1)}, u32[]{:S(2)}, u32[]{:S(2)}) %collective-permute-start.24) | collective-permute-done | bytes 81952 | tf_op jit(solution)/shard_map/ppermute | solution.py:163
  164.3 1.6 collective-permute-start.28
  165.9 1.5 collective-permute-start.30
  167.7 1.9 collective-permute-done.28
  169.9 1.7 collective-permute-start.33
  172.7 11.3 %collective-permute-done.30 = f32[352,512]{1,0:T(8,128)S(1)} collective-permute-done((f32[352,512]{1,0:T(8,128)S(1)}, f32[352,512]{1,0:T(8,128)S(1)}, u32[]{:S(2)}, u32[]{:S(2)}) %collective-permute-start.30) | collective-permute-done | bytes 720928 | tf_op jit(solution)/shard_map/ppermute | solution.py:163
  186.8 5.3 %shard_map.76 = (f32[512,512]{1,0:T(8,128)S(1)}, f32[512,512]{1,0:T(8,128)S(1)}, f32[512,512]{1,0:T(8,128)S(1)}) custom-call(f32[512,512]{1,0:T(8,128)S(1)} %fusion.21.work_in, f32[512,512]{1,0:T(8,128)S(1)} %broadcast_in_dim.11.rest_in.inverse_in, f32[512,512]{1,0:T(8,128)S(1)} %broadcast_in_dim.11.rest_in.inverse_in), custom_call_target="tpu_custom_call" | custom-call | flops 1000000 | bytes 100000 | tf_op jit(solution)/shard_map/pallas_call | solution.py:82
  192.1 4.9 %shard_map.77 = (f32[512,512]{1,0:T(8,128)S(1)}, f32[512,512]{1,0:T(8,128)S(1)}, f32[512,512]{1,0:T(8,128)S(1)}) custom-call(f32[512,512]{1,0:T(8,128)S(1)} %get-tuple-element.133.work_in, f32[512,512]{1,0:T(8,128)S(1)} %get-tuple-element.134.rest_in, f32[512,512]{1,0:T(8,128)S(1)} %get-tuple-element.135.inverse_in), custom_call_target="tpu_custom_call" | custom-call | flops 1000000 | bytes 100000 | tf_op jit(solution)/shard_map/pallas_call | solution.py:82
  197.2 2.2 collective-permute-done.31
  199.4 3.8 %collective-permute-start.34 = (f32[320,512]{1,0:T(8,128)S(1)}, f32[320,512]{1,0:T(8,128)S(1)}, u32[]{:S(2)}, u32[]{:S(2)}) collective-permute-start(f32[320,512]{1,0:T(8,128)S(1)} %collective-permute-done.33), channel_id=1, source_target_pairs={{0,1},{1,2},{2,3},{3,0},{4,5},{5,6},{6,7},{7,4},{8,9},{9,10},{10,1... | collective-permute-start | bytes 1966088 | tf_op jit(solution)/shard_map/ppermute | solution.py:172
  204.0 4.5 %shard_map.78 = (f32[512,512]{1,0:T(8,128)S(1)}, f32[512,512]{1,0:T(8,128)S(1)}, f32[512,512]{1,0:T(8,128)S(1)}) custom-call(f32[512,512]{1,0:T(8,128)S(1)} %get-tuple-element.139.work_in, f32[512,512]{1,0:T(8,128)S(1)} %get-tuple-element.140.rest_in, f32[512,512]{1,0:T(8,128)S(1)} %get-tuple-element.141.inverse_in), custom_call_target="tpu_custom_call" | custom-call | flops 1000000 | bytes 100000 | tf_op jit(solution)/shard_map/pallas_call | solution.py:82
  208.5 3.6 %shard_map.79 = (f32[512,512]{1,0:T(8,128)}, f32[512,512]{1,0:T(8,128)}, f32[512,512]{1,0:T(8,128)S(1)}) custom-call(f32[512,512]{1,0:T(8,128)S(1)} %get-tuple-element.142.work_in, f32[512,512]{1,0:T(8,128)S(1)} %get-tuple-element.143.rest_in, f32[512,512]{1,0:T(8,128)S(1)} %get-tuple-element.144.inverse_in), custom_call_target="tpu_custom_call" | custom-call | flops 1000000 | bytes 100000 | tf_op jit(solution)/shard_map/pallas_call | solution.py:82
  212.1 1.5 fusion.6
  213.6 1.5 fusion.15
  216.4 2.7 collective-permute-start.37
  224.8 4.2 %collective-permute-done.37 = f32[320,512]{1,0:T(8,128)S(1)} collective-permute-done((f32[320,512]{1,0:T(8,128)S(1)}, f32[320,512]{1,0:T(8,128)S(1)}, u32[]{:S(2)}, u32[]{:S(2)}) %collective-permute-start.37) | collective-permute-done | bytes 655392 | tf_op jit(solution)/shard_map/ppermute | solution.py:172
  230.6 1.5 fusion.4
  232.1 1.5 fusion.2
  237.0 1.6 fusion.10.basis_ref
  240.6 1.8 fusion.67
  243.1 2.1 collective-permute-done.39
  246.4 1.9 collective-permute-start.40
  248.4 2.2 copy-done.1
  250.6 10.3 %shard_map.80 = f32[512,1536]{1,0:T(8,128)S(1)} custom-call(s32[8]{0:T(128)S(1)} %stack.65.starts_ref, bf16[4096,512]{1,0:T(8,128)(2,1)S(1)} %copy-done.1, bf16[4096,3584]{1,0:T(8,128)(2,1)} %bitcast.109), custom_call_target="tpu_custom_call" | custom-call | flops 1000000 | bytes 100000 | tf_op jit(solution)/shard_map/pallas_call | solution.py:129
  262.7 1.4 collective-permute-start.43
  264.1 12.8 %shard_map.81 = f32[512,2048]{1,0:T(8,128)S(1)} custom-call(s32[8]{0:T(128)S(1)} %stack.65.starts_ref, bf16[4096,512]{1,0:T(8,128)(2,1)S(1)} %copy-done.1, bf16[4096,3584]{1,0:T(8,128)(2,1)} %bitcast.110), custom_call_target="tpu_custom_call" | custom-call | flops 1000000 | bytes 100000 | tf_op jit(solution)/shard_map/pallas_call | solution.py:129
  278.3 1.8 collective-permute-start.45
  282.1 7.0 %collective-permute-done.46 = f32[1,2,1,64,768]{4,3,2,1,0:T(8,128)S(1)} collective-permute-done((f32[1,2,1,64,768]{4,3,2,1,0:T(8,128)S(1)}, f32[1,2,1,64,768]{4,3,2,1,0:T(8,128)S(1)}, u32[]{:S(2)}, u32[]{:S(2)}) %collective-permute-start.46) | collective-permute-done | bytes 393248 | tf_op jit(solution)/shard_map/ppermute | solution.py:163
  289.7 1.8 collective-permute-start.51
  295.3 2.3 collective-permute-done.51
  297.6 11.6 %collective-permute-done.50 = f32[1,1,1,64,768]{4,3,2,1,0:T(8,128)S(1)} collective-permute-done((f32[1,1,1,64,768]{4,3,2,1,0:T(8,128)S(1)}, f32[1,1,1,64,768]{4,3,2,1,0:T(8,128)S(1)}, u32[]{:S(2)}, u32[]{:S(2)}) %collective-permute-start.50) | collective-permute-done | bytes 196640 | tf_op jit(solution)/shard_map/ppermute | solution.py:163
  311.3 4.6 %collective-permute-done.53 = f32[1,1,1,64,1024]{4,3,2,1,0:T(8,128)S(1)} collective-permute-done((f32[1,1,1,64,1024]{4,3,2,1,0:T(8,128)S(1)}, f32[1,1,1,64,1024]{4,3,2,1,0:T(8,128)S(1)}, u32[]{:S(2)}, u32[]{:S(2)}) %collective-permute-start.53) | collective-permute-done | bytes 262176 | tf_op jit(solution)/shard_map/ppermute | solution.py:163
  (211 shorter events, 61.6 us)
Async XLA Ops:
  2.4 23.9 %collective-permute-start = (f32[2,2,1,64,896]{4,3,2,1,0:T(8,128)S(1)}, f32[2,2,1,64,896]{4,3,2,1,0:T(8,128)}, u32[]{:S(2)}, u32[]{:S(2)}) collective-permute-start(f32[2,2,1,64,896]{4,3,2,1,0:T(8,128)S(1)} %constant_dynamic-slice_fusion.24), channel_id=1, source_target_pairs={{0,4},{4,0},{1,5},{5,1},{2,6},{6,2},{3,7},{7,3},{8,12},{12,8},{9,1... | collective-permute-start | bytes 2752520 | tf_op jit(solution)/shard_map/ppermute | solution.py:163
  30.0 35.0 %collective-permute-start.2 = (f32[704,512]{1,0:T(8,128)}, f32[704,512]{1,0:T(8,128)S(1)}, u32[]{:S(2)}, u32[]{:S(2)}) collective-permute-start(f32[704,512]{1,0:T(8,128)} %get-tuple-element.188), channel_id=1, source_target_pairs={{0,8},{8,0},{16,24},{24,16},{1,9},{9,1},{17,25},{25,17},{2,10},{10... | collective-permute-start | bytes 4325384 | tf_op jit(solution)/shard_map/ppermute | solution.py:163
  32.5 34.0 %collective-permute-start.3 = (f32[704,512]{1,0:T(8,128)}, f32[704,512]{1,0:T(8,128)}, u32[]{:S(2)}, u32[]{:S(2)}) collective-permute-start(f32[704,512]{1,0:T(8,128)} %get-tuple-element.187), channel_id=1, source_target_pairs={{0,16},{8,24},{16,0},{24,8},{1,17},{9,25},{17,1},{25,9},{2,18},{10... | collective-permute-start | bytes 4325384 | tf_op jit(solution)/shard_map/ppermute | solution.py:163
  36.0 18.7 %collective-permute-start.1 = (f32[320,512]{1,0:T(8,128)}, f32[320,512]{1,0:T(8,128)}, u32[]{:S(2)}, u32[]{:S(2)}) collective-permute-start(f32[320,512]{1,0:T(8,128)} %constant_dynamic-slice_fusion.23), channel_id=1, source_target_pairs={{0,1},{1,2},{2,3},{3,0},{4,5},{5,6},{6,7},{7,4},{8,9},{9,10},{10,1... | collective-permute-start | bytes 1966088 | tf_op jit(solution)/shard_map/ppermute | solution.py:172
  56.1 17.6 %collective-permute-start.4 = (f32[320,512]{1,0:T(8,128)S(1)}, f32[320,512]{1,0:T(8,128)S(1)}, u32[]{:S(2)}, u32[]{:S(2)}) collective-permute-start(f32[320,512]{1,0:T(8,128)S(1)} %dynamic-slice_add_fusion.8), channel_id=1, source_target_pairs={{0,1},{1,2},{2,3},{3,0},{4,5},{5,6},{6,7},{7,4},{8,9},{9,10},{10,1... | collective-permute-start | bytes 1966088 | tf_op jit(solution)/shard_map/ppermute | solution.py:172
  69.5 17.5 %collective-permute-start.6 = (f32[352,512]{1,0:T(8,128)S(1)}, f32[352,512]{1,0:T(8,128)S(1)}, u32[]{:S(2)}, u32[]{:S(2)}) collective-permute-start(f32[352,512]{1,0:T(8,128)S(1)} %constant_dynamic-slice_fusion.19), channel_id=1, source_target_pairs={{0,8},{8,0},{16,24},{24,16},{1,9},{9,1},{17,25},{25,17},{2,10},{10... | collective-permute-start | bytes 2162696 | tf_op jit(solution)/shard_map/ppermute | solution.py:163
  69.9 19.1 %collective-permute-start.5 = (f32[352,512]{1,0:T(8,128)S(1)}, f32[352,512]{1,0:T(8,128)S(1)}, u32[]{:S(2)}, u32[]{:S(2)}) collective-permute-start(f32[352,512]{1,0:T(8,128)S(1)} %constant_dynamic-slice_fusion.20), channel_id=1, source_target_pairs={{0,16},{8,24},{16,0},{24,8},{1,17},{9,25},{17,1},{25,9},{2,18},{10... | collective-permute-start | bytes 2162696 | tf_op jit(solution)/shard_map/ppermute | solution.py:163
  72.0 17.4 %copy-start.2 = (f32[8,32,896]{2,1,0:T(8,128)}, f32[8,32,896]{2,1,0:T(8,128)S(1)}, u32[]{:S(2)}) copy-start(f32[8,32,896]{2,1,0:T(8,128)S(1)} %get-tuple-element.199) | copy-start | bytes 2752516
  74.9 18.7 %collective-permute-start.7 = (f32[320,512]{1,0:T(8,128)S(1)}, f32[320,512]{1,0:T(8,128)S(1)}, u32[]{:S(2)}, u32[]{:S(2)}) collective-permute-start(f32[320,512]{1,0:T(8,128)S(1)} %dynamic-slice_add_fusion.7), channel_id=1, source_target_pairs={{0,1},{1,2},{2,3},{3,0},{4,5},{5,6},{6,7},{7,4},{8,9},{9,10},{10,1... | collective-permute-start | bytes 1966088 | tf_op jit(solution)/shard_map/ppermute | solution.py:172
  76.1 21.2 %collective-permute-start.11 = (f32[1,2,2,32,896]{4,3,2,1,0:T(8,128)}, f32[1,2,2,32,896]{4,3,2,1,0:T(8,128)}, u32[]{:S(2)}, u32[]{:S(2)}) collective-permute-start(f32[1,2,2,32,896]{4,3,2,1,0:T(8,128)} %constant_dynamic-slice_fusion.16), channel_id=1, source_target_pairs={{0,16},{8,24},{16,0},{24,8},{1,17},{9,25},{17,1},{25,9},{2,18},{10... | collective-permute-start | bytes 1376264 | tf_op jit(solution)/shard_map/ppermute | solution.py:163
  89.4 18.4 %collective-permute-start.8 = (f32[2,1,176,512]{3,2,1,0:T(8,128)S(1)}, f32[2,1,176,512]{3,2,1,0:T(8,128)}, u32[]{:S(2)}, u32[]{:S(2)}) collective-permute-start(f32[2,1,176,512]{3,2,1,0:T(8,128)S(1)} %fusion.27), channel_id=1, source_target_pairs={{0,1},{1,0},{2,3},{3,2},{4,5},{5,4},{6,7},{7,6},{8,9},{9,8},{10,11... | collective-permute-start | bytes 2162696 | tf_op jit(solution)/shard_map/ppermute | solution.py:163
  92.1 12.3 %collective-permute-start.10 = (f32[2,1,2,32,896]{4,3,2,1,0:T(8,128)}, f32[2,1,2,32,896]{4,3,2,1,0:T(8,128)}, u32[]{:S(2)}, u32[]{:S(2)}) collective-permute-start(f32[2,1,2,32,896]{4,3,2,1,0:T(8,128)} %constant_dynamic-slice_fusion.17), channel_id=1, source_target_pairs={{0,8},{8,0},{16,24},{24,16},{1,9},{9,1},{17,25},{25,17},{2,10},{10... | collective-permute-start | bytes 1376264 | tf_op jit(solution)/shard_map/ppermute | solution.py:163
  94.8 0.8 copy-start.4
  96.4 11.5 %collective-permute-start.9 = (f32[160,512]{1,0:T(8,128)}, f32[160,512]{1,0:T(8,128)S(1)}, u32[]{:S(2)}, u32[]{:S(2)}) collective-permute-start(f32[160,512]{1,0:T(8,128)} %constant_dynamic-slice_fusion.18), channel_id=1, source_target_pairs={{0,8},{8,0},{16,24},{24,16},{1,9},{9,1},{17,25},{25,17},{2,10},{10... | collective-permute-start | bytes 983048 | tf_op jit(solution)/shard_map/ppermute | solution.py:163
  107.9 3.4 %copy-start.6 = (f32[160,512]{1,0:T(8,128)}, f32[160,512]{1,0:T(8,128)S(1)}, u32[]{:S(2)}) copy-start(f32[160,512]{1,0:T(8,128)S(1)} %collective-permute-done.9) | copy-start | bytes 983044
  112.0 7.4 %copy-start.5 = (f32[320,512]{1,0:T(8,128)S(1)}, f32[320,512]{1,0:T(8,128)}, u32[]{:S(2)}) copy-start(f32[320,512]{1,0:T(8,128)} %copy-done.4) | copy-start | bytes 1966084
  112.0 7.4 %copy-start.7 = (f32[160,512]{1,0:T(8,128)S(1)}, f32[160,512]{1,0:T(8,128)}, u32[]{:S(2)}) copy-start(f32[160,512]{1,0:T(8,128)} %copy-done.6) | copy-start | bytes 983044
  112.0 18.4 %collective-permute-start.15 = (f32[2,1,2,32,896]{4,3,2,1,0:T(8,128)}, f32[2,1,2,32,896]{4,3,2,1,0:T(8,128)}, u32[]{:S(2)}, u32[]{:S(2)}) collective-permute-start(f32[2,1,2,32,896]{4,3,2,1,0:T(8,128)} %fusion.48), channel_id=1, source_target_pairs={{0,8},{8,0},{16,24},{24,16},{1,9},{9,1},{17,25},{25,17},{2,10},{10... | collective-permute-start | bytes 1376264 | tf_op jit(solution)/shard_map/ppermute | solution.py:163
  115.3 15.1 %collective-permute-start.14 = (f32[1,2,2,32,896]{4,3,2,1,0:T(8,128)}, f32[1,2,2,32,896]{4,3,2,1,0:T(8,128)}, u32[]{:S(2)}, u32[]{:S(2)}) collective-permute-start(f32[1,2,2,32,896]{4,3,2,1,0:T(8,128)} %fusion.50), channel_id=1, source_target_pairs={{0,16},{8,24},{16,0},{24,8},{1,17},{9,25},{17,1},{25,9},{2,18},{10... | collective-permute-start | bytes 1376264 | tf_op jit(solution)/shard_map/ppermute | solution.py:163
  116.8 13.6 %collective-permute-start.12 = (f32[1,1,176,512]{3,2,1,0:T(8,128)}, f32[1,1,176,512]{3,2,1,0:T(8,128)S(1)}, u32[]{:S(2)}, u32[]{:S(2)}) collective-permute-start(f32[1,1,176,512]{3,2,1,0:T(8,128)} %constant_dynamic-slice_fusion.15), channel_id=1, source_target_pairs={{0,2},{1,3},{2,0},{3,1},{4,6},{5,7},{6,4},{7,5},{8,10},{9,11},{10,... | collective-permute-start | bytes 1081352 | tf_op jit(solution)/shard_map/ppermute | solution.py:163
  119.5 8.9 %collective-permute-start.13 = (f32[80,512]{1,0:T(8,128)S(1)}, f32[80,512]{1,0:T(8,128)}, u32[]{:S(2)}, u32[]{:S(2)}) collective-permute-start(f32[80,512]{1,0:T(8,128)S(1)} %constant_dynamic-slice_fusion.14), channel_id=1, source_target_pairs={{0,16},{8,24},{16,0},{24,8},{1,17},{9,25},{17,1},{25,9},{2,18},{10... | collective-permute-start | bytes 491528 | tf_op jit(solution)/shard_map/ppermute | solution.py:163
  131.4 5.4 %collective-permute-start.17 = (f32[80,512]{1,0:T(8,128)S(1)}, f32[80,512]{1,0:T(8,128)S(1)}, u32[]{:S(2)}, u32[]{:S(2)}) collective-permute-start(f32[80,512]{1,0:T(8,128)S(1)} %dynamic-slice_add_fusion.15), channel_id=1, source_target_pairs={{0,16},{8,24},{16,0},{24,8},{1,17},{9,25},{17,1},{25,9},{2,18},{10... | collective-permute-start | bytes 491528 | tf_op jit(solution)/shard_map/ppermute | solution.py:163
  134.1 15.2 %collective-permute-start.22 = (f32[176,512]{1,0:T(8,128)S(1)}, f32[176,512]{1,0:T(8,128)S(1)}, u32[]{:S(2)}, u32[]{:S(2)}) collective-permute-start(f32[176,512]{1,0:T(8,128)S(1)} %add_bitcast_fusion), channel_id=1, source_target_pairs={{0,2},{1,3},{2,0},{3,1},{4,6},{5,7},{6,4},{7,5},{8,10},{9,11},{10,... | collective-permute-start | bytes 1081352 | tf_op jit(solution)/shard_map/ppermute | solution.py:163
  135.5 1.7 collective-permute-start.16
  136.7 34.9 %slice-start = ((s8[8388608]{0:T(1024)(128)(4,1)}), s8[4194304]{0:T(1024)(128)(4,1)S(1)}, s32[]{:S(2)}) async-start(s8[8388608]{0:T(1024)(128)(4,1)} %bitcast.111), calls=%async_computation | async-start | bytes 8388608
  137.2 13.3 %collective-permute-start.21 = (f32[160,512]{1,0:T(8,128)S(1)}, f32[160,512]{1,0:T(8,128)S(1)}, u32[]{:S(2)}, u32[]{:S(2)}) collective-permute-start(f32[160,512]{1,0:T(8,128)S(1)} %pad_maximum_fusion.15), channel_id=1, source_target_pairs={{0,8},{8,0},{16,24},{24,16},{1,9},{9,1},{17,25},{25,17},{2,10},{10... | collective-permute-start | bytes 983048 | tf_op jit(solution)/shard_map/ppermute | solution.py:163
  139.1 10.6 %collective-permute-start.18 = (f32[160,128]{1,0:T(8,128)S(1)}, f32[160,128]{1,0:T(8,128)S(1)}, u32[]{:S(2)}, u32[]{:S(2)}) collective-permute-start(f32[160,128]{1,0:T(8,128)S(1)} %get-tuple-element.251), channel_id=1, source_target_pairs={{0,8},{8,0},{16,24},{24,16},{1,9},{9,1},{17,25},{25,17},{2,10},{10... | collective-permute-start | bytes 245768 | tf_op jit(solution)/shard_map/ppermute | solution.py:163
  139.5 10.1 %collective-permute-start.19 = (f32[160,128]{1,0:T(8,128)S(1)}, f32[160,128]{1,0:T(8,128)S(1)}, u32[]{:S(2)}, u32[]{:S(2)}) collective-permute-start(f32[160,128]{1,0:T(8,128)S(1)} %get-tuple-element.250), channel_id=1, source_target_pairs={{0,16},{8,24},{16,0},{24,8},{1,17},{9,25},{17,1},{25,9},{2,18},{10... | collective-permute-start | bytes 245768 | tf_op jit(solution)/shard_map/ppermute | solution.py:163
  140.6 10.0 %collective-permute-start.20 = (f32[160,128]{1,0:T(8,128)S(1)}, f32[160,128]{1,0:T(8,128)S(1)}, u32[]{:S(2)}, u32[]{:S(2)}) collective-permute-start(f32[160,128]{1,0:T(8,128)S(1)} %get-tuple-element.249), channel_id=1, source_target_pairs={{0,24},{8,16},{16,8},{24,0},{1,25},{9,17},{17,9},{25,1},{2,26},{10... | collective-permute-start | bytes 245768 | tf_op jit(solution)/shard_map/ppermute | solution.py:163
  142.6 29.0 %slice-start.1 = ((s8[8388608]{0:T(1024)(128)(4,1)}), s8[4194304]{0:T(1024)(128)(4,1)S(1)}, s32[]{:S(2)}) async-start(s8[8388608]{0:T(1024)(128)(4,1)} %bitcast.111), calls=%async_computation.1 | async-start | bytes 8388608
  150.6 5.8 %collective-permute-start.23 = (f32[160,128]{1,0:T(8,128)S(1)}, f32[160,128]{1,0:T(8,128)S(1)}, u32[]{:S(2)}, u32[]{:S(2)}) collective-permute-start(f32[160,128]{1,0:T(8,128)S(1)} %bitcast_add_fusion), channel_id=1, source_target_pairs={{0,1},{1,0},{2,3},{3,2},{4,5},{5,4},{6,7},{7,6},{8,9},{9,8},{10,11... | collective-permute-start | bytes 245768 | tf_op jit(solution)/shard_map/ppermute | solution.py:163
  153.8 8.5 %collective-permute-start.24 = (f32[160,128]{1,0:T(8,128)S(1)}, f32[160,128]{1,0:T(8,128)S(1)}, u32[]{:S(2)}, u32[]{:S(2)}) collective-permute-start(f32[160,128]{1,0:T(8,128)S(1)} %bitcast_add_fusion), channel_id=1, source_target_pairs={{0,2},{1,3},{2,0},{3,1},{4,6},{5,7},{6,4},{7,5},{8,10},{9,11},{10,... | collective-permute-start | bytes 245768 | tf_op jit(solution)/shard_map/ppermute | solution.py:163
  153.8 8.5 %collective-permute-start.25 = (f32[160,128]{1,0:T(8,128)S(1)}, f32[160,128]{1,0:T(8,128)S(1)}, u32[]{:S(2)}, u32[]{:S(2)}) collective-permute-start(f32[160,128]{1,0:T(8,128)S(1)} %bitcast_add_fusion), channel_id=1, source_target_pairs={{0,3},{1,2},{2,1},{3,0},{4,7},{5,6},{6,5},{7,4},{8,11},{9,10},{10,... | collective-permute-start | bytes 245768 | tf_op jit(solution)/shard_map/ppermute | solution.py:163
  162.3 5.1 %collective-permute-start.26 = (f32[160,128]{1,0:T(8,128)S(1)}, f32[160,128]{1,0:T(8,128)S(1)}, u32[]{:S(2)}, u32[]{:S(2)}) collective-permute-start(f32[160,128]{1,0:T(8,128)S(1)} %select_add_fusion), channel_id=1, source_target_pairs={{0,8},{8,0},{16,24},{24,16},{1,9},{9,1},{17,25},{25,17},{2,10},{10... | collective-permute-start | bytes 245768 | tf_op jit(solution)/shard_map/ppermute | solution.py:163
  163.3 4.4 %collective-permute-start.27 = (f32[160,128]{1,0:T(8,128)S(1)}, f32[160,128]{1,0:T(8,128)S(1)}, u32[]{:S(2)}, u32[]{:S(2)}) collective-permute-start(f32[160,128]{1,0:T(8,128)S(1)} %select_add_fusion), channel_id=1, source_target_pairs={{0,16},{8,24},{16,0},{24,8},{1,17},{9,25},{17,1},{25,9},{2,18},{10... | collective-permute-start | bytes 245768 | tf_op jit(solution)/shard_map/ppermute | solution.py:163
  164.3 5.3 %collective-permute-start.28 = (f32[160,128]{1,0:T(8,128)S(1)}, f32[160,128]{1,0:T(8,128)S(1)}, u32[]{:S(2)}, u32[]{:S(2)}) collective-permute-start(f32[160,128]{1,0:T(8,128)S(1)} %select_add_fusion), channel_id=1, source_target_pairs={{0,24},{8,16},{16,8},{24,0},{1,25},{9,17},{17,9},{25,1},{2,26},{10... | collective-permute-start | bytes 245768 | tf_op jit(solution)/shard_map/ppermute | solution.py:163
  165.9 18.1 %collective-permute-start.30 = (f32[352,512]{1,0:T(8,128)S(1)}, f32[352,512]{1,0:T(8,128)S(1)}, u32[]{:S(2)}, u32[]{:S(2)}) collective-permute-start(f32[352,512]{1,0:T(8,128)S(1)} %pad_maximum_fusion.11), channel_id=1, source_target_pairs={{0,1},{1,0},{2,3},{3,2},{4,5},{5,4},{6,7},{7,6},{8,9},{9,8},{10,11... | collective-permute-start | bytes 2162696 | tf_op jit(solution)/shard_map/ppermute | solution.py:163
  169.7 3.0 collective-permute-start.29
  169.9 27.2 %collective-permute-start.33 = (f32[320,512]{1,0:T(8,128)S(1)}, f32[320,512]{1,0:T(8,128)S(1)}, u32[]{:S(2)}, u32[]{:S(2)}) collective-permute-start(f32[320,512]{1,0:T(8,128)S(1)} %pad_maximum_fusion.14), channel_id=1, source_target_pairs={{0,1},{1,2},{2,3},{3,0},{4,5},{5,6},{6,7},{7,4},{8,9},{9,10},{10,1... | collective-permute-start | bytes 1966088 | tf_op jit(solution)/shard_map/ppermute | solution.py:172
  184.3 12.9 %collective-permute-start.32 = (f32[352,512]{1,0:T(8,128)S(1)}, f32[352,512]{1,0:T(8,128)S(1)}, u32[]{:S(2)}, u32[]{:S(2)}) collective-permute-start(f32[352,512]{1,0:T(8,128)S(1)} %bitcast.140), channel_id=1, source_target_pairs={{0,8},{8,0},{16,24},{24,16},{1,9},{9,1},{17,25},{25,17},{2,10},{10... | collective-permute-start | bytes 2162696 | tf_op jit(solution)/shard_map/ppermute | solution.py:163
  185.4 14.0 %collective-permute-start.31 = (f32[352,512]{1,0:T(8,128)S(1)}, f32[352,512]{1,0:T(8,128)S(1)}, u32[]{:S(2)}, u32[]{:S(2)}) collective-permute-start(f32[352,512]{1,0:T(8,128)S(1)} %bitcast.141), channel_id=1, source_target_pairs={{0,16},{8,24},{16,0},{24,8},{1,17},{9,25},{17,1},{25,9},{2,18},{10... | collective-permute-start | bytes 2162696 | tf_op jit(solution)/shard_map/ppermute | solution.py:163
  199.4 15.7 %collective-permute-start.34 = (f32[320,512]{1,0:T(8,128)S(1)}, f32[320,512]{1,0:T(8,128)S(1)}, u32[]{:S(2)}, u32[]{:S(2)}) collective-permute-start(f32[320,512]{1,0:T(8,128)S(1)} %collective-permute-done.33), channel_id=1, source_target_pairs={{0,1},{1,2},{2,3},{3,0},{4,5},{5,6},{6,7},{7,4},{8,9},{9,10},{10,1... | collective-permute-start | bytes 1966088 | tf_op jit(solution)/shard_map/ppermute | solution.py:172
  203.7 25.9 %collective-permute-start.36 = (f32[704,512]{1,0:T(8,128)S(1)}, f32[704,512]{1,0:T(8,128)S(1)}, u32[]{:S(2)}, u32[]{:S(2)}) collective-permute-start(f32[704,512]{1,0:T(8,128)S(1)} %pad_maximum_fusion.5), channel_id=1, source_target_pairs={{0,16},{8,24},{16,0},{24,8},{1,17},{9,25},{17,1},{25,9},{2,18},{10... | collective-permute-start | bytes 4325384 | tf_op jit(solution)/shard_map/ppermute | solution.py:163
  203.9 26.7 %collective-permute-start.35 = (f32[704,512]{1,0:T(8,128)S(1)}, f32[704,512]{1,0:T(8,128)S(1)}, u32[]{:S(2)}, u32[]{:S(2)}) collective-permute-start(f32[704,512]{1,0:T(8,128)S(1)} %pad_maximum_fusion.4), channel_id=1, source_target_pairs={{0,8},{8,0},{16,24},{24,16},{1,9},{9,1},{17,25},{25,17},{2,10},{10... | collective-permute-start | bytes 4325384 | tf_op jit(solution)/shard_map/ppermute | solution.py:163
  216.4 12.6 %collective-permute-start.37 = (f32[320,512]{1,0:T(8,128)S(1)}, f32[320,512]{1,0:T(8,128)S(1)}, u32[]{:S(2)}, u32[]{:S(2)}) collective-permute-start(f32[320,512]{1,0:T(8,128)S(1)} %collective-permute-done.34), channel_id=1, source_target_pairs={{0,1},{1,2},{2,3},{3,0},{4,5},{5,6},{6,7},{7,4},{8,9},{9,10},{10,1... | collective-permute-start | bytes 1966088 | tf_op jit(solution)/shard_map/ppermute | solution.py:172
  234.7 3.9 %collective-permute-start.38 = (f32[512,512]{1,0:T(8,128)S(1)}, f32[512,512]{1,0:T(8,128)S(1)}, u32[]{:S(2)}, u32[]{:S(2)}) collective-permute-start(f32[512,512]{1,0:T(8,128)S(1)} %add_add_fusion), channel_id=1, source_target_pairs={{0,4},{4,0},{1,5},{5,1},{2,6},{6,2},{3,7},{7,3},{8,12},{12,8},{9,1... | collective-permute-start | bytes 3145736 | tf_op jit(solution)/shard_map/ppermute | solution.py:163
  238.5 2.0 copy-start
  242.5 2.7 collective-permute-start.39
  245.6 15.3 %collective-permute-start.41 = (f32[1,2,2,32,896]{4,3,2,1,0:T(8,128)S(1)}, f32[1,2,2,32,896]{4,3,2,1,0:T(8,128)}, u32[]{:S(2)}, u32[]{:S(2)}) collective-permute-start(f32[1,2,2,32,896]{4,3,2,1,0:T(8,128)S(1)} %constant_dynamic-slice_fusion.10), channel_id=1, source_target_pairs={{0,16},{8,24},{16,0},{24,8},{1,17},{9,25},{17,1},{25,9},{2,18},{10... | collective-permute-start | bytes 1376264 | tf_op jit(solution)/shard_map/ppermute | solution.py:163
  246.4 14.5 %collective-permute-start.40 = (f32[2,1,2,32,896]{4,3,2,1,0:T(8,128)S(1)}, f32[2,1,2,32,896]{4,3,2,1,0:T(8,128)S(1)}, u32[]{:S(2)}, u32[]{:S(2)}) collective-permute-start(f32[2,1,2,32,896]{4,3,2,1,0:T(8,128)S(1)} %constant_dynamic-slice_fusion.11), channel_id=1, source_target_pairs={{0,8},{8,0},{16,24},{24,16},{1,9},{9,1},{17,25},{25,17},{2,10},{10... | collective-permute-start | bytes 1376264 | tf_op jit(solution)/shard_map/ppermute | solution.py:163
  248.4 2.2 copy-start.1
  261.0 15.8 %collective-permute-start.42 = (f32[2,2,1,64,1536]{4,3,2,1,0:T(8,128)S(1)}, f32[2,2,1,64,1536]{4,3,2,1,0:T(8,128)S(1)}, u32[]{:S(2)}, u32[]{:S(2)}) collective-permute-start(f32[2,2,1,64,1536]{4,3,2,1,0:T(8,128)S(1)} %constant_dynamic-slice_fusion.9), channel_id=1, source_target_pairs={{0,4},{4,0},{1,5},{5,1},{2,6},{6,2},{3,7},{7,3},{8,12},{12,8},{9,1... | collective-permute-start | bytes 4718600 | tf_op jit(solution)/shard_map/ppermute | solution.py:163
  262.3 14.6 %collective-permute-start.44 = (f32[2,1,2,32,896]{4,3,2,1,0:T(8,128)S(1)}, f32[2,1,2,32,896]{4,3,2,1,0:T(8,128)S(1)}, u32[]{:S(2)}, u32[]{:S(2)}) collective-permute-start(f32[2,1,2,32,896]{4,3,2,1,0:T(8,128)S(1)} %fusion.44), channel_id=1, source_target_pairs={{0,8},{8,0},{16,24},{24,16},{1,9},{9,1},{17,25},{25,17},{2,10},{10... | collective-permute-start | bytes 1376264 | tf_op jit(solution)/shard_map/ppermute | solution.py:163
  262.7 14.2 %collective-permute-start.43 = (f32[1,2,2,32,896]{4,3,2,1,0:T(8,128)S(1)}, f32[1,2,2,32,896]{4,3,2,1,0:T(8,128)S(1)}, u32[]{:S(2)}, u32[]{:S(2)}) collective-permute-start(f32[1,2,2,32,896]{4,3,2,1,0:T(8,128)S(1)} %fusion.46), channel_id=1, source_target_pairs={{0,16},{8,24},{16,0},{24,8},{1,17},{9,25},{17,1},{25,9},{2,18},{10... | collective-permute-start | bytes 1376264 | tf_op jit(solution)/shard_map/ppermute | solution.py:163
  277.0 12.6 %collective-permute-start.47 = (f32[2,2,1,64,2048]{4,3,2,1,0:T(8,128)S(1)}, f32[2,2,1,64,2048]{4,3,2,1,0:T(8,128)S(1)}, u32[]{:S(2)}, u32[]{:S(2)}) collective-permute-start(f32[2,2,1,64,2048]{4,3,2,1,0:T(8,128)S(1)} %constant_dynamic-slice_fusion.6), channel_id=1, source_target_pairs={{0,4},{4,0},{1,5},{5,1},{2,6},{6,2},{3,7},{7,3},{8,12},{12,8},{9,1... | collective-permute-start | bytes 6291464 | tf_op jit(solution)/shard_map/ppermute | solution.py:163
  277.5 11.6 %collective-permute-start.46 = (f32[1,2,1,64,768]{4,3,2,1,0:T(8,128)S(1)}, f32[1,2,1,64,768]{4,3,2,1,0:T(8,128)S(1)}, u32[]{:S(2)}, u32[]{:S(2)}) collective-permute-start(f32[1,2,1,64,768]{4,3,2,1,0:T(8,128)S(1)} %constant_dynamic-slice_fusion.7), channel_id=1, source_target_pairs={{0,16},{8,24},{16,0},{24,8},{1,17},{9,25},{17,1},{25,9},{2,18},{10... | collective-permute-start | bytes 1179656 | tf_op jit(solution)/shard_map/ppermute | solution.py:163
  278.3 11.3 %collective-permute-start.45 = (f32[2,1,1,64,768]{4,3,2,1,0:T(8,128)S(1)}, f32[2,1,1,64,768]{4,3,2,1,0:T(8,128)S(1)}, u32[]{:S(2)}, u32[]{:S(2)}) collective-permute-start(f32[2,1,1,64,768]{4,3,2,1,0:T(8,128)S(1)} %constant_dynamic-slice_fusion.8), channel_id=1, source_target_pairs={{0,8},{8,0},{16,24},{24,16},{1,9},{9,1},{17,25},{25,17},{2,10},{10... | collective-permute-start | bytes 1179656 | tf_op jit(solution)/shard_map/ppermute | solution.py:163
  289.7 7.9 %collective-permute-start.51 = (f32[1,1,1,64,768]{4,3,2,1,0:T(8,128)S(1)}, f32[1,1,1,64,768]{4,3,2,1,0:T(8,128)S(1)}, u32[]{:S(2)}, u32[]{:S(2)}) collective-permute-start(f32[1,1,1,64,768]{4,3,2,1,0:T(8,128)S(1)} %constant_dynamic-slice_fusion.2), channel_id=1, source_target_pairs={{0,8},{8,0},{16,24},{24,16},{1,9},{9,1},{17,25},{25,17},{2,10},{10... | collective-permute-start | bytes 589832 | tf_op jit(solution)/shard_map/ppermute | solution.py:163
  292.1 17.2 %collective-permute-start.49 = (f32[1,2,1,64,1024]{4,3,2,1,0:T(8,128)S(1)}, f32[1,2,1,64,1024]{4,3,2,1,0:T(8,128)S(1)}, u32[]{:S(2)}, u32[]{:S(2)}) collective-permute-start(f32[1,2,1,64,1024]{4,3,2,1,0:T(8,128)S(1)} %constant_dynamic-slice_fusion.4), channel_id=1, source_target_pairs={{0,16},{8,24},{16,0},{24,8},{1,17},{9,25},{17,1},{25,9},{2,18},{10... | collective-permute-start | bytes 1572872 | tf_op jit(solution)/shard_map/ppermute | solution.py:163
  292.7 16.6 %collective-permute-start.48 = (f32[2,1,1,64,1024]{4,3,2,1,0:T(8,128)S(1)}, f32[2,1,1,64,1024]{4,3,2,1,0:T(8,128)S(1)}, u32[]{:S(2)}, u32[]{:S(2)}) collective-permute-start(f32[2,1,1,64,1024]{4,3,2,1,0:T(8,128)S(1)} %constant_dynamic-slice_fusion.5), channel_id=1, source_target_pairs={{0,8},{8,0},{16,24},{24,16},{1,9},{9,1},{17,25},{25,17},{2,10},{10... | collective-permute-start | bytes 1572872 | tf_op jit(solution)/shard_map/ppermute | solution.py:163
  293.9 15.4 %collective-permute-start.50 = (f32[1,1,1,64,768]{4,3,2,1,0:T(8,128)S(1)}, f32[1,1,1,64,768]{4,3,2,1,0:T(8,128)S(1)}, u32[]{:S(2)}, u32[]{:S(2)}) collective-permute-start(f32[1,1,1,64,768]{4,3,2,1,0:T(8,128)S(1)} %constant_dynamic-slice_fusion.3), channel_id=1, source_target_pairs={{0,16},{8,24},{16,0},{24,8},{1,17},{9,25},{17,1},{25,9},{2,18},{10... | collective-permute-start | bytes 589832 | tf_op jit(solution)/shard_map/ppermute | solution.py:163
  309.4 6.4 %collective-permute-start.53 = (f32[1,1,1,64,1024]{4,3,2,1,0:T(8,128)S(1)}, f32[1,1,1,64,1024]{4,3,2,1,0:T(8,128)S(1)}, u32[]{:S(2)}, u32[]{:S(2)}) collective-permute-start(f32[1,1,1,64,1024]{4,3,2,1,0:T(8,128)S(1)} %constant_dynamic-slice_fusion), channel_id=1, source_target_pairs={{0,8},{8,0},{16,24},{24,16},{1,9},{9,1},{17,25},{25,17},{2,10},{10... | collective-permute-start | bytes 786440 | tf_op jit(solution)/shard_map/ppermute | solution.py:163
  309.9 6.4 %collective-permute-start.52 = (f32[1,1,1,64,1024]{4,3,2,1,0:T(8,128)S(1)}, f32[1,1,1,64,1024]{4,3,2,1,0:T(8,128)S(1)}, u32[]{:S(2)}, u32[]{:S(2)}) collective-permute-start(f32[1,1,1,64,1024]{4,3,2,1,0:T(8,128)S(1)} %constant_dynamic-slice_fusion.1), channel_id=1, source_target_pairs={{0,16},{8,24},{16,0},{24,8},{1,17},{9,25},{17,1},{25,9},{2,18},{10... | collective-permute-start | bytes 786440 | tf_op jit(solution)/shard_map/ppermute | solution.py:163
  317.5 1.2 copy-start.3

commit v6 on v5

--- a/solution.py
+++ b/solution.py
@@ -532,11 +532,12 @@
     back.start_row()
     for turn in turns:
         turn.finish()
-    front[0].got, front[1].got, back.got = join(front[0].got, front[1].got, back.got)
+    (back.got,) = join(back.got)
     back.finish()
     back = back.halves()
     for part, bit in zip(back, (low, high), strict=True):
         part.start("dp", bit)
+    front[0].got, front[1].got = join(front[0].got, front[1].got)
     for part, bit in zip(front, (high, low), strict=True):
         part.finish()
         part.start("dp", bit)

time: 325 us -> 325 us (level)
  no operation moved by 1% of the time
where the time goes in v6:
time: 325 us; the launch traced here: 319 us
  waiting for transfers between devices  126 us (39%)
  starting transfers between devices  61.2 us (19%)
  matrix products  45.9 us (14%)
  Pallas kernels  41.3 us (13%)
  other arithmetic  26.2 us (8%)
  local copies, waits for them, and re-layouts  16.2 us (5%)
    ppermute x48, waiting for transfers between devices, flipped(): lax.ppermute(value, axis, [(i, i ^ mask) for i in range(lax.axis_size(axi...  104 us
    ppermute x48, starting transfers between devices, flipped(): lax.ppermute(value, axis, [(i, i ^ mask) for i in range(lax.axis_size(axi...  50.9 us
    dot_general x1, matrix products, local(): whole = jnp.dot(grad, test_values, preferred_element_type=jnp.float32)  23.4 us
    pallas_call x2, Pallas kernels, projection(): pl.pallas_call(functools.partial(projection_kernel, sizes, first, tile),...  23.1 us
    dot_general x19, matrix products, contract(): lax.dot_general(a, b, (((a_dim,), (b_dim,)), ((), ())), precision=precisi...  22.5 us
    ppermute x6, waiting for transfers between devices, shifted(): return lax.ppermute(value, axis, [(i, (i + 1) % size) for i in range(size)])  22 us
    pallas_call x4, Pallas kernels, cholesky_step(): pl.pallas_call(functools.partial(cholesky_kernel, index), out_shape=[whol...  18.2 us
    ppermute x6, starting transfers between devices, shifted(): return lax.ppermute(value, axis, [(i, (i + 1) % size) for i in range(size)])  10.3 us
  transfers between devices with their start and end apart: 54, of which 33 were waited for; matrix products, arithmetic and copies ran while one was open for 20% of the time, Pallas kernels for 13%

profile of v6, /device:TPU:0, one launch (start us, length us, event | category | flops | bytes accessed | tf_op | source)
XLA Modules:
  0.0 319.0 jit_solution(14987375847622047089)
XLA Ops:
  0.6 1.6 pad_maximum_fusion
  3.0 23.4 %fusion = f32[4096,512]{1,0:T(8,128)} fusion(s32[3584,512]{1,0:T(8,128)} %param.6, bf16[1,4096,3584]{2,1,0:T(8,128)(2,1)} %param.5), kind=kOutput, calls=%fused_computation | convolution fusion | flops 15034220544 | bytes 45088768 | tf_op jit(solution)/shard_map/dot_general | solution.py:363
  26.3 3.6 %constant_dynamic-slice_fusion.21 = (f32[704,512]{1,0:T(8,128)}, f32[704,512]{1,0:T(8,128)}) fusion(f32[4096,512]{1,0:T(8,128)} %fusion, s32[]{:T(128)S(6)} %select_n.546, s32[]{:T(128)S(6)} %select_n.545), kind=kLoop, calls=%fused_computation.208 | loop fusion | bytes 5767176 | tf_op jit(solution)/shard_map/dynamic_slice | solution.py:370
  30.0 2.5 collective-permute-start.2
  32.5 1.5 collective-permute-start.3
  34.0 2.0 constant_dynamic-slice_fusion.23
  36.0 1.6 collective-permute-start.1
  38.9 15.8 %collective-permute-done.1 = f32[320,512]{1,0:T(8,128)} collective-permute-done((f32[320,512]{1,0:T(8,128)}, f32[320,512]{1,0:T(8,128)}, u32[]{:S(2)}, u32[]{:S(2)}) %collective-permute-start.1) | collective-permute-done | bytes 655392 | tf_op jit(solution)/shard_map/ppermute | solution.py:172
  54.7 1.4 dynamic-slice_add_fusion.8
  56.2 8.8 %collective-permute-done.2 = f32[704,512]{1,0:T(8,128)S(1)} collective-permute-done((f32[704,512]{1,0:T(8,128)}, f32[704,512]{1,0:T(8,128)S(1)}, u32[]{:S(2)}, u32[]{:S(2)}) %collective-permute-start.2) | collective-permute-done | bytes 1441824 | tf_op jit(solution)/shard_map/ppermute | solution.py:163
  64.9 1.6 collective-permute-done.3
  66.5 2.9 dynamic-slice_add_fusion.2
  69.9 1.8 collective-permute-start.5
  72.0 1.7 collective-permute-done.4
  76.6 10.3 %collective-permute-done.6 = f32[352,512]{1,0:T(8,128)S(1)} collective-permute-done((f32[352,512]{1,0:T(8,128)S(1)}, f32[352,512]{1,0:T(8,128)S(1)}, u32[]{:S(2)}, u32[]{:S(2)}) %collective-permute-start.6) | collective-permute-done | bytes 720928 | tf_op jit(solution)/shard_map/ppermute | solution.py:163
  87.0 2.1 collective-permute-done.5
  89.4 1.9 collective-permute-start.8
  92.1 1.5 collective-permute-start.10
  97.4 7.1 %collective-permute-done.10 = f32[2,1,2,32,896]{4,3,2,1,0:T(8,128)} collective-permute-done((f32[2,1,2,32,896]{4,3,2,1,0:T(8,128)}, f32[2,1,2,32,896]{4,3,2,1,0:T(8,128)}, u32[]{:S(2)}, u32[]{:S(2)}) %collective-permute-start.10) | collective-permute-done | bytes 458784 | tf_op jit(solution)/shard_map/ppermute | solution.py:163
  104.4 3.4 %collective-permute-done.9 = f32[160,512]{1,0:T(8,128)S(1)} collective-permute-done((f32[160,512]{1,0:T(8,128)}, f32[160,512]{1,0:T(8,128)S(1)}, u32[]{:S(2)}, u32[]{:S(2)}) %collective-permute-start.9) | collective-permute-done | bytes 327712 | tf_op jit(solution)/shard_map/ppermute | solution.py:163
  107.9 1.4 fusion.29
  112.0 1.4 collective-permute-start.15
  115.3 1.5 collective-permute-start.14
  116.8 2.6 collective-permute-start.12
  120.1 8.4 %collective-permute-done.13 = f32[80,512]{1,0:T(8,128)} collective-permute-done((f32[80,512]{1,0:T(8,128)S(1)}, f32[80,512]{1,0:T(8,128)}, u32[]{:S(2)}, u32[]{:S(2)}) %collective-permute-start.13) | collective-permute-done | bytes 163872 | tf_op jit(solution)/shard_map/ppermute | solution.py:163
  128.4 2.0 collective-permute-done.12
  131.4 1.6 collective-permute-start.17
  137.2 1.7 collective-permute-start.21
  140.6 2.0 collective-permute-start.20
  142.7 6.5 %collective-permute-done.22 = f32[176,512]{1,0:T(8,128)S(1)} collective-permute-done((f32[176,512]{1,0:T(8,128)S(1)}, f32[176,512]{1,0:T(8,128)S(1)}, u32[]{:S(2)}, u32[]{:S(2)}) %collective-permute-start.22) | collective-permute-done | bytes 360480 | tf_op jit(solution)/shard_map/ppermute | solution.py:163
  150.6 3.2 %collective-permute-start.23 = (f32[160,128]{1,0:T(8,128)S(1)}, f32[160,128]{1,0:T(8,128)S(1)}, u32[]{:S(2)}, u32[]{:S(2)}) collective-permute-start(f32[160,128]{1,0:T(8,128)S(1)} %bitcast_add_fusion), channel_id=1, source_target_pairs={{0,1},{1,0},{2,3},{3,2},{4,5},{5,4},{6,7},{7,6},{8,9},{9,8},{10,11... | collective-permute-start | bytes 245768 | tf_op jit(solution)/shard_map/ppermute | solution.py:163
  153.8 2.4 collective-permute-start.25
  156.4 5.9 %collective-permute-done.24 = f32[160,128]{1,0:T(8,128)S(1)} collective-permute-done((f32[160,128]{1,0:T(8,128)S(1)}, f32[160,128]{1,0:T(8,128)S(1)}, u32[]{:S(2)}, u32[]{:S(2)}) %collective-permute-start.24) | collective-permute-done | bytes 81952 | tf_op jit(solution)/shard_map/ppermute | solution.py:163
  164.3 1.6 collective-permute-start.28
  165.9 1.5 collective-permute-start.30
  167.7 1.9 collective-permute-done.28
  169.9 1.7 collective-permute-start.33
  172.7 11.3 %collective-permute-done.30 = f32[352,512]{1,0:T(8,128)S(1)} collective-permute-done((f32[352,512]{1,0:T(8,128)S(1)}, f32[352,512]{1,0:T(8,128)S(1)}, u32[]{:S(2)}, u32[]{:S(2)}) %collective-permute-start.30) | collective-permute-done | bytes 720928 | tf_op jit(solution)/shard_map/ppermute | solution.py:163
  186.8 5.3 %shard_map.76 = (f32[512,512]{1,0:T(8,128)S(1)}, f32[512,512]{1,0:T(8,128)S(1)}, f32[512,512]{1,0:T(8,128)S(1)}) custom-call(f32[512,512]{1,0:T(8,128)S(1)} %fusion.21.work_in, f32[512,512]{1,0:T(8,128)S(1)} %broadcast_in_dim.11.rest_in.inverse_in, f32[512,512]{1,0:T(8,128)S(1)} %broadcast_in_dim.11.rest_in.inverse_in), custom_call_target="tpu_custom_call" | custom-call | flops 1000000 | bytes 100000 | tf_op jit(solution)/shard_map/pallas_call | solution.py:82
  192.1 4.9 %shard_map.77 = (f32[512,512]{1,0:T(8,128)S(1)}, f32[512,512]{1,0:T(8,128)S(1)}, f32[512,512]{1,0:T(8,128)S(1)}) custom-call(f32[512,512]{1,0:T(8,128)S(1)} %get-tuple-element.134.work_in, f32[512,512]{1,0:T(8,128)S(1)} %get-tuple-element.135.rest_in, f32[512,512]{1,0:T(8,128)S(1)} %get-tuple-element.136.inverse_in), custom_call_target="tpu_custom_call" | custom-call | flops 1000000 | bytes 100000 | tf_op jit(solution)/shard_map/pallas_call | solution.py:82
  197.2 2.2 collective-permute-done.31
  199.4 3.8 %collective-permute-start.34 = (f32[320,512]{1,0:T(8,128)S(1)}, f32[320,512]{1,0:T(8,128)S(1)}, u32[]{:S(2)}, u32[]{:S(2)}) collective-permute-start(f32[320,512]{1,0:T(8,128)S(1)} %collective-permute-done.33), channel_id=1, source_target_pairs={{0,1},{1,2},{2,3},{3,0},{4,5},{5,6},{6,7},{7,4},{8,9},{9,10},{10,1... | collective-permute-start | bytes 1966088 | tf_op jit(solution)/shard_map/ppermute | solution.py:172
  204.0 4.5 %shard_map.78 = (f32[512,512]{1,0:T(8,128)S(1)}, f32[512,512]{1,0:T(8,128)S(1)}, f32[512,512]{1,0:T(8,128)S(1)}) custom-call(f32[512,512]{1,0:T(8,128)S(1)} %get-tuple-element.140.work_in, f32[512,512]{1,0:T(8,128)S(1)} %get-tuple-element.141.rest_in, f32[512,512]{1,0:T(8,128)S(1)} %get-tuple-element.142.inverse_in), custom_call_target="tpu_custom_call" | custom-call | flops 1000000 | bytes 100000 | tf_op jit(solution)/shard_map/pallas_call | solution.py:82
  208.5 3.6 %shard_map.79 = (f32[512,512]{1,0:T(8,128)}, f32[512,512]{1,0:T(8,128)}, f32[512,512]{1,0:T(8,128)S(1)}) custom-call(f32[512,512]{1,0:T(8,128)S(1)} %get-tuple-element.143.work_in, f32[512,512]{1,0:T(8,128)S(1)} %get-tuple-element.144.rest_in, f32[512,512]{1,0:T(8,128)S(1)} %get-tuple-element.145.inverse_in), custom_call_target="tpu_custom_call" | custom-call | flops 1000000 | bytes 100000 | tf_op jit(solution)/shard_map/pallas_call | solution.py:82
  212.1 1.5 fusion.6
  213.6 1.5 fusion.15
  216.4 2.7 collective-permute-start.37
  224.8 4.2 %collective-permute-done.37 = f32[320,512]{1,0:T(8,128)S(1)} collective-permute-done((f32[320,512]{1,0:T(8,128)S(1)}, f32[320,512]{1,0:T(8,128)S(1)}, u32[]{:S(2)}, u32[]{:S(2)}) %collective-permute-start.37) | collective-permute-done | bytes 655392 | tf_op jit(solution)/shard_map/ppermute | solution.py:172
  230.6 1.5 fusion.4
  232.1 1.5 fusion.2
  237.0 1.6 fusion.10.basis_ref
  240.6 1.8 fusion.67
  243.1 2.1 collective-permute-done.39
  246.4 1.9 collective-permute-start.40
  248.4 2.2 copy-done.1
  250.6 10.3 %shard_map.80 = f32[512,1536]{1,0:T(8,128)S(1)} custom-call(s32[8]{0:T(128)S(1)} %stack.65.starts_ref, bf16[4096,512]{1,0:T(8,128)(2,1)S(1)} %copy-done.1, bf16[4096,3584]{1,0:T(8,128)(2,1)} %bitcast.109), custom_call_target="tpu_custom_call" | custom-call | flops 1000000 | bytes 100000 | tf_op jit(solution)/shard_map/pallas_call | solution.py:129
  262.7 1.4 collective-permute-start.43
  264.1 12.8 %shard_map.81 = f32[512,2048]{1,0:T(8,128)S(1)} custom-call(s32[8]{0:T(128)S(1)} %stack.65.starts_ref, bf16[4096,512]{1,0:T(8,128)(2,1)S(1)} %copy-done.1, bf16[4096,3584]{1,0:T(8,128)(2,1)} %bitcast.110), custom_call_target="tpu_custom_call" | custom-call | flops 1000000 | bytes 100000 | tf_op jit(solution)/shard_map/pallas_call | solution.py:129
  278.3 1.8 collective-permute-start.45
  282.1 7.0 %collective-permute-done.46 = f32[1,2,1,64,768]{4,3,2,1,0:T(8,128)S(1)} collective-permute-done((f32[1,2,1,64,768]{4,3,2,1,0:T(8,128)S(1)}, f32[1,2,1,64,768]{4,3,2,1,0:T(8,128)S(1)}, u32[]{:S(2)}, u32[]{:S(2)}) %collective-permute-start.46) | collective-permute-done | bytes 393248 | tf_op jit(solution)/shard_map/ppermute | solution.py:163
  289.7 1.8 collective-permute-start.51
  295.3 2.3 collective-permute-done.51
  297.6 11.6 %collective-permute-done.50 = f32[1,1,1,64,768]{4,3,2,1,0:T(8,128)S(1)} collective-permute-done((f32[1,1,1,64,768]{4,3,2,1,0:T(8,128)S(1)}, f32[1,1,1,64,768]{4,3,2,1,0:T(8,128)S(1)}, u32[]{:S(2)}, u32[]{:S(2)}) %collective-permute-start.50) | collective-permute-done | bytes 196640 | tf_op jit(solution)/shard_map/ppermute | solution.py:163
  311.3 4.6 %collective-permute-done.53 = f32[1,1,1,64,1024]{4,3,2,1,0:T(8,128)S(1)} collective-permute-done((f32[1,1,1,64,1024]{4,3,2,1,0:T(8,128)S(1)}, f32[1,1,1,64,1024]{4,3,2,1,0:T(8,128)S(1)}, u32[]{:S(2)}, u32[]{:S(2)}) %collective-permute-start.53) | collective-permute-done | bytes 262176 | tf_op jit(solution)/shard_map/ppermute | solution.py:163
  (211 shorter events, 61.6 us)
Async XLA Ops:
  2.4 23.9 %collective-permute-start = (f32[2,2,1,64,896]{4,3,2,1,0:T(8,128)S(1)}, f32[2,2,1,64,896]{4,3,2,1,0:T(8,128)}, u32[]{:S(2)}, u32[]{:S(2)}) collective-permute-start(f32[2,2,1,64,896]{4,3,2,1,0:T(8,128)S(1)} %constant_dynamic-slice_fusion.24), channel_id=1, source_target_pairs={{0,4},{4,0},{1,5},{5,1},{2,6},{6,2},{3,7},{7,3},{8,12},{12,8},{9,1... | collective-permute-start | bytes 2752520 | tf_op jit(solution)/shard_map/ppermute | solution.py:163
  30.0 35.0 %collective-permute-start.2 = (f32[704,512]{1,0:T(8,128)}, f32[704,512]{1,0:T(8,128)S(1)}, u32[]{:S(2)}, u32[]{:S(2)}) collective-permute-start(f32[704,512]{1,0:T(8,128)} %get-tuple-element.188), channel_id=1, source_target_pairs={{0,8},{8,0},{16,24},{24,16},{1,9},{9,1},{17,25},{25,17},{2,10},{10... | collective-permute-start | bytes 4325384 | tf_op jit(solution)/shard_map/ppermute | solution.py:163
  32.5 34.0 %collective-permute-start.3 = (f32[704,512]{1,0:T(8,128)}, f32[704,512]{1,0:T(8,128)}, u32[]{:S(2)}, u32[]{:S(2)}) collective-permute-start(f32[704,512]{1,0:T(8,128)} %get-tuple-element.187), channel_id=1, source_target_pairs={{0,16},{8,24},{16,0},{24,8},{1,17},{9,25},{17,1},{25,9},{2,18},{10... | collective-permute-start | bytes 4325384 | tf_op jit(solution)/shard_map/ppermute | solution.py:163
  36.0 18.7 %collective-permute-start.1 = (f32[320,512]{1,0:T(8,128)}, f32[320,512]{1,0:T(8,128)}, u32[]{:S(2)}, u32[]{:S(2)}) collective-permute-start(f32[320,512]{1,0:T(8,128)} %constant_dynamic-slice_fusion.23), channel_id=1, source_target_pairs={{0,1},{1,2},{2,3},{3,0},{4,5},{5,6},{6,7},{7,4},{8,9},{9,10},{10,1... | collective-permute-start | bytes 1966088 | tf_op jit(solution)/shard_map/ppermute | solution.py:172
  56.1 17.6 %collective-permute-start.4 = (f32[320,512]{1,0:T(8,128)S(1)}, f32[320,512]{1,0:T(8,128)S(1)}, u32[]{:S(2)}, u32[]{:S(2)}) collective-permute-start(f32[320,512]{1,0:T(8,128)S(1)} %dynamic-slice_add_fusion.8), channel_id=1, source_target_pairs={{0,1},{1,2},{2,3},{3,0},{4,5},{5,6},{6,7},{7,4},{8,9},{9,10},{10,1... | collective-permute-start | bytes 1966088 | tf_op jit(solution)/shard_map/ppermute | solution.py:172
  69.5 17.5 %collective-permute-start.6 = (f32[352,512]{1,0:T(8,128)S(1)}, f32[352,512]{1,0:T(8,128)S(1)}, u32[]{:S(2)}, u32[]{:S(2)}) collective-permute-start(f32[352,512]{1,0:T(8,128)S(1)} %constant_dynamic-slice_fusion.19), channel_id=1, source_target_pairs={{0,8},{8,0},{16,24},{24,16},{1,9},{9,1},{17,25},{25,17},{2,10},{10... | collective-permute-start | bytes 2162696 | tf_op jit(solution)/shard_map/ppermute | solution.py:163
  69.9 19.1 %collective-permute-start.5 = (f32[352,512]{1,0:T(8,128)S(1)}, f32[352,512]{1,0:T(8,128)S(1)}, u32[]{:S(2)}, u32[]{:S(2)}) collective-permute-start(f32[352,512]{1,0:T(8,128)S(1)} %constant_dynamic-slice_fusion.20), channel_id=1, source_target_pairs={{0,16},{8,24},{16,0},{24,8},{1,17},{9,25},{17,1},{25,9},{2,18},{10... | collective-permute-start | bytes 2162696 | tf_op jit(solution)/shard_map/ppermute | solution.py:163
  72.0 17.4 %copy-start.2 = (f32[8,32,896]{2,1,0:T(8,128)}, f32[8,32,896]{2,1,0:T(8,128)S(1)}, u32[]{:S(2)}) copy-start(f32[8,32,896]{2,1,0:T(8,128)S(1)} %get-tuple-element.199) | copy-start | bytes 2752516
  74.9 18.7 %collective-permute-start.7 = (f32[320,512]{1,0:T(8,128)S(1)}, f32[320,512]{1,0:T(8,128)S(1)}, u32[]{:S(2)}, u32[]{:S(2)}) collective-permute-start(f32[320,512]{1,0:T(8,128)S(1)} %dynamic-slice_add_fusion.7), channel_id=1, source_target_pairs={{0,1},{1,2},{2,3},{3,0},{4,5},{5,6},{6,7},{7,4},{8,9},{9,10},{10,1... | collective-permute-start | bytes 1966088 | tf_op jit(solution)/shard_map/ppermute | solution.py:172
  76.1 21.2 %collective-permute-start.11 = (f32[1,2,2,32,896]{4,3,2,1,0:T(8,128)}, f32[1,2,2,32,896]{4,3,2,1,0:T(8,128)}, u32[]{:S(2)}, u32[]{:S(2)}) collective-permute-start(f32[1,2,2,32,896]{4,3,2,1,0:T(8,128)} %constant_dynamic-slice_fusion.16), channel_id=1, source_target_pairs={{0,16},{8,24},{16,0},{24,8},{1,17},{9,25},{17,1},{25,9},{2,18},{10... | collective-permute-start | bytes 1376264 | tf_op jit(solution)/shard_map/ppermute | solution.py:163
  89.4 18.4 %collective-permute-start.8 = (f32[2,1,176,512]{3,2,1,0:T(8,128)S(1)}, f32[2,1,176,512]{3,2,1,0:T(8,128)}, u32[]{:S(2)}, u32[]{:S(2)}) collective-permute-start(f32[2,1,176,512]{3,2,1,0:T(8,128)S(1)} %fusion.27), channel_id=1, source_target_pairs={{0,1},{1,0},{2,3},{3,2},{4,5},{5,4},{6,7},{7,6},{8,9},{9,8},{10,11... | collective-permute-start | bytes 2162696 | tf_op jit(solution)/shard_map/ppermute | solution.py:163
  92.1 12.3 %collective-permute-start.10 = (f32[2,1,2,32,896]{4,3,2,1,0:T(8,128)}, f32[2,1,2,32,896]{4,3,2,1,0:T(8,128)}, u32[]{:S(2)}, u32[]{:S(2)}) collective-permute-start(f32[2,1,2,32,896]{4,3,2,1,0:T(8,128)} %constant_dynamic-slice_fusion.17), channel_id=1, source_target_pairs={{0,8},{8,0},{16,24},{24,16},{1,9},{9,1},{17,25},{25,17},{2,10},{10... | collective-permute-start | bytes 1376264 | tf_op jit(solution)/shard_map/ppermute | solution.py:163
  94.8 0.8 copy-start.4
  96.4 11.5 %collective-permute-start.9 = (f32[160,512]{1,0:T(8,128)}, f32[160,512]{1,0:T(8,128)S(1)}, u32[]{:S(2)}, u32[]{:S(2)}) collective-permute-start(f32[160,512]{1,0:T(8,128)} %constant_dynamic-slice_fusion.18), channel_id=1, source_target_pairs={{0,8},{8,0},{16,24},{24,16},{1,9},{9,1},{17,25},{25,17},{2,10},{10... | collective-permute-start | bytes 983048 | tf_op jit(solution)/shard_map/ppermute | solution.py:163
  107.9 3.4 %copy-start.6 = (f32[160,512]{1,0:T(8,128)}, f32[160,512]{1,0:T(8,128)S(1)}, u32[]{:S(2)}) copy-start(f32[160,512]{1,0:T(8,128)S(1)} %collective-permute-done.9) | copy-start | bytes 983044
  112.0 7.4 %copy-start.5 = (f32[320,512]{1,0:T(8,128)S(1)}, f32[320,512]{1,0:T(8,128)}, u32[]{:S(2)}) copy-start(f32[320,512]{1,0:T(8,128)} %copy-done.4) | copy-start | bytes 1966084
  112.0 7.4 %copy-start.7 = (f32[160,512]{1,0:T(8,128)S(1)}, f32[160,512]{1,0:T(8,128)}, u32[]{:S(2)}) copy-start(f32[160,512]{1,0:T(8,128)} %copy-done.6) | copy-start | bytes 983044
  112.0 18.4 %collective-permute-start.15 = (f32[2,1,2,32,896]{4,3,2,1,0:T(8,128)}, f32[2,1,2,32,896]{4,3,2,1,0:T(8,128)}, u32[]{:S(2)}, u32[]{:S(2)}) collective-permute-start(f32[2,1,2,32,896]{4,3,2,1,0:T(8,128)} %fusion.48), channel_id=1, source_target_pairs={{0,8},{8,0},{16,24},{24,16},{1,9},{9,1},{17,25},{25,17},{2,10},{10... | collective-permute-start | bytes 1376264 | tf_op jit(solution)/shard_map/ppermute | solution.py:163
  115.3 15.1 %collective-permute-start.14 = (f32[1,2,2,32,896]{4,3,2,1,0:T(8,128)}, f32[1,2,2,32,896]{4,3,2,1,0:T(8,128)}, u32[]{:S(2)}, u32[]{:S(2)}) collective-permute-start(f32[1,2,2,32,896]{4,3,2,1,0:T(8,128)} %fusion.50), channel_id=1, source_target_pairs={{0,16},{8,24},{16,0},{24,8},{1,17},{9,25},{17,1},{25,9},{2,18},{10... | collective-permute-start | bytes 1376264 | tf_op jit(solution)/shard_map/ppermute | solution.py:163
  116.8 13.6 %collective-permute-start.12 = (f32[1,1,176,512]{3,2,1,0:T(8,128)}, f32[1,1,176,512]{3,2,1,0:T(8,128)S(1)}, u32[]{:S(2)}, u32[]{:S(2)}) collective-permute-start(f32[1,1,176,512]{3,2,1,0:T(8,128)} %constant_dynamic-slice_fusion.15), channel_id=1, source_target_pairs={{0,2},{1,3},{2,0},{3,1},{4,6},{5,7},{6,4},{7,5},{8,10},{9,11},{10,... | collective-permute-start | bytes 1081352 | tf_op jit(solution)/shard_map/ppermute | solution.py:163
  119.5 8.9 %collective-permute-start.13 = (f32[80,512]{1,0:T(8,128)S(1)}, f32[80,512]{1,0:T(8,128)}, u32[]{:S(2)}, u32[]{:S(2)}) collective-permute-start(f32[80,512]{1,0:T(8,128)S(1)} %constant_dynamic-slice_fusion.14), channel_id=1, source_target_pairs={{0,16},{8,24},{16,0},{24,8},{1,17},{9,25},{17,1},{25,9},{2,18},{10... | collective-permute-start | bytes 491528 | tf_op jit(solution)/shard_map/ppermute | solution.py:163
  131.4 5.4 %collective-permute-start.17 = (f32[80,512]{1,0:T(8,128)S(1)}, f32[80,512]{1,0:T(8,128)S(1)}, u32[]{:S(2)}, u32[]{:S(2)}) collective-permute-start(f32[80,512]{1,0:T(8,128)S(1)} %dynamic-slice_add_fusion.15), channel_id=1, source_target_pairs={{0,16},{8,24},{16,0},{24,8},{1,17},{9,25},{17,1},{25,9},{2,18},{10... | collective-permute-start | bytes 491528 | tf_op jit(solution)/shard_map/ppermute | solution.py:163
  134.1 15.2 %collective-permute-start.22 = (f32[176,512]{1,0:T(8,128)S(1)}, f32[176,512]{1,0:T(8,128)S(1)}, u32[]{:S(2)}, u32[]{:S(2)}) collective-permute-start(f32[176,512]{1,0:T(8,128)S(1)} %add_bitcast_fusion), channel_id=1, source_target_pairs={{0,2},{1,3},{2,0},{3,1},{4,6},{5,7},{6,4},{7,5},{8,10},{9,11},{10,... | collective-permute-start | bytes 1081352 | tf_op jit(solution)/shard_map/ppermute | solution.py:163
  135.5 1.7 collective-permute-start.16
  136.7 34.9 %slice-start = ((s8[8388608]{0:T(1024)(128)(4,1)}), s8[4194304]{0:T(1024)(128)(4,1)S(1)}, s32[]{:S(2)}) async-start(s8[8388608]{0:T(1024)(128)(4,1)} %bitcast.111), calls=%async_computation | async-start | bytes 8388608
  137.2 13.3 %collective-permute-start.21 = (f32[160,512]{1,0:T(8,128)S(1)}, f32[160,512]{1,0:T(8,128)S(1)}, u32[]{:S(2)}, u32[]{:S(2)}) collective-permute-start(f32[160,512]{1,0:T(8,128)S(1)} %pad_maximum_fusion.15), channel_id=1, source_target_pairs={{0,8},{8,0},{16,24},{24,16},{1,9},{9,1},{17,25},{25,17},{2,10},{10... | collective-permute-start | bytes 983048 | tf_op jit(solution)/shard_map/ppermute | solution.py:163
  139.1 10.6 %collective-permute-start.18 = (f32[160,128]{1,0:T(8,128)S(1)}, f32[160,128]{1,0:T(8,128)S(1)}, u32[]{:S(2)}, u32[]{:S(2)}) collective-permute-start(f32[160,128]{1,0:T(8,128)S(1)} %get-tuple-element.251), channel_id=1, source_target_pairs={{0,8},{8,0},{16,24},{24,16},{1,9},{9,1},{17,25},{25,17},{2,10},{10... | collective-permute-start | bytes 245768 | tf_op jit(solution)/shard_map/ppermute | solution.py:163
  139.5 10.1 %collective-permute-start.19 = (f32[160,128]{1,0:T(8,128)S(1)}, f32[160,128]{1,0:T(8,128)S(1)}, u32[]{:S(2)}, u32[]{:S(2)}) collective-permute-start(f32[160,128]{1,0:T(8,128)S(1)} %get-tuple-element.250), channel_id=1, source_target_pairs={{0,16},{8,24},{16,0},{24,8},{1,17},{9,25},{17,1},{25,9},{2,18},{10... | collective-permute-start | bytes 245768 | tf_op jit(solution)/shard_map/ppermute | solution.py:163
  140.6 10.0 %collective-permute-start.20 = (f32[160,128]{1,0:T(8,128)S(1)}, f32[160,128]{1,0:T(8,128)S(1)}, u32[]{:S(2)}, u32[]{:S(2)}) collective-permute-start(f32[160,128]{1,0:T(8,128)S(1)} %get-tuple-element.249), channel_id=1, source_target_pairs={{0,24},{8,16},{16,8},{24,0},{1,25},{9,17},{17,9},{25,1},{2,26},{10... | collective-permute-start | bytes 245768 | tf_op jit(solution)/shard_map/ppermute | solution.py:163
  142.6 29.0 %slice-start.1 = ((s8[8388608]{0:T(1024)(128)(4,1)}), s8[4194304]{0:T(1024)(128)(4,1)S(1)}, s32[]{:S(2)}) async-start(s8[8388608]{0:T(1024)(128)(4,1)} %bitcast.111), calls=%async_computation.1 | async-start | bytes 8388608
  150.6 5.8 %collective-permute-start.23 = (f32[160,128]{1,0:T(8,128)S(1)}, f32[160,128]{1,0:T(8,128)S(1)}, u32[]{:S(2)}, u32[]{:S(2)}) collective-permute-start(f32[160,128]{1,0:T(8,128)S(1)} %bitcast_add_fusion), channel_id=1, source_target_pairs={{0,1},{1,0},{2,3},{3,2},{4,5},{5,4},{6,7},{7,6},{8,9},{9,8},{10,11... | collective-permute-start | bytes 245768 | tf_op jit(solution)/shard_map/ppermute | solution.py:163
  153.8 8.5 %collective-permute-start.24 = (f32[160,128]{1,0:T(8,128)S(1)}, f32[160,128]{1,0:T(8,128)S(1)}, u32[]{:S(2)}, u32[]{:S(2)}) collective-permute-start(f32[160,128]{1,0:T(8,128)S(1)} %bitcast_add_fusion), channel_id=1, source_target_pairs={{0,2},{1,3},{2,0},{3,1},{4,6},{5,7},{6,4},{7,5},{8,10},{9,11},{10,... | collective-permute-start | bytes 245768 | tf_op jit(solution)/shard_map/ppermute | solution.py:163
  153.8 8.5 %collective-permute-start.25 = (f32[160,128]{1,0:T(8,128)S(1)}, f32[160,128]{1,0:T(8,128)S(1)}, u32[]{:S(2)}, u32[]{:S(2)}) collective-permute-start(f32[160,128]{1,0:T(8,128)S(1)} %bitcast_add_fusion), channel_id=1, source_target_pairs={{0,3},{1,2},{2,1},{3,0},{4,7},{5,6},{6,5},{7,4},{8,11},{9,10},{10,... | collective-permute-start | bytes 245768 | tf_op jit(solution)/shard_map/ppermute | solution.py:163
  162.3 5.1 %collective-permute-start.26 = (f32[160,128]{1,0:T(8,128)S(1)}, f32[160,128]{1,0:T(8,128)S(1)}, u32[]{:S(2)}, u32[]{:S(2)}) collective-permute-start(f32[160,128]{1,0:T(8,128)S(1)} %select_add_fusion), channel_id=1, source_target_pairs={{0,8},{8,0},{16,24},{24,16},{1,9},{9,1},{17,25},{25,17},{2,10},{10... | collective-permute-start | bytes 245768 | tf_op jit(solution)/shard_map/ppermute | solution.py:163
  163.3 4.4 %collective-permute-start.27 = (f32[160,128]{1,0:T(8,128)S(1)}, f32[160,128]{1,0:T(8,128)S(1)}, u32[]{:S(2)}, u32[]{:S(2)}) collective-permute-start(f32[160,128]{1,0:T(8,128)S(1)} %select_add_fusion), channel_id=1, source_target_pairs={{0,16},{8,24},{16,0},{24,8},{1,17},{9,25},{17,1},{25,9},{2,18},{10... | collective-permute-start | bytes 245768 | tf_op jit(solution)/shard_map/ppermute | solution.py:163
  164.3 5.3 %collective-permute-start.28 = (f32[160,128]{1,0:T(8,128)S(1)}, f32[160,128]{1,0:T(8,128)S(1)}, u32[]{:S(2)}, u32[]{:S(2)}) collective-permute-start(f32[160,128]{1,0:T(8,128)S(1)} %select_add_fusion), channel_id=1, source_target_pairs={{0,24},{8,16},{16,8},{24,0},{1,25},{9,17},{17,9},{25,1},{2,26},{10... | collective-permute-start | bytes 245768 | tf_op jit(solution)/shard_map/ppermute | solution.py:163
  165.9 18.1 %collective-permute-start.30 = (f32[352,512]{1,0:T(8,128)S(1)}, f32[352,512]{1,0:T(8,128)S(1)}, u32[]{:S(2)}, u32[]{:S(2)}) collective-permute-start(f32[352,512]{1,0:T(8,128)S(1)} %pad_maximum_fusion.11), channel_id=1, source_target_pairs={{0,1},{1,0},{2,3},{3,2},{4,5},{5,4},{6,7},{7,6},{8,9},{9,8},{10,11... | collective-permute-start | bytes 2162696 | tf_op jit(solution)/shard_map/ppermute | solution.py:163
  169.7 3.0 collective-permute-start.29
  169.9 27.2 %collective-permute-start.33 = (f32[320,512]{1,0:T(8,128)S(1)}, f32[320,512]{1,0:T(8,128)S(1)}, u32[]{:S(2)}, u32[]{:S(2)}) collective-permute-start(f32[320,512]{1,0:T(8,128)S(1)} %pad_maximum_fusion.14), channel_id=1, source_target_pairs={{0,1},{1,2},{2,3},{3,0},{4,5},{5,6},{6,7},{7,4},{8,9},{9,10},{10,1... | collective-permute-start | bytes 1966088 | tf_op jit(solution)/shard_map/ppermute | solution.py:172
  184.3 12.9 %collective-permute-start.32 = (f32[352,512]{1,0:T(8,128)S(1)}, f32[352,512]{1,0:T(8,128)S(1)}, u32[]{:S(2)}, u32[]{:S(2)}) collective-permute-start(f32[352,512]{1,0:T(8,128)S(1)} %bitcast.140), channel_id=1, source_target_pairs={{0,8},{8,0},{16,24},{24,16},{1,9},{9,1},{17,25},{25,17},{2,10},{10... | collective-permute-start | bytes 2162696 | tf_op jit(solution)/shard_map/ppermute | solution.py:163
  185.4 14.0 %collective-permute-start.31 = (f32[352,512]{1,0:T(8,128)S(1)}, f32[352,512]{1,0:T(8,128)S(1)}, u32[]{:S(2)}, u32[]{:S(2)}) collective-permute-start(f32[352,512]{1,0:T(8,128)S(1)} %bitcast.141), channel_id=1, source_target_pairs={{0,16},{8,24},{16,0},{24,8},{1,17},{9,25},{17,1},{25,9},{2,18},{10... | collective-permute-start | bytes 2162696 | tf_op jit(solution)/shard_map/ppermute | solution.py:163
  199.4 15.7 %collective-permute-start.34 = (f32[320,512]{1,0:T(8,128)S(1)}, f32[320,512]{1,0:T(8,128)S(1)}, u32[]{:S(2)}, u32[]{:S(2)}) collective-permute-start(f32[320,512]{1,0:T(8,128)S(1)} %collective-permute-done.33), channel_id=1, source_target_pairs={{0,1},{1,2},{2,3},{3,0},{4,5},{5,6},{6,7},{7,4},{8,9},{9,10},{10,1... | collective-permute-start | bytes 1966088 | tf_op jit(solution)/shard_map/ppermute | solution.py:172
  203.7 25.9 %collective-permute-start.36 = (f32[704,512]{1,0:T(8,128)S(1)}, f32[704,512]{1,0:T(8,128)S(1)}, u32[]{:S(2)}, u32[]{:S(2)}) collective-permute-start(f32[704,512]{1,0:T(8,128)S(1)} %pad_maximum_fusion.5), channel_id=1, source_target_pairs={{0,16},{8,24},{16,0},{24,8},{1,17},{9,25},{17,1},{25,9},{2,18},{10... | collective-permute-start | bytes 4325384 | tf_op jit(solution)/shard_map/ppermute | solution.py:163
  203.9 26.7 %collective-permute-start.35 = (f32[704,512]{1,0:T(8,128)S(1)}, f32[704,512]{1,0:T(8,128)S(1)}, u32[]{:S(2)}, u32[]{:S(2)}) collective-permute-start(f32[704,512]{1,0:T(8,128)S(1)} %pad_maximum_fusion.4), channel_id=1, source_target_pairs={{0,8},{8,0},{16,24},{24,16},{1,9},{9,1},{17,25},{25,17},{2,10},{10... | collective-permute-start | bytes 4325384 | tf_op jit(solution)/shard_map/ppermute | solution.py:163
  216.4 12.6 %collective-permute-start.37 = (f32[320,512]{1,0:T(8,128)S(1)}, f32[320,512]{1,0:T(8,128)S(1)}, u32[]{:S(2)}, u32[]{:S(2)}) collective-permute-start(f32[320,512]{1,0:T(8,128)S(1)} %collective-permute-done.34), channel_id=1, source_target_pairs={{0,1},{1,2},{2,3},{3,0},{4,5},{5,6},{6,7},{7,4},{8,9},{9,10},{10,1... | collective-permute-start | bytes 1966088 | tf_op jit(solution)/shard_map/ppermute | solution.py:172
  234.7 3.9 %collective-permute-start.38 = (f32[512,512]{1,0:T(8,128)S(1)}, f32[512,512]{1,0:T(8,128)S(1)}, u32[]{:S(2)}, u32[]{:S(2)}) collective-permute-start(f32[512,512]{1,0:T(8,128)S(1)} %add_add_fusion), channel_id=1, source_target_pairs={{0,4},{4,0},{1,5},{5,1},{2,6},{6,2},{3,7},{7,3},{8,12},{12,8},{9,1... | collective-permute-start | bytes 3145736 | tf_op jit(solution)/shard_map/ppermute | solution.py:163
  238.5 2.0 copy-start
  242.5 2.7 collective-permute-start.39
  245.6 15.3 %collective-permute-start.41 = (f32[1,2,2,32,896]{4,3,2,1,0:T(8,128)S(1)}, f32[1,2,2,32,896]{4,3,2,1,0:T(8,128)}, u32[]{:S(2)}, u32[]{:S(2)}) collective-permute-start(f32[1,2,2,32,896]{4,3,2,1,0:T(8,128)S(1)} %constant_dynamic-slice_fusion.10), channel_id=1, source_target_pairs={{0,16},{8,24},{16,0},{24,8},{1,17},{9,25},{17,1},{25,9},{2,18},{10... | collective-permute-start | bytes 1376264 | tf_op jit(solution)/shard_map/ppermute | solution.py:163
  246.4 14.5 %collective-permute-start.40 = (f32[2,1,2,32,896]{4,3,2,1,0:T(8,128)S(1)}, f32[2,1,2,32,896]{4,3,2,1,0:T(8,128)S(1)}, u32[]{:S(2)}, u32[]{:S(2)}) collective-permute-start(f32[2,1,2,32,896]{4,3,2,1,0:T(8,128)S(1)} %constant_dynamic-slice_fusion.11), channel_id=1, source_target_pairs={{0,8},{8,0},{16,24},{24,16},{1,9},{9,1},{17,25},{25,17},{2,10},{10... | collective-permute-start | bytes 1376264 | tf_op jit(solution)/shard_map/ppermute | solution.py:163
  248.4 2.2 copy-start.1
  261.0 15.8 %collective-permute-start.42 = (f32[2,2,1,64,1536]{4,3,2,1,0:T(8,128)S(1)}, f32[2,2,1,64,1536]{4,3,2,1,0:T(8,128)S(1)}, u32[]{:S(2)}, u32[]{:S(2)}) collective-permute-start(f32[2,2,1,64,1536]{4,3,2,1,0:T(8,128)S(1)} %constant_dynamic-slice_fusion.9), channel_id=1, source_target_pairs={{0,4},{4,0},{1,5},{5,1},{2,6},{6,2},{3,7},{7,3},{8,12},{12,8},{9,1... | collective-permute-start | bytes 4718600 | tf_op jit(solution)/shard_map/ppermute | solution.py:163
  262.3 14.6 %collective-permute-start.44 = (f32[2,1,2,32,896]{4,3,2,1,0:T(8,128)S(1)}, f32[2,1,2,32,896]{4,3,2,1,0:T(8,128)S(1)}, u32[]{:S(2)}, u32[]{:S(2)}) collective-permute-start(f32[2,1,2,32,896]{4,3,2,1,0:T(8,128)S(1)} %fusion.44), channel_id=1, source_target_pairs={{0,8},{8,0},{16,24},{24,16},{1,9},{9,1},{17,25},{25,17},{2,10},{10... | collective-permute-start | bytes 1376264 | tf_op jit(solution)/shard_map/ppermute | solution.py:163
  262.7 14.2 %collective-permute-start.43 = (f32[1,2,2,32,896]{4,3,2,1,0:T(8,128)S(1)}, f32[1,2,2,32,896]{4,3,2,1,0:T(8,128)S(1)}, u32[]{:S(2)}, u32[]{:S(2)}) collective-permute-start(f32[1,2,2,32,896]{4,3,2,1,0:T(8,128)S(1)} %fusion.46), channel_id=1, source_target_pairs={{0,16},{8,24},{16,0},{24,8},{1,17},{9,25},{17,1},{25,9},{2,18},{10... | collective-permute-start | bytes 1376264 | tf_op jit(solution)/shard_map/ppermute | solution.py:163
  277.0 14.5 %collective-permute-start.47 = (f32[2,2,1,64,2048]{4,3,2,1,0:T(8,128)S(1)}, f32[2,2,1,64,2048]{4,3,2,1,0:T(8,128)S(1)}, u32[]{:S(2)}, u32[]{:S(2)}) collective-permute-start(f32[2,2,1,64,2048]{4,3,2,1,0:T(8,128)S(1)} %constant_dynamic-slice_fusion.6), channel_id=1, source_target_pairs={{0,4},{4,0},{1,5},{5,1},{2,6},{6,2},{3,7},{7,3},{8,12},{12,8},{9,1... | collective-permute-start | bytes 6291464 | tf_op jit(solution)/shard_map/ppermute | solution.py:163
  277.5 11.6 %collective-permute-start.46 = (f32[1,2,1,64,768]{4,3,2,1,0:T(8,128)S(1)}, f32[1,2,1,64,768]{4,3,2,1,0:T(8,128)S(1)}, u32[]{:S(2)}, u32[]{:S(2)}) collective-permute-start(f32[1,2,1,64,768]{4,3,2,1,0:T(8,128)S(1)} %constant_dynamic-slice_fusion.7), channel_id=1, source_target_pairs={{0,16},{8,24},{16,0},{24,8},{1,17},{9,25},{17,1},{25,9},{2,18},{10... | collective-permute-start | bytes 1179656 | tf_op jit(solution)/shard_map/ppermute | solution.py:163
  278.3 11.3 %collective-permute-start.45 = (f32[2,1,1,64,768]{4,3,2,1,0:T(8,128)S(1)}, f32[2,1,1,64,768]{4,3,2,1,0:T(8,128)S(1)}, u32[]{:S(2)}, u32[]{:S(2)}) collective-permute-start(f32[2,1,1,64,768]{4,3,2,1,0:T(8,128)S(1)} %constant_dynamic-slice_fusion.8), channel_id=1, source_target_pairs={{0,8},{8,0},{16,24},{24,16},{1,9},{9,1},{17,25},{25,17},{2,10},{10... | collective-permute-start | bytes 1179656 | tf_op jit(solution)/shard_map/ppermute | solution.py:163
  289.7 7.9 %collective-permute-start.51 = (f32[1,1,1,64,768]{4,3,2,1,0:T(8,128)S(1)}, f32[1,1,1,64,768]{4,3,2,1,0:T(8,128)S(1)}, u32[]{:S(2)}, u32[]{:S(2)}) collective-permute-start(f32[1,1,1,64,768]{4,3,2,1,0:T(8,128)S(1)} %constant_dynamic-slice_fusion.2), channel_id=1, source_target_pairs={{0,8},{8,0},{16,24},{24,16},{1,9},{9,1},{17,25},{25,17},{2,10},{10... | collective-permute-start | bytes 589832 | tf_op jit(solution)/shard_map/ppermute | solution.py:163
  292.1 17.2 %collective-permute-start.49 = (f32[1,2,1,64,1024]{4,3,2,1,0:T(8,128)S(1)}, f32[1,2,1,64,1024]{4,3,2,1,0:T(8,128)S(1)}, u32[]{:S(2)}, u32[]{:S(2)}) collective-permute-start(f32[1,2,1,64,1024]{4,3,2,1,0:T(8,128)S(1)} %constant_dynamic-slice_fusion.4), channel_id=1, source_target_pairs={{0,16},{8,24},{16,0},{24,8},{1,17},{9,25},{17,1},{25,9},{2,18},{10... | collective-permute-start | bytes 1572872 | tf_op jit(solution)/shard_map/ppermute | solution.py:163
  292.7 16.6 %collective-permute-start.48 = (f32[2,1,1,64,1024]{4,3,2,1,0:T(8,128)S(1)}, f32[2,1,1,64,1024]{4,3,2,1,0:T(8,128)S(1)}, u32[]{:S(2)}, u32[]{:S(2)}) collective-permute-start(f32[2,1,1,64,1024]{4,3,2,1,0:T(8,128)S(1)} %constant_dynamic-slice_fusion.5), channel_id=1, source_target_pairs={{0,8},{8,0},{16,24},{24,16},{1,9},{9,1},{17,25},{25,17},{2,10},{10... | collective-permute-start | bytes 1572872 | tf_op jit(solution)/shard_map/ppermute | solution.py:163
  293.9 15.4 %collective-permute-start.50 = (f32[1,1,1,64,768]{4,3,2,1,0:T(8,128)S(1)}, f32[1,1,1,64,768]{4,3,2,1,0:T(8,128)S(1)}, u32[]{:S(2)}, u32[]{:S(2)}) collective-permute-start(f32[1,1,1,64,768]{4,3,2,1,0:T(8,128)S(1)} %constant_dynamic-slice_fusion.3), channel_id=1, source_target_pairs={{0,16},{8,24},{16,0},{24,8},{1,17},{9,25},{17,1},{25,9},{2,18},{10... | collective-permute-start | bytes 589832 | tf_op jit(solution)/shard_map/ppermute | solution.py:163
  309.4 6.4 %collective-permute-start.53 = (f32[1,1,1,64,1024]{4,3,2,1,0:T(8,128)S(1)}, f32[1,1,1,64,1024]{4,3,2,1,0:T(8,128)S(1)}, u32[]{:S(2)}, u32[]{:S(2)}) collective-permute-start(f32[1,1,1,64,1024]{4,3,2,1,0:T(8,128)S(1)} %constant_dynamic-slice_fusion), channel_id=1, source_target_pairs={{0,8},{8,0},{16,24},{24,16},{1,9},{9,1},{17,25},{25,17},{2,10},{10... | collective-permute-start | bytes 786440 | tf_op jit(solution)/shard_map/ppermute | solution.py:163
  309.9 6.4 %collective-permute-start.52 = (f32[1,1,1,64,1024]{4,3,2,1,0:T(8,128)S(1)}, f32[1,1,1,64,1024]{4,3,2,1,0:T(8,128)S(1)}, u32[]{:S(2)}, u32[]{:S(2)}) collective-permute-start(f32[1,1,1,64,1024]{4,3,2,1,0:T(8,128)S(1)} %constant_dynamic-slice_fusion.1), channel_id=1, source_target_pairs={{0,16},{8,24},{16,0},{24,8},{1,17},{9,25},{17,1},{25,9},{2,18},{10... | collective-permute-start | bytes 786440 | tf_op jit(solution)/shard_map/ppermute | solution.py:163
  317.5 1.2 copy-start.3
